TPU v7x, 32 devices: a whole 2x2x4 slice. The times are simulated.
32 devices in a mesh: seq: 8 (over y, x, core), head: 4 (over z).
Axes of the slice: x: 2, y: 2, z: 4, core: 2. Of those that a mesh axis runs over, the one named last changes fastest.
Arguments:
- query_rows: bfloat16 [4096, 4096], P('seq', 'head'), may hold values from -6 to 6
- key_rows: bfloat16 [4096, 4096], P('seq', 'head'), may hold values from -6 to 6
- value_rows: bfloat16 [4096, 4096], P('seq', 'head'), may hold values from -6 to 6
- out_weight: bfloat16 [4096, 4096], P('seq', 'head'), may hold values from -0.09375 to 0.09375
- target_rows: bfloat16 [4096, 4096], P('seq', 'head'), may hold values from -6 to 6
Outputs:
- output: bfloat16 [4096, 4096], P('seq', 'head')
- grad_query: bfloat16 [4096, 4096], P('seq', 'head')
- grad_key: bfloat16 [4096, 4096], P('seq', 'head')
- grad_value: bfloat16 [4096, 4096], P('seq', 'head')
- grad_weight: float32 [4096, 4096], P('seq', 'head')
All inputs are finite; a program needn't handle non-finite values.
Results may differ from a plain program's by a relative error of at most 0.019.
Values may be sent and summed in bfloat16 or wider, within the bound.
No kernel may reach another device: no remote copies, remote signals or barrier semaphores. Data moves between devices by JAX's collectives and lax.ppermute only.
A program may use at most 64 MiB of HBM per device.

v0:
```python
import math

import jax
import jax.numpy as jnp
from jax import lax
from jax.sharding import PartitionSpec as P

DH = 128
BLK = 512


EXACT = lax.Precision.HIGHEST


def on_device(query_rows, key_rows, value_rows, out_weight, target_rows):
    rows_dev = query_rows.shape[0]
    feature_width = query_rows.shape[1]
    local_heads = feature_width // DH
    block_count = rows_dev // BLK
    seq_count = lax.axis_size("seq")
    total_rows = rows_dev * seq_count
    seq_index = lax.axis_index("seq")
    positions = (seq_index * rows_dev + jnp.arange(rows_dev, dtype=jnp.int32) + 1).astype(
        jnp.float32
    )
    query_scale = lax.rsqrt(jnp.float32(DH) * positions)
    scaled = (query_rows.astype(jnp.float32) * query_scale[:, None]).astype(jnp.bfloat16)
    shaped = (block_count, BLK, local_heads, DH)
    query_blocks = scaled.reshape(shaped)
    key_blocks = key_rows.reshape(shaped)
    value_blocks = value_rows.reshape(shaped)
    causal = jnp.tril(jnp.ones((BLK, BLK), dtype=bool))
    device_ids = jnp.arange(seq_count, dtype=jnp.int32)
    block_kv = jnp.einsum(
        "bshd,bshe->bhde", key_blocks, value_blocks, preferred_element_type=jnp.float32
    )
    local_total = jnp.sum(block_kv, axis=0)
    every_state = lax.all_gather(
        local_total[None].astype(jnp.bfloat16), "seq", axis=0, tiled=True
    ).astype(jnp.float32)
    lower = (device_ids < seq_index)[:, None, None, None]
    earlier = jnp.sum(jnp.where(lower, every_state, 0.0), axis=0)
    running_kv = jnp.cumsum(block_kv, axis=0)
    before = earlier[None] + jnp.concatenate([jnp.zeros_like(block_kv), running_kv[:-1]], axis=0)
    inter = jnp.einsum("bthd,bhde->bthe", query_blocks.astype(jnp.float32), before, precision=EXACT)
    scores = jnp.einsum(
        "bthd,bshd->bhts", query_blocks, key_blocks, preferred_element_type=jnp.float32
    )
    scores = jnp.where(causal, scores, 0.0).astype(jnp.bfloat16)
    intra = jnp.einsum("bhts,bshe->bthe", scores, value_blocks, preferred_element_type=jnp.float32)
    attended = (inter + intra).astype(jnp.bfloat16).reshape(rows_dev, feature_width)
    whole_weight = lax.all_gather(out_weight, "seq", axis=0, tiled=True)
    partial_out = lax.dot_general(
        attended, whole_weight, (((1,), (1,)), ((), ())), preferred_element_type=jnp.float32
    )
    summed = lax.psum_scatter(
        partial_out.astype(jnp.bfloat16), "head", scatter_dimension=1, tiled=True
    )
    residual = (summed.astype(jnp.float32) - target_rows.astype(jnp.float32)).astype(jnp.bfloat16)
    residual_full = lax.all_gather(residual, "head", axis=1, tiled=True)
    grad_attended = jnp.dot(residual_full, whole_weight, preferred_element_type=jnp.float32).astype(
        jnp.bfloat16
    )
    weight_factor = 1.0 / math.sqrt(total_rows)
    product = lax.dot_general(
        residual_full, attended, (((0,), (0,)), ((), ())), preferred_element_type=jnp.float32
    )
    grad_weight = lax.psum_scatter(
        (product * weight_factor).astype(jnp.bfloat16), "seq", scatter_dimension=0, tiled=True
    ).astype(jnp.float32)
    grad_blocks = grad_attended.reshape(shaped)
    block_qg = jnp.einsum(
        "bthd,bthe->bhde", query_blocks, grad_blocks, preferred_element_type=jnp.float32
    )
    local_grad = jnp.sum(block_qg, axis=0)
    every_grad = lax.all_gather(
        local_grad[None].astype(jnp.bfloat16), "seq", axis=0, tiled=True
    ).astype(jnp.float32)
    upper = (device_ids > seq_index)[:, None, None, None]
    later = jnp.sum(jnp.where(upper, every_grad, 0.0), axis=0)
    running_qg = jnp.cumsum(block_qg[::-1], axis=0)[::-1]
    after = later[None] + jnp.concatenate([running_qg[1:], jnp.zeros_like(block_qg)], axis=0)
    mixed = jnp.einsum(
        "bthe,bshe->bhts", grad_blocks, value_blocks, preferred_element_type=jnp.float32
    )
    mixed = jnp.where(causal, mixed, 0.0).astype(jnp.bfloat16)
    grad_scaled = jnp.einsum(
        "bthe,bhde->bthd", grad_blocks.astype(jnp.float32), before, precision=EXACT
    )
    grad_scaled = grad_scaled + jnp.einsum(
        "bhts,bshd->bthd", mixed, key_blocks, preferred_element_type=jnp.float32
    )
    grad_key = jnp.einsum(
        "bshe,bhde->bshd", value_blocks.astype(jnp.float32), after, precision=EXACT
    )
    grad_key = grad_key + jnp.einsum(
        "bhts,bthd->bshd", mixed, query_blocks, preferred_element_type=jnp.float32
    )
    grad_value = jnp.einsum(
        "bshd,bhde->bshe", key_blocks.astype(jnp.float32), after, precision=EXACT
    )
    grad_value = grad_value + jnp.einsum(
        "bhts,bthe->bshe", scores, grad_blocks, preferred_element_type=jnp.float32
    )
    grad_query = (grad_scaled.reshape(rows_dev, feature_width) * query_scale[:, None]).astype(
        jnp.bfloat16
    )
    return (
        summed,
        grad_query,
        grad_key.astype(jnp.bfloat16).reshape(rows_dev, feature_width),
        grad_value.astype(jnp.bfloat16).reshape(rows_dev, feature_width),
        grad_weight,
    )


def solution(mesh):
    placed = (
        P("seq", "head"),
        P("seq", "head"),
        P("seq", "head"),
        P("seq", "head"),
        P("seq", "head"),
    )
    return jax.shard_map(
        on_device,
        mesh=mesh,
        in_specs=placed,
        out_specs=(
            P("seq", "head"),
            P("seq", "head"),
            P("seq", "head"),
            P("seq", "head"),
            P("seq", "head"),
        ),
        check_vma=False,
    )
```

profile of v0, /device:TPU:0, one launch (start us, length us, event | category | flops | bytes accessed | tf_op | source)
XLA Modules:
  0.0 392.4 jit_solution(6562584442265369691)
XLA Ops:
  7.2 0.0 copy-start
  7.2 0.0 all-gather.11.cloned.1.call-start
  7.2 1.6 copy.58
  8.8 0.7 copy.31
  9.5 0.0 copy-done
  9.5 0.0 copy-start.5
  9.5 1.2 convolution_convert_fusion.3
  10.7 0.0 all-gather.11.cloned.1.call-update
  10.7 0.0 all-gather.7.cloned.1.call-start
  10.7 0.7 all-gather.7.cloned.1.call-update
  11.4 0.0 reduce-scatter.3.cloned.1.call-start
  11.5 0.0 copy-done.5
  11.5 1.5 multiply_convert_fusion.2
  13.0 0.5 copy.54
  13.6 0.1 iota_compare_fusion
  13.6 4.6 %select_convert_fusion.1 = bf16[8,512,512]{2,1,0:T(8,128)(2,1)} fusion(pred[512,512]{1,0:T(8,128)(4,1)S(1)} %iota_compare_fusion, bf16[512,8,128]{0,2,1:T(8,128)(2,1)S(1)} %bitcast.92, bf16[512,1024]{1,0:T(8,128)(2,1)} %param.6), kind=kOutput, calls=%fused_computation.2 | convolution fusion | flops 541065216 | bytes 6553600 | tf_op jit(solution)/shard_map/bthd,bshd->bhts/dot_general | solution.py:46
  18.2 23.2 %all-gather.11.cloned.1.call-done = bf16[64,128,128]{2,1,0:T(8,128)(2,1)} async-done(((bf16[8,128,128]{2,1,0:T(8,128)(2,1)}), bf16[64,128,128]{2,1,0:T(8,128)(2,1)}) %all-gather.11.cloned.1.call-update) | async-done | bytes 2097168 | tf_op jit(solution)/shard_map/all_gather | solution.py:38
  41.4 0.0 copy-start.1
  41.4 2.3 fusion.1
  43.7 0.0 copy-start.4
  43.7 0.8 copy-done.4
  44.5 1.1 fusion.15
  45.6 0.0 copy-done.1
  45.6 1.5 fusion.2
  47.1 0.0 copy-start.9
  47.1 50.6 %all-gather.7.cloned.1.call-done = bf16[4096,1024]{1,0:T(8,128)(2,1)} async-done(((bf16[512,1024]{1,0:T(8,128)(2,1)}), bf16[4096,1024]{1,0:T(8,128)(2,1)}) %all-gather.7.cloned.1.call-update) | async-done | bytes 8388624 | tf_op jit(solution)/shard_map/all_gather | solution.py:52
  97.8 0.0 copy-done.9
  97.8 9.6 %convolution_convert_fusion = bf16[512,4096]{1,0:T(8,128)(2,1)} fusion(bf16[512,1024]{0,1:T(8,128)(2,1)S(1)} %bitcast.107, bf16[4096,1024]{1,0:T(8,128)(2,1)} %all-gather.7.cloned.1.call-done), kind=kOutput, calls=%fused_computation.3 | convolution fusion | flops 4297064448 | bytes 13631488 | tf_op jit(solution)/shard_map/dot_general | solution.py:53
  107.4 0.0 reduce-scatter.3.cloned.1.call-update
  107.4 0.0 all-gather.9.cloned.1.call-start
  107.4 76.9 %reduce-scatter.3.cloned.1.call-done = bf16[512,1024]{1,0:T(8,128)(2,1)} async-done(((bf16[512,4096]{1,0:T(8,128)(2,1)}), bf16[512,1024]{1,0:T(8,128)(2,1)}) %reduce-scatter.3.cloned.1.call-update) | async-done | bytes 1048592 | tf_op jit(solution)/shard_map/reduce_scatter | solution.py:56
  184.3 0.0 copy-done.8
  184.3 2.6 subtract_convert_fusion
  186.9 0.0 all-gather.9.cloned.1.call-update
  186.9 0.2 all-gather.13.cloned.1.call-start
  187.2 81.2 %all-gather.9.cloned.1.call-done = bf16[512,4096]{1,0:T(8,128)(2,1)} async-done(((bf16[512,1024]{1,0:T(8,128)(2,1)}), bf16[512,4096]{1,0:T(8,128)(2,1)}) %all-gather.9.cloned.1.call-update) | async-done | bytes 4194320 | tf_op jit(solution)/shard_map/all_gather | solution.py:60
  268.4 10.1 %convolution_convert_fusion.1 = bf16[512,1024]{1,0:T(8,128)(2,1)} fusion(bf16[512,4096]{1,0:T(8,128)(2,1)} %all-gather.9.cloned.1.call-done, bf16[4096,1024]{1,0:T(8,128)(2,1)} %all-gather.7.cloned.1.call-done), kind=kOutput, calls=%fused_computation.16 | convolution fusion | flops 4295491584 | bytes 13631488 | tf_op jit(solution)/shard_map/dot_general | solution.py:61
  278.5 1.5 copy.55
  280.0 1.1 convolution_convert_fusion.2
  281.1 0.0 all-gather.13.cloned.1.call-update
  281.1 0.0 reduce-scatter.5.cloned.1.call-start
  281.2 10.3 %multiply_convert_fusion = bf16[4096,1024]{1,0:T(8,128)(2,1)} fusion(bf16[512,4096]{1,0:T(8,128)(2,1)} %all-gather.9.cloned.1.call-done, bf16[512,1024]{0,1:T(8,128)(2,1)} %bitcast.108), kind=kOutput, calls=%fused_computation | convolution fusion | flops 4303355904 | bytes 13631488 | tf_op jit(solution)/shard_map/dot_general | solution.py:65
  291.5 0.0 reduce-scatter.5.cloned.1.call-update
  291.5 2.0 fusion.16
  293.6 0.0 copy-start.6
  293.6 1.4 select_convert_fusion
  295.0 0.0 copy-done.6
  295.0 0.0 copy-start.2
  295.0 2.8 bitcast_add_fusion
  297.8 0.0 copy-done.2
  297.8 3.1 copy.42
  300.9 2.7 multiply_convert_fusion.1
  303.6 0.0 copy-start.3
  303.6 4.4 %fusion.18 = f32[8,128,512]{2,1,0:T(8,128)} fusion(bf16[512,8,128]{0,2,1:T(8,128)(2,1)S(1)} %bitcast.99, bf16[8,512,512]{2,1,0:T(8,128)(2,1)} %select_convert_fusion.1), kind=kOutput, calls=%fused_computation.38 | convolution fusion | flops 536870912 | bytes 7340032 | tf_op jit(solution)/shard_map/bhts,bthe->bshe/dot_general | solution.py:102
  308.1 0.0 copy-done.3
  308.1 2.0 fusion.17
  310.1 2.1 fusion
  312.2 0.0 copy-done.7
  312.2 3.6 add_convert_fusion
  315.9 2.5 copy.51
  318.3 3.1 add_convert_fusion.1
  321.4 1.3 copy.50
  322.7 60.0 %reduce-scatter.5.cloned.1.call-done = bf16[512,1024]{1,0:T(8,128)(2,1)} async-done(((bf16[4096,1024]{1,0:T(8,128)(2,1)}), bf16[512,1024]{1,0:T(8,128)(2,1)}) %reduce-scatter.5.cloned.1.call-update) | async-done | bytes 1048592 | tf_op jit(solution)/shard_map/reduce_scatter | solution.py:68
  382.8 2.8 convert_element_type.125
  (6 shorter events, 0.0 us)
Async XLA Ops:
  7.2 2.3 copy-start
  7.2 34.3 %all-gather.11.cloned.1.call-start = ((), (), s32[]{:S(2)}) async-start(), calls=%async_computation.6 | async-start | bytes 2359296 | tf_op jit(solution)/shard_map/all_gather | solution.py:38
  9.5 2.0 copy-start.5
  10.7 87.1 %all-gather.7.cloned.1.call-start = ((), (), s32[]{:S(2)}) async-start(), calls=%async_computation.2 | async-start | bytes 9437184 | tf_op jit(solution)/shard_map/all_gather | solution.py:52
  11.4 172.9 %reduce-scatter.3.cloned.1.call-start = ((), (), s32[]{:S(2)}) async-start(), calls=%async_computation.3 | async-start | bytes 5242880 | tf_op jit(solution)/shard_map/reduce_scatter | solution.py:56
  41.4 4.1 %copy-start.1 = (bf16[8,512,512]{2,1,0:T(8,128)(2,1)S(1)}, bf16[8,512,512]{2,1,0:T(8,128)(2,1)}, u32[]{:S(2)}) copy-start(bf16[8,512,512]{2,1,0:T(8,128)(2,1)} %select_convert_fusion.1) | copy-start | bytes 12582916
  43.7 0.8 copy-start.4
  47.1 50.6 %copy-start.9 = (bf16[8,128,512]{2,1,0:T(8,128)(2,1)}, bf16[8,128,512]{2,1,0:T(8,128)(2,1)S(1)}, u32[]{:S(2)}) copy-start(bf16[8,128,512]{2,1,0:T(8,128)(2,1)S(1)} %fusion.2) | copy-start | bytes 3145732
  107.4 77.0 %copy-start.8 = (bf16[512,1024]{1,0:T(8,128)(2,1)S(1)}, bf16[512,1024]{1,0:T(8,128)(2,1)}, u32[]{:S(2)}) copy-start(bf16[512,1024]{1,0:T(8,128)(2,1)} %param.9) | copy-start | bytes 3145732
  107.4 161.0 %all-gather.9.cloned.1.call-start = ((), (), s32[]{:S(2)}) async-start(), calls=%async_computation.4 | async-start | bytes 5242880 | tf_op jit(solution)/shard_map/all_gather | solution.py:60
  186.9 123.2 %all-gather.13.cloned.1.call-start = ((), (), s32[]{:S(2)}) async-start(), calls=%async_computation.7 | async-start | bytes 2359296 | tf_op jit(solution)/shard_map/all_gather | solution.py:76
  281.1 101.6 %reduce-scatter.5.cloned.1.call-start = ((), (), s32[]{:S(2)}) async-start(), calls=%async_computation.5 | async-start | bytes 9437184 | tf_op jit(solution)/shard_map/reduce_scatter | solution.py:68
  293.6 1.4 copy-start.6
  295.0 2.8 copy-start.2
  303.6 4.4 %copy-start.3 = (bf16[8,512,512]{2,1,0:T(8,128)(2,1)S(1)}, bf16[8,512,512]{2,1,0:T(8,128)(2,1)}, u32[]{:S(2)}) copy-start(bf16[8,512,512]{2,1,0:T(8,128)(2,1)} %copy-done.2) | copy-start | bytes 12582916
  308.1 4.2 %copy-start.7 = (bf16[512,1024]{1,0:T(8,128)(2,1)S(1)}, bf16[512,1024]{1,0:T(8,128)(2,1)}, u32[]{:S(2)}) copy-start(bf16[512,1024]{1,0:T(8,128)(2,1)} %param.6) | copy-start | bytes 3145732
Sparse Core Ops, SparseCore 0:
  10.8 30.5 all-gather.10
  43.3 54.3 all-gather.6
  107.5 76.7 reduce-scatter.2
  187.1 81.2 all-gather.8
  281.3 26.4 all-gather.12
  311.4 71.2 reduce-scatter.4
where the time goes:
time: 393 us; the launch traced here: 392 us
  waiting for transfers between devices  293 us (75%)
  matrix products  58.9 us (15%)
  between operations  14.3 us (4%)
  other arithmetic  14.1 us (4%)
  local copies, waits for them, and re-layouts  12 us (3%)
    all_gather x1, waiting for transfers between devices, on_device(): residual_full = lax.all_gather(residual, 'head', axis=1, tiled=True)  81.2 us
    reduce_scatter x1, waiting for transfers between devices, on_device(): lax.psum_scatter(partial_out.astype(jnp.bfloat16), 'head', scatter_dimens...  76.9 us
    reduce_scatter x1, waiting for transfers between devices, on_device(): lax.psum_scatter((product * weight_factor).astype(jnp.bfloat16), 'seq', s...  60 us
    all_gather x1, waiting for transfers between devices, on_device(): whole_weight = lax.all_gather(out_weight, 'seq', axis=0, tiled=True)  50.6 us
    all_gather x1, waiting for transfers between devices, on_device(): lax.all_gather(local_total[None].astype(jnp.bfloat16), 'seq', axis=0, til...  23.2 us
    dot_general x1, matrix products, on_device(): lax.dot_general(residual_full, attended, (((0,), (0,)), ((), ())), prefer...  10.3 us
    dot_general x1, matrix products, on_device(): jnp.dot(residual_full, whole_weight, preferred_element_type=jnp.float32)  10.1 us
    dot_general x1, matrix products, on_device(): lax.dot_general(attended, whole_weight, (((1,), (1,)), ((), ())), preferr...  9.62 us
  transfers between devices with their start and end apart: 6, of which 5 were waited for; matrix products, arithmetic and copies ran while one was open for 13% of the time, Pallas kernels for 0%

commit v1 on v0

v1 whole, which is shorter than its diff:
```python
import functools
import math

import jax
import jax.numpy as jnp
from jax import lax
from jax.experimental import pallas as pl
from jax.experimental.pallas import tpu as pltpu
from jax.sharding import PartitionSpec as P

DH = 128
CHUNKS = 2
F32 = jnp.float32
BF16 = jnp.bfloat16
VMEM_LIMIT = 16 * 1024 * 1024

NT = (((1,), (1,)), ((), ()))
TN = (((0,), (0,)), ((), ()))
NN = (((1,), (0,)), ((), ()))


def dot(a, b, dims):
    return lax.dot_general(a, b, dims, preferred_element_type=F32)


def split_dot(a, state, dims):
    high = state.astype(BF16)
    low = (state - high.astype(F32)).astype(BF16)
    return dot(a, high, dims) + dot(a, low, dims)


def causal_mask(rows):
    t = lax.broadcasted_iota(jnp.int32, (rows, rows), 0)
    s = lax.broadcasted_iota(jnp.int32, (rows, rows), 1)
    return s <= t


def outer_kernel(a_ref, b_ref, out_ref):
    out_ref[0] = dot(a_ref[...], b_ref[...], TN)


def forward_kernel(q_ref, k_ref, v_ref, scale_ref, scaled_ref, intra_ref):
    scaled = (q_ref[...].astype(F32) * scale_ref[...]).astype(BF16)
    scaled_ref[...] = scaled
    scores = dot(scaled, k_ref[...], NT)
    scores = jnp.where(causal_mask(scores.shape[0]), scores, 0.0).astype(BF16)
    intra_ref[...] = dot(scores, v_ref[...], NN)


def attended_kernel(scaled_ref, intra_ref, state_ref, out_ref):
    inter = split_dot(scaled_ref[...], state_ref[0], NN)
    out_ref[...] = (inter + intra_ref[...]).astype(BF16)


def backward_kernel(
    scaled_ref, k_ref, v_ref, g_ref, scale_ref, state_ref, dq_ref, dk_ref, dv_ref
):
    scaled, keys, values, grads = scaled_ref[...], k_ref[...], v_ref[...], g_ref[...]
    mask = causal_mask(scaled.shape[0])
    mixed = jnp.where(mask, dot(grads, values, NT), 0.0).astype(BF16)
    dq = split_dot(grads, state_ref[0], NT) + dot(mixed, keys, NN)
    dq_ref[...] = (dq * scale_ref[...]).astype(BF16)
    dk_ref[...] = dot(mixed, scaled, TN)
    scores = jnp.where(mask, dot(scaled, keys, NT), 0.0).astype(BF16)
    dv_ref[...] = dot(scores, grads, TN)


def finish_kernel(k_ref, v_ref, dk_part_ref, dv_part_ref, after_ref, dk_ref, dv_ref):
    after = after_ref[0]
    dk_ref[...] = (split_dot(v_ref[...], after, NT) + dk_part_ref[...]).astype(BF16)
    dv_ref[...] = (split_dot(k_ref[...], after, NN) + dv_part_ref[...]).astype(BF16)


def per_head(kernel, rows, heads, ins, outs, macs):
    specs = {
        "h": pl.BlockSpec((rows, DH), lambda h: (0, h)),
        "m": pl.BlockSpec((1, DH, DH), lambda h: (h, 0, 0)),
        "s": pl.BlockSpec((rows, 1), lambda h: (0, 0)),
    }
    shapes = {"h": (rows, heads * DH), "m": (heads, DH, DH)}
    return pl.pallas_call(
        kernel,
        grid=(heads,),
        in_specs=[specs[kind] for kind in ins],
        out_specs=[specs[kind] for kind, unused in outs],
        out_shape=[jax.ShapeDtypeStruct(shapes[kind], dtype) for kind, dtype in outs],
        compiler_params=pltpu.CompilerParams(vmem_limit_bytes=VMEM_LIMIT),
        cost_estimate=pl.CostEstimate(
            flops=2 * macs * heads,
            bytes_accessed=rows * heads * DH * 2 * (len(ins) + len(outs)),
            transcendentals=0,
        ),
    )


def core_swap(value):
    count = lax.axis_size("seq")
    return lax.ppermute(value, "seq", [(j, j ^ 1) for j in range(count)])


def chip_swap(value, delta):
    count = lax.axis_size("seq")
    return lax.ppermute(value, "seq", [(j, j ^ (2 * delta)) for j in range(count)])


def line_permutes(active):
    even = [pair for pair in active if min(pair) % 2 == 0]
    odd = [pair for pair in active if min(pair) % 2 == 1]
    return even, odd


def line_step(values, active):
    return [
        lax.ppermute(value, "head", pairs) if pairs else None
        for value, pairs in zip(values, line_permutes(active))
    ]


def line_sum(part_for):
    count = lax.axis_size("head")
    mine = lax.axis_index("head")
    got = [None, None]
    for step in range(1, count):
        active = [(j, j + 1) for j in range(count - 1) if j <= step - 1]
        active += [(j, j - 1) for j in range(1, count) if count - 1 - j <= step - 1]
        values = []
        for parity, pairs in enumerate(line_permutes(active)):
            if not pairs:
                values.append(None)
                continue
            target = jnp.where(mine % 2 == parity, mine + count - step, mine - count + step)
            value = part_for(jnp.clip(target, 0, count - 1))
            if got[1 - parity] is not None:
                value = (value.astype(F32) + got[1 - parity].astype(F32)).astype(BF16)
            values.append(value)
        got = line_step(values, active)
    total = part_for(mine).astype(F32)
    for value in got:
        if value is not None:
            total = total + value.astype(F32)
    return total


def line_gather(value):
    count = lax.axis_size("head")
    mine = lax.axis_index("head")
    zero = jnp.zeros_like(value)
    up, down = {}, {}
    got = [None, None]
    first = None
    for step in range(1, count):
        active = [(j, j + 1) for j in range(count - 1) if j >= step - 1]
        active += [(j, j - 1) for j in range(1, count) if j + step - 1 <= count - 1]
        values = [
            value if step == 1 else (zero if got[1 - parity] is None else got[1 - parity])
            for parity in (0, 1)
        ]
        got = line_step(values, active)
        if first is None:
            first = [item for item in got if item is not None]
        even, odd = [zero if item is None else item for item in got]
        up[step] = jnp.where(mine % 2 == 1, even, odd)
        down[step] = jnp.where(mine % 2 == 0, even, odd)
    pieces = [value]
    for back in range(1, count):
        pieces.append(jnp.where(mine >= back, up[back], down[count - back]))
    return pieces, first


def earlier_or_later(total, lower):
    position = lax.axis_index("seq")
    chips = lax.axis_size("seq") // 2
    chip, core = position // 2, position % 2
    half_heads = total.shape[0] // 2
    mine = total.astype(BF16)
    other = core_swap(mine)
    both = (mine.astype(F32) + other.astype(F32)).astype(BF16)
    half = lax.dynamic_slice_in_dim(both, core * half_heads, half_heads, 0)
    summed = jnp.zeros(half.shape, F32)
    for delta in range(1, chips):
        partner = chip ^ delta
        counts = (partner < chip) if lower else (partner > chip)
        summed = summed + jnp.where(counts, chip_swap(half, delta).astype(F32), 0.0)
    summed = summed.astype(BF16)
    swapped = core_swap(summed)
    first = jnp.where(core == 0, summed, swapped)
    second = jnp.where(core == 0, swapped, summed)
    whole = jnp.concatenate([first, second], axis=0).astype(F32)
    return whole + jnp.where(core == (1 if lower else 0), other.astype(F32), 0.0)


def on_device(query_rows, key_rows, value_rows, out_weight, target_rows):
    rows, width = query_rows.shape
    heads = width // DH
    groups = lax.axis_size("head")
    seq_count = lax.axis_size("seq")
    chips = seq_count // 2
    share = chips // groups
    position = lax.axis_index("seq")
    chip, core = position // 2, position % 2
    mine = lax.axis_index("head")
    held = out_weight.shape[0]
    part = held // CHUNKS
    call = functools.partial(per_head, rows=rows, heads=heads)

    weight_parts = []
    for c in range(CHUNKS):
        own = out_weight[c * part : (c + 1) * part]
        if c:
            own, unused = lax.optimization_barrier((own, weight_parts[-1]))
        pieces = [own] + [chip_swap(own, delta) for delta in range(1, chips)]
        weight_parts.append(jnp.concatenate(pieces, axis=0))

    positions = (position * rows + jnp.arange(rows, dtype=jnp.int32) + 1).astype(F32)
    scale = lax.rsqrt(F32(DH) * positions)[:, None]
    (key_value,) = call(outer_kernel, ins="hh", outs=[("m", F32)], macs=rows * DH * DH)(
        key_rows, value_rows
    )
    before = earlier_or_later(key_value, True)
    scaled, intra = call(
        forward_kernel, ins="hhhs", outs=[("h", BF16), ("h", F32)], macs=2 * rows * rows * DH
    )(query_rows, key_rows, value_rows, scale)
    (attended,) = call(attended_kernel, ins="hhm", outs=[("h", BF16)], macs=2 * rows * DH * DH)(
        scaled, intra, before
    )
    both_attended = jnp.concatenate([attended, core_swap(attended)], axis=0)

    targets = target_rows.reshape(rows, share, 2, held)
    own_target = lax.dynamic_index_in_dim(targets, core, 2, keepdims=False)
    sent_target = lax.dynamic_index_in_dim(targets, 1 - core, 2, keepdims=False)
    both_targets = jnp.concatenate([own_target, core_swap(sent_target)], axis=0)

    def columns_for(array, group):
        pieces = [
            lax.dynamic_slice_in_dim(array, ((group * share + j) ^ chip) * part, part, 1)
            for j in range(share)
        ]
        return pieces[0] if share == 1 else jnp.concatenate(pieces, axis=1)

    outputs = []
    residuals = []
    gate = None
    for c in range(CHUNKS):
        partial_out = dot(both_attended, weight_parts[c], NT).astype(BF16)
        if gate is not None:
            partial_out, *gate = lax.optimization_barrier((partial_out, *gate))
        summed = line_sum(functools.partial(columns_for, partial_out)).astype(BF16)
        target = both_targets[:, :, c * part : (c + 1) * part].reshape(2 * rows, share * part)
        residual = (summed.astype(F32) - target.astype(F32)).astype(BF16)
        pieces, gate = line_gather(residual)
        stacked = jnp.stack(pieces)
        ordered = []
        for delta in range(chips):
            piece_chip = chip ^ delta
            back = lax.rem(mine - piece_chip // share + groups, groups)
            piece = lax.dynamic_index_in_dim(stacked, back, 0, keepdims=False)
            ordered.append(
                lax.dynamic_slice_in_dim(piece, (piece_chip % share) * part, part, 1)
                if share > 1
                else piece
            )
        residuals.append(jnp.concatenate(ordered, axis=1))
        own_output = summed[:rows].reshape(rows, share, part)
        other_output = core_swap(summed[rows:]).reshape(rows, share, part)
        first = jnp.where(core == 0, own_output, other_output)
        second = jnp.where(core == 0, other_output, own_output)
        outputs.append(jnp.stack([first, second], axis=2))
    output = jnp.concatenate(outputs, axis=3).reshape(rows, width)

    weight_factor = 1.0 / math.sqrt(rows * seq_count)
    grad_both = jnp.zeros((2 * rows, width), F32)
    grad_weights = []
    for c in range(CHUNKS):
        grad_both = grad_both + dot(residuals[c], weight_parts[c], NN)
        product = (dot(residuals[c], both_attended, TN) * weight_factor).astype(BF16)
        total = product[:part].astype(F32)
        for delta in range(1, chips):
            piece = product[delta * part : (delta + 1) * part]
            total = total + chip_swap(piece, delta).astype(F32)
        grad_weights.append(total)
    grad_weight = jnp.concatenate(grad_weights, axis=0)
    swapped_grad = core_swap(grad_both[rows:].astype(BF16))
    grad_attended = (grad_both[:rows] + swapped_grad.astype(F32)).astype(BF16)

    (query_grad,) = call(outer_kernel, ins="hh", outs=[("m", F32)], macs=rows * DH * DH)(
        scaled, grad_attended
    )
    after = earlier_or_later(query_grad, False)
    grad_query, key_part, value_part = call(
        backward_kernel,
        ins="hhhhsm",
        outs=[("h", BF16), ("h", F32), ("h", F32)],
        macs=5 * rows * rows * DH,
    )(scaled, key_rows, value_rows, grad_attended, scale, before)
    grad_key, grad_value = call(
        finish_kernel, ins="hhhhm", outs=[("h", BF16), ("h", BF16)], macs=4 * rows * DH * DH
    )(key_rows, value_rows, key_part, value_part, after)
    return output, grad_query, grad_key, grad_value, grad_weight


def solution(mesh):
    placed = P("seq", "head")
    return jax.shard_map(
        on_device,
        mesh=mesh,
        in_specs=(placed,) * 5,
        out_specs=(placed,) * 5,
        check_vma=False,
    )
```

time: 393 us -> 298 us (0.76)
  waiting for transfers between devices: 293 us -> 108 us
  starting transfers between devices: 0.42 us -> 75.6 us
  matrix products: 58.9 us -> 23.8 us
  Pallas kernels: 0 us -> 31.1 us
  other arithmetic: 14.1 us -> 31.2 us
  local copies, waits for them, and re-layouts: 12 us -> 26.3 us
  between operations: 14.3 us -> 1.41 us
    all_gather x4 -> x0, waiting for transfers between devices: 155 us -> none  [the longest x1 81.2 us: on_device(): residual_full = lax.all_gather(residual, 'head', axis=1, tiled=True)]
    reduce_scatter x2 -> x0, waiting for transfers between devices: 137 us -> none  [the longest x1 76.9 us: on_device(): lax.psum_scatter(partial_out.astype(jnp.bfloat16), 'head', scatter_dimens...]
    ppermute x0 -> x47, waiting for transfers between devices: none -> 108 us  [the longest x18 56.9 us: chip_swap(): lax.ppermute(value, 'seq', [(j, j ^ 2 * delta) for j in range(count)])]
    ppermute x0 -> x47, starting transfers between devices: none -> 75.6 us  [the longest x20 51.4 us: line_step(): lax.ppermute(value, 'head', pairs)]
    dot_general x15 -> x6, matrix products: 58.9 us -> 23.8 us  [dot(): return lax.dot_general(a, b, dims, preferred_element_type=F32)]
    pallas_call x0 -> x6, Pallas kernels: none -> 31.1 us  [the longest x1 11.2 us: on_device(): call(backward_kernel, ins='hhhhsm', outs=[('h', BF16), ('h', F32), ('h',...]
    another operation x0 -> x8, other arithmetic: none -> 7.68 us  [the longest x6 6.56 us: on_device(): stacked = jnp.stack(pieces)]
    slice x0 -> x6, local copies, waits for them, and re-layouts: none -> 6.79 us  [the longest x2 2.35 us: on_device(): piece = product[delta * part:(delta + 1) * part]]
  transfers between devices with their start and end apart: 6 -> 47, of which waited for: 5 -> 20; matrix products, arithmetic and copies ran while one was open for 13% -> 22% of each run, Pallas kernels for 0% -> 7%
where the time goes in v1:
time: 298 us; the launch traced here: 297 us
  waiting for transfers between devices  108 us (36%)
  starting transfers between devices  75.6 us (25%)
  other arithmetic  31.2 us (10%)
  Pallas kernels  31.1 us (10%)
  local copies, waits for them, and re-layouts  26.3 us (9%)
  matrix products  23.8 us (8%)
    ppermute x18, waiting for transfers between devices, chip_swap(): lax.ppermute(value, 'seq', [(j, j ^ 2 * delta) for j in range(count)])  56.9 us
    ppermute x20, starting transfers between devices, line_step(): lax.ppermute(value, 'head', pairs)  51.4 us
    ppermute x20, waiting for transfers between devices, line_step(): lax.ppermute(value, 'head', pairs)  49.5 us
    dot_general x6, matrix products, dot(): return lax.dot_general(a, b, dims, preferred_element_type=F32)  23.8 us
    ppermute x18, starting transfers between devices, chip_swap(): lax.ppermute(value, 'seq', [(j, j ^ 2 * delta) for j in range(count)])  22.8 us
    unnamed x70, local copies, waits for them, and re-layouts  12.7 us
    pallas_call x1, Pallas kernels, on_device(): call(backward_kernel, ins='hhhhsm', outs=[('h', BF16), ('h', F32), ('h',...  11.2 us
    convert_element_type x4, other arithmetic, line_sum(): value = (value.astype(F32) + got[1 - parity].astype(F32)).astype(BF16)  7.67 us
  transfers between devices with their start and end apart: 47, of which 20 were waited for; matrix products, arithmetic and copies ran while one was open for 22% of the time, Pallas kernels for 7%

profile of v1, /device:TPU:0, one launch (start us, length us, event | category | flops | bytes accessed | tf_op | source)
XLA Modules:
  0.0 297.0 jit_solution(603251606175061904)
XLA Ops:
  3.1 2.5 shard_map.93
  7.4 2.9 collective-permute-start.1
  10.3 1.5 collective-permute-start.2
  11.9 2.4 collective-permute-done.1
  14.2 4.2 %collective-permute-done.2 = bf16[4,128,128]{2,1,0:T(8,128)(2,1)S(1)} collective-permute-done((bf16[4,128,128]{2,1,0:T(8,128)(2,1)S(1)}, bf16[4,128,128]{2,1,0:T(8,128)(2,1)S(1)}, u32[]{:S(2)}, u32[]{:S(2)}) %collective-permute-start.2) | collective-permute-done | bytes 131104 | tf_op jit(solution)/shard_map/ppermute | solution.py:103
  19.9 5.8 %shard_map.92 = (bf16[512,1024]{1,0:T(8,128)(2,1)S(1)}, f32[512,1024]{1,0:T(8,128)S(1)}) custom-call(bf16[512,1024]{1,0:T(8,128)(2,1)S(1)} %copy-done.6, bf16[512,1024]{1,0:T(8,128)(2,1)S(1)} %copy-done.1, bf16[512,1024]{1,0:T(8,128)(2,1)S(1)} %copy-done.3, f32[512,1]{1,0:T(8,128)S(1)} %multiply_rsqrt_fusion.scale_ref), custom_call_target="tpu_custom_call" | custom-call | flops 1073741824 | bytes 6291456 | tf_op jit(solution)/shard_map/pallas_call | solution.py:220
  26.8 4.1 %shard_map.94 = bf16[512,1024]{1,0:T(8,128)(2,1)} custom-call(bf16[512,1024]{1,0:T(8,128)(2,1)S(1)} %get-tuple-element.14.scaled_ref.a_ref, f32[512,1024]{1,0:T(8,128)S(1)} %get-tuple-element.15.intra_ref, f32[8,128,128]{2,1,0:T(8,128)S(1)} %select_add_fusion.1.state_ref), custom_call_target="tpu_custom_call" | custom-call | flops 268435456 | bytes 4194304 | tf_op jit(solution)/shard_map/pallas_call | solution.py:223
  34.5 1.4 collective-permute-start.8
  35.9 11.6 %collective-permute-done.6 = bf16[256,1024]{1,0:T(8,128)(2,1)} collective-permute-done((bf16[256,1024]{1,0:T(8,128)(2,1)}, bf16[256,1024]{1,0:T(8,128)(2,1)}, u32[]{:S(2)}, u32[]{:S(2)}) %collective-permute-start.6) | collective-permute-done | bytes 524320 | tf_op jit(solution)/shard_map/ppermute | solution.py:103
  47.6 9.6 %collective-permute-done.7 = bf16[256,1024]{1,0:T(8,128)(2,1)} collective-permute-done((bf16[256,1024]{1,0:T(8,128)(2,1)}, bf16[256,1024]{1,0:T(8,128)(2,1)}, u32[]{:S(2)}, u32[]{:S(2)}) %collective-permute-start.7) | collective-permute-done | bytes 524320 | tf_op jit(solution)/shard_map/ppermute | solution.py:103
  57.2 1.6 collective-permute-done.8
  58.8 4.5 %convolution_convert_fusion.1 = bf16[1024,1024]{0,1:T(8,128)(2,1)S(1)} fusion(bf16[512,1024]{1,0:T(8,128)(2,1)} %collective-permute-done.5, bf16[512,1024]{1,0:T(8,128)(2,1)} %shard_map.94, bf16[256,1024]{1,0:T(8,128)(2,1)} %collective-permute-done.8, bf16[256,1024]{1,0:T(8,128)(2,1)} %collective-permute-done.7, ...), kind=kOutput, calls=%fused_computation.14 | convolution fusion | flops 2161115136 | bytes 6291456 | tf_op jit(solution)/shard_map/dot_general | solution.py:23
  65.7 4.3 %collective-permute-start.9 = (bf16[1024,256]{0,1:T(8,128)(2,1)}, bf16[1024,256]{0,1:T(8,128)(2,1)}, u32[]{:S(2)}, u32[]{:S(2)}) collective-permute-start(bf16[1024,256]{0,1:T(8,128)(2,1)} %get-tuple-element.57), channel_id=1, source_target_pairs={{0,1},{3,2},{4,5},{7,6},{8,9},{11,10},{12,13},{15,14},{16,17},{19,... | collective-permute-start | bytes 1572872 | tf_op jit(solution)/shard_map/ppermute | solution.py:114
  70.0 2.1 collective-permute-start.12
  72.0 9.8 %collective-permute-done.9 = bf16[1024,256]{0,1:T(8,128)(2,1)} collective-permute-done((bf16[1024,256]{0,1:T(8,128)(2,1)}, bf16[1024,256]{0,1:T(8,128)(2,1)}, u32[]{:S(2)}, u32[]{:S(2)}) %collective-permute-start.9) | collective-permute-done | bytes 524320 | tf_op jit(solution)/shard_map/ppermute | solution.py:114
  81.8 2.2 add_convert_fusion.7
  84.0 1.5 collective-permute-start.10
  86.3 1.5 collective-permute-start.16
  87.8 2.3 copy.20
  90.1 2.2 dynamic-slice_bitcast_fusion.9
  92.3 2.9 add_convert_fusion.6
  95.2 6.6 %collective-permute-start.11 = (bf16[1024,256]{0,1:T(8,128)(2,1)}, bf16[1024,256]{0,1:T(8,128)(2,1)}, u32[]{:S(2)}, u32[]{:S(2)}) collective-permute-start(bf16[1024,256]{0,1:T(8,128)(2,1)} %get-tuple-element.55), channel_id=1, source_target_pairs={{0,1},{2,3},{1,0},{3,2},{4,5},{6,7},{5,4},{7,6},{8,9},{10,11},{9,8... | collective-permute-start | bytes 1572872 | tf_op jit(solution)/shard_map/ppermute | solution.py:114
  101.8 1.4 collective-permute-start.13
  107.4 5.3 %collective-permute-done.11 = bf16[1024,256]{0,1:T(8,128)(2,1)} collective-permute-done((bf16[1024,256]{0,1:T(8,128)(2,1)}, bf16[1024,256]{0,1:T(8,128)(2,1)}, u32[]{:S(2)}, u32[]{:S(2)}) %collective-permute-start.11) | collective-permute-done | bytes 524320 | tf_op jit(solution)/shard_map/ppermute | solution.py:114
  112.7 2.6 fusion.2
  115.3 3.6 %collective-permute-start.19 = (bf16[1024,256]{0,1:T(8,128)(2,1)S(1)}, bf16[1024,256]{0,1:T(8,128)(2,1)}, u32[]{:S(2)}, u32[]{:S(2)}) collective-permute-start(bf16[1024,256]{0,1:T(8,128)(2,1)S(1)} %get-tuple-element.35), channel_id=1, source_target_pairs={{0,1},{2,3},{1,0},{3,2},{4,5},{6,7},{5,4},{7,6},{8,9},{10,11},{9,8... | collective-permute-start | bytes 1572872 | tf_op jit(solution)/shard_map/ppermute | solution.py:114
  118.9 1.4 collective-permute-start.20
  120.4 4.7 %convolution_convert_fusion = bf16[1024,1024]{0,1:T(8,128)(2,1)S(1)} fusion(bf16[1024,1024]{1,0:T(8,128)(2,1)S(1)} %constant_dynamic-update-slice_fusion, bf16[512,1024]{1,0:T(8,128)(2,1)} %collective-permute-done.5, bf16[512,1024]{1,0:T(8,128)(2,1)} %shard_map.94), kind=kOutput, calls=%fused_computation.13 | convolution fusion | flops 2152726528 | bytes 6291456 | tf_op jit(solution)/shard_map/dot_general | solution.py:23
  125.2 3.5 %collective-permute-done.19 = bf16[1024,256]{0,1:T(8,128)(2,1)} collective-permute-done((bf16[1024,256]{0,1:T(8,128)(2,1)S(1)}, bf16[1024,256]{0,1:T(8,128)(2,1)}, u32[]{:S(2)}, u32[]{:S(2)}) %collective-permute-start.19) | collective-permute-done | bytes 524320 | tf_op jit(solution)/shard_map/ppermute | solution.py:114
  129.5 5.5 %collective-permute-start.21 = (bf16[1024,256]{0,1:T(8,128)(2,1)S(1)}, bf16[1024,256]{0,1:T(8,128)(2,1)S(1)}, u32[]{:S(2)}, u32[]{:S(2)}) collective-permute-start(bf16[1024,256]{0,1:T(8,128)(2,1)S(1)} %get-tuple-element.53), channel_id=1, source_target_pairs={{0,1},{3,2},{4,5},{7,6},{8,9},{11,10},{12,13},{15,14},{16,17},{19,... | collective-permute-start | bytes 1572872 | tf_op jit(solution)/shard_map/ppermute | solution.py:114
  135.1 1.5 collective-permute-start.27
  137.9 6.1 %collective-permute-start.24 = (bf16[1024,256]{0,1:T(8,128)(2,1)}, bf16[1024,256]{0,1:T(8,128)(2,1)}, u32[]{:S(2)}, u32[]{:S(2)}) collective-permute-start(bf16[1024,256]{0,1:T(8,128)(2,1)} %get-tuple-element.54), channel_id=1, source_target_pairs={{0,1},{3,2},{4,5},{7,6},{8,9},{11,10},{12,13},{15,14},{16,17},{19,... | collective-permute-start | bytes 1572872 | tf_op jit(solution)/shard_map/ppermute | solution.py:114
  144.0 2.4 collective-permute-done.21
  147.4 1.5 collective-permute-start.22
  152.7 1.7 collective-permute-done.24
  154.4 1.6 add_convert_fusion.2
  156.0 7.0 %collective-permute-start.23 = (bf16[1024,256]{0,1:T(8,128)(2,1)S(1)}, bf16[1024,256]{0,1:T(8,128)(2,1)S(1)}, u32[]{:S(2)}, u32[]{:S(2)}) collective-permute-start(bf16[1024,256]{0,1:T(8,128)(2,1)S(1)} %get-tuple-element.51), channel_id=1, source_target_pairs={{0,1},{2,3},{1,0},{3,2},{4,5},{6,7},{5,4},{7,6},{8,9},{10,11},{9,8... | collective-permute-start | bytes 1572872 | tf_op jit(solution)/shard_map/ppermute | solution.py:114
  163.8 3.7 %collective-permute-done.28 = bf16[1024,256]{0,1:T(8,128)(2,1)S(1)} collective-permute-done((bf16[1024,256]{0,1:T(8,128)(2,1)}, bf16[1024,256]{0,1:T(8,128)(2,1)S(1)}, u32[]{:S(2)}, u32[]{:S(2)}) %collective-permute-start.28) | collective-permute-done | bytes 524320 | tf_op jit(solution)/shard_map/ppermute | solution.py:114
  169.3 9.2 %collective-permute-done.23 = bf16[1024,256]{0,1:T(8,128)(2,1)S(1)} collective-permute-done((bf16[1024,256]{0,1:T(8,128)(2,1)S(1)}, bf16[1024,256]{0,1:T(8,128)(2,1)S(1)}, u32[]{:S(2)}, u32[]{:S(2)}) %collective-permute-start.23) | collective-permute-done | bytes 524320 | tf_op jit(solution)/shard_map/ppermute | solution.py:114
  178.5 2.3 fusion.1
  180.8 3.9 %multiply_convert_fusion.1 = bf16[1024,1024]{1,0:T(8,128)(2,1)S(1)} fusion(bf16[1024,256]{0,1:T(8,128)(2,1)S(1)} %get-tuple-element.44, bf16[1024,256]{0,1:T(8,128)(2,1)S(1)} %get-tuple-element.45, bf16[1024,256]{0,1:T(8,128)(2,1)S(1)} %get-tuple-element.46, bf16[1024,256]{0,1:T(8,128)(2,1)S(1)} %get-tuple-element.43, ...), kind=kOutput, calls=%fused_computation.1 | convolution fusion | flops 2162163712 | bytes 6291456 | tf_op jit(solution)/shard_map/dot_general | solution.py:23
  184.8 1.5 collective-permute-start.31
  188.2 1.8 collective-permute-start.42
  190.0 4.8 %collective-permute-done.30 = bf16[1024,256]{0,1:T(8,128)(2,1)} collective-permute-done((bf16[1024,256]{0,1:T(8,128)(2,1)}, bf16[1024,256]{0,1:T(8,128)(2,1)}, u32[]{:S(2)}, u32[]{:S(2)}) %collective-permute-start.30) | collective-permute-done | bytes 524320 | tf_op jit(solution)/shard_map/ppermute | solution.py:114
  194.9 1.4 collective-permute-start.32
  197.0 2.1 collective-permute-start.43
  203.9 9.4 %collective-permute-done.42 = bf16[256,1024]{1,0:T(8,128)(2,1)} collective-permute-done((bf16[256,1024]{1,0:T(8,128)(2,1)}, bf16[256,1024]{1,0:T(8,128)(2,1)}, u32[]{:S(2)}, u32[]{:S(2)}) %collective-permute-start.42) | collective-permute-done | bytes 524320 | tf_op jit(solution)/shard_map/ppermute | solution.py:103
  213.3 2.8 convert_add_fusion.1
  217.2 9.1 %collective-permute-done.33 = bf16[1024,256]{0,1:T(8,128)(2,1)S(1)} collective-permute-done((bf16[1024,256]{0,1:T(8,128)(2,1)}, bf16[1024,256]{0,1:T(8,128)(2,1)S(1)}, u32[]{:S(2)}, u32[]{:S(2)}) %collective-permute-start.33) | collective-permute-done | bytes 524320 | tf_op jit(solution)/shard_map/ppermute | solution.py:114
  230.5 2.4 fusion.6
  233.0 4.0 %convolution_add_fusion = f32[1024,1024]{1,0:T(8,128)S(1)} fusion(f32[1024,1024]{1,0:T(8,128)S(1)} %fusion.6, bf16[1024,256]{0,1:T(8,128)(2,1)S(1)} %copy-done.25, bf16[1024,256]{0,1:T(8,128)(2,1)S(1)} %copy-done.27, bf16[1024,256]{0,1:T(8,128)(2,1)S(1)} %copy-done.29, bf16[1024,256]{0,1:T(8,128)(2,1)S(1)} %copy-done.23, ...), kind=kOutput, calls=%fused_computation.12 | convolution fusion | flops 2165309440 | bytes 12582912 | tf_op jit(solution)/shard_map/dot_general | solution.py:23
  238.3 4.3 %multiply_convert_fusion = bf16[1024,1024]{1,0:T(8,128)(2,1)S(1)} fusion(bf16[1024,256]{0,1:T(8,128)(2,1)S(1)} %get-tuple-element.48, bf16[1024,256]{0,1:T(8,128)(2,1)S(1)} %get-tuple-element.49, bf16[1024,256]{0,1:T(8,128)(2,1)S(1)} %get-tuple-element.50, bf16[1024,256]{0,1:T(8,128)(2,1)S(1)} %get-tuple-element.47, ...), kind=kOutput, calls=%fused_computation | convolution fusion | flops 2162163712 | bytes 6291456 | tf_op jit(solution)/shard_map/dot_general | solution.py:23
  244.7 1.8 collective-permute-start.45
  248.4 2.3 copy.18
  250.7 2.2 fusion.g_ref.b_ref
  252.9 2.5 shard_map.96
  255.5 3.4 %collective-permute-done.44 = bf16[256,1024]{1,0:T(8,128)(2,1)} collective-permute-done((bf16[256,1024]{1,0:T(8,128)(2,1)}, bf16[256,1024]{1,0:T(8,128)(2,1)}, u32[]{:S(2)}, u32[]{:S(2)}) %collective-permute-start.44) | collective-permute-done | bytes 524320 | tf_op jit(solution)/shard_map/ppermute | solution.py:103
  258.9 11.0 %collective-permute-done.45 = bf16[256,1024]{1,0:T(8,128)(2,1)} collective-permute-done((bf16[256,1024]{1,0:T(8,128)(2,1)}, bf16[256,1024]{1,0:T(8,128)(2,1)}, u32[]{:S(2)}, u32[]{:S(2)}) %collective-permute-start.45) | collective-permute-done | bytes 524320 | tf_op jit(solution)/shard_map/ppermute | solution.py:103
  269.9 1.8 convert_add_fusion
  271.9 1.5 collective-permute-start.37
  275.4 1.5 pad_maximum_fusion.6
  277.8 2.8 collective-permute-done.38
  280.7 11.2 %shard_map.95 = (bf16[512,1024]{1,0:T(8,128)(2,1)}, f32[512,1024]{1,0:T(8,128)S(1)}, f32[512,1024]{1,0:T(8,128)S(1)}) custom-call(bf16[512,1024]{1,0:T(8,128)(2,1)S(1)} %get-tuple-element.14.scaled_ref.a_ref, bf16[512,1024]{1,0:T(8,128)(2,1)S(1)} %copy-done.1, bf16[512,1024]{1,0:T(8,128)(2,1)S(1)} %copy-done.3, bf16[512,1024]{1,0:T(8,128)(2,1)S(1)} %fusion.g_ref.b_ref, ...), custom_call_target="tpu_custom_call" | custom-call | flops 2684354560 | bytes 9437184 | tf_op jit(solution)/shard_map/pallas_call | solution.py:289
  292.0 5.0 %shard_map.97 = (bf16[512,1024]{1,0:T(8,128)(2,1)}, bf16[512,1024]{1,0:T(8,128)(2,1)}) custom-call(bf16[512,1024]{1,0:T(8,128)(2,1)S(1)} %copy-done.1, bf16[512,1024]{1,0:T(8,128)(2,1)S(1)} %copy-done.3, f32[512,1024]{1,0:T(8,128)S(1)} %get-tuple-element.19.dk_part_ref, f32[512,1024]{1,0:T(8,128)S(1)} %get-tuple-element.20.dv_part_ref, ...), custom_call_target="tpu_custom_call" | custom-call | flops 536870912 | bytes 7340032 | tf_op jit(solution)/shard_map/pallas_call | solution.py:295
  (157 shorter events, 48.5 us)
Async XLA Ops:
  5.6 13.1 %copy-start.1 = (bf16[512,1024]{1,0:T(8,128)(2,1)S(1)}, bf16[512,1024]{1,0:T(8,128)(2,1)}, u32[]{:S(2)}) copy-start(bf16[512,1024]{1,0:T(8,128)(2,1)} %k_ref.5) | copy-start | bytes 3145732
  5.6 13.1 %copy-start.3 = (bf16[512,1024]{1,0:T(8,128)(2,1)S(1)}, bf16[512,1024]{1,0:T(8,128)(2,1)}, u32[]{:S(2)}) copy-start(bf16[512,1024]{1,0:T(8,128)(2,1)} %v_ref.5) | copy-start | bytes 3145732
  5.6 1.7 collective-permute-start
  7.3 11.3 %copy-start.20 = (bf16[8,128,128]{2,1,0:T(8,128)(2,1)}, bf16[8,128,128]{2,1,0:T(8,128)(2,1)S(1)}, u32[]{:S(2)}) copy-start(bf16[8,128,128]{2,1,0:T(8,128)(2,1)S(1)} %collective-permute-done) | copy-start | bytes 786436
  7.4 6.8 %collective-permute-start.1 = (bf16[4,128,128]{2,1,0:T(8,128)(2,1)S(1)}, bf16[4,128,128]{2,1,0:T(8,128)(2,1)S(1)}, u32[]{:S(2)}, u32[]{:S(2)}) collective-permute-start(bf16[4,128,128]{2,1,0:T(8,128)(2,1)S(1)} %fusion.8), channel_id=1, source_target_pairs={{0,8},{4,12},{8,0},{12,4},{16,24},{20,28},{24,16},{28,20},{1,9},{5... | collective-permute-start | bytes 393224 | tf_op jit(solution)/shard_map/ppermute | solution.py:103
  10.3 8.1 %collective-permute-start.2 = (bf16[4,128,128]{2,1,0:T(8,128)(2,1)S(1)}, bf16[4,128,128]{2,1,0:T(8,128)(2,1)S(1)}, u32[]{:S(2)}, u32[]{:S(2)}) collective-permute-start(bf16[4,128,128]{2,1,0:T(8,128)(2,1)S(1)} %fusion.8), channel_id=1, source_target_pairs={{0,16},{4,20},{8,24},{12,28},{16,0},{20,4},{24,8},{28,12},{1,17},{... | collective-permute-start | bytes 393224 | tf_op jit(solution)/shard_map/ppermute | solution.py:103
  11.9 6.5 %collective-permute-start.3 = (bf16[4,128,128]{2,1,0:T(8,128)(2,1)S(1)}, bf16[4,128,128]{2,1,0:T(8,128)(2,1)S(1)}, u32[]{:S(2)}, u32[]{:S(2)}) collective-permute-start(bf16[4,128,128]{2,1,0:T(8,128)(2,1)S(1)} %fusion.8), channel_id=1, source_target_pairs={{0,24},{4,28},{8,16},{12,20},{16,8},{20,12},{24,0},{28,4},{1,25},{... | collective-permute-start | bytes 393224 | tf_op jit(solution)/shard_map/ppermute | solution.py:103
  18.5 7.2 %collective-permute-start.4 = (bf16[4,128,128]{2,1,0:T(8,128)(2,1)S(1)}, bf16[4,128,128]{2,1,0:T(8,128)(2,1)}, u32[]{:S(2)}, u32[]{:S(2)}) collective-permute-start(bf16[4,128,128]{2,1,0:T(8,128)(2,1)S(1)} %add_convert_fusion.9), channel_id=1, source_target_pairs={{0,4},{4,0},{8,12},{12,8},{16,20},{20,16},{24,28},{28,24},{1,5},{5... | collective-permute-start | bytes 393224 | tf_op jit(solution)/shard_map/ppermute | solution.py:98
  19.9 6.7 %copy-start.21 = (bf16[8,128,128]{2,1,0:T(8,128)(2,1)S(1)}, bf16[8,128,128]{2,1,0:T(8,128)(2,1)}, u32[]{:S(2)}) copy-start(bf16[8,128,128]{2,1,0:T(8,128)(2,1)} %copy-done.20) | copy-start | bytes 786436
  30.9 27.9 %collective-permute-start.5 = (bf16[512,1024]{1,0:T(8,128)(2,1)}, bf16[512,1024]{1,0:T(8,128)(2,1)}, u32[]{:S(2)}, u32[]{:S(2)}) collective-permute-start(bf16[512,1024]{1,0:T(8,128)(2,1)} %shard_map.94), channel_id=1, source_target_pairs={{0,4},{4,0},{8,12},{12,8},{16,20},{20,16},{24,28},{28,24},{1,5},{5... | collective-permute-start | bytes 3145736 | tf_op jit(solution)/shard_map/ppermute | solution.py:98
  32.5 15.1 %collective-permute-start.6 = (bf16[256,1024]{1,0:T(8,128)(2,1)}, bf16[256,1024]{1,0:T(8,128)(2,1)}, u32[]{:S(2)}, u32[]{:S(2)}) collective-permute-start(bf16[256,1024]{1,0:T(8,128)(2,1)} %get-tuple-element.63), channel_id=1, source_target_pairs={{0,8},{4,12},{8,0},{12,4},{16,24},{20,28},{24,16},{28,20},{1,9},{5... | collective-permute-start | bytes 1572872 | tf_op jit(solution)/shard_map/ppermute | solution.py:103
  33.7 23.5 %collective-permute-start.7 = (bf16[256,1024]{1,0:T(8,128)(2,1)}, bf16[256,1024]{1,0:T(8,128)(2,1)}, u32[]{:S(2)}, u32[]{:S(2)}) collective-permute-start(bf16[256,1024]{1,0:T(8,128)(2,1)} %get-tuple-element.63), channel_id=1, source_target_pairs={{0,16},{4,20},{8,24},{12,28},{16,0},{20,4},{24,8},{28,12},{1,17},{... | collective-permute-start | bytes 1572872 | tf_op jit(solution)/shard_map/ppermute | solution.py:103
  34.5 24.3 %collective-permute-start.8 = (bf16[256,1024]{1,0:T(8,128)(2,1)}, bf16[256,1024]{1,0:T(8,128)(2,1)}, u32[]{:S(2)}, u32[]{:S(2)}) collective-permute-start(bf16[256,1024]{1,0:T(8,128)(2,1)} %get-tuple-element.63), channel_id=1, source_target_pairs={{0,24},{4,28},{8,16},{12,20},{16,8},{20,12},{24,0},{28,4},{1,25},{... | collective-permute-start | bytes 1572872 | tf_op jit(solution)/shard_map/ppermute | solution.py:103
  65.7 16.2 %collective-permute-start.9 = (bf16[1024,256]{0,1:T(8,128)(2,1)}, bf16[1024,256]{0,1:T(8,128)(2,1)}, u32[]{:S(2)}, u32[]{:S(2)}) collective-permute-start(bf16[1024,256]{0,1:T(8,128)(2,1)} %get-tuple-element.57), channel_id=1, source_target_pairs={{0,1},{3,2},{4,5},{7,6},{8,9},{11,10},{12,13},{15,14},{16,17},{19,... | collective-permute-start | bytes 1572872 | tf_op jit(solution)/shard_map/ppermute | solution.py:114
  70.0 22.3 %collective-permute-start.12 = (bf16[1024,256]{0,1:T(8,128)(2,1)}, bf16[1024,256]{0,1:T(8,128)(2,1)}, u32[]{:S(2)}, u32[]{:S(2)}) collective-permute-start(bf16[1024,256]{0,1:T(8,128)(2,1)} %get-tuple-element.58), channel_id=1, source_target_pairs={{0,1},{3,2},{4,5},{7,6},{8,9},{11,10},{12,13},{15,14},{16,17},{19,... | collective-permute-start | bytes 1572872 | tf_op jit(solution)/shard_map/ppermute | solution.py:114
  84.0 8.3 %collective-permute-start.10 = (bf16[1024,256]{0,1:T(8,128)(2,1)}, bf16[1024,256]{0,1:T(8,128)(2,1)}, u32[]{:S(2)}, u32[]{:S(2)}) collective-permute-start(bf16[1024,256]{0,1:T(8,128)(2,1)} %add_convert_fusion.7), channel_id=1, source_target_pairs={{1,2},{2,1},{5,6},{6,5},{9,10},{10,9},{13,14},{14,13},{17,18},{18,... | collective-permute-start | bytes 1572872 | tf_op jit(solution)/shard_map/ppermute | solution.py:114
  85.5 18.9 %collective-permute-start.15 = (bf16[256,1024]{1,0:T(8,128)(2,1)}, bf16[256,1024]{1,0:T(8,128)(2,1)}, u32[]{:S(2)}, u32[]{:S(2)}) collective-permute-start(bf16[256,1024]{1,0:T(8,128)(2,1)} %get-tuple-element.16), channel_id=1, source_target_pairs={{0,8},{4,12},{8,0},{12,4},{16,24},{20,28},{24,16},{28,20},{1,9},{5... | collective-permute-start | bytes 1572872 | tf_op jit(solution)/shard_map/ppermute | solution.py:103
  86.3 20.0 %collective-permute-start.16 = (bf16[256,1024]{1,0:T(8,128)(2,1)}, bf16[256,1024]{1,0:T(8,128)(2,1)}, u32[]{:S(2)}, u32[]{:S(2)}) collective-permute-start(bf16[256,1024]{1,0:T(8,128)(2,1)} %get-tuple-element.16), channel_id=1, source_target_pairs={{0,16},{4,20},{8,24},{12,28},{16,0},{20,4},{24,8},{28,12},{1,17},{... | collective-permute-start | bytes 1572872 | tf_op jit(solution)/shard_map/ppermute | solution.py:103
  92.3 15.0 %collective-permute-start.18 = (bf16[512,1,512]{0,2,1:T(8,128)(2,1)}, bf16[512,1,512]{0,2,1:T(8,128)(2,1)}, u32[]{:S(2)}, u32[]{:S(2)}) collective-permute-start(bf16[512,1,512]{0,2,1:T(8,128)(2,1)} %get-tuple-element.66), channel_id=1, source_target_pairs={{0,4},{4,0},{8,12},{12,8},{16,20},{20,16},{24,28},{28,24},{1,5},{5... | collective-permute-start | bytes 1572872 | tf_op jit(solution)/shard_map/ppermute | solution.py:98
  95.2 17.5 %collective-permute-start.11 = (bf16[1024,256]{0,1:T(8,128)(2,1)}, bf16[1024,256]{0,1:T(8,128)(2,1)}, u32[]{:S(2)}, u32[]{:S(2)}) collective-permute-start(bf16[1024,256]{0,1:T(8,128)(2,1)} %get-tuple-element.55), channel_id=1, source_target_pairs={{0,1},{2,3},{1,0},{3,2},{4,5},{6,7},{5,4},{7,6},{8,9},{10,11},{9,8... | collective-permute-start | bytes 1572872 | tf_op jit(solution)/shard_map/ppermute | solution.py:114
  101.8 10.9 %collective-permute-start.13 = (bf16[1024,256]{0,1:T(8,128)(2,1)}, bf16[1024,256]{0,1:T(8,128)(2,1)}, u32[]{:S(2)}, u32[]{:S(2)}) collective-permute-start(bf16[1024,256]{0,1:T(8,128)(2,1)} %get-tuple-element.56), channel_id=1, source_target_pairs={{1,2},{2,1},{5,6},{6,5},{9,10},{10,9},{13,14},{14,13},{17,18},{18,... | collective-permute-start | bytes 1572872 | tf_op jit(solution)/shard_map/ppermute | solution.py:114
  103.3 9.4 %copy-start.10 = (bf16[512,1,512]{0,2,1:T(8,128)(2,1)S(1)}, bf16[512,1,512]{0,2,1:T(8,128)(2,1)}, u32[]{:S(2)}) copy-start(bf16[512,1,512]{0,2,1:T(8,128)(2,1)} %get-tuple-element.65) | copy-start | bytes 1572868
  104.4 16.0 %collective-permute-start.17 = (bf16[256,1024]{1,0:T(8,128)(2,1)}, bf16[256,1024]{1,0:T(8,128)(2,1)S(1)}, u32[]{:S(2)}, u32[]{:S(2)}) collective-permute-start(bf16[256,1024]{1,0:T(8,128)(2,1)} %get-tuple-element.16), channel_id=1, source_target_pairs={{0,24},{4,28},{8,16},{12,20},{16,8},{20,12},{24,0},{28,4},{1,25},{... | collective-permute-start | bytes 1572872 | tf_op jit(solution)/shard_map/ppermute | solution.py:103
  115.3 9.8 %copy-start.17 = (bf16[1024,256]{0,1:T(8,128)(2,1)}, bf16[1024,256]{0,1:T(8,128)(2,1)S(1)}, u32[]{:S(2)}) copy-start(bf16[1024,256]{0,1:T(8,128)(2,1)S(1)} %get-tuple-element.35) | copy-start | bytes 1572868
  115.3 13.4 %collective-permute-start.19 = (bf16[1024,256]{0,1:T(8,128)(2,1)S(1)}, bf16[1024,256]{0,1:T(8,128)(2,1)}, u32[]{:S(2)}, u32[]{:S(2)}) collective-permute-start(bf16[1024,256]{0,1:T(8,128)(2,1)S(1)} %get-tuple-element.35), channel_id=1, source_target_pairs={{0,1},{2,3},{1,0},{3,2},{4,5},{6,7},{5,4},{7,6},{8,9},{10,11},{9,8... | collective-permute-start | bytes 1572872 | tf_op jit(solution)/shard_map/ppermute | solution.py:114
  118.9 9.7 %collective-permute-start.20 = (bf16[1024,256]{0,1:T(8,128)(2,1)S(1)}, bf16[1024,256]{0,1:T(8,128)(2,1)}, u32[]{:S(2)}, u32[]{:S(2)}) collective-permute-start(bf16[1024,256]{0,1:T(8,128)(2,1)S(1)} %get-tuple-element.35), channel_id=1, source_target_pairs={{1,2},{2,1},{5,6},{6,5},{9,10},{10,9},{13,14},{14,13},{17,18},{18,... | collective-permute-start | bytes 1572872 | tf_op jit(solution)/shard_map/ppermute | solution.py:114
  125.2 21.3 %copy-start.7 = (bf16[1024,1024]{0,1:T(8,128)(2,1)}, bf16[1024,1024]{0,1:T(8,128)(2,1)S(1)}, u32[]{:S(2)}) copy-start(bf16[1024,1024]{0,1:T(8,128)(2,1)S(1)} %convolution_convert_fusion) | copy-start | bytes 6291460
  129.5 16.9 %collective-permute-start.21 = (bf16[1024,256]{0,1:T(8,128)(2,1)S(1)}, bf16[1024,256]{0,1:T(8,128)(2,1)S(1)}, u32[]{:S(2)}, u32[]{:S(2)}) collective-permute-start(bf16[1024,256]{0,1:T(8,128)(2,1)S(1)} %get-tuple-element.53), channel_id=1, source_target_pairs={{0,1},{3,2},{4,5},{7,6},{8,9},{11,10},{12,13},{15,14},{16,17},{19,... | collective-permute-start | bytes 1572872 | tf_op jit(solution)/shard_map/ppermute | solution.py:114
  135.1 15.0 %collective-permute-start.27 = (bf16[1024,256]{0,1:T(8,128)(2,1)}, bf16[1024,256]{0,1:T(8,128)(2,1)}, u32[]{:S(2)}, u32[]{:S(2)}) collective-permute-start(bf16[1024,256]{0,1:T(8,128)(2,1)} %collective-permute-done.19), channel_id=1, source_target_pairs={{1,2},{2,1},{5,6},{6,5},{9,10},{10,9},{13,14},{14,13},{17,18},{18,... | collective-permute-start | bytes 1572872 | tf_op jit(solution)/shard_map/ppermute | solution.py:114
  136.6 14.8 %collective-permute-start.29 = (bf16[1024,256]{0,1:T(8,128)(2,1)}, bf16[1024,256]{0,1:T(8,128)(2,1)}, u32[]{:S(2)}, u32[]{:S(2)}) collective-permute-start(bf16[1024,256]{0,1:T(8,128)(2,1)} %collective-permute-done.20), channel_id=1, source_target_pairs={{2,3},{1,0},{6,7},{5,4},{10,11},{9,8},{14,15},{13,12},{18,19},{17,... | collective-permute-start | bytes 1572872 | tf_op jit(solution)/shard_map/ppermute | solution.py:114
  137.9 16.5 %collective-permute-start.24 = (bf16[1024,256]{0,1:T(8,128)(2,1)}, bf16[1024,256]{0,1:T(8,128)(2,1)}, u32[]{:S(2)}, u32[]{:S(2)}) collective-permute-start(bf16[1024,256]{0,1:T(8,128)(2,1)} %get-tuple-element.54), channel_id=1, source_target_pairs={{0,1},{3,2},{4,5},{7,6},{8,9},{11,10},{12,13},{15,14},{16,17},{19,... | collective-permute-start | bytes 1572872 | tf_op jit(solution)/shard_map/ppermute | solution.py:114
  147.4 7.0 %collective-permute-start.22 = (bf16[1024,256]{0,1:T(8,128)(2,1)}, bf16[1024,256]{0,1:T(8,128)(2,1)}, u32[]{:S(2)}, u32[]{:S(2)}) collective-permute-start(bf16[1024,256]{0,1:T(8,128)(2,1)} %add_convert_fusion.3), channel_id=1, source_target_pairs={{1,2},{2,1},{5,6},{6,5},{9,10},{10,9},{13,14},{14,13},{17,18},{18,... | collective-permute-start | bytes 1572872 | tf_op jit(solution)/shard_map/ppermute | solution.py:114
  148.9 5.5 %copy-start.8 = (bf16[1024,1024]{0,1:T(8,128)(2,1)S(1)}, bf16[1024,1024]{0,1:T(8,128)(2,1)}, u32[]{:S(2)}) copy-start(bf16[1024,1024]{0,1:T(8,128)(2,1)} %copy-done.7) | copy-start | bytes 6291460
  150.0 46.3 %collective-permute-start.14 = (bf16[512,256]{0,1:T(8,128)(2,1)S(1)}, bf16[512,256]{0,1:T(8,128)(2,1)S(1)}, u32[]{:S(2)}, u32[]{:S(2)}) collective-permute-start(bf16[512,256]{0,1:T(8,128)(2,1)S(1)} %slice.74), channel_id=1, source_target_pairs={{0,4},{4,0},{8,12},{12,8},{16,20},{20,16},{24,28},{28,24},{1,5},{5... | collective-permute-start | bytes 786440 | tf_op jit(solution)/shard_map/ppermute | solution.py:98
  150.1 17.4 %collective-permute-start.28 = (bf16[1024,256]{0,1:T(8,128)(2,1)}, bf16[1024,256]{0,1:T(8,128)(2,1)S(1)}, u32[]{:S(2)}, u32[]{:S(2)}) collective-permute-start(bf16[1024,256]{0,1:T(8,128)(2,1)} %collective-permute-done.27), channel_id=1, source_target_pairs={{2,3},{1,0},{6,7},{5,4},{10,11},{9,8},{14,15},{13,12},{18,19},{17,... | collective-permute-start | bytes 1572872 | tf_op jit(solution)/shard_map/ppermute | solution.py:114
  156.0 12.8 %copy-start.18 = (bf16[1024,256]{0,1:T(8,128)(2,1)S(1)}, bf16[1024,256]{0,1:T(8,128)(2,1)}, u32[]{:S(2)}) copy-start(bf16[1024,256]{0,1:T(8,128)(2,1)} %copy-done.17) | copy-start | bytes 1572868
  156.0 22.5 %collective-permute-start.23 = (bf16[1024,256]{0,1:T(8,128)(2,1)S(1)}, bf16[1024,256]{0,1:T(8,128)(2,1)S(1)}, u32[]{:S(2)}, u32[]{:S(2)}) collective-permute-start(bf16[1024,256]{0,1:T(8,128)(2,1)S(1)} %get-tuple-element.51), channel_id=1, source_target_pairs={{0,1},{2,3},{1,0},{3,2},{4,5},{6,7},{5,4},{7,6},{8,9},{10,11},{9,8... | collective-permute-start | bytes 1572872 | tf_op jit(solution)/shard_map/ppermute | solution.py:114
  163.0 15.6 %collective-permute-start.25 = (bf16[1024,256]{0,1:T(8,128)(2,1)S(1)}, bf16[1024,256]{0,1:T(8,128)(2,1)S(1)}, u32[]{:S(2)}, u32[]{:S(2)}) collective-permute-start(bf16[1024,256]{0,1:T(8,128)(2,1)S(1)} %get-tuple-element.52), channel_id=1, source_target_pairs={{1,2},{2,1},{5,6},{6,5},{9,10},{10,9},{13,14},{14,13},{17,18},{18,... | collective-permute-start | bytes 1572872 | tf_op jit(solution)/shard_map/ppermute | solution.py:114
  169.1 9.4 %copy-start.11 = (bf16[512,1,512]{0,2,1:T(8,128)(2,1)S(1)}, bf16[512,1,512]{0,2,1:T(8,128)(2,1)}, u32[]{:S(2)}) copy-start(bf16[512,1,512]{0,2,1:T(8,128)(2,1)} %get-tuple-element.65) | copy-start | bytes 1572868
  169.3 15.4 %copy-start.22 = (bf16[1024,256]{0,1:T(8,128)(2,1)}, bf16[1024,256]{0,1:T(8,128)(2,1)S(1)}, u32[]{:S(2)}) copy-start(bf16[1024,256]{0,1:T(8,128)(2,1)S(1)} %get-tuple-element.43) | copy-start | bytes 1572868
  169.3 15.4 %copy-start.24 = (bf16[1024,256]{0,1:T(8,128)(2,1)}, bf16[1024,256]{0,1:T(8,128)(2,1)S(1)}, u32[]{:S(2)}) copy-start(bf16[1024,256]{0,1:T(8,128)(2,1)S(1)} %get-tuple-element.44) | copy-start | bytes 1572868
  169.3 15.4 %copy-start.26 = (bf16[1024,256]{0,1:T(8,128)(2,1)}, bf16[1024,256]{0,1:T(8,128)(2,1)S(1)}, u32[]{:S(2)}) copy-start(bf16[1024,256]{0,1:T(8,128)(2,1)S(1)} %get-tuple-element.45) | copy-start | bytes 1572868
  169.3 15.4 %copy-start.28 = (bf16[1024,256]{0,1:T(8,128)(2,1)}, bf16[1024,256]{0,1:T(8,128)(2,1)S(1)}, u32[]{:S(2)}) copy-start(bf16[1024,256]{0,1:T(8,128)(2,1)S(1)} %get-tuple-element.46) | copy-start | bytes 1572868
  180.8 14.0 %collective-permute-start.30 = (bf16[1024,256]{0,1:T(8,128)(2,1)}, bf16[1024,256]{0,1:T(8,128)(2,1)}, u32[]{:S(2)}, u32[]{:S(2)}) collective-permute-start(bf16[1024,256]{0,1:T(8,128)(2,1)} %get-tuple-element.33), channel_id=1, source_target_pairs={{0,1},{2,3},{1,0},{3,2},{4,5},{6,7},{5,4},{7,6},{8,9},{10,11},{9,8... | collective-permute-start | bytes 1572872 | tf_op jit(solution)/shard_map/ppermute | solution.py:114
  184.8 14.4 %collective-permute-start.31 = (bf16[1024,256]{0,1:T(8,128)(2,1)}, bf16[1024,256]{0,1:T(8,128)(2,1)}, u32[]{:S(2)}, u32[]{:S(2)}) collective-permute-start(bf16[1024,256]{0,1:T(8,128)(2,1)} %get-tuple-element.33), channel_id=1, source_target_pairs={{1,2},{2,1},{5,6},{6,5},{9,10},{10,9},{13,14},{14,13},{17,18},{18,... | collective-permute-start | bytes 1572872 | tf_op jit(solution)/shard_map/ppermute | solution.py:114
  187.4 15.1 %collective-permute-start.41 = (bf16[256,1024]{1,0:T(8,128)(2,1)}, bf16[256,1024]{1,0:T(8,128)(2,1)}, u32[]{:S(2)}, u32[]{:S(2)}) collective-permute-start(bf16[256,1024]{1,0:T(8,128)(2,1)} %get-tuple-element.37), channel_id=1, source_target_pairs={{0,8},{4,12},{8,0},{12,4},{16,24},{20,28},{24,16},{28,20},{1,9},{5... | collective-permute-start | bytes 1572872 | tf_op jit(solution)/shard_map/ppermute | solution.py:103
  188.2 25.1 %collective-permute-start.42 = (bf16[256,1024]{1,0:T(8,128)(2,1)}, bf16[256,1024]{1,0:T(8,128)(2,1)}, u32[]{:S(2)}, u32[]{:S(2)}) collective-permute-start(bf16[256,1024]{1,0:T(8,128)(2,1)} %get-tuple-element.39), channel_id=1, source_target_pairs={{0,16},{4,20},{8,24},{12,28},{16,0},{20,4},{24,8},{28,12},{1,17},{... | collective-permute-start | bytes 1572872 | tf_op jit(solution)/shard_map/ppermute | solution.py:103
  194.9 7.7 %collective-permute-start.32 = (bf16[1024,256]{0,1:T(8,128)(2,1)}, bf16[1024,256]{0,1:T(8,128)(2,1)}, u32[]{:S(2)}, u32[]{:S(2)}) collective-permute-start(bf16[1024,256]{0,1:T(8,128)(2,1)} %collective-permute-done.30), channel_id=1, source_target_pairs={{1,2},{2,1},{5,6},{6,5},{9,10},{10,9},{13,14},{14,13},{17,18},{18,... | collective-permute-start | bytes 1572872 | tf_op jit(solution)/shard_map/ppermute | solution.py:114
  197.0 16.3 %collective-permute-start.43 = (bf16[256,1024]{1,0:T(8,128)(2,1)}, bf16[256,1024]{1,0:T(8,128)(2,1)}, u32[]{:S(2)}, u32[]{:S(2)}) collective-permute-start(bf16[256,1024]{1,0:T(8,128)(2,1)} %get-tuple-element.38), channel_id=1, source_target_pairs={{0,24},{4,28},{8,16},{12,20},{16,8},{20,12},{24,0},{28,4},{1,25},{... | collective-permute-start | bytes 1572872 | tf_op jit(solution)/shard_map/ppermute | solution.py:103
  199.1 17.0 %collective-permute-start.34 = (bf16[1024,256]{0,1:T(8,128)(2,1)}, bf16[1024,256]{0,1:T(8,128)(2,1)S(1)}, u32[]{:S(2)}, u32[]{:S(2)}) collective-permute-start(bf16[1024,256]{0,1:T(8,128)(2,1)} %collective-permute-done.31), channel_id=1, source_target_pairs={{2,3},{1,0},{6,7},{5,4},{10,11},{9,8},{14,15},{13,12},{18,19},{17,... | collective-permute-start | bytes 1572872 | tf_op jit(solution)/shard_map/ppermute | solution.py:114
  202.5 44.8 %collective-permute-start.26 = (bf16[512,256]{0,1:T(8,128)(2,1)S(1)}, bf16[512,256]{0,1:T(8,128)(2,1)S(1)}, u32[]{:S(2)}, u32[]{:S(2)}) collective-permute-start(bf16[512,256]{0,1:T(8,128)(2,1)S(1)} %slice.78), channel_id=1, source_target_pairs={{0,4},{4,0},{8,12},{12,8},{16,20},{20,16},{24,28},{28,24},{1,5},{5... | collective-permute-start | bytes 786440 | tf_op jit(solution)/shard_map/ppermute | solution.py:98
  202.6 23.7 %collective-permute-start.33 = (bf16[1024,256]{0,1:T(8,128)(2,1)}, bf16[1024,256]{0,1:T(8,128)(2,1)S(1)}, u32[]{:S(2)}, u32[]{:S(2)}) collective-permute-start(bf16[1024,256]{0,1:T(8,128)(2,1)} %collective-permute-done.32), channel_id=1, source_target_pairs={{2,3},{1,0},{6,7},{5,4},{10,11},{9,8},{14,15},{13,12},{18,19},{17,... | collective-permute-start | bytes 1572872 | tf_op jit(solution)/shard_map/ppermute | solution.py:114
  237.0 5.6 %copy-start.13 = (f32[1024,1024]{1,0:T(8,128)}, f32[1024,1024]{1,0:T(8,128)S(1)}, u32[]{:S(2)}) copy-start(f32[1024,1024]{1,0:T(8,128)S(1)} %convolution_add_fusion) | copy-start | bytes 12582916
  238.3 12.4 %collective-permute-start.35 = (bf16[512,1024]{1,0:T(8,128)(2,1)}, bf16[512,1024]{1,0:T(8,128)(2,1)}, u32[]{:S(2)}, u32[]{:S(2)}) collective-permute-start(bf16[512,1024]{1,0:T(8,128)(2,1)} %slice.109), channel_id=1, source_target_pairs={{0,4},{4,0},{8,12},{12,8},{16,20},{20,16},{24,28},{28,24},{1,5},{5... | collective-permute-start | bytes 3145736 | tf_op jit(solution)/shard_map/ppermute | solution.py:98
  243.8 15.1 %collective-permute-start.44 = (bf16[256,1024]{1,0:T(8,128)(2,1)}, bf16[256,1024]{1,0:T(8,128)(2,1)}, u32[]{:S(2)}, u32[]{:S(2)}) collective-permute-start(bf16[256,1024]{1,0:T(8,128)(2,1)} %get-tuple-element.40), channel_id=1, source_target_pairs={{0,8},{4,12},{8,0},{12,4},{16,24},{20,28},{24,16},{28,20},{1,9},{5... | collective-permute-start | bytes 1572872 | tf_op jit(solution)/shard_map/ppermute | solution.py:103
  244.7 25.2 %collective-permute-start.45 = (bf16[256,1024]{1,0:T(8,128)(2,1)}, bf16[256,1024]{1,0:T(8,128)(2,1)}, u32[]{:S(2)}, u32[]{:S(2)}) collective-permute-start(bf16[256,1024]{1,0:T(8,128)(2,1)} %get-tuple-element.42), channel_id=1, source_target_pairs={{0,16},{4,20},{8,24},{12,28},{16,0},{20,4},{24,8},{28,12},{1,17},{... | collective-permute-start | bytes 1572872 | tf_op jit(solution)/shard_map/ppermute | solution.py:103
  246.5 23.4 %collective-permute-start.46 = (bf16[256,1024]{1,0:T(8,128)(2,1)}, bf16[256,1024]{1,0:T(8,128)(2,1)}, u32[]{:S(2)}, u32[]{:S(2)}) collective-permute-start(bf16[256,1024]{1,0:T(8,128)(2,1)} %get-tuple-element.41), channel_id=1, source_target_pairs={{0,24},{4,28},{8,16},{12,20},{16,8},{20,12},{24,0},{28,4},{1,25},{... | collective-permute-start | bytes 1572872 | tf_op jit(solution)/shard_map/ppermute | solution.py:103
  255.4 20.0 %copy-start.12 = (f32[256,1024]{1,0:T(8,128)S(1)}, f32[256,1024]{1,0:T(8,128)}, u32[]{:S(2)}) copy-start(f32[256,1024]{1,0:T(8,128)} %convert_add_fusion.1) | copy-start | bytes 3145732
  255.5 16.3 %collective-permute-start.36 = (bf16[8,128,128]{2,1,0:T(8,128)(2,1)S(1)}, bf16[8,128,128]{2,1,0:T(8,128)(2,1)S(1)}, u32[]{:S(2)}, u32[]{:S(2)}) collective-permute-start(bf16[8,128,128]{2,1,0:T(8,128)(2,1)S(1)} %convert_element_type.259), channel_id=1, source_target_pairs={{0,4},{4,0},{8,12},{12,8},{16,20},{20,16},{24,28},{28,24},{1,5},{5... | collective-permute-start | bytes 786440 | tf_op jit(solution)/shard_map/ppermute | solution.py:98
  271.9 8.9 %copy-start.5 = (f32[8,128,128]{2,1,0:T(8,128)S(1)}, f32[8,128,128]{2,1,0:T(8,128)}, u32[]{:S(2)}) copy-start(f32[8,128,128]{2,1,0:T(8,128)} %copy-done.4) | copy-start | bytes 1572868
  271.9 5.9 %collective-permute-start.37 = (bf16[4,128,128]{2,1,0:T(8,128)(2,1)S(1)}, bf16[4,128,128]{2,1,0:T(8,128)(2,1)S(1)}, u32[]{:S(2)}, u32[]{:S(2)}) collective-permute-start(bf16[4,128,128]{2,1,0:T(8,128)(2,1)S(1)} %fusion.7), channel_id=1, source_target_pairs={{0,8},{4,12},{8,0},{12,4},{16,24},{20,28},{24,16},{28,20},{1,9},{5... | collective-permute-start | bytes 393224 | tf_op jit(solution)/shard_map/ppermute | solution.py:103
  273.4 7.2 %collective-permute-start.38 = (bf16[4,128,128]{2,1,0:T(8,128)(2,1)S(1)}, bf16[4,128,128]{2,1,0:T(8,128)(2,1)S(1)}, u32[]{:S(2)}, u32[]{:S(2)}) collective-permute-start(bf16[4,128,128]{2,1,0:T(8,128)(2,1)S(1)} %fusion.7), channel_id=1, source_target_pairs={{0,16},{4,20},{8,24},{12,28},{16,0},{20,4},{24,8},{28,12},{1,17},{... | collective-permute-start | bytes 393224 | tf_op jit(solution)/shard_map/ppermute | solution.py:103
  274.0 6.5 %collective-permute-start.39 = (bf16[4,128,128]{2,1,0:T(8,128)(2,1)S(1)}, bf16[4,128,128]{2,1,0:T(8,128)(2,1)S(1)}, u32[]{:S(2)}, u32[]{:S(2)}) collective-permute-start(bf16[4,128,128]{2,1,0:T(8,128)(2,1)S(1)} %fusion.7), channel_id=1, source_target_pairs={{0,24},{4,28},{8,16},{12,20},{16,8},{20,12},{24,0},{28,4},{1,25},{... | collective-permute-start | bytes 393224 | tf_op jit(solution)/shard_map/ppermute | solution.py:103
  280.6 11.3 %collective-permute-start.40 = (bf16[4,128,128]{2,1,0:T(8,128)(2,1)S(1)}, bf16[4,128,128]{2,1,0:T(8,128)(2,1)S(1)}, u32[]{:S(2)}, u32[]{:S(2)}) collective-permute-start(bf16[4,128,128]{2,1,0:T(8,128)(2,1)S(1)} %add_convert_fusion.8), channel_id=1, source_target_pairs={{0,4},{4,0},{8,12},{12,8},{16,20},{20,16},{24,28},{28,24},{1,5},{5... | collective-permute-start | bytes 393224 | tf_op jit(solution)/shard_map/ppermute | solution.py:98
  (16 other events, 41.6 us)

commit v2 on v1

v2 whole, which is shorter than its diff:
```python
import functools
import math

import jax
import jax.numpy as jnp
from jax import lax
from jax.experimental import pallas as pl
from jax.experimental.pallas import tpu as pltpu
from jax.sharding import PartitionSpec as P

DH = 128
CHUNKS = 2
F32 = jnp.float32
BF16 = jnp.bfloat16
VMEM_LIMIT = 16 * 1024 * 1024

NT = (((1,), (1,)), ((), ()))
TN = (((0,), (0,)), ((), ()))
NN = (((1,), (0,)), ((), ()))


def dot(a, b, dims):
    return lax.dot_general(a, b, dims, preferred_element_type=F32)


def split_dot(a, state, dims):
    high = state.astype(BF16)
    low = (state - high.astype(F32)).astype(BF16)
    return dot(a, high, dims) + dot(a, low, dims)


def causal_mask(rows):
    t = lax.broadcasted_iota(jnp.int32, (rows, rows), 0)
    s = lax.broadcasted_iota(jnp.int32, (rows, rows), 1)
    return s <= t


def head_columns(ref):
    return [ref.at[:, h * DH : (h + 1) * DH] for h in range(ref.shape[1] // DH)]


def outer_kernel(a_ref, b_ref, out_ref):
    for h, (a, b) in enumerate(zip(head_columns(a_ref), head_columns(b_ref))):
        out_ref[h] = dot(a[...], b[...], TN)


def forward_kernel(q_ref, k_ref, v_ref, scale_ref, scaled_ref, intra_ref):
    scaled_ref[...] = (q_ref[...].astype(F32) * scale_ref[...]).astype(BF16)
    mask = causal_mask(scaled_ref.shape[0])
    refs = (scaled_ref, k_ref, v_ref, intra_ref)
    for scaled, keys, values, intra in zip(*map(head_columns, refs)):
        scores = jnp.where(mask, dot(scaled[...], keys[...], NT), 0.0).astype(BF16)
        intra[...] = dot(scores, values[...], NN)


def attended_kernel(scaled_ref, intra_ref, state_ref, out_ref):
    refs = (scaled_ref, intra_ref, out_ref)
    for h, (scaled, intra, out) in enumerate(zip(*map(head_columns, refs))):
        out[...] = (split_dot(scaled[...], state_ref[h], NN) + intra[...]).astype(BF16)


def backward_kernel(
    scaled_ref, k_ref, v_ref, g_ref, scale_ref, state_ref, dq_ref, dk_ref, dv_ref
):
    mask = causal_mask(scaled_ref.shape[0])
    refs = (scaled_ref, k_ref, v_ref, g_ref, dq_ref, dk_ref, dv_ref)
    for h, (scaled, keys, values, grads, dq, dk, dv) in enumerate(zip(*map(head_columns, refs))):
        mixed = jnp.where(mask, dot(grads[...], values[...], NT), 0.0).astype(BF16)
        total = split_dot(grads[...], state_ref[h], NT) + dot(mixed, keys[...], NN)
        dq[...] = (total * scale_ref[...]).astype(BF16)
        dk[...] = dot(mixed, scaled[...], TN)
        scores = jnp.where(mask, dot(scaled[...], keys[...], NT), 0.0).astype(BF16)
        dv[...] = dot(scores, grads[...], TN)


def finish_kernel(k_ref, v_ref, dk_part_ref, dv_part_ref, after_ref, dk_ref, dv_ref):
    refs = (k_ref, v_ref, dk_part_ref, dv_part_ref, dk_ref, dv_ref)
    for h, (keys, values, dk_part, dv_part, dk, dv) in enumerate(zip(*map(head_columns, refs))):
        dk[...] = (split_dot(values[...], after_ref[h], NT) + dk_part[...]).astype(BF16)
        dv[...] = (split_dot(keys[...], after_ref[h], NN) + dv_part[...]).astype(BF16)


def per_head(kernel, rows, heads, ins, outs, macs, step=2):
    if heads % step:
        step = 1
    specs = {
        "h": pl.BlockSpec((rows, step * DH), lambda h: (0, h)),
        "m": pl.BlockSpec((step, DH, DH), lambda h: (h, 0, 0)),
        "s": pl.BlockSpec((rows, 1), lambda h: (0, 0)),
    }
    shapes = {"h": (rows, heads * DH), "m": (heads, DH, DH)}
    return pl.pallas_call(
        kernel,
        grid=(heads // step,),
        in_specs=[specs[kind] for kind in ins],
        out_specs=[specs[kind] for kind, unused in outs],
        out_shape=[jax.ShapeDtypeStruct(shapes[kind], dtype) for kind, dtype in outs],
        compiler_params=pltpu.CompilerParams(vmem_limit_bytes=VMEM_LIMIT),
        cost_estimate=pl.CostEstimate(
            flops=2 * macs * heads,
            bytes_accessed=rows * heads * DH * 2 * (len(ins) + len(outs)),
            transcendentals=0,
        ),
    )


def project_kernel(pieces, half, own_ref, other_ref, *refs):
    def fill(a_ref):
        for piece in range(pieces):
            refs[-1][piece] = dot(a_ref[...], refs[piece][...], NT).astype(BF16)

    pl.when(pl.program_id(0) < half)(lambda: fill(own_ref))
    pl.when(pl.program_id(0) >= half)(lambda: fill(other_ref))


def project(own, other, pieces):
    rows, width = own.shape
    features = pieces[0].shape[0]
    step = min(rows, 256)
    half = rows // step
    return pl.pallas_call(
        functools.partial(project_kernel, len(pieces), half),
        grid=(2 * half,),
        in_specs=[
            pl.BlockSpec((step, width), lambda r: (jnp.minimum(r, half - 1), 0)),
            pl.BlockSpec((step, width), lambda r: (jnp.maximum(r - half, 0), 0)),
        ]
        + [pl.BlockSpec((features, width), lambda r: (0, 0)) for unused in pieces],
        out_specs=pl.BlockSpec((len(pieces), step, features), lambda r: (0, r, 0)),
        out_shape=jax.ShapeDtypeStruct((len(pieces), 2 * rows, features), BF16),
        compiler_params=pltpu.CompilerParams(vmem_limit_bytes=VMEM_LIMIT),
        cost_estimate=pl.CostEstimate(
            flops=4 * rows * width * features * len(pieces),
            bytes_accessed=8 * rows * width,
            transcendentals=0,
        ),
    )(own, other, *pieces)


def products_kernel(count, chips, share, before, factor, meta_ref, *refs):
    candidates, (own_ref, other_ref), rest = refs[:count], refs[count : count + 2], refs[count + 2 :]
    pieces, rest = rest[:chips], rest[chips:]
    earlier, (first_ref, second_ref, grad_ref, total, weight_ref) = rest[:before], rest[before:]
    rows = own_ref.shape[0]
    part = weight_ref.shape[1]
    for delta, piece in enumerate(pieces):
        weight_ref[delta] = piece[...]
    if before:
        total[:rows] = earlier[0][...]
        total[rows:] = earlier[1][...]
    for j, candidate in enumerate(candidates):

        @pl.when(meta_ref[j * (share + 1)] == 1)
        def unused(j=j, candidate=candidate):
            for u in range(share):
                delta = meta_ref[j * (share + 1) + 1 + u]
                values = candidate[:, u * part : (u + 1) * part]
                product = dot(values, weight_ref[delta], NN)
                if j == 0 and u == 0 and not before:
                    total[...] = product
                else:
                    total[...] += product
                grad = dot(values[:rows], own_ref[...], TN) + dot(values[rows:], other_ref[...], TN)
                grad_ref[delta] = (grad * factor).astype(BF16)

    first_ref[...] = total[:rows]
    second_ref[...] = total[rows:].astype(second_ref.dtype)


def products(meta, candidates, own, other, weights, earlier, second_type, factor, share):
    rows, width = own.shape
    chips, part = len(weights), weights[0].shape[0]
    step = 256 if width % 256 == 0 else DH
    block = pl.BlockSpec((rows, step), lambda k, unused: (0, k))
    pieces = pl.BlockSpec((chips, part, step), lambda k, unused: (0, 0, k))
    return pl.pallas_call(
        functools.partial(products_kernel, len(candidates), chips, share, len(earlier), factor),
        grid_spec=pltpu.PrefetchScalarGridSpec(
            num_scalar_prefetch=1,
            grid=(width // step,),
            in_specs=[pl.BlockSpec(c.shape, lambda k, unused: (0, 0)) for c in candidates]
            + [block, block]
            + [pl.BlockSpec((part, step), lambda k, unused: (0, k)) for unused in weights]
            + [block for unused in earlier],
            out_specs=[block, block, pieces],
            scratch_shapes=[pltpu.VMEM((2 * rows, step), F32), pltpu.VMEM((chips, part, step), BF16)],
        ),
        out_shape=[
            jax.ShapeDtypeStruct((rows, width), F32),
            jax.ShapeDtypeStruct((rows, width), second_type),
            jax.ShapeDtypeStruct((chips, part, width), BF16),
        ],
        compiler_params=pltpu.CompilerParams(vmem_limit_bytes=2 * VMEM_LIMIT),
        cost_estimate=pl.CostEstimate(
            flops=8 * rows * width * part * chips,
            bytes_accessed=16 * rows * width,
            transcendentals=0,
        ),
    )(meta, *candidates, own, other, *weights, *earlier)


def core_swap(value):
    count = lax.axis_size("seq")
    return lax.ppermute(value, "seq", [(j, j ^ 1) for j in range(count)])


def chip_swap(value, delta):
    count = lax.axis_size("seq")
    return lax.ppermute(value, "seq", [(j, j ^ (2 * delta)) for j in range(count)])


def line_permutes(active):
    even = [pair for pair in active if min(pair) % 2 == 0]
    odd = [pair for pair in active if min(pair) % 2 == 1]
    return even, odd


def line_step(values, active):
    return [
        lax.ppermute(value, "head", pairs) if pairs else None
        for value, pairs in zip(values, line_permutes(active))
    ]


def line_sum(part_for, beside):
    count = lax.axis_size("head")
    mine = lax.axis_index("head")
    got = [None, None]
    for step in range(1, count):
        active = [(j, j + 1) for j in range(count - 1) if j <= step - 1]
        active += [(j, j - 1) for j in range(1, count) if count - 1 - j <= step - 1]
        values = []
        for parity, pairs in enumerate(line_permutes(active)):
            if not pairs:
                values.append(None)
                continue
            target = jnp.where(mine % 2 == parity, mine + count - step, mine - count + step)
            value = part_for(jnp.clip(target, 0, count - 1))
            if got[1 - parity] is not None:
                value = (value.astype(F32) + got[1 - parity].astype(F32)).astype(BF16)
            values.append(value)
        got = line_step(values, active)
        if beside.get(step):
            got, unused = lax.optimization_barrier((got, beside[step]))
    total = part_for(mine).astype(F32)
    for value in got:
        if value is not None:
            total = total + value.astype(F32)
    return total


def line_gather(value, tied):
    tied = dict(tied)
    count = lax.axis_size("head")
    mine = lax.axis_index("head")
    found, arrived = [(value, mine >= 0, mine)], {}
    got = [value, value]
    for step in range(1, count):
        active = [(j, j + 1) for j in range(count - 1) if j >= step - 1]
        active += [(j, j - 1) for j in range(1, count) if j + step - 1 <= count - 1]
        new = line_step([value if got[1 - q] is None else got[1 - q] for q in (0, 1)], active)
        if step in tied:
            new, tied[step] = lax.optimization_barrier((new, tied[step]))
        got = new
        arrived[step] = [item for item in got if item is not None]
        for parity, item in enumerate(got):
            if item is None:
                continue
            source = jnp.where(mine % 2 == parity, mine + step, mine - step)
            found.append((item, (source >= 0) & (source < count), source))
    return found, arrived, tied


def swapped_halves(total):
    core = lax.rem(lax.axis_index("seq"), 2)
    half_heads = total.shape[0] // 2
    mine = total.astype(BF16)
    other = core_swap(mine)
    both = mine.astype(F32) + other.astype(F32)
    half = lax.dynamic_slice_in_dim(both, core * half_heads, half_heads, 0).astype(BF16)
    return half, other


def sum_of_others(half, arrived, other, lower):
    position = lax.axis_index("seq")
    chip, core = lax.div(position, 2), lax.rem(position, 2)
    summed = jnp.zeros(half.shape, F32)
    for delta, item in enumerate(arrived, 1):
        partner = chip ^ delta
        counts = (partner < chip) if lower else (partner > chip)
        summed = summed + jnp.where(counts, item.astype(F32), 0.0)
    summed = summed.astype(BF16)
    swapped = core_swap(summed)
    first = jnp.where(core == 0, summed, swapped)
    second = jnp.where(core == 0, swapped, summed)
    whole = jnp.concatenate([first, second], axis=0).astype(F32)
    return whole + jnp.where(core == (1 if lower else 0), other.astype(F32), 0.0)


def near_pieces(own):
    chips = lax.axis_size("seq") // 2
    if chips != 4:
        pieces = [own] + [chip_swap(own, delta) for delta in range(1, chips)]
        return pieces[1:], lambda arrived: [own, *arrived]
    half = own.shape[0] // 2

    def rest(arrived):
        first = chip_swap(arrived[0][:half], 2)
        second = chip_swap(arrived[1][half:], 1)
        return [own, *arrived, jnp.concatenate([first, second], axis=0)]

    return [chip_swap(own, 1), chip_swap(own, 2)], rest


def scatter_start(grads):
    chips, part = grads.shape[:2]
    if chips != 4:
        sent = [chip_swap(grads[delta], delta) for delta in range(1, chips)]
        return sent, lambda arrived: (arrived, lambda final: added(grads[0], *final))
    half = part // 2
    upper, lower = slice(0, half), slice(half, part)
    sent = [chip_swap(grads[1::2, upper], 1), chip_swap(grads[2:, lower], 2)]

    def second(arrived):
        by_x, by_y = arrived
        upper_sum = added(grads[2, upper], by_x[1]).astype(BF16)
        lower_sum = added(grads[1, lower], by_y[1]).astype(BF16)

        def finish(final):
            return jnp.concatenate(
                [
                    added(grads[0, upper], by_x[0], final[0]),
                    added(grads[0, lower], by_y[0], final[1]),
                ],
                axis=0,
            )

        return [chip_swap(upper_sum, 2), chip_swap(lower_sum, 1)], finish

    return sent, second


def added(*values):
    return sum(value.astype(F32) for value in values)


def on_device(query_rows, key_rows, value_rows, out_weight, target_rows):
    rows, width = query_rows.shape
    heads = width // DH
    groups = lax.axis_size("head")
    seq_count = lax.axis_size("seq")
    chips = seq_count // 2
    share = chips // groups
    position = lax.axis_index("seq")
    chip, core = lax.div(position, 2), lax.rem(position, 2)
    held = out_weight.shape[0]
    part = held // CHUNKS
    call = functools.partial(per_head, rows=rows, heads=heads)
    barrier = lax.optimization_barrier
    outer = call(outer_kernel, ins="hh", outs=[("m", F32)], macs=rows * DH * DH, step=4)

    positions = (position * rows + jnp.arange(rows, dtype=jnp.int32) + 1).astype(F32)
    scale = lax.rsqrt(F32(DH) * positions)[:, None]
    (key_value,) = outer(key_rows, value_rows)
    half, other = swapped_halves(key_value)
    arrived = [chip_swap(half, delta) for delta in range(1, chips)]
    near, rest = near_pieces(out_weight[:part])
    scaled, intra = call(
        forward_kernel, ins="hhhs", outs=[("h", BF16), ("h", F32)], macs=2 * rows * rows * DH
    )(query_rows, key_rows, value_rows, scale)
    arrived, near, scaled, intra = barrier((arrived, near, scaled, intra))
    pieces = rest(near)
    before = sum_of_others(half, arrived, other, True)
    (attended,) = call(
        attended_kernel, ins="hhm", outs=[("h", BF16)], macs=2 * rows * DH * DH, step=4
    )(scaled, intra, before)
    other_attended = core_swap(attended)

    targets = target_rows.reshape(rows, share, 2, held)
    own_target = lax.dynamic_index_in_dim(targets, core, 2, keepdims=False)
    sent_target = lax.dynamic_index_in_dim(targets, 1 - core, 2, keepdims=False)
    both_targets = jnp.concatenate([own_target, core_swap(sent_target)], axis=0)

    outputs, grad_parts = [], []
    gate, totals, sent, gathered = None, (), None, {}
    factor = 1.0 / math.sqrt(rows * seq_count)
    for c in range(CHUNKS):
        last = c == CHUNKS - 1
        if c:
            own_rows, unused = barrier((out_weight[c * part : (c + 1) * part], pieces[-1]))
            near, rest = near_pieces(own_rows)
            pieces = rest(near)
        partial_out = project(attended, other_attended, pieces)
        if gate is not None:
            partial_out, gate, outputs[-1] = barrier((partial_out, gate, outputs[-1]))

        def part_for(group, partial_out=partial_out):
            found = [
                lax.dynamic_index_in_dim(partial_out, (group * share + j) ^ chip, 0, keepdims=False)
                for j in range(share)
            ]
            return found[0] if share == 1 else jnp.concatenate(found, axis=1)

        summed = line_sum(part_for, {step - 1: items for step, items in gathered.items() if step > 1}).astype(BF16)
        target = both_targets[:, :, c * part : (c + 1) * part].reshape(2 * rows, share * part)
        residual = (summed.astype(F32) - target.astype(F32)).astype(BF16)
        own_output = summed[:rows].reshape(rows, share, part)
        other_output = core_swap(summed[rows:]).reshape(rows, share, part)
        first = jnp.where(core == 0, own_output, other_output)
        second = jnp.where(core == 0, other_output, own_output)
        outputs.append(jnp.stack([first, second], axis=2))
        output = jnp.concatenate(outputs, axis=3).reshape(rows, width) if last else None
        found, gathered, tied = line_gather(
            residual, {1: totals, 2: (sent, output)}
        )
        totals, (sent, output) = tied[1], tied[2]
        gate = gathered[1]
        meta = []
        for unused, valid, source in found:
            meta.append(valid.astype(jnp.int32))
            meta += [
                jnp.clip((source * share + j) ^ chip, 0, chips - 1).astype(jnp.int32)
                for j in range(share)
            ]
        items = [item for item, unused, unused in found]
        if sent is not None:
            sent, finish = second_step(sent)
            items, sent = barrier((items, sent))
            grad_parts.append(finish(sent))
        *totals, grads = products(
            jnp.stack(meta),
            items,
            attended,
            other_attended,
            pieces,
            totals,
            BF16 if last else F32,
            factor,
            share,
        )
        sent, second_step = scatter_start(grads)

    grad_attended = (totals[0] + core_swap(totals[1]).astype(F32)).astype(BF16)
    (query_grad,) = outer(scaled, grad_attended)
    half, other = swapped_halves(query_grad)
    arrived = [chip_swap(half, delta) for delta in range(1, chips)]
    grad_query, key_part, value_part = call(
        backward_kernel,
        ins="hhhhsm",
        outs=[("h", BF16), ("h", F32), ("h", F32)],
        macs=5 * rows * rows * DH,
    )(scaled, key_rows, value_rows, grad_attended, scale, before)
    arrived, key_part, value_part, grad_query, sent = barrier(
        (arrived, key_part, value_part, grad_query, sent)
    )
    sent, finish = second_step(sent)
    after = sum_of_others(half, arrived, other, False)
    sent, after = barrier((sent, after))
    grad_key, grad_value = call(
        finish_kernel, ins="hhhhm", outs=[("h", BF16), ("h", BF16)], macs=4 * rows * DH * DH
    )(key_rows, value_rows, key_part, value_part, after)
    grad_weight = jnp.concatenate([*grad_parts, finish(sent)], axis=0)
    return output, grad_query, grad_key, grad_value, grad_weight


def solution(mesh):
    placed = P("seq", "head")
    return jax.shard_map(
        on_device,
        mesh=mesh,
        in_specs=(placed,) * 5,
        out_specs=(placed,) * 5,
        check_vma=False,
    )
```

time: 298 us -> 290 us (0.973)
  matrix products: 23.8 us -> 0 us
  local copies, waits for them, and re-layouts: 26.3 us -> 47.9 us
  Pallas kernels: 31.1 us -> 51.9 us
  waiting for transfers between devices: 108 us -> 89.1 us
  other arithmetic: 31.2 us -> 20.9 us
    pallas_call x2 -> x6, Pallas kernels: 4.97 us -> 33.8 us  [the longest x2 22.3 us: products(): pl.pallas_call(functools.partial(products_kernel, len(candidates), chips,...]
    dot_general x6 -> x0, matrix products: 23.8 us -> none  [dot(): return lax.dot_general(a, b, dims, preferred_element_type=F32)]
    ppermute x18 -> x22, waiting for transfers between devices: 56.9 us -> 40.3 us  [chip_swap(): lax.ppermute(value, 'seq', [(j, j ^ 2 * delta) for j in range(count)])]
    unnamed x70 -> x109, local copies, waits for them, and re-layouts: 12.7 us -> 28.7 us
    another operation x6 -> x0, other arithmetic: 6.56 us -> none  [on_device(): stacked = jnp.stack(pieces)]
    ppermute x18 -> x22, starting transfers between devices: 22.8 us -> 26.8 us  [chip_swap(): lax.ppermute(value, 'seq', [(j, j ^ 2 * delta) for j in range(count)])]
    slice x4 -> x7, local copies, waits for them, and re-layouts: 4.71 us -> 8.32 us  [the longest x2 2.81 us: rest(): first = chip_swap(arrived[0][:half], 2)]
  transfers between devices with their start and end apart: 47 -> 51, of which waited for: 20 -> 27; matrix products, arithmetic and copies ran while one was open for 22% -> 13% of each run, Pallas kernels for 7% -> 10%
where the time goes in v2:
time: 290 us; the launch traced here: 288 us
  waiting for transfers between devices  89.1 us (31%)
  starting transfers between devices  77 us (27%)
  Pallas kernels  51.9 us (18%)
  local copies, waits for them, and re-layouts  47.9 us (17%)
  other arithmetic  20.9 us (7%)
    ppermute x20, starting transfers between devices, line_step(): lax.ppermute(value, 'head', pairs)  49.1 us
    ppermute x20, waiting for transfers between devices, line_step(): lax.ppermute(value, 'head', pairs)  47.3 us
    ppermute x22, waiting for transfers between devices, chip_swap(): lax.ppermute(value, 'seq', [(j, j ^ 2 * delta) for j in range(count)])  40.3 us
    unnamed x109, local copies, waits for them, and re-layouts  28.7 us
    ppermute x22, starting transfers between devices, chip_swap(): lax.ppermute(value, 'seq', [(j, j ^ 2 * delta) for j in range(count)])  26.8 us
    pallas_call x2, Pallas kernels, products(): pl.pallas_call(functools.partial(products_kernel, len(candidates), chips,...  22.3 us
    pallas_call x2, Pallas kernels, project(): pl.pallas_call(functools.partial(project_kernel, len(pieces), half), grid...  9.78 us
    pallas_call x1, Pallas kernels, on_device(): call(backward_kernel, ins='hhhhsm', outs=[('h', BF16), ('h', F32), ('h',...  9.43 us
  transfers between devices with their start and end apart: 51, of which 27 were waited for; matrix products, arithmetic and copies ran while one was open for 13% of the time, Pallas kernels for 10%

profile of v2, /device:TPU:0, one launch (start us, length us, event | category | flops | bytes accessed | tf_op | source)
XLA Modules:
  0.0 288.2 jit_solution(12476575068869870547)
XLA Ops:
  5.6 2.7 collective-permute-start.5
  8.3 1.5 collective-permute-start.4
  10.6 2.0 collective-permute-start.2
  12.6 1.5 collective-permute-start.1
  15.4 4.1 %shard_map.93 = (bf16[512,1024]{1,0:T(8,128)(2,1)S(1)}, f32[512,1024]{1,0:T(8,128)S(1)}) custom-call(bf16[512,1024]{1,0:T(8,128)(2,1)S(1)} %copy-done.30, bf16[512,1024]{1,0:T(8,128)(2,1)S(1)} %copy-done.1, bf16[512,1024]{1,0:T(8,128)(2,1)S(1)} %copy-done.3, f32[512,1]{1,0:T(8,128)S(1)} %multiply_rsqrt_fusion.scale_ref), custom_call_target="tpu_custom_call" | custom-call | flops 1073741824 | bytes 6291456 | tf_op jit(solution)/shard_map/pallas_call | solution.py:368
  20.8 4.8 %collective-permute-done.3 = bf16[4,128,128]{2,1,0:T(8,128)(2,1)S(1)} collective-permute-done((bf16[4,128,128]{2,1,0:T(8,128)(2,1)}, bf16[4,128,128]{2,1,0:T(8,128)(2,1)S(1)}, u32[]{:S(2)}, u32[]{:S(2)}) %collective-permute-start.3) | collective-permute-done | bytes 131104 | tf_op jit(solution)/shard_map/ppermute | solution.py:209
  26.7 1.5 collective-permute-done.1
  31.7 1.6 copy-done.14
  37.2 1.8 collective-permute-start.9
  39.0 5.4 %collective-permute-done.8 = bf16[128,1024]{1,0:T(8,128)(2,1)S(1)} collective-permute-done((bf16[128,1024]{1,0:T(8,128)(2,1)S(1)}, bf16[128,1024]{1,0:T(8,128)(2,1)S(1)}, u32[]{:S(2)}, u32[]{:S(2)}) %collective-permute-start.8) | collective-permute-done | bytes 262176 | tf_op jit(solution)/shard_map/ppermute | solution.py:209
  46.9 5.0 %shard_map.96 = bf16[4,1024,256]{2,1,0:T(8,128)(2,1)S(1)} custom-call(bf16[512,1024]{1,0:T(8,128)(2,1)S(1)} %copy-done.16, bf16[512,1024]{1,0:T(8,128)(2,1)} %collective-permute-done.7.other_ref.refs_7_, bf16[256,1024]{1,0:T(8,128)(2,1)} %get-tuple-element.156.refs_0_.refs_8_, bf16[256,1024]{1,0:T(8,128)(2,1)} %collective-permute-done.4.refs_1_.refs_9_, ...), custom_call_target="tpu_custom_call" | custom-call | flops 2147483648 | bytes 4194304 | tf_op jit(solution)/shard_map/pallas_call | solution.py:121
  52.9 4.5 %collective-permute-start.14 = (bf16[1024,256]{1,0:T(8,128)(2,1)}, bf16[1024,256]{1,0:T(8,128)(2,1)}, u32[]{:S(2)}, u32[]{:S(2)}) collective-permute-start(bf16[1024,256]{1,0:T(8,128)(2,1)} %get-tuple-element.153), channel_id=1, source_target_pairs={{0,1},{3,2},{4,5},{7,6},{8,9},{11,10},{12,13},{15,14},{16,17},{19,... | collective-permute-start | bytes 1572872 | tf_op jit(solution)/shard_map/ppermute | solution.py:220
  57.4 2.2 collective-permute-start.17
  59.5 9.7 %collective-permute-done.14 = bf16[1024,256]{1,0:T(8,128)(2,1)} collective-permute-done((bf16[1024,256]{1,0:T(8,128)(2,1)}, bf16[1024,256]{1,0:T(8,128)(2,1)}, u32[]{:S(2)}, u32[]{:S(2)}) %collective-permute-start.14) | collective-permute-done | bytes 524320 | tf_op jit(solution)/shard_map/ppermute | solution.py:220
  69.3 2.0 fusion.8
  71.2 1.4 collective-permute-start.15
  72.7 2.6 reshape.97
  75.3 1.5 collective-permute-start.10
  76.8 4.7 %constant_dynamic-slice_fusion.1 = (bf16[512,1,1,512]{3,2,0,1:T(2,128)(2,1)}, bf16[512,1,1,512]{3,2,0,1:T(2,128)(2,1)S(1)}) fusion(bf16[512,1,2,512]{3,2,0,1:T(2,128)(2,1)} %reshape.97, s32[]{:T(128)S(6)} %select_n.231, s32[]{:T(128)S(6)} %select_n.232), kind=kLoop, calls=%fused_computation.72 | loop fusion | bytes 2097160 | tf_op jit(solution)/shard_map/jit(dynamic_index_in_dim)/dynamic_slice | solution.py:380
  82.5 1.5 collective-permute-start.11
  84.0 2.5 fusion.9
  86.5 4.5 %collective-permute-start.16 = (bf16[1024,256]{1,0:T(8,128)(2,1)}, bf16[1024,256]{1,0:T(8,128)(2,1)}, u32[]{:S(2)}, u32[]{:S(2)}) collective-permute-start(bf16[1024,256]{1,0:T(8,128)(2,1)} %get-tuple-element.151), channel_id=1, source_target_pairs={{0,1},{2,3},{1,0},{3,2},{4,5},{6,7},{5,4},{7,6},{8,9},{10,11},{9,8... | collective-permute-start | bytes 1572872 | tf_op jit(solution)/shard_map/ppermute | solution.py:220
  91.0 1.5 collective-permute-start.18
  92.5 1.7 slice.128
  94.7 2.1 copy.26
  98.7 4.0 %collective-permute-done.12 = bf16[128,1024]{1,0:T(8,128)(2,1)} collective-permute-done((bf16[128,1024]{1,0:T(8,128)(2,1)}, bf16[128,1024]{1,0:T(8,128)(2,1)}, u32[]{:S(2)}, u32[]{:S(2)}) %collective-permute-start.12) | collective-permute-done | bytes 262176 | tf_op jit(solution)/shard_map/ppermute | solution.py:209
  103.7 1.8 fusion.6
  106.8 6.3 %collective-permute-start.20 = (bf16[1024,256]{1,0:T(8,128)(2,1)S(1)}, bf16[1024,256]{1,0:T(8,128)(2,1)S(1)}, u32[]{:S(2)}, u32[]{:S(2)}) collective-permute-start(bf16[1024,256]{1,0:T(8,128)(2,1)S(1)} %get-tuple-element.133.refs_0_), channel_id=1, source_target_pairs={{0,1},{2,3},{1,0},{3,2},{4,5},{6,7},{5,4},{7,6},{8,9},{10,11},{9,8... | collective-permute-start | bytes 1572872 | tf_op jit(solution)/shard_map/ppermute | solution.py:220
  113.1 4.8 %shard_map.95 = bf16[4,1024,256]{2,1,0:T(8,128)(2,1)S(1)} custom-call(bf16[512,1024]{1,0:T(8,128)(2,1)S(1)} %copy-done.17, bf16[512,1024]{1,0:T(8,128)(2,1)} %collective-permute-done.7.other_ref.refs_7_, bf16[256,1024]{1,0:T(8,128)(2,1)S(1)} %copy-done.20, bf16[256,1024]{1,0:T(8,128)(2,1)} %collective-permute-done.10.refs_1_.refs_9_, ...), custom_call_target="tpu_custom_call" | custom-call | flops 2147483648 | bytes 4194304 | tf_op jit(solution)/shard_map/pallas_call | solution.py:121
  118.9 6.0 %collective-permute-done.20.refs_1_ = bf16[1024,256]{1,0:T(8,128)(2,1)S(1)} collective-permute-done((bf16[1024,256]{1,0:T(8,128)(2,1)S(1)}, bf16[1024,256]{1,0:T(8,128)(2,1)S(1)}, u32[]{:S(2)}, u32[]{:S(2)}) %collective-permute-start.20) | collective-permute-done | bytes 524320 | tf_op jit(solution)/shard_map/ppermute | solution.py:220
  127.0 6.5 %collective-permute-start.24 = (bf16[1024,256]{1,0:T(8,128)(2,1)S(1)}, bf16[1024,256]{1,0:T(8,128)(2,1)S(1)}, u32[]{:S(2)}, u32[]{:S(2)}) collective-permute-start(bf16[1024,256]{1,0:T(8,128)(2,1)S(1)} %get-tuple-element.149), channel_id=1, source_target_pairs={{0,1},{3,2},{4,5},{7,6},{8,9},{11,10},{12,13},{15,14},{16,17},{19,... | collective-permute-start | bytes 1572872 | tf_op jit(solution)/shard_map/ppermute | solution.py:220
  134.9 7.3 %collective-permute-done.25.refs_3_ = bf16[1024,256]{1,0:T(8,128)(2,1)S(1)} collective-permute-done((bf16[1024,256]{1,0:T(8,128)(2,1)S(1)}, bf16[1024,256]{1,0:T(8,128)(2,1)S(1)}, u32[]{:S(2)}, u32[]{:S(2)}) %collective-permute-start.25) | collective-permute-done | bytes 524320 | tf_op jit(solution)/shard_map/ppermute | solution.py:220
  142.1 1.5 collective-permute-start.28
  143.6 2.3 collective-permute-done.24
  146.7 8.0 %collective-permute-done.23 = bf16[1024,256]{1,0:T(8,128)(2,1)S(1)} collective-permute-done((bf16[1024,256]{1,0:T(8,128)(2,1)S(1)}, bf16[1024,256]{1,0:T(8,128)(2,1)S(1)}, u32[]{:S(2)}, u32[]{:S(2)}) %collective-permute-start.23) | collective-permute-done | bytes 524320 | tf_op jit(solution)/shard_map/ppermute | solution.py:220
  157.1 4.1 %collective-permute-start.29 = (bf16[1024,256]{1,0:T(8,128)(2,1)}, bf16[1024,256]{1,0:T(8,128)(2,1)}, u32[]{:S(2)}, u32[]{:S(2)}) collective-permute-start(bf16[1024,256]{1,0:T(8,128)(2,1)} %get-tuple-element.147), channel_id=1, source_target_pairs={{0,1},{2,3},{1,0},{3,2},{4,5},{6,7},{5,4},{7,6},{8,9},{10,11},{9,8... | collective-permute-start | bytes 1572872 | tf_op jit(solution)/shard_map/ppermute | solution.py:220
  161.2 1.5 collective-permute-start.30
  162.8 5.8 %collective-permute-done.29 = bf16[1024,256]{1,0:T(8,128)(2,1)} collective-permute-done((bf16[1024,256]{1,0:T(8,128)(2,1)}, bf16[1024,256]{1,0:T(8,128)(2,1)}, u32[]{:S(2)}, u32[]{:S(2)}) %collective-permute-start.29) | collective-permute-done | bytes 524320 | tf_op jit(solution)/shard_map/ppermute | solution.py:220
  168.6 1.6 fusion
  170.3 1.5 collective-permute-start.32
  171.8 5.0 %collective-permute-start.31 = (bf16[1024,256]{1,0:T(8,128)(2,1)S(1)}, bf16[1024,256]{1,0:T(8,128)(2,1)}, u32[]{:S(2)}, u32[]{:S(2)}) collective-permute-start(bf16[1024,256]{1,0:T(8,128)(2,1)S(1)} %get-tuple-element.92.refs_0_), channel_id=1, source_target_pairs={{0,1},{2,3},{1,0},{3,2},{4,5},{6,7},{5,4},{7,6},{8,9},{10,11},{9,8... | collective-permute-start | bytes 1572872 | tf_op jit(solution)/shard_map/ppermute | solution.py:220
  178.9 10.3 %shard_map.97 = (f32[512,1024]{1,0:T(8,128)S(1)}, f32[512,1024]{1,0:T(8,128)S(1)}, bf16[4,256,1024]{2,1,0:T(8,128)(2,1)S(1)}) custom-call(s32[12]{0:T(128)S(1)} %stack.109.meta_ref, bf16[1024,256]{1,0:T(8,128)(2,1)S(1)} %copy-done.23, bf16[1024,256]{1,0:T(8,128)(2,1)S(1)} %copy-done.34, bf16[1024,256]{1,0:T(8,128)(2,1)S(1)} %copy-done.32, ...), custom_call_target="tpu_custom_call" | custom-call | flops 4294967296 | bytes 8388608 | tf_op jit(solution)/shard_map/pallas_call | solution.py:176
  191.8 1.5 collective-permute-start.36
  195.1 1.5 collective-permute-start.34
  197.7 2.3 copy.19
  200.0 6.5 %collective-permute-done.36 = bf16[2,128,1024]{2,1,0:T(8,128)(2,1)} collective-permute-done((bf16[2,128,1024]{2,1,0:T(8,128)(2,1)}, bf16[2,128,1024]{2,1,0:T(8,128)(2,1)}, u32[]{:S(2)}, u32[]{:S(2)}) %collective-permute-start.36) | collective-permute-done | bytes 524320 | tf_op jit(solution)/shard_map/ppermute | solution.py:209
  207.7 2.1 collective-permute-done.33.refs_3_
  212.3 1.6 collective-permute-start.40
  214.4 5.3 %collective-permute-done.40 = bf16[128,1024]{1,0:T(8,128)(2,1)S(1)} collective-permute-done((bf16[128,1024]{1,0:T(8,128)(2,1)S(1)}, bf16[128,1024]{1,0:T(8,128)(2,1)S(1)}, u32[]{:S(2)}, u32[]{:S(2)}) %collective-permute-start.40) | collective-permute-done | bytes 262176 | tf_op jit(solution)/shard_map/ppermute | solution.py:209
  221.7 5.0 %collective-permute-done.38.refs_5_ = bf16[1024,256]{1,0:T(8,128)(2,1)S(1)} collective-permute-done((bf16[1024,256]{1,0:T(8,128)(2,1)}, bf16[1024,256]{1,0:T(8,128)(2,1)S(1)}, u32[]{:S(2)}, u32[]{:S(2)}) %collective-permute-start.38) | collective-permute-done | bytes 524320 | tf_op jit(solution)/shard_map/ppermute | solution.py:220
  231.0 1.6 copy-done.42
  232.6 1.6 copy-done.44
  234.2 11.9 %shard_map.98 = (f32[512,1024]{1,0:T(8,128)S(1)}, bf16[512,1024]{1,0:T(8,128)(2,1)}, bf16[4,256,1024]{2,1,0:T(8,128)(2,1)S(1)}) custom-call(s32[12]{0:T(128)S(1)} %stack.109.meta_ref, bf16[1024,256]{1,0:T(8,128)(2,1)S(1)} %copy-done.25, bf16[1024,256]{1,0:T(8,128)(2,1)} %collective-permute-done.31.refs_1_, ...), custom_call_target="tpu_custom_call" | custom-call | flops 4294967296 | bytes 8388608 | tf_op jit(solution)/shard_map/pallas_call | solution.py:176
  248.7 2.3 copy.20
  253.0 1.5 collective-permute-start.46
  254.5 1.7 add_convert_fusion.b_ref.g_ref
  258.9 1.5 collective-permute-start.45
  260.9 1.5 collective-permute-start.43
  262.5 9.4 %shard_map.100 = (bf16[512,1024]{1,0:T(8,128)(2,1)}, f32[512,1024]{1,0:T(8,128)S(1)}, f32[512,1024]{1,0:T(8,128)S(1)}) custom-call(bf16[512,1024]{1,0:T(8,128)(2,1)S(1)} %copy-done.6, bf16[512,1024]{1,0:T(8,128)(2,1)S(1)} %copy-done.1, bf16[512,1024]{1,0:T(8,128)(2,1)S(1)} %copy-done.4, bf16[512,1024]{1,0:T(8,128)(2,1)S(1)} %add_convert_fusion.b_ref.g_ref, ...), custom_call_target="tpu_custom_call" | custom-call | flops 2684354560 | bytes 9437184 | tf_op jit(solution)/shard_map/pallas_call | solution.py:447
  273.1 1.6 collective-permute-start.49
  274.6 1.5 collective-permute-start.48
  276.3 5.6 %collective-permute-done.49 = bf16[128,1024]{1,0:T(8,128)(2,1)S(1)} collective-permute-done((bf16[128,1024]{1,0:T(8,128)(2,1)S(1)}, bf16[128,1024]{1,0:T(8,128)(2,1)S(1)}, u32[]{:S(2)}, u32[]{:S(2)}) %collective-permute-start.49) | collective-permute-done | bytes 262176 | tf_op jit(solution)/shard_map/ppermute | solution.py:209
  283.3 3.4 %shard_map.101 = (bf16[512,1024]{1,0:T(8,128)(2,1)}, bf16[512,1024]{1,0:T(8,128)(2,1)}) custom-call(bf16[512,1024]{1,0:T(8,128)(2,1)S(1)} %copy-done.1, bf16[512,1024]{1,0:T(8,128)(2,1)S(1)} %copy-done.4, f32[512,1024]{1,0:T(8,128)S(1)} %get-tuple-element.107.dk_part_ref, f32[512,1024]{1,0:T(8,128)S(1)} %get-tuple-element.108.dv_part_ref, ...), custom_call_target="tpu_custom_call" | custom-call | flops 536870912 | bytes 7340032 | tf_op jit(solution)/shard_map/pallas_call | solution.py:459
  286.7 1.6 pad_maximum_fusion
  (203 shorter events, 62.0 us)
Async XLA Ops:
  4.0 5.8 %collective-permute-start = (bf16[8,128,128]{2,1,0:T(8,128)(2,1)S(1)}, bf16[8,128,128]{2,1,0:T(8,128)(2,1)S(1)}, u32[]{:S(2)}, u32[]{:S(2)}) collective-permute-start(bf16[8,128,128]{2,1,0:T(8,128)(2,1)S(1)} %convert_element_type.310), channel_id=1, source_target_pairs={{0,4},{4,0},{8,12},{12,8},{16,20},{20,16},{24,28},{28,24},{1,5},{5... | collective-permute-start | bytes 786440 | tf_op jit(solution)/shard_map/ppermute | solution.py:204
  5.6 22.5 %collective-permute-start.5 = (bf16[256,1024]{1,0:T(8,128)(2,1)}, bf16[256,1024]{1,0:T(8,128)(2,1)}, u32[]{:S(2)}, u32[]{:S(2)}) collective-permute-start(bf16[256,1024]{1,0:T(8,128)(2,1)} %get-tuple-element.156.refs_0_.refs_8_), channel_id=1, source_target_pairs={{0,16},{4,20},{8,24},{12,28},{16,0},{20,4},{24,8},{28,12},{1,17},{... | collective-permute-start | bytes 1572872 | tf_op jit(solution)/shard_map/ppermute | solution.py:209
  8.3 19.8 %collective-permute-start.4 = (bf16[256,1024]{1,0:T(8,128)(2,1)}, bf16[256,1024]{1,0:T(8,128)(2,1)}, u32[]{:S(2)}, u32[]{:S(2)}) collective-permute-start(bf16[256,1024]{1,0:T(8,128)(2,1)} %get-tuple-element.156.refs_0_.refs_8_), channel_id=1, source_target_pairs={{0,8},{4,12},{8,0},{12,4},{16,24},{20,28},{24,16},{28,20},{1,9},{5... | collective-permute-start | bytes 1572872 | tf_op jit(solution)/shard_map/ppermute | solution.py:209
  10.6 15.0 %collective-permute-start.3 = (bf16[4,128,128]{2,1,0:T(8,128)(2,1)}, bf16[4,128,128]{2,1,0:T(8,128)(2,1)S(1)}, u32[]{:S(2)}, u32[]{:S(2)}) collective-permute-start(bf16[4,128,128]{2,1,0:T(8,128)(2,1)} %fusion.20), channel_id=1, source_target_pairs={{0,24},{4,28},{8,16},{12,20},{16,8},{20,12},{24,0},{28,4},{1,25},{... | collective-permute-start | bytes 393224 | tf_op jit(solution)/shard_map/ppermute | solution.py:209
  10.6 16.1 %collective-permute-start.2 = (bf16[4,128,128]{2,1,0:T(8,128)(2,1)}, bf16[4,128,128]{2,1,0:T(8,128)(2,1)}, u32[]{:S(2)}, u32[]{:S(2)}) collective-permute-start(bf16[4,128,128]{2,1,0:T(8,128)(2,1)} %fusion.20), channel_id=1, source_target_pairs={{0,16},{4,20},{8,24},{12,28},{16,0},{20,4},{24,8},{28,12},{1,17},{... | collective-permute-start | bytes 393224 | tf_op jit(solution)/shard_map/ppermute | solution.py:209
  12.6 15.6 %collective-permute-start.1 = (bf16[4,128,128]{2,1,0:T(8,128)(2,1)}, bf16[4,128,128]{2,1,0:T(8,128)(2,1)}, u32[]{:S(2)}, u32[]{:S(2)}) collective-permute-start(bf16[4,128,128]{2,1,0:T(8,128)(2,1)} %fusion.20), channel_id=1, source_target_pairs={{0,8},{4,12},{8,0},{12,4},{16,24},{20,28},{24,16},{28,20},{1,9},{5... | collective-permute-start | bytes 393224 | tf_op jit(solution)/shard_map/ppermute | solution.py:209
  20.8 13.7 %copy-start.5 = (bf16[512,1024]{1,0:T(8,128)(2,1)}, bf16[512,1024]{1,0:T(8,128)(2,1)S(1)}, u32[]{:S(2)}) copy-start(bf16[512,1024]{1,0:T(8,128)(2,1)S(1)} %get-tuple-element.65.scaled_ref.a_ref) | copy-start | bytes 3145732
  29.2 1.4 collective-permute-start.6
  34.5 10.9 %collective-permute-start.7 = (bf16[512,1024]{1,0:T(8,128)(2,1)S(1)}, bf16[512,1024]{1,0:T(8,128)(2,1)}, u32[]{:S(2)}, u32[]{:S(2)}) collective-permute-start(bf16[512,1024]{1,0:T(8,128)(2,1)S(1)} %shard_map.94.own_ref.refs_6_), channel_id=1, source_target_pairs={{0,4},{4,0},{8,12},{12,8},{16,20},{20,16},{24,28},{28,24},{1,5},{5... | collective-permute-start | bytes 3145736 | tf_op jit(solution)/shard_map/ppermute | solution.py:204
  35.9 8.5 %collective-permute-start.8 = (bf16[128,1024]{1,0:T(8,128)(2,1)S(1)}, bf16[128,1024]{1,0:T(8,128)(2,1)S(1)}, u32[]{:S(2)}, u32[]{:S(2)}) collective-permute-start(bf16[128,1024]{1,0:T(8,128)(2,1)S(1)} %slice.98), channel_id=1, source_target_pairs={{0,16},{4,20},{8,24},{12,28},{16,0},{20,4},{24,8},{28,12},{1,17},{... | collective-permute-start | bytes 786440 | tf_op jit(solution)/shard_map/ppermute | solution.py:209
  37.2 8.2 %collective-permute-start.9 = (bf16[128,1024]{1,0:T(8,128)(2,1)S(1)}, bf16[128,1024]{1,0:T(8,128)(2,1)S(1)}, u32[]{:S(2)}, u32[]{:S(2)}) collective-permute-start(bf16[128,1024]{1,0:T(8,128)(2,1)S(1)} %slice.99), channel_id=1, source_target_pairs={{0,8},{4,12},{8,0},{12,4},{16,24},{20,28},{24,16},{28,20},{1,9},{5... | collective-permute-start | bytes 786440 | tf_op jit(solution)/shard_map/ppermute | solution.py:209
  52.9 16.4 %collective-permute-start.14 = (bf16[1024,256]{1,0:T(8,128)(2,1)}, bf16[1024,256]{1,0:T(8,128)(2,1)}, u32[]{:S(2)}, u32[]{:S(2)}) collective-permute-start(bf16[1024,256]{1,0:T(8,128)(2,1)} %get-tuple-element.153), channel_id=1, source_target_pairs={{0,1},{3,2},{4,5},{7,6},{8,9},{11,10},{12,13},{15,14},{16,17},{19,... | collective-permute-start | bytes 1572872 | tf_op jit(solution)/shard_map/ppermute | solution.py:220
  57.4 26.6 %collective-permute-start.17 = (bf16[1024,256]{1,0:T(8,128)(2,1)}, bf16[1024,256]{1,0:T(8,128)(2,1)}, u32[]{:S(2)}, u32[]{:S(2)}) collective-permute-start(bf16[1024,256]{1,0:T(8,128)(2,1)} %get-tuple-element.154), channel_id=1, source_target_pairs={{0,1},{3,2},{4,5},{7,6},{8,9},{11,10},{12,13},{15,14},{16,17},{19,... | collective-permute-start | bytes 1572872 | tf_op jit(solution)/shard_map/ppermute | solution.py:220
  71.2 12.7 %collective-permute-start.15 = (bf16[1024,256]{1,0:T(8,128)(2,1)}, bf16[1024,256]{1,0:T(8,128)(2,1)}, u32[]{:S(2)}, u32[]{:S(2)}) collective-permute-start(bf16[1024,256]{1,0:T(8,128)(2,1)} %fusion.8), channel_id=1, source_target_pairs={{1,2},{2,1},{5,6},{6,5},{9,10},{10,9},{13,14},{14,13},{17,18},{18,... | collective-permute-start | bytes 1572872 | tf_op jit(solution)/shard_map/ppermute | solution.py:220
  75.3 17.2 %collective-permute-start.10 = (bf16[256,1024]{1,0:T(8,128)(2,1)}, bf16[256,1024]{1,0:T(8,128)(2,1)}, u32[]{:S(2)}, u32[]{:S(2)}) collective-permute-start(bf16[256,1024]{1,0:T(8,128)(2,1)} %get-tuple-element.72.refs_0_.refs_8_), channel_id=1, source_target_pairs={{0,8},{4,12},{8,0},{12,4},{16,24},{20,28},{24,16},{28,20},{1,9},{5... | collective-permute-start | bytes 1572872 | tf_op jit(solution)/shard_map/ppermute | solution.py:209
  82.4 21.2 %collective-permute-start.19 = (bf16[512,1,512]{2,0,1:T(8,128)(2,1)}, bf16[512,1,512]{2,0,1:T(8,128)(2,1)}, u32[]{:S(2)}, u32[]{:S(2)}) collective-permute-start(bf16[512,1,512]{2,0,1:T(8,128)(2,1)} %bitcast.85), channel_id=1, source_target_pairs={{0,4},{4,0},{8,12},{12,8},{16,20},{20,16},{24,28},{28,24},{1,5},{5... | collective-permute-start | bytes 1572872 | tf_op jit(solution)/shard_map/ppermute | solution.py:204
  82.5 14.7 %collective-permute-start.11 = (bf16[256,1024]{1,0:T(8,128)(2,1)}, bf16[256,1024]{1,0:T(8,128)(2,1)}, u32[]{:S(2)}, u32[]{:S(2)}) collective-permute-start(bf16[256,1024]{1,0:T(8,128)(2,1)} %get-tuple-element.72.refs_0_.refs_8_), channel_id=1, source_target_pairs={{0,16},{4,20},{8,24},{12,28},{16,0},{20,4},{24,8},{28,12},{1,17},{... | collective-permute-start | bytes 1572872 | tf_op jit(solution)/shard_map/ppermute | solution.py:209
  86.5 17.2 %collective-permute-start.16 = (bf16[1024,256]{1,0:T(8,128)(2,1)}, bf16[1024,256]{1,0:T(8,128)(2,1)}, u32[]{:S(2)}, u32[]{:S(2)}) collective-permute-start(bf16[1024,256]{1,0:T(8,128)(2,1)} %get-tuple-element.151), channel_id=1, source_target_pairs={{0,1},{2,3},{1,0},{3,2},{4,5},{6,7},{5,4},{7,6},{8,9},{10,11},{9,8... | collective-permute-start | bytes 1572872 | tf_op jit(solution)/shard_map/ppermute | solution.py:220
  91.0 12.7 %collective-permute-start.18 = (bf16[1024,256]{1,0:T(8,128)(2,1)}, bf16[1024,256]{1,0:T(8,128)(2,1)}, u32[]{:S(2)}, u32[]{:S(2)}) collective-permute-start(bf16[1024,256]{1,0:T(8,128)(2,1)} %get-tuple-element.152), channel_id=1, source_target_pairs={{1,2},{2,1},{5,6},{6,5},{9,10},{10,9},{13,14},{14,13},{17,18},{18,... | collective-permute-start | bytes 1572872 | tf_op jit(solution)/shard_map/ppermute | solution.py:220
  94.2 8.5 %collective-permute-start.12 = (bf16[128,1024]{1,0:T(8,128)(2,1)}, bf16[128,1024]{1,0:T(8,128)(2,1)}, u32[]{:S(2)}, u32[]{:S(2)}) collective-permute-start(bf16[128,1024]{1,0:T(8,128)(2,1)} %slice.128), channel_id=1, source_target_pairs={{0,16},{4,20},{8,24},{12,28},{16,0},{20,4},{24,8},{28,12},{1,17},{... | collective-permute-start | bytes 786440 | tf_op jit(solution)/shard_map/ppermute | solution.py:209
  98.1 8.0 %collective-permute-start.13 = (bf16[128,1024]{1,0:T(8,128)(2,1)S(1)}, bf16[128,1024]{1,0:T(8,128)(2,1)S(1)}, u32[]{:S(2)}, u32[]{:S(2)}) collective-permute-start(bf16[128,1024]{1,0:T(8,128)(2,1)S(1)} %slice.129), channel_id=1, source_target_pairs={{0,8},{4,12},{8,0},{12,4},{16,24},{20,28},{24,16},{28,20},{1,9},{5... | collective-permute-start | bytes 786440 | tf_op jit(solution)/shard_map/ppermute | solution.py:209
  105.5 12.4 %collective-permute-start.22 = (bf16[512,256]{1,0:T(8,128)(2,1)S(1)}, bf16[512,256]{1,0:T(8,128)(2,1)S(1)}, u32[]{:S(2)}, u32[]{:S(2)}) collective-permute-start(bf16[512,256]{1,0:T(8,128)(2,1)S(1)} %slice.133), channel_id=1, source_target_pairs={{0,4},{4,0},{8,12},{12,8},{16,20},{20,16},{24,28},{28,24},{1,5},{5... | collective-permute-start | bytes 786440 | tf_op jit(solution)/shard_map/ppermute | solution.py:204
  106.1 12.8 %collective-permute-start.21 = (bf16[1024,256]{1,0:T(8,128)(2,1)S(1)}, bf16[1024,256]{1,0:T(8,128)(2,1)S(1)}, u32[]{:S(2)}, u32[]{:S(2)}) collective-permute-start(bf16[1024,256]{1,0:T(8,128)(2,1)S(1)} %get-tuple-element.133.refs_0_), channel_id=1, source_target_pairs={{1,2},{2,1},{5,6},{6,5},{9,10},{10,9},{13,14},{14,13},{17,18},{18,... | collective-permute-start | bytes 1572872 | tf_op jit(solution)/shard_map/ppermute | solution.py:220
  106.8 18.1 %collective-permute-start.20 = (bf16[1024,256]{1,0:T(8,128)(2,1)S(1)}, bf16[1024,256]{1,0:T(8,128)(2,1)S(1)}, u32[]{:S(2)}, u32[]{:S(2)}) collective-permute-start(bf16[1024,256]{1,0:T(8,128)(2,1)S(1)} %get-tuple-element.133.refs_0_), channel_id=1, source_target_pairs={{0,1},{2,3},{1,0},{3,2},{4,5},{6,7},{5,4},{7,6},{8,9},{10,11},{9,8... | collective-permute-start | bytes 1572872 | tf_op jit(solution)/shard_map/ppermute | solution.py:220
  118.9 38.2 %copy-start.31 = (bf16[1024,256]{1,0:T(8,128)(2,1)}, bf16[1024,256]{1,0:T(8,128)(2,1)S(1)}, u32[]{:S(2)}) copy-start(bf16[1024,256]{1,0:T(8,128)(2,1)S(1)} %collective-permute-done.21.refs_2_) | copy-start | bytes 1572868
  124.9 32.2 %copy-start.33 = (bf16[1024,256]{1,0:T(8,128)(2,1)}, bf16[1024,256]{1,0:T(8,128)(2,1)S(1)}, u32[]{:S(2)}) copy-start(bf16[1024,256]{1,0:T(8,128)(2,1)S(1)} %collective-permute-done.20.refs_1_) | copy-start | bytes 1572868
  124.9 9.9 %collective-permute-start.26 = (bf16[1024,256]{1,0:T(8,128)(2,1)S(1)}, bf16[1024,256]{1,0:T(8,128)(2,1)S(1)}, u32[]{:S(2)}, u32[]{:S(2)}) collective-permute-start(bf16[1024,256]{1,0:T(8,128)(2,1)S(1)} %collective-permute-done.20.refs_1_), channel_id=1, source_target_pairs={{1,2},{2,1},{5,6},{6,5},{9,10},{10,9},{13,14},{14,13},{17,18},{18,... | collective-permute-start | bytes 1572872 | tf_op jit(solution)/shard_map/ppermute | solution.py:220
  125.6 16.5 %collective-permute-start.25 = (bf16[1024,256]{1,0:T(8,128)(2,1)S(1)}, bf16[1024,256]{1,0:T(8,128)(2,1)S(1)}, u32[]{:S(2)}, u32[]{:S(2)}) collective-permute-start(bf16[1024,256]{1,0:T(8,128)(2,1)S(1)} %collective-permute-done.21.refs_2_), channel_id=1, source_target_pairs={{2,3},{1,0},{6,7},{5,4},{10,11},{9,8},{14,15},{13,12},{18,19},{17,... | collective-permute-start | bytes 1572872 | tf_op jit(solution)/shard_map/ppermute | solution.py:220
  127.0 18.8 %collective-permute-start.24 = (bf16[1024,256]{1,0:T(8,128)(2,1)S(1)}, bf16[1024,256]{1,0:T(8,128)(2,1)S(1)}, u32[]{:S(2)}, u32[]{:S(2)}) collective-permute-start(bf16[1024,256]{1,0:T(8,128)(2,1)S(1)} %get-tuple-element.149), channel_id=1, source_target_pairs={{0,1},{3,2},{4,5},{7,6},{8,9},{11,10},{12,13},{15,14},{16,17},{19,... | collective-permute-start | bytes 1572872 | tf_op jit(solution)/shard_map/ppermute | solution.py:220
  133.5 21.1 %collective-permute-start.23 = (bf16[1024,256]{1,0:T(8,128)(2,1)S(1)}, bf16[1024,256]{1,0:T(8,128)(2,1)S(1)}, u32[]{:S(2)}, u32[]{:S(2)}) collective-permute-start(bf16[1024,256]{1,0:T(8,128)(2,1)S(1)} %get-tuple-element.150), channel_id=1, source_target_pairs={{0,1},{3,2},{4,5},{7,6},{8,9},{11,10},{12,13},{15,14},{16,17},{19,... | collective-permute-start | bytes 1572872 | tf_op jit(solution)/shard_map/ppermute | solution.py:220
  134.8 22.2 %copy-start.35 = (bf16[1024,256]{1,0:T(8,128)(2,1)}, bf16[1024,256]{1,0:T(8,128)(2,1)S(1)}, u32[]{:S(2)}) copy-start(bf16[1024,256]{1,0:T(8,128)(2,1)S(1)} %collective-permute-done.26.refs_4_) | copy-start | bytes 1572868
  142.1 15.0 %copy-start.37 = (bf16[1024,256]{1,0:T(8,128)(2,1)}, bf16[1024,256]{1,0:T(8,128)(2,1)S(1)}, u32[]{:S(2)}) copy-start(bf16[1024,256]{1,0:T(8,128)(2,1)S(1)} %collective-permute-done.25.refs_3_) | copy-start | bytes 1572868
  142.1 13.7 %collective-permute-start.28 = (bf16[1024,256]{1,0:T(8,128)(2,1)S(1)}, bf16[1024,256]{1,0:T(8,128)(2,1)S(1)}, u32[]{:S(2)}, u32[]{:S(2)}) collective-permute-start(bf16[1024,256]{1,0:T(8,128)(2,1)S(1)} %collective-permute-done.26.refs_4_), channel_id=1, source_target_pairs={{2,3},{1,0},{6,7},{5,4},{10,11},{9,8},{14,15},{13,12},{18,19},{17,... | collective-permute-start | bytes 1572872 | tf_op jit(solution)/shard_map/ppermute | solution.py:220
  146.0 9.8 %collective-permute-start.27 = (bf16[1024,256]{1,0:T(8,128)(2,1)S(1)}, bf16[1024,256]{1,0:T(8,128)(2,1)S(1)}, u32[]{:S(2)}, u32[]{:S(2)}) collective-permute-start(bf16[1024,256]{1,0:T(8,128)(2,1)S(1)} %fusion.2), channel_id=1, source_target_pairs={{1,2},{2,1},{5,6},{6,5},{9,10},{10,9},{13,14},{14,13},{17,18},{18,... | collective-permute-start | bytes 1572872 | tf_op jit(solution)/shard_map/ppermute | solution.py:220
  157.1 11.5 %collective-permute-start.29 = (bf16[1024,256]{1,0:T(8,128)(2,1)}, bf16[1024,256]{1,0:T(8,128)(2,1)}, u32[]{:S(2)}, u32[]{:S(2)}) collective-permute-start(bf16[1024,256]{1,0:T(8,128)(2,1)} %get-tuple-element.147), channel_id=1, source_target_pairs={{0,1},{2,3},{1,0},{3,2},{4,5},{6,7},{5,4},{7,6},{8,9},{10,11},{9,8... | collective-permute-start | bytes 1572872 | tf_op jit(solution)/shard_map/ppermute | solution.py:220
  161.2 7.5 %collective-permute-start.30 = (bf16[1024,256]{1,0:T(8,128)(2,1)}, bf16[1024,256]{1,0:T(8,128)(2,1)}, u32[]{:S(2)}, u32[]{:S(2)}) collective-permute-start(bf16[1024,256]{1,0:T(8,128)(2,1)} %get-tuple-element.148), channel_id=1, source_target_pairs={{1,2},{2,1},{5,6},{6,5},{9,10},{10,9},{13,14},{14,13},{17,18},{18,... | collective-permute-start | bytes 1572872 | tf_op jit(solution)/shard_map/ppermute | solution.py:220
  162.7 14.1 %copy-start.18 = (bf16[512,1024]{1,0:T(8,128)(2,1)S(1)}, bf16[512,1024]{1,0:T(8,128)(2,1)}, u32[]{:S(2)}) copy-start(bf16[512,1024]{1,0:T(8,128)(2,1)} %copy-done.15) | copy-start | bytes 3145732
  162.8 14.1 %copy-start.23 = (bf16[1024,256]{1,0:T(8,128)(2,1)S(1)}, bf16[1024,256]{1,0:T(8,128)(2,1)}, u32[]{:S(2)}) copy-start(bf16[1024,256]{1,0:T(8,128)(2,1)} %copy-done.22) | copy-start | bytes 1572868
  162.8 14.0 %copy-start.29 = (bf16[256,1024]{1,0:T(8,128)(2,1)S(1)}, bf16[256,1024]{1,0:T(8,128)(2,1)}, u32[]{:S(2)}) copy-start(bf16[256,1024]{1,0:T(8,128)(2,1)} %copy-done.28) | copy-start | bytes 1572868
  162.8 14.0 %copy-start.32 = (bf16[1024,256]{1,0:T(8,128)(2,1)S(1)}, bf16[1024,256]{1,0:T(8,128)(2,1)}, u32[]{:S(2)}) copy-start(bf16[1024,256]{1,0:T(8,128)(2,1)} %copy-done.31) | copy-start | bytes 1572868
  162.8 14.0 %copy-start.34 = (bf16[1024,256]{1,0:T(8,128)(2,1)S(1)}, bf16[1024,256]{1,0:T(8,128)(2,1)}, u32[]{:S(2)}) copy-start(bf16[1024,256]{1,0:T(8,128)(2,1)} %copy-done.33) | copy-start | bytes 1572868
  162.8 14.0 %copy-start.36 = (bf16[1024,256]{1,0:T(8,128)(2,1)S(1)}, bf16[1024,256]{1,0:T(8,128)(2,1)}, u32[]{:S(2)}) copy-start(bf16[1024,256]{1,0:T(8,128)(2,1)} %copy-done.35) | copy-start | bytes 1572868
  170.3 19.0 %copy-start.24 = (bf16[1024,256]{1,0:T(8,128)(2,1)}, bf16[1024,256]{1,0:T(8,128)(2,1)S(1)}, u32[]{:S(2)}) copy-start(bf16[1024,256]{1,0:T(8,128)(2,1)S(1)} %get-tuple-element.92.refs_0_) | copy-start | bytes 1572868
  170.3 23.5 %collective-permute-start.32 = (bf16[1024,256]{1,0:T(8,128)(2,1)S(1)}, bf16[1024,256]{1,0:T(8,128)(2,1)}, u32[]{:S(2)}, u32[]{:S(2)}) collective-permute-start(bf16[1024,256]{1,0:T(8,128)(2,1)S(1)} %get-tuple-element.92.refs_0_), channel_id=1, source_target_pairs={{1,2},{2,1},{5,6},{6,5},{9,10},{10,9},{13,14},{14,13},{17,18},{18,... | collective-permute-start | bytes 1572872 | tf_op jit(solution)/shard_map/ppermute | solution.py:220
  171.8 22.0 %collective-permute-start.31 = (bf16[1024,256]{1,0:T(8,128)(2,1)S(1)}, bf16[1024,256]{1,0:T(8,128)(2,1)}, u32[]{:S(2)}, u32[]{:S(2)}) collective-permute-start(bf16[1024,256]{1,0:T(8,128)(2,1)S(1)} %get-tuple-element.92.refs_0_), channel_id=1, source_target_pairs={{0,1},{2,3},{1,0},{3,2},{4,5},{6,7},{5,4},{7,6},{8,9},{10,11},{9,8... | collective-permute-start | bytes 1572872 | tf_op jit(solution)/shard_map/ppermute | solution.py:220
  190.6 6.0 %collective-permute-start.37 = (bf16[512,256]{1,0:T(8,128)(2,1)S(1)}, bf16[512,256]{1,0:T(8,128)(2,1)S(1)}, u32[]{:S(2)}, u32[]{:S(2)}) collective-permute-start(bf16[512,256]{1,0:T(8,128)(2,1)S(1)} %slice.135), channel_id=1, source_target_pairs={{0,4},{4,0},{8,12},{12,8},{16,20},{20,16},{24,28},{28,24},{1,5},{5... | collective-permute-start | bytes 786440 | tf_op jit(solution)/shard_map/ppermute | solution.py:204
  191.8 14.7 %collective-permute-start.36 = (bf16[2,128,1024]{2,1,0:T(8,128)(2,1)}, bf16[2,128,1024]{2,1,0:T(8,128)(2,1)}, u32[]{:S(2)}, u32[]{:S(2)}) collective-permute-start(bf16[2,128,1024]{2,1,0:T(8,128)(2,1)} %get-tuple-element.145), channel_id=1, source_target_pairs={{0,16},{4,20},{8,24},{12,28},{16,0},{20,4},{24,8},{28,12},{1,17},{... | collective-permute-start | bytes 1572872 | tf_op jit(solution)/shard_map/ppermute | solution.py:209
  193.3 14.4 %collective-permute-start.35 = (bf16[2,128,1024]{2,1,0:T(8,128)(2,1)}, bf16[2,128,1024]{2,1,0:T(8,128)(2,1)}, u32[]{:S(2)}, u32[]{:S(2)}) collective-permute-start(bf16[2,128,1024]{2,1,0:T(8,128)(2,1)} %get-tuple-element.146), channel_id=1, source_target_pairs={{0,8},{4,12},{8,0},{12,4},{16,24},{20,28},{24,16},{28,20},{1,9},{5... | collective-permute-start | bytes 1572872 | tf_op jit(solution)/shard_map/ppermute | solution.py:209
  193.8 16.0 %collective-permute-start.33 = (bf16[1024,256]{1,0:T(8,128)(2,1)}, bf16[1024,256]{1,0:T(8,128)(2,1)}, u32[]{:S(2)}, u32[]{:S(2)}) collective-permute-start(bf16[1024,256]{1,0:T(8,128)(2,1)} %collective-permute-done.32.refs_2_), channel_id=1, source_target_pairs={{2,3},{1,0},{6,7},{5,4},{10,11},{9,8},{14,15},{13,12},{18,19},{17,... | collective-permute-start | bytes 1572872 | tf_op jit(solution)/shard_map/ppermute | solution.py:220
  195.1 14.7 %collective-permute-start.34 = (bf16[1024,256]{1,0:T(8,128)(2,1)}, bf16[1024,256]{1,0:T(8,128)(2,1)}, u32[]{:S(2)}, u32[]{:S(2)}) collective-permute-start(bf16[1024,256]{1,0:T(8,128)(2,1)} %collective-permute-done.31.refs_1_), channel_id=1, source_target_pairs={{1,2},{2,1},{5,6},{6,5},{9,10},{10,9},{13,14},{14,13},{17,18},{18,... | collective-permute-start | bytes 1572872 | tf_op jit(solution)/shard_map/ppermute | solution.py:220
  209.8 16.8 %collective-permute-start.38 = (bf16[1024,256]{1,0:T(8,128)(2,1)}, bf16[1024,256]{1,0:T(8,128)(2,1)S(1)}, u32[]{:S(2)}, u32[]{:S(2)}) collective-permute-start(bf16[1024,256]{1,0:T(8,128)(2,1)} %collective-permute-done.34.refs_4_), channel_id=1, source_target_pairs={{2,3},{1,0},{6,7},{5,4},{10,11},{9,8},{14,15},{13,12},{18,19},{17,... | collective-permute-start | bytes 1572872 | tf_op jit(solution)/shard_map/ppermute | solution.py:220
  212.3 7.4 %collective-permute-start.40 = (bf16[128,1024]{1,0:T(8,128)(2,1)S(1)}, bf16[128,1024]{1,0:T(8,128)(2,1)S(1)}, u32[]{:S(2)}, u32[]{:S(2)}) collective-permute-start(bf16[128,1024]{1,0:T(8,128)(2,1)S(1)} %get-tuple-element.143), channel_id=1, source_target_pairs={{0,8},{4,12},{8,0},{12,4},{16,24},{20,28},{24,16},{28,20},{1,9},{5... | collective-permute-start | bytes 786440 | tf_op jit(solution)/shard_map/ppermute | solution.py:209
  213.9 7.0 %collective-permute-start.39 = (bf16[128,1024]{1,0:T(8,128)(2,1)S(1)}, bf16[128,1024]{1,0:T(8,128)(2,1)S(1)}, u32[]{:S(2)}, u32[]{:S(2)}) collective-permute-start(bf16[128,1024]{1,0:T(8,128)(2,1)S(1)} %get-tuple-element.144), channel_id=1, source_target_pairs={{0,16},{4,20},{8,24},{12,28},{16,0},{20,4},{24,8},{28,12},{1,17},{... | collective-permute-start | bytes 786440 | tf_op jit(solution)/shard_map/ppermute | solution.py:209
  248.7 5.8 %collective-permute-start.41 = (bf16[512,1024]{1,0:T(8,128)(2,1)}, bf16[512,1024]{1,0:T(8,128)(2,1)}, u32[]{:S(2)}, u32[]{:S(2)}) collective-permute-start(bf16[512,1024]{1,0:T(8,128)(2,1)} %get-tuple-element.101), channel_id=1, source_target_pairs={{0,4},{4,0},{8,12},{12,8},{16,20},{20,16},{24,28},{28,24},{1,5},{5... | collective-permute-start | bytes 3145736 | tf_op jit(solution)/shard_map/ppermute | solution.py:204
  252.4 19.5 %collective-permute-start.47 = (bf16[2,128,1024]{2,1,0:T(8,128)(2,1)S(1)}, bf16[2,128,1024]{2,1,0:T(8,128)(2,1)S(1)}, u32[]{:S(2)}, u32[]{:S(2)}) collective-permute-start(bf16[2,128,1024]{2,1,0:T(8,128)(2,1)S(1)} %get-tuple-element.141), channel_id=1, source_target_pairs={{0,16},{4,20},{8,24},{12,28},{16,0},{20,4},{24,8},{28,12},{1,17},{... | collective-permute-start | bytes 1572872 | tf_op jit(solution)/shard_map/ppermute | solution.py:209
  253.0 18.9 %collective-permute-start.46 = (bf16[2,128,1024]{2,1,0:T(8,128)(2,1)S(1)}, bf16[2,128,1024]{2,1,0:T(8,128)(2,1)S(1)}, u32[]{:S(2)}, u32[]{:S(2)}) collective-permute-start(bf16[2,128,1024]{2,1,0:T(8,128)(2,1)S(1)} %get-tuple-element.142), channel_id=1, source_target_pairs={{0,8},{4,12},{8,0},{12,4},{16,24},{20,28},{24,16},{28,20},{1,9},{5... | collective-permute-start | bytes 1572872 | tf_op jit(solution)/shard_map/ppermute | solution.py:209
  257.2 1.6 collective-permute-start.42
  258.9 14.0 %copy-start.8 = (bf16[4,256,1024]{2,1,0:T(8,128)(2,1)S(1)}, bf16[4,256,1024]{2,1,0:T(8,128)(2,1)}, u32[]{:S(2)}) copy-start(bf16[4,256,1024]{2,1,0:T(8,128)(2,1)} %copy-done.7) | copy-start | bytes 6291460
  258.9 13.0 %collective-permute-start.45 = (bf16[4,128,128]{2,1,0:T(8,128)(2,1)S(1)}, bf16[4,128,128]{2,1,0:T(8,128)(2,1)S(1)}, u32[]{:S(2)}, u32[]{:S(2)}) collective-permute-start(bf16[4,128,128]{2,1,0:T(8,128)(2,1)S(1)} %fusion.19), channel_id=1, source_target_pairs={{0,24},{4,28},{8,16},{12,20},{16,8},{20,12},{24,0},{28,4},{1,25},{... | collective-permute-start | bytes 393224 | tf_op jit(solution)/shard_map/ppermute | solution.py:209
  260.4 12.0 %collective-permute-start.44 = (bf16[4,128,128]{2,1,0:T(8,128)(2,1)S(1)}, bf16[4,128,128]{2,1,0:T(8,128)(2,1)S(1)}, u32[]{:S(2)}, u32[]{:S(2)}) collective-permute-start(bf16[4,128,128]{2,1,0:T(8,128)(2,1)S(1)} %fusion.19), channel_id=1, source_target_pairs={{0,16},{4,20},{8,24},{12,28},{16,0},{20,4},{24,8},{28,12},{1,17},{... | collective-permute-start | bytes 393224 | tf_op jit(solution)/shard_map/ppermute | solution.py:209
  260.9 11.7 %collective-permute-start.43 = (bf16[4,128,128]{2,1,0:T(8,128)(2,1)S(1)}, bf16[4,128,128]{2,1,0:T(8,128)(2,1)S(1)}, u32[]{:S(2)}, u32[]{:S(2)}) collective-permute-start(bf16[4,128,128]{2,1,0:T(8,128)(2,1)S(1)} %fusion.19), channel_id=1, source_target_pairs={{0,8},{4,12},{8,0},{12,4},{16,24},{20,28},{24,16},{28,20},{1,9},{5... | collective-permute-start | bytes 393224 | tf_op jit(solution)/shard_map/ppermute | solution.py:209
  272.8 3.4 %collective-permute-start.50 = (bf16[4,128,128]{2,1,0:T(8,128)(2,1)S(1)}, bf16[4,128,128]{2,1,0:T(8,128)(2,1)S(1)}, u32[]{:S(2)}, u32[]{:S(2)}) collective-permute-start(bf16[4,128,128]{2,1,0:T(8,128)(2,1)S(1)} %add_convert_fusion.5), channel_id=1, source_target_pairs={{0,4},{4,0},{8,12},{12,8},{16,20},{20,16},{24,28},{28,24},{1,5},{5... | collective-permute-start | bytes 393224 | tf_op jit(solution)/shard_map/ppermute | solution.py:204
  273.1 8.8 %collective-permute-start.49 = (bf16[128,1024]{1,0:T(8,128)(2,1)S(1)}, bf16[128,1024]{1,0:T(8,128)(2,1)S(1)}, u32[]{:S(2)}, u32[]{:S(2)}) collective-permute-start(bf16[128,1024]{1,0:T(8,128)(2,1)S(1)} %get-tuple-element.139), channel_id=1, source_target_pairs={{0,8},{4,12},{8,0},{12,4},{16,24},{20,28},{24,16},{28,20},{1,9},{5... | collective-permute-start | bytes 786440 | tf_op jit(solution)/shard_map/ppermute | solution.py:209
  274.6 8.4 %collective-permute-start.48 = (bf16[128,1024]{1,0:T(8,128)(2,1)S(1)}, bf16[128,1024]{1,0:T(8,128)(2,1)S(1)}, u32[]{:S(2)}, u32[]{:S(2)}) collective-permute-start(bf16[128,1024]{1,0:T(8,128)(2,1)S(1)} %get-tuple-element.140), channel_id=1, source_target_pairs={{0,16},{4,20},{8,24},{12,28},{16,0},{20,4},{24,8},{28,12},{1,17},{... | collective-permute-start | bytes 786440 | tf_op jit(solution)/shard_map/ppermute | solution.py:209
  (39 other events, 138.1 us)

commit v3 on v2

--- a/solution.py
+++ b/solution.py
@@ -19,6 +19,10 @@
 NN = (((1,), (0,)), ((), ()))
 
 
+def in_hbm(values):
+    return [pltpu.with_memory_space_constraint(value, pltpu.HBM) for value in values]
+
+
 def dot(a, b, dims):
     return lax.dot_general(a, b, dims, preferred_element_type=F32)
 
@@ -29,12 +33,6 @@
     return dot(a, high, dims) + dot(a, low, dims)
 
 
-def causal_mask(rows):
-    t = lax.broadcasted_iota(jnp.int32, (rows, rows), 0)
-    s = lax.broadcasted_iota(jnp.int32, (rows, rows), 1)
-    return s <= t
-
-
 def head_columns(ref):
     return [ref.at[:, h * DH : (h + 1) * DH] for h in range(ref.shape[1] // DH)]
 
@@ -44,13 +42,25 @@
         out_ref[h] = dot(a[...], b[...], TN)
 
 
+def halves(rows):
+    middle = rows // 2
+    return [(slice(0, middle), slice(0, middle)), (slice(middle, rows), slice(0, rows))]
+
+
+def masked(product):
+    rows, columns = product.shape
+    t = lax.broadcasted_iota(jnp.int32, product.shape, 0) + (columns - rows)
+    s = lax.broadcasted_iota(jnp.int32, product.shape, 1)
+    return jnp.where(s <= t, product, 0.0).astype(BF16)
+
+
 def forward_kernel(q_ref, k_ref, v_ref, scale_ref, scaled_ref, intra_ref):
     scaled_ref[...] = (q_ref[...].astype(F32) * scale_ref[...]).astype(BF16)
-    mask = causal_mask(scaled_ref.shape[0])
     refs = (scaled_ref, k_ref, v_ref, intra_ref)
     for scaled, keys, values, intra in zip(*map(head_columns, refs)):
-        scores = jnp.where(mask, dot(scaled[...], keys[...], NT), 0.0).astype(BF16)
-        intra[...] = dot(scores, values[...], NN)
+        for own, upto in halves(scaled_ref.shape[0]):
+            scores = masked(dot(scaled[own], keys[upto], NT))
+            intra[own] = dot(scores, values[upto], NN)
 
 
 def attended_kernel(scaled_ref, intra_ref, state_ref, out_ref):
@@ -62,15 +72,23 @@
 def backward_kernel(
     scaled_ref, k_ref, v_ref, g_ref, scale_ref, state_ref, dq_ref, dk_ref, dv_ref
 ):
-    mask = causal_mask(scaled_ref.shape[0])
+    rows = scaled_ref.shape[0]
     refs = (scaled_ref, k_ref, v_ref, g_ref, dq_ref, dk_ref, dv_ref)
     for h, (scaled, keys, values, grads, dq, dk, dv) in enumerate(zip(*map(head_columns, refs))):
-        mixed = jnp.where(mask, dot(grads[...], values[...], NT), 0.0).astype(BF16)
-        total = split_dot(grads[...], state_ref[h], NT) + dot(mixed, keys[...], NN)
-        dq[...] = (total * scale_ref[...]).astype(BF16)
-        dk[...] = dot(mixed, scaled[...], TN)
-        scores = jnp.where(mask, dot(scaled[...], keys[...], NT), 0.0).astype(BF16)
-        dv[...] = dot(scores, grads[...], TN)
+        inter = split_dot(grads[...], state_ref[h], NT)
+        for own, upto in reversed(halves(rows)):
+            mixed = masked(dot(grads[own], values[upto], NT))
+            scores = masked(dot(scaled[own], keys[upto], NT))
+            total = inter[own] + dot(mixed, keys[upto], NN)
+            dq[own] = (total * scale_ref[own]).astype(BF16)
+            key_part = dot(mixed, scaled[own], TN)
+            value_part = dot(scores, grads[own], TN)
+            if upto.stop == rows:
+                dk[...] = key_part
+                dv[...] = value_part
+            else:
+                dk[upto] += key_part
+                dv[upto] += value_part
 
 
 def finish_kernel(k_ref, v_ref, dk_part_ref, dv_part_ref, after_ref, dk_ref, dv_ref):
@@ -89,12 +107,15 @@
         "s": pl.BlockSpec((rows, 1), lambda h: (0, 0)),
     }
     shapes = {"h": (rows, heads * DH), "m": (heads, DH, DH)}
-    return pl.pallas_call(
+    call = pl.pallas_call(
         kernel,
         grid=(heads // step,),
         in_specs=[specs[kind] for kind in ins],
         out_specs=[specs[kind] for kind, unused in outs],
-        out_shape=[jax.ShapeDtypeStruct(shapes[kind], dtype) for kind, dtype in outs],
+        out_shape=[
+            (pltpu.HBM if kind == "h" else jax.ShapeDtypeStruct)(shapes[kind], dtype)
+            for kind, dtype in outs
+        ],
         compiler_params=pltpu.CompilerParams(vmem_limit_bytes=VMEM_LIMIT),
         cost_estimate=pl.CostEstimate(
             flops=2 * macs * heads,
@@ -102,6 +123,13 @@
             transcendentals=0,
         ),
     )
+
+    def on_values(*values):
+        return call(
+            *[in_hbm([value])[0] if kind == "h" else value for kind, value in zip(ins, values)]
+        )
+
+    return on_values
 
 
 def project_kernel(pieces, half, own_ref, other_ref, *refs):
@@ -134,69 +162,151 @@
             bytes_accessed=8 * rows * width,
             transcendentals=0,
         ),
-    )(own, other, *pieces)
-
-
-def products_kernel(count, chips, share, before, factor, meta_ref, *refs):
+    )(*in_hbm([own, other, *pieces]))
+
+
+def products_kernel(count, late, chips, before, factor, meta_ref, *refs):
     candidates, (own_ref, other_ref), rest = refs[:count], refs[count : count + 2], refs[count + 2 :]
-    pieces, rest = rest[:chips], rest[chips:]
-    earlier, (first_ref, second_ref, grad_ref, total, weight_ref) = rest[:before], rest[before:]
+    weights, rest = rest[:chips], rest[chips:]
+    earlier, rest = rest[:before], rest[before:]
+    first_ref, second_ref, grad_ref, gathered, turned, semaphores = rest
     rows = own_ref.shape[0]
-    part = weight_ref.shape[1]
-    for delta, piece in enumerate(pieces):
-        weight_ref[delta] = piece[...]
+    part = weights[0].shape[0]
+
+    @pl.when(pl.program_id(0) == 0)
+    def unused():
+        copies = []
+        for j, candidate in enumerate(candidates):
+            for u in range(candidate.shape[1] // part):
+                copies.append(
+                    (
+                        meta_ref[2 * len(copies)] == 1,
+                        pltpu.make_async_copy(
+                            candidate.at[:, u * part : (u + 1) * part],
+                            gathered.at[meta_ref[2 * len(copies) + 1]],
+                            semaphores.at[len(copies)],
+                        ),
+                    )
+                )
+        for valid, copy in copies:
+            pl.when(valid)(copy.start)
+        for j in range(len(copies), len(copies) + late):
+
+            @pl.when(meta_ref[2 * j] == 1)
+            def unused_zero(j=j):
+                gathered[meta_ref[2 * j + 1]] = jnp.zeros(gathered.shape[1:], BF16)
+
+        for valid, copy in copies:
+            pl.when(valid)(copy.wait)
+        for delta in range(chips):
+            turned[delta * part : (delta + 1) * part, :] = gathered[delta].T
+
+    residuals = jnp.concatenate([gathered[delta] for delta in range(chips)], axis=1)
+    weight = jnp.concatenate([piece[...] for piece in weights], axis=0)
+    total = dot(residuals, weight, NN)
+    first, second = total[:rows], total[rows:]
     if before:
-        total[:rows] = earlier[0][...]
-        total[rows:] = earlier[1][...]
-    for j, candidate in enumerate(candidates):
-
-        @pl.when(meta_ref[j * (share + 1)] == 1)
-        def unused(j=j, candidate=candidate):
-            for u in range(share):
-                delta = meta_ref[j * (share + 1) + 1 + u]
-                values = candidate[:, u * part : (u + 1) * part]
-                product = dot(values, weight_ref[delta], NN)
-                if j == 0 and u == 0 and not before:
-                    total[...] = product
-                else:
-                    total[...] += product
-                grad = dot(values[:rows], own_ref[...], TN) + dot(values[rows:], other_ref[...], TN)
-                grad_ref[delta] = (grad * factor).astype(BF16)
-
-    first_ref[...] = total[:rows]
-    second_ref[...] = total[rows:].astype(second_ref.dtype)
-
-
-def products(meta, candidates, own, other, weights, earlier, second_type, factor, share):
+        first, second = first + earlier[0][...], second + earlier[1][...]
+    first_ref[...] = first
+    second_ref[...] = second
+    grad = dot(turned[:, :rows], own_ref[...], NN) + dot(turned[:, rows:], other_ref[...], NN)
+    grad = (grad * factor).astype(BF16)
+    for delta in range(chips):
+        grad_ref[delta] = grad[delta * part : (delta + 1) * part]
+
+
+def products(meta, candidates, late, own, other, weights, earlier, factor):
     rows, width = own.shape
     chips, part = len(weights), weights[0].shape[0]
     step = 256 if width % 256 == 0 else DH
     block = pl.BlockSpec((rows, step), lambda k, unused: (0, k))
     pieces = pl.BlockSpec((chips, part, step), lambda k, unused: (0, 0, k))
+    copies = sum(c.shape[1] for c in candidates) // part
     return pl.pallas_call(
-        functools.partial(products_kernel, len(candidates), chips, share, len(earlier), factor),
+        functools.partial(products_kernel, len(candidates), late, chips, len(earlier), factor),
         grid_spec=pltpu.PrefetchScalarGridSpec(
             num_scalar_prefetch=1,
             grid=(width // step,),
-            in_specs=[pl.BlockSpec(c.shape, lambda k, unused: (0, 0)) for c in candidates]
+            in_specs=[pl.BlockSpec(memory_space=pltpu.HBM) for unused in candidates]
             + [block, block]
             + [pl.BlockSpec((part, step), lambda k, unused: (0, k)) for unused in weights]
             + [block for unused in earlier],
             out_specs=[block, block, pieces],
-            scratch_shapes=[pltpu.VMEM((2 * rows, step), F32), pltpu.VMEM((chips, part, step), BF16)],
+            scratch_shapes=[
+                pltpu.VMEM((chips, 2 * rows, part), BF16),
+                pltpu.VMEM((chips * part, 2 * rows), BF16),
+                pltpu.SemaphoreType.DMA((copies,)),
+            ],
         ),
         out_shape=[
-            jax.ShapeDtypeStruct((rows, width), F32),
-            jax.ShapeDtypeStruct((rows, width), second_type),
-            jax.ShapeDtypeStruct((chips, part, width), BF16),
+            pltpu.HBM((rows, width), F32),
+            pltpu.HBM((rows, width), F32),
+            pltpu.HBM((chips, part, width), BF16),
         ],
-        compiler_params=pltpu.CompilerParams(vmem_limit_bytes=2 * VMEM_LIMIT),
+        compiler_params=pltpu.CompilerParams(vmem_limit_bytes=32 * rows * chips * part),
         cost_estimate=pl.CostEstimate(
             flops=8 * rows * width * part * chips,
             bytes_accessed=16 * rows * width,
             transcendentals=0,
         ),
-    )(meta, *candidates, own, other, *weights, *earlier)
+    )(meta, *in_hbm([*candidates, own, other, *weights, *earlier]))
+
+
+def late_kernel(
+    chips, factor, second_type, meta_ref, piece_ref, own_ref, other_ref, first_in, second_in, grad_in, *refs
+):
+    weights, (first_ref, second_ref, grad_ref) = refs[:chips], refs[chips:]
+    rows = own_ref.shape[0]
+    valid, place = meta_ref[0] == 1, meta_ref[1]
+
+    @pl.when(jnp.logical_not(valid))
+    def unused_pass():
+        first_ref[...] = first_in[...]
+        second_ref[...] = second_in[...].astype(second_type)
+        grad_ref[...] = grad_in[...]
+
+    for delta, weight in enumerate(weights):
+
+        @pl.when(valid & (place == delta))
+        def unused_add(weight=weight):
+            total = dot(piece_ref[...], weight[...], NN)
+            first_ref[...] = first_in[...] + total[:rows]
+            second_ref[...] = (second_in[...] + total[rows:]).astype(second_type)
+
+    @pl.when(valid)
+    def unused_grad():
+        grad = dot(piece_ref[:rows], own_ref[...], TN) + dot(piece_ref[rows:], other_ref[...], TN)
+        grad_ref[0] = (grad * factor).astype(BF16)
+
+
+def late_products(meta, piece, own, other, weights, totals, grads, second_type, factor):
+    rows, width = own.shape
+    chips, part = len(weights), weights[0].shape[0]
+    step = min(width, 512)
+    block = pl.BlockSpec((rows, step), lambda k, unused: (0, k))
+    slot = pl.BlockSpec((1, part, step), lambda k, meta: (meta[1], 0, k))
+    return pl.pallas_call(
+        functools.partial(late_kernel, chips, factor, second_type),
+        grid_spec=pltpu.PrefetchScalarGridSpec(
+            num_scalar_prefetch=1,
+            grid=(width // step,),
+            in_specs=[pl.BlockSpec(piece.shape, lambda k, unused: (0, 0)), block, block, block, block, slot]
+            + [pl.BlockSpec((part, step), lambda k, unused: (0, k)) for unused in weights],
+            out_specs=[block, block, slot],
+        ),
+        out_shape=[
+            pltpu.HBM((rows, width), F32),
+            pltpu.HBM((rows, width), second_type),
+            pltpu.HBM(grads.shape, BF16),
+        ],
+        input_output_aliases={6: 2},
+        compiler_params=pltpu.CompilerParams(vmem_limit_bytes=VMEM_LIMIT),
+        cost_estimate=pl.CostEstimate(
+            flops=8 * rows * width * part,
+            bytes_accessed=16 * rows * width,
+            transcendentals=0,
+        ),
+    )(meta, piece, *in_hbm([own, other, *totals, grads, *weights]))
 
 
 def core_swap(value):
@@ -236,7 +346,9 @@
                 continue
             target = jnp.where(mine % 2 == parity, mine + count - step, mine - count + step)
             value = part_for(jnp.clip(target, 0, count - 1))
-            if got[1 - parity] is not None:
+            if step > 1 and got[1 - parity] is None:
+                value, unused = lax.optimization_barrier((value, got[parity]))
+            elif step > 1:
                 value = (value.astype(F32) + got[1 - parity].astype(F32)).astype(BF16)
             values.append(value)
         got = line_step(values, active)
@@ -354,7 +466,8 @@
     position = lax.axis_index("seq")
     chip, core = lax.div(position, 2), lax.rem(position, 2)
     held = out_weight.shape[0]
-    part = held // CHUNKS
+    chunks = CHUNKS if held % (CHUNKS * DH) == 0 else 1
+    part = held // chunks
     call = functools.partial(per_head, rows=rows, heads=heads)
     barrier = lax.optimization_barrier
     outer = call(outer_kernel, ins="hh", outs=[("m", F32)], macs=rows * DH * DH, step=4)
@@ -368,24 +481,39 @@
     scaled, intra = call(
         forward_kernel, ins="hhhs", outs=[("h", BF16), ("h", F32)], macs=2 * rows * rows * DH
     )(query_rows, key_rows, value_rows, scale)
-    arrived, near, scaled, intra = barrier((arrived, near, scaled, intra))
+    def features_of(array, group, first, count):
+        found = [
+            lax.dynamic_slice_in_dim(array, (2 * j + group) * held + first, count, 1)
+            for j in range(share)
+        ]
+        return found[0] if share == 1 else jnp.concatenate(found, axis=1)
+
+    def chunk_of(array, c):
+        found = [array[:, j * held + c * part : j * held + (c + 1) * part] for j in range(share)]
+        return found[0] if share == 1 else jnp.concatenate(found, axis=1)
+
+    other_targets = core_swap(features_of(target_rows, 1 - core, 0, held))
+    targets = [
+        jnp.concatenate(
+            [features_of(target_rows, core, c * part, part), chunk_of(other_targets, c)], axis=0
+        )
+        for c in range(chunks)
+    ]
+    near, scaled, intra = barrier((near, scaled, intra))
     pieces = rest(near)
+    arrived, targets, scaled = barrier((arrived, targets, scaled))
     before = sum_of_others(half, arrived, other, True)
+    before, pieces = barrier((before, pieces))
     (attended,) = call(
         attended_kernel, ins="hhm", outs=[("h", BF16)], macs=2 * rows * DH * DH, step=4
     )(scaled, intra, before)
     other_attended = core_swap(attended)
 
-    targets = target_rows.reshape(rows, share, 2, held)
-    own_target = lax.dynamic_index_in_dim(targets, core, 2, keepdims=False)
-    sent_target = lax.dynamic_index_in_dim(targets, 1 - core, 2, keepdims=False)
-    both_targets = jnp.concatenate([own_target, core_swap(sent_target)], axis=0)
-
     outputs, grad_parts = [], []
     gate, totals, sent, gathered = None, (), None, {}
     factor = 1.0 / math.sqrt(rows * seq_count)
-    for c in range(CHUNKS):
-        last = c == CHUNKS - 1
+    for c in range(chunks):
+        last = c == chunks - 1
         if c:
             own_rows, unused = barrier((out_weight[c * part : (c + 1) * part], pieces[-1]))
             near, rest = near_pieces(own_rows)
@@ -402,42 +530,81 @@
             return found[0] if share == 1 else jnp.concatenate(found, axis=1)
 
         summed = line_sum(part_for, {step - 1: items for step, items in gathered.items() if step > 1}).astype(BF16)
-        target = both_targets[:, :, c * part : (c + 1) * part].reshape(2 * rows, share * part)
-        residual = (summed.astype(F32) - target.astype(F32)).astype(BF16)
-        own_output = summed[:rows].reshape(rows, share, part)
-        other_output = core_swap(summed[rows:]).reshape(rows, share, part)
-        first = jnp.where(core == 0, own_output, other_output)
-        second = jnp.where(core == 0, other_output, own_output)
-        outputs.append(jnp.stack([first, second], axis=2))
-        output = jnp.concatenate(outputs, axis=3).reshape(rows, width) if last else None
+        residual = (summed.astype(F32) - targets[c].astype(F32)).astype(BF16)
+        own_output = summed[:rows]
+        other_output = core_swap(summed[rows:])
+        outputs.append(
+            [
+                jnp.where(core == 0, own_output, other_output),
+                jnp.where(core == 0, other_output, own_output),
+            ]
+        )
+        output = None
+        if last:
+            output = jnp.concatenate(
+                [
+                    piece[group][:, j * part : (j + 1) * part]
+                    for j in range(share)
+                    for group in (0, 1)
+                    for piece in outputs
+                ],
+                axis=1,
+            )
         found, gathered, tied = line_gather(
             residual, {1: totals, 2: (sent, output)}
         )
         totals, (sent, output) = tied[1], tied[2]
         gate = gathered[1]
-        meta = []
-        for unused, valid, source in found:
-            meta.append(valid.astype(jnp.int32))
-            meta += [
-                jnp.clip((source * share + j) ^ chip, 0, chips - 1).astype(jnp.int32)
+        weights = pieces
+        on_time = found[:-1] if last and len(found) > 1 else found
+        metas = [
+            [
+                value
                 for j in range(share)
+                for value in (
+                    valid.astype(jnp.int32),
+                    jnp.clip((source * share + j) ^ chip, 0, chips - 1).astype(jnp.int32),
+                )
             ]
-        items = [item for item, unused, unused in found]
-        if sent is not None:
-            sent, finish = second_step(sent)
-            items, sent = barrier((items, sent))
-            grad_parts.append(finish(sent))
+            for unused, valid, source in found
+        ]
+        late = found[len(on_time) :]
+        if not last:
+            items = [item for item, unused, unused in on_time]
+            if sent is not None:
+                sent, finish = second_step(sent)
+                items, sent = barrier((items, sent))
+                grad_parts.append(finish(sent))
+        else:
+            items = [item for item, unused, unused in on_time]
         *totals, grads = products(
-            jnp.stack(meta),
+            jnp.stack(sum(metas, [])),
             items,
+            len(late) * share,
             attended,
             other_attended,
-            pieces,
+            weights,
             totals,
-            BF16 if last else F32,
             factor,
-            share,
         )
+        if late:
+            item = late[0][0]
+            if sent is not None:
+                sent, finish = second_step(sent)
+                item, sent, totals = barrier((item, sent, totals))
+                grad_parts.append(finish(sent))
+            for j in range(share):
+                *totals, grads = late_products(
+                    jnp.stack(metas[-1][2 * j : 2 * j + 2]),
+                    item[:, j * part : (j + 1) * part] if share > 1 else item,
+                    attended,
+                    other_attended,
+                    weights,
+                    totals,
+                    grads,
+                    BF16 if j == share - 1 else F32,
+                    factor,
+                )
         sent, second_step = scatter_start(grads)
 
     grad_attended = (totals[0] + core_swap(totals[1]).astype(F32)).astype(BF16)
@@ -455,10 +622,10 @@
     )
     sent, finish = second_step(sent)
     after = sum_of_others(half, arrived, other, False)
-    sent, after = barrier((sent, after))
     grad_key, grad_value = call(
         finish_kernel, ins="hhhhm", outs=[("h", BF16), ("h", BF16)], macs=4 * rows * DH * DH
     )(key_rows, value_rows, key_part, value_part, after)
+    sent, grad_key, grad_value = barrier((sent, grad_key, grad_value))
     grad_weight = jnp.concatenate([*grad_parts, finish(sent)], axis=0)
     return output, grad_query, grad_key, grad_value, grad_weight
 

time: 290 us -> 258 us (0.89)
  local copies, waits for them, and re-layouts: 47.9 us -> 13.4 us
  waiting for transfers between devices: 89.1 us -> 74 us
  Pallas kernels: 51.9 us -> 66.7 us
  starting transfers between devices: 77 us -> 81.9 us
    unnamed x109 -> x59, local copies, waits for them, and re-layouts: 28.7 us -> 2.68 us
    ppermute x22, waiting for transfers between devices: 40.3 us -> 25.7 us  [chip_swap(): lax.ppermute(value, 'seq', [(j, j ^ 2 * delta) for j in range(count)])]
    pallas_call x8 -> x9, Pallas kernels: 42.1 us -> 56.1 us  [the longest x6 28 us: on_values(): call(*[in_hbm([value])[0] if kind == 'h' else value for kind, value in zi...]
    ppermute x20, starting transfers between devices: 49.1 us -> 54.1 us  [line_step(): lax.ppermute(value, 'head', pairs)]
    dynamic_slice x1 -> x2, local copies, waits for them, and re-layouts: 4.75 us -> 0.9 us  [features_of(): lax.dynamic_slice_in_dim(array, (2 * j + group) * held + first, count, 1)]
    ppermute x20, waiting for transfers between devices: 47.3 us -> 44 us  [line_step(): lax.ppermute(value, 'head', pairs)]
  transfers between devices with their start and end apart: 51 -> 51, of which waited for: 27 -> 21; matrix products, arithmetic and copies ran while one was open for 13% -> 8% of each run, Pallas kernels for 10% -> 20%
where the time goes in v3:
time: 258 us; the launch traced here: 256 us
  starting transfers between devices  81.9 us (32%)
  waiting for transfers between devices  74 us (29%)
  Pallas kernels  66.7 us (26%)
  other arithmetic  18.6 us (7%)
  local copies, waits for them, and re-layouts  13.4 us (5%)
    ppermute x20, starting transfers between devices, line_step(): lax.ppermute(value, 'head', pairs)  54.1 us
    ppermute x20, waiting for transfers between devices, line_step(): lax.ppermute(value, 'head', pairs)  44 us
    pallas_call x6, Pallas kernels, on_values(): call(*[in_hbm([value])[0] if kind == 'h' else value for kind, value in zi...  28 us
    ppermute x22, starting transfers between devices, chip_swap(): lax.ppermute(value, 'seq', [(j, j ^ 2 * delta) for j in range(count)])  26.7 us
    ppermute x22, waiting for transfers between devices, chip_swap(): lax.ppermute(value, 'seq', [(j, j ^ 2 * delta) for j in range(count)])  25.7 us
    pallas_call x2, Pallas kernels, products(): pl.pallas_call(functools.partial(products_kernel, len(candidates), late,...  21.9 us
    pallas_call x2, Pallas kernels, project(): pl.pallas_call(functools.partial(project_kernel, len(pieces), half), grid...  10.6 us
    pallas_call x1, Pallas kernels, late_products(): pl.pallas_call(functools.partial(late_kernel, chips, factor, second_type)...  6.22 us
  transfers between devices with their start and end apart: 51, of which 21 were waited for; matrix products, arithmetic and copies ran while one was open for 8% of the time, Pallas kernels for 20%

profile of v3, /device:TPU:0, one launch (start us, length us, event | category | flops | bytes accessed | tf_op | source)
XLA Modules:
  0.0 256.1 jit_solution(8695664837072923313)
XLA Ops:
  0.6 2.1 fusion.20
  2.8 3.0 %collective-permute-start.6 = (bf16[256,1024]{1,0:T(8,128)(2,1)}, bf16[256,1024]{1,0:T(8,128)(2,1)S(1)}, u32[]{:S(2)}, u32[]{:S(2)}) collective-permute-start(bf16[256,1024]{1,0:T(8,128)(2,1)} %get-tuple-element.88.refs_0_.refs_8_), channel_id=1, source_target_pairs={{0,16},{4,20},{8,24},{12,28},{16,0},{20,4},{24,8},{28,12},{1,17},{... | collective-permute-start | bytes 1572872 | tf_op jit(solution)/shard_map/ppermute | solution.py:319
  5.7 1.5 collective-permute-start.5
  8.1 1.9 shard_map.92
  10.7 6.2 %shard_map.93 = (bf16[512,1024]{1,0:T(8,128)(2,1)}, f32[512,1024]{1,0:T(8,128)}) custom-call(bf16[512,1024]{1,0:T(8,128)(2,1)} %q_ref.1, bf16[512,1024]{1,0:T(8,128)(2,1)} %k_ref.5, bf16[512,1024]{1,0:T(8,128)(2,1)} %v_ref.5, f32[512,1]{1,0:T(8,128)S(1)} %multiply_rsqrt_fusion.scale_ref), custom_call_target="tpu_custom_call" | custom-call | flops 1073741824 | bytes 6291456 | tf_op jit(solution)/shard_map/pallas_call | solution.py:128
  17.2 2.0 collective-permute-start.2
  19.2 1.5 collective-permute-start.1
  21.7 2.7 %collective-permute-done.3 = bf16[4,128,128]{2,1,0:T(8,128)(2,1)S(1)} collective-permute-done((bf16[4,128,128]{2,1,0:T(8,128)(2,1)S(1)}, bf16[4,128,128]{2,1,0:T(8,128)(2,1)S(1)}, u32[]{:S(2)}, u32[]{:S(2)}) %collective-permute-start.3) | collective-permute-done | bytes 131104 | tf_op jit(solution)/shard_map/ppermute | solution.py:319
  26.7 1.4 collective-permute-start.9
  29.3 6.2 %collective-permute-done.9 = bf16[128,1024]{1,0:T(8,128)(2,1)S(1)} collective-permute-done((bf16[128,1024]{1,0:T(8,128)(2,1)S(1)}, bf16[128,1024]{1,0:T(8,128)(2,1)S(1)}, u32[]{:S(2)}, u32[]{:S(2)}) %collective-permute-start.9) | collective-permute-done | bytes 262176 | tf_op jit(solution)/shard_map/ppermute | solution.py:319
  37.3 3.1 %shard_map.94.own_ref.refs_6_.refs_5_ = bf16[512,1024]{1,0:T(8,128)(2,1)} custom-call(bf16[512,1024]{1,0:T(8,128)(2,1)} %get-tuple-element.78.scaled_ref.a_ref, f32[512,1024]{1,0:T(8,128)} %get-tuple-element.79.intra_ref, f32[8,128,128]{2,1,0:T(8,128)S(1)} %select_add_fusion.1.state_ref), custom_call_target="tpu_custom_call" | custom-call | flops 268435456 | bytes 4194304 | tf_op jit(solution)/shard_map/pallas_call | solution.py:128
  40.4 3.0 %collective-permute-done.10.other_ref.refs_7_.refs_6_ = bf16[512,1024]{1,0:T(8,128)(2,1)} collective-permute-done((bf16[512,1024]{1,0:T(8,128)(2,1)}, bf16[512,1024]{1,0:T(8,128)(2,1)}, u32[]{:S(2)}, u32[]{:S(2)}) %collective-permute-start.10) | collective-permute-done | bytes 1048608 | tf_op jit(solution)/shard_map/ppermute | solution.py:314
  43.4 5.3 %shard_map.96 = bf16[4,1024,256]{2,1,0:T(8,128)(2,1)S(1)} custom-call(bf16[512,1024]{1,0:T(8,128)(2,1)} %shard_map.94.own_ref.refs_6_.refs_5_, bf16[512,1024]{1,0:T(8,128)(2,1)} %collective-permute-done.10.other_ref.refs_7_.refs_6_, bf16[256,1024]{1,0:T(8,128)(2,1)} %get-tuple-element.88.refs_0_.refs_8_, ...), custom_call_target="tpu_custom_call" | custom-call | flops 2147483648 | bytes 4194304 | tf_op jit(solution)/shard_map/pallas_call | solution.py:149
  48.7 1.1 dynamic-slice_bitcast_fusion.3
  49.8 4.3 %collective-permute-start.15 = (bf16[1024,256]{1,0:T(8,128)(2,1)}, bf16[1024,256]{1,0:T(8,128)(2,1)}, u32[]{:S(2)}, u32[]{:S(2)}) collective-permute-start(bf16[1024,256]{1,0:T(8,128)(2,1)} %get-tuple-element.167), channel_id=1, source_target_pairs={{0,1},{3,2},{4,5},{7,6},{8,9},{11,10},{12,13},{15,14},{16,17},{19,... | collective-permute-start | bytes 1572872 | tf_op jit(solution)/shard_map/ppermute | solution.py:330
  54.1 10.9 %collective-permute-done.15 = bf16[1024,256]{1,0:T(8,128)(2,1)} collective-permute-done((bf16[1024,256]{1,0:T(8,128)(2,1)}, bf16[1024,256]{1,0:T(8,128)(2,1)}, u32[]{:S(2)}, u32[]{:S(2)}) %collective-permute-start.15) | collective-permute-done | bytes 524320 | tf_op jit(solution)/shard_map/ppermute | solution.py:330
  65.1 2.0 fusion.6
  67.0 1.5 collective-permute-start.16
  68.6 7.2 %collective-permute-start.18 = (bf16[1024,256]{1,0:T(8,128)(2,1)}, bf16[1024,256]{1,0:T(8,128)(2,1)}, u32[]{:S(2)}, u32[]{:S(2)}) collective-permute-start(bf16[1024,256]{1,0:T(8,128)(2,1)} %get-tuple-element.91), channel_id=1, source_target_pairs={{0,1},{3,2},{4,5},{7,6},{8,9},{11,10},{12,13},{15,14},{16,17},{19,... | collective-permute-start | bytes 1572872 | tf_op jit(solution)/shard_map/ppermute | solution.py:330
  76.6 1.3 collective-permute-start.12
  77.9 7.7 %collective-permute-done.18 = bf16[1024,256]{1,0:T(8,128)(2,1)} collective-permute-done((bf16[1024,256]{1,0:T(8,128)(2,1)}, bf16[1024,256]{1,0:T(8,128)(2,1)}, u32[]{:S(2)}, u32[]{:S(2)}) %collective-permute-start.18) | collective-permute-done | bytes 524320 | tf_op jit(solution)/shard_map/ppermute | solution.py:330
  85.6 2.5 fusion.7
  88.1 2.5 collective-permute-start.17
  90.6 1.5 collective-permute-start.19
  92.1 1.7 slice.130
  96.9 3.5 %collective-permute-done.13 = bf16[128,1024]{1,0:T(8,128)(2,1)} collective-permute-done((bf16[128,1024]{1,0:T(8,128)(2,1)}, bf16[128,1024]{1,0:T(8,128)(2,1)}, u32[]{:S(2)}, u32[]{:S(2)}) %collective-permute-start.13) | collective-permute-done | bytes 262176 | tf_op jit(solution)/shard_map/ppermute | solution.py:319
  101.4 1.6 subtract_convert_fusion.1
  103.8 5.0 %collective-permute-start.20 = (bf16[1024,256]{1,0:T(8,128)(2,1)S(1)}, bf16[1024,256]{1,0:T(8,128)(2,1)S(1)}, u32[]{:S(2)}, u32[]{:S(2)}) collective-permute-start(bf16[1024,256]{1,0:T(8,128)(2,1)S(1)} %get-tuple-element.147.refs_0_), channel_id=1, source_target_pairs={{0,1},{2,3},{1,0},{3,2},{4,5},{6,7},{5,4},{7,6},{8,9},{10,11},{9,8... | collective-permute-start | bytes 1572872 | tf_op jit(solution)/shard_map/ppermute | solution.py:330
  109.7 5.3 %shard_map.95 = bf16[4,1024,256]{2,1,0:T(8,128)(2,1)S(1)} custom-call(bf16[512,1024]{1,0:T(8,128)(2,1)} %shard_map.94.own_ref.refs_6_.refs_5_, bf16[512,1024]{1,0:T(8,128)(2,1)} %collective-permute-done.10.other_ref.refs_7_.refs_6_, bf16[256,1024]{1,0:T(8,128)(2,1)} %copy-done.3, bf16[256,1024]{1,0:T(8,128)(2,1)} %collective-permute-done.11.refs_1_.refs_8_, ...), custom_call_target="tpu_custom_call" | custom-call | flops 2147483648 | bytes 4194304 | tf_op jit(solution)/shard_map/pallas_call | solution.py:149
  116.0 1.8 collective-permute-done.20.refs_1_
  118.5 1.3 collective-permute-start.24
  119.9 6.6 %collective-permute-start.23 = (bf16[1024,256]{1,0:T(8,128)(2,1)S(1)}, bf16[1024,256]{1,0:T(8,128)(2,1)S(1)}, u32[]{:S(2)}, u32[]{:S(2)}) collective-permute-start(bf16[1024,256]{1,0:T(8,128)(2,1)S(1)} %get-tuple-element.163), channel_id=1, source_target_pairs={{0,1},{3,2},{4,5},{7,6},{8,9},{11,10},{12,13},{15,14},{16,17},{19,... | collective-permute-start | bytes 1572872 | tf_op jit(solution)/shard_map/ppermute | solution.py:330
  126.5 6.5 %collective-permute-done.24.refs_3_ = bf16[1024,256]{1,0:T(8,128)(2,1)S(1)} collective-permute-done((bf16[1024,256]{1,0:T(8,128)(2,1)S(1)}, bf16[1024,256]{1,0:T(8,128)(2,1)S(1)}, u32[]{:S(2)}, u32[]{:S(2)}) %collective-permute-start.24) | collective-permute-done | bytes 524320 | tf_op jit(solution)/shard_map/ppermute | solution.py:330
  133.1 1.3 collective-permute-start.28
  135.3 7.1 %collective-permute-start.26 = (bf16[1024,256]{1,0:T(8,128)(2,1)S(1)}, bf16[1024,256]{1,0:T(8,128)(2,1)S(1)}, u32[]{:S(2)}, u32[]{:S(2)}) collective-permute-start(bf16[1024,256]{1,0:T(8,128)(2,1)S(1)} %get-tuple-element.99), channel_id=1, source_target_pairs={{0,1},{3,2},{4,5},{7,6},{8,9},{11,10},{12,13},{15,14},{16,17},{19,... | collective-permute-start | bytes 1572872 | tf_op jit(solution)/shard_map/ppermute | solution.py:330
  142.4 2.4 collective-permute-done.28.refs_5_
  145.6 4.9 %collective-permute-done.26 = bf16[1024,256]{1,0:T(8,128)(2,1)S(1)} collective-permute-done((bf16[1024,256]{1,0:T(8,128)(2,1)S(1)}, bf16[1024,256]{1,0:T(8,128)(2,1)S(1)}, u32[]{:S(2)}, u32[]{:S(2)}) %collective-permute-start.26) | collective-permute-done | bytes 524320 | tf_op jit(solution)/shard_map/ppermute | solution.py:330
  150.5 1.3 fusion.2
  151.8 2.5 collective-permute-start.29
  154.3 1.4 collective-permute-start.30
  155.8 6.1 %collective-permute-done.29 = bf16[1024,256]{1,0:T(8,128)(2,1)} collective-permute-done((bf16[1024,256]{1,0:T(8,128)(2,1)}, bf16[1024,256]{1,0:T(8,128)(2,1)}, u32[]{:S(2)}, u32[]{:S(2)}) %collective-permute-start.29) | collective-permute-done | bytes 524320 | tf_op jit(solution)/shard_map/ppermute | solution.py:330
  161.9 1.5 subtract_convert_fusion
  164.1 5.7 %collective-permute-start.31 = (bf16[1024,256]{1,0:T(8,128)(2,1)S(1)}, bf16[1024,256]{1,0:T(8,128)(2,1)S(1)}, u32[]{:S(2)}, u32[]{:S(2)}) collective-permute-start(bf16[1024,256]{1,0:T(8,128)(2,1)S(1)} %get-tuple-element.145.refs_0_), channel_id=1, source_target_pairs={{0,1},{2,3},{1,0},{3,2},{4,5},{6,7},{5,4},{7,6},{8,9},{10,11},{9,8... | collective-permute-start | bytes 1572872 | tf_op jit(solution)/shard_map/ppermute | solution.py:330
  169.8 10.6 %shard_map.97 = (f32[512,1024]{1,0:T(8,128)}, f32[512,1024]{1,0:T(8,128)}, bf16[4,256,1024]{2,1,0:T(8,128)(2,1)}) custom-call(s32[12]{0:T(128)S(1)} %stack.93.meta_ref, bf16[1024,256]{1,0:T(8,128)(2,1)} %copy-done.13, bf16[1024,256]{1,0:T(8,128)(2,1)} %copy-done.21, bf16[1024,256]{1,0:T(8,128)(2,1)} %copy-done.20, bf16[1024,256]{1,0:T(8,128)(2,1)} %copy-done.23, ...), custom_call_target="tpu_custom_call" | custom-call | flops 4294967296 | bytes 8388608 | tf_op jit(solution)/shard_map/pallas_call | solution.py:225
  180.5 1.3 fusion.19
  181.8 1.1 collective-permute-start.36
  184.0 1.3 collective-permute-start.33
  186.3 1.1 pad_maximum_fusion.1
  187.4 8.7 %collective-permute-done.36 = bf16[2,128,1024]{2,1,0:T(8,128)(2,1)S(1)} collective-permute-done((bf16[2,128,1024]{2,1,0:T(8,128)(2,1)S(1)}, bf16[2,128,1024]{2,1,0:T(8,128)(2,1)S(1)}, u32[]{:S(2)}, u32[]{:S(2)}) %collective-permute-start.36) | collective-permute-done | bytes 524320 | tf_op jit(solution)/shard_map/ppermute | solution.py:319
  197.0 2.7 %collective-permute-done.33.refs_3_ = bf16[1024,256]{1,0:T(8,128)(2,1)S(1)} collective-permute-done((bf16[1024,256]{1,0:T(8,128)(2,1)S(1)}, bf16[1024,256]{1,0:T(8,128)(2,1)S(1)}, u32[]{:S(2)}, u32[]{:S(2)}) %collective-permute-start.33) | collective-permute-done | bytes 524320 | tf_op jit(solution)/shard_map/ppermute | solution.py:330
  199.6 1.3 collective-permute-start.38
  203.2 11.3 %shard_map.98 = (f32[512,1024]{1,0:T(8,128)}, f32[512,1024]{1,0:T(8,128)}, bf16[4,256,1024]{2,1,0:T(8,128)(2,1)}) custom-call(s32[12]{0:T(128)S(1)} %stack.93.meta_ref, bf16[1024,256]{1,0:T(8,128)(2,1)} %copy-done.14, bf16[1024,256]{1,0:T(8,128)(2,1)} %copy-done.26, bf16[1024,256]{1,0:T(8,128)(2,1)} %copy-done.25, bf16[1024,256]{1,0:T(8,128)(2,1)} %copy-done.28, ...), custom_call_target="tpu_custom_call" | custom-call | flops 4294967296 | bytes 8388608 | tf_op jit(solution)/shard_map/pallas_call | solution.py:225
  215.4 6.2 %shard_map.99 = (f32[512,1024]{1,0:T(8,128)}, bf16[512,1024]{1,0:T(8,128)(2,1)}, bf16[4,256,1024]{2,1,0:T(8,128)(2,1)}) custom-call(s32[2]{0:T(128)S(1)} %pad_add_fusion.meta_ref, bf16[1024,256]{1,0:T(8,128)(2,1)S(1)} %collective-permute-done.38.piece_ref, bf16[512,1024]{1,0:T(8,128)(2,1)} %shard_map.94.own_ref.refs_6_.refs_5_, ...), custom_call_target="tpu_custom_call", output_to_operand_aliasing={{2}: (6, {})} | custom-call | flops 1073741824 | bytes 8388608 | tf_op jit(solution)/shard_map/pallas_call | solution.py:288
  221.7 1.4 fusion.18
  224.0 1.2 collective-permute-start.46
  225.2 2.6 %add_convert_fusion.b_ref.g_ref = bf16[512,1024]{1,0:T(8,128)(2,1)} fusion(f32[512,1024]{1,0:T(8,128)S(1)} %copy-done.2, bf16[512,1024]{1,0:T(8,128)(2,1)} %collective-permute-done.41), kind=kLoop, calls=%fused_computation.1 | loop fusion | flops 1572864 | bytes 4194304 | tf_op jit(solution)/shard_map/convert_element_type | solution.py:610
  227.8 2.1 shard_map.100
  230.3 1.2 collective-permute-done.42
  231.6 1.6 collective-permute-start.45
  234.0 1.2 collective-permute-start.43
  235.1 9.3 %shard_map.101 = (bf16[512,1024]{1,0:T(8,128)(2,1)}, f32[512,1024]{1,0:T(8,128)}, f32[512,1024]{1,0:T(8,128)}) custom-call(bf16[512,1024]{1,0:T(8,128)(2,1)} %get-tuple-element.78.scaled_ref.a_ref, bf16[512,1024]{1,0:T(8,128)(2,1)} %k_ref.5, bf16[512,1024]{1,0:T(8,128)(2,1)} %v_ref.5, bf16[512,1024]{1,0:T(8,128)(2,1)} %add_convert_fusion.b_ref.g_ref, ...), custom_call_target="tpu_custom_call" | custom-call | flops 2684354560 | bytes 9437184 | tf_op jit(solution)/shard_map/pallas_call | solution.py:128
  245.8 1.3 collective-permute-start.48
  247.2 5.4 %shard_map.102 = (bf16[512,1024]{1,0:T(8,128)(2,1)}, bf16[512,1024]{1,0:T(8,128)(2,1)}) custom-call(bf16[512,1024]{1,0:T(8,128)(2,1)} %k_ref.5, bf16[512,1024]{1,0:T(8,128)(2,1)} %v_ref.5, f32[512,1024]{1,0:T(8,128)} %get-tuple-element.132.dk_part_ref, f32[512,1024]{1,0:T(8,128)} %get-tuple-element.133.dv_part_ref, f32[8,128,128]{2,1,0:T(8,128)S(1)} %select_add_fusion.after_ref), custom_call_target="tpu_custom_call" | custom-call | flops 536870912 | bytes 7340032 | tf_op jit(solution)/shard_map/pallas_call | solution.py:128
  254.5 1.6 pad_maximum_fusion
  (155 shorter events, 30.2 us)
Async XLA Ops:
  2.8 73.8 %copy-start.3 = (bf16[256,1024]{1,0:T(8,128)(2,1)}, bf16[256,1024]{1,0:T(8,128)(2,1)S(1)}, u32[]{:S(2)}) copy-start(bf16[256,1024]{1,0:T(8,128)(2,1)S(1)} %get-tuple-element.87.refs_0_.refs_7_) | copy-start | bytes 1572868
  2.8 16.4 %collective-permute-start.6 = (bf16[256,1024]{1,0:T(8,128)(2,1)}, bf16[256,1024]{1,0:T(8,128)(2,1)S(1)}, u32[]{:S(2)}, u32[]{:S(2)}) collective-permute-start(bf16[256,1024]{1,0:T(8,128)(2,1)} %get-tuple-element.88.refs_0_.refs_8_), channel_id=1, source_target_pairs={{0,16},{4,20},{8,24},{12,28},{16,0},{20,4},{24,8},{28,12},{1,17},{... | collective-permute-start | bytes 1572872 | tf_op jit(solution)/shard_map/ppermute | solution.py:319
  5.7 14.9 %collective-permute-start.5 = (bf16[256,1024]{1,0:T(8,128)(2,1)}, bf16[256,1024]{1,0:T(8,128)(2,1)}, u32[]{:S(2)}, u32[]{:S(2)}) collective-permute-start(bf16[256,1024]{1,0:T(8,128)(2,1)} %get-tuple-element.88.refs_0_.refs_8_), channel_id=1, source_target_pairs={{0,8},{4,12},{8,0},{12,4},{16,24},{20,28},{24,16},{28,20},{1,9},{5... | collective-permute-start | bytes 1572872 | tf_op jit(solution)/shard_map/ppermute | solution.py:319
  8.1 12.6 %collective-permute-start.4 = (bf16[512,512]{1,0:T(8,128)(2,1)}, bf16[512,512]{1,0:T(8,128)(2,1)S(1)}, u32[]{:S(2)}, u32[]{:S(2)}) collective-permute-start(bf16[512,512]{1,0:T(8,128)(2,1)} %constant_dynamic-slice_fusion.1), channel_id=1, source_target_pairs={{0,4},{4,0},{8,12},{12,8},{16,20},{20,16},{24,28},{28,24},{1,5},{5... | collective-permute-start | bytes 1572872 | tf_op jit(solution)/shard_map/ppermute | solution.py:314
  10.1 6.9 %collective-permute-start = (bf16[8,128,128]{2,1,0:T(8,128)(2,1)S(1)}, bf16[8,128,128]{2,1,0:T(8,128)(2,1)S(1)}, u32[]{:S(2)}, u32[]{:S(2)}) collective-permute-start(bf16[8,128,128]{2,1,0:T(8,128)(2,1)S(1)} %convert_element_type.304), channel_id=1, source_target_pairs={{0,4},{4,0},{8,12},{12,8},{16,20},{20,16},{24,28},{28,24},{1,5},{5... | collective-permute-start | bytes 786440 | tf_op jit(solution)/shard_map/ppermute | solution.py:314
  17.1 7.4 %collective-permute-start.3 = (bf16[4,128,128]{2,1,0:T(8,128)(2,1)S(1)}, bf16[4,128,128]{2,1,0:T(8,128)(2,1)S(1)}, u32[]{:S(2)}, u32[]{:S(2)}) collective-permute-start(bf16[4,128,128]{2,1,0:T(8,128)(2,1)S(1)} %fusion.15), channel_id=1, source_target_pairs={{0,24},{4,28},{8,16},{12,20},{16,8},{20,12},{24,0},{28,4},{1,25},{... | collective-permute-start | bytes 393224 | tf_op jit(solution)/shard_map/ppermute | solution.py:319
  17.2 8.3 %collective-permute-start.2 = (bf16[4,128,128]{2,1,0:T(8,128)(2,1)S(1)}, bf16[4,128,128]{2,1,0:T(8,128)(2,1)S(1)}, u32[]{:S(2)}, u32[]{:S(2)}) collective-permute-start(bf16[4,128,128]{2,1,0:T(8,128)(2,1)S(1)} %fusion.15), channel_id=1, source_target_pairs={{0,16},{4,20},{8,24},{12,28},{16,0},{20,4},{24,8},{28,12},{1,17},{... | collective-permute-start | bytes 393224 | tf_op jit(solution)/shard_map/ppermute | solution.py:319
  19.2 6.3 %collective-permute-start.1 = (bf16[4,128,128]{2,1,0:T(8,128)(2,1)S(1)}, bf16[4,128,128]{2,1,0:T(8,128)(2,1)S(1)}, u32[]{:S(2)}, u32[]{:S(2)}) collective-permute-start(bf16[4,128,128]{2,1,0:T(8,128)(2,1)S(1)} %fusion.15), channel_id=1, source_target_pairs={{0,8},{4,12},{8,0},{12,4},{16,24},{20,28},{24,16},{28,20},{1,9},{5... | collective-permute-start | bytes 393224 | tf_op jit(solution)/shard_map/ppermute | solution.py:319
  25.6 3.6 %collective-permute-start.7 = (bf16[4,128,128]{2,1,0:T(8,128)(2,1)S(1)}, bf16[4,128,128]{2,1,0:T(8,128)(2,1)S(1)}, u32[]{:S(2)}, u32[]{:S(2)}) collective-permute-start(bf16[4,128,128]{2,1,0:T(8,128)(2,1)S(1)} %add_convert_fusion.6), channel_id=1, source_target_pairs={{0,4},{4,0},{8,12},{12,8},{16,20},{20,16},{24,28},{28,24},{1,5},{5... | collective-permute-start | bytes 393224 | tf_op jit(solution)/shard_map/ppermute | solution.py:314
  26.7 8.8 %collective-permute-start.9 = (bf16[128,1024]{1,0:T(8,128)(2,1)S(1)}, bf16[128,1024]{1,0:T(8,128)(2,1)S(1)}, u32[]{:S(2)}, u32[]{:S(2)}) collective-permute-start(bf16[128,1024]{1,0:T(8,128)(2,1)S(1)} %slice.100), channel_id=1, source_target_pairs={{0,8},{4,12},{8,0},{12,4},{16,24},{20,28},{24,16},{28,20},{1,9},{5... | collective-permute-start | bytes 786440 | tf_op jit(solution)/shard_map/ppermute | solution.py:319
  28.1 8.4 %collective-permute-start.8 = (bf16[128,1024]{1,0:T(8,128)(2,1)S(1)}, bf16[128,1024]{1,0:T(8,128)(2,1)S(1)}, u32[]{:S(2)}, u32[]{:S(2)}) collective-permute-start(bf16[128,1024]{1,0:T(8,128)(2,1)S(1)} %slice.99), channel_id=1, source_target_pairs={{0,16},{4,20},{8,24},{12,28},{16,0},{20,4},{24,8},{28,12},{1,17},{... | collective-permute-start | bytes 786440 | tf_op jit(solution)/shard_map/ppermute | solution.py:319
  40.4 3.0 %collective-permute-start.10 = (bf16[512,1024]{1,0:T(8,128)(2,1)}, bf16[512,1024]{1,0:T(8,128)(2,1)}, u32[]{:S(2)}, u32[]{:S(2)}) collective-permute-start(bf16[512,1024]{1,0:T(8,128)(2,1)} %shard_map.94.own_ref.refs_6_.refs_5_), channel_id=1, source_target_pairs={{0,4},{4,0},{8,12},{12,8},{16,20},{20,16},{24,28},{28,24},{1,5},{5... | collective-permute-start | bytes 3145736 | tf_op jit(solution)/shard_map/ppermute | solution.py:314
  49.8 15.3 %collective-permute-start.15 = (bf16[1024,256]{1,0:T(8,128)(2,1)}, bf16[1024,256]{1,0:T(8,128)(2,1)}, u32[]{:S(2)}, u32[]{:S(2)}) collective-permute-start(bf16[1024,256]{1,0:T(8,128)(2,1)} %get-tuple-element.167), channel_id=1, source_target_pairs={{0,1},{3,2},{4,5},{7,6},{8,9},{11,10},{12,13},{15,14},{16,17},{19,... | collective-permute-start | bytes 1572872 | tf_op jit(solution)/shard_map/ppermute | solution.py:330
  67.0 10.8 %collective-permute-start.16 = (bf16[1024,256]{1,0:T(8,128)(2,1)}, bf16[1024,256]{1,0:T(8,128)(2,1)}, u32[]{:S(2)}, u32[]{:S(2)}) collective-permute-start(bf16[1024,256]{1,0:T(8,128)(2,1)} %fusion.6), channel_id=1, source_target_pairs={{1,2},{2,1},{5,6},{6,5},{9,10},{10,9},{13,14},{14,13},{17,18},{18,... | collective-permute-start | bytes 1572872 | tf_op jit(solution)/shard_map/ppermute | solution.py:330
  68.6 17.1 %collective-permute-start.18 = (bf16[1024,256]{1,0:T(8,128)(2,1)}, bf16[1024,256]{1,0:T(8,128)(2,1)}, u32[]{:S(2)}, u32[]{:S(2)}) collective-permute-start(bf16[1024,256]{1,0:T(8,128)(2,1)} %get-tuple-element.91), channel_id=1, source_target_pairs={{0,1},{3,2},{4,5},{7,6},{8,9},{11,10},{12,13},{15,14},{16,17},{19,... | collective-permute-start | bytes 1572872 | tf_op jit(solution)/shard_map/ppermute | solution.py:330
  75.8 16.3 %collective-permute-start.11 = (bf16[256,1024]{1,0:T(8,128)(2,1)S(1)}, bf16[256,1024]{1,0:T(8,128)(2,1)}, u32[]{:S(2)}, u32[]{:S(2)}) collective-permute-start(bf16[256,1024]{1,0:T(8,128)(2,1)S(1)} %get-tuple-element.87.refs_0_.refs_7_), channel_id=1, source_target_pairs={{0,8},{4,12},{8,0},{12,4},{16,24},{20,28},{24,16},{28,20},{1,9},{5... | collective-permute-start | bytes 1572872 | tf_op jit(solution)/shard_map/ppermute | solution.py:319
  76.6 18.3 %collective-permute-start.12 = (bf16[256,1024]{1,0:T(8,128)(2,1)S(1)}, bf16[256,1024]{1,0:T(8,128)(2,1)}, u32[]{:S(2)}, u32[]{:S(2)}) collective-permute-start(bf16[256,1024]{1,0:T(8,128)(2,1)S(1)} %get-tuple-element.87.refs_0_.refs_7_), channel_id=1, source_target_pairs={{0,16},{4,20},{8,24},{12,28},{16,0},{20,4},{24,8},{28,12},{1,17},{... | collective-permute-start | bytes 1572872 | tf_op jit(solution)/shard_map/ppermute | solution.py:319
  88.1 13.3 %collective-permute-start.17 = (bf16[1024,256]{1,0:T(8,128)(2,1)}, bf16[1024,256]{1,0:T(8,128)(2,1)}, u32[]{:S(2)}, u32[]{:S(2)}) collective-permute-start(bf16[1024,256]{1,0:T(8,128)(2,1)} %get-tuple-element.165), channel_id=1, source_target_pairs={{0,1},{2,3},{1,0},{3,2},{4,5},{6,7},{5,4},{7,6},{8,9},{10,11},{9,8... | collective-permute-start | bytes 1572872 | tf_op jit(solution)/shard_map/ppermute | solution.py:330
  90.6 10.8 %collective-permute-start.19 = (bf16[1024,256]{1,0:T(8,128)(2,1)}, bf16[1024,256]{1,0:T(8,128)(2,1)}, u32[]{:S(2)}, u32[]{:S(2)}) collective-permute-start(bf16[1024,256]{1,0:T(8,128)(2,1)} %get-tuple-element.166), channel_id=1, source_target_pairs={{1,2},{2,1},{5,6},{6,5},{9,10},{10,9},{13,14},{14,13},{17,18},{18,... | collective-permute-start | bytes 1572872 | tf_op jit(solution)/shard_map/ppermute | solution.py:330
  93.7 6.7 %collective-permute-start.13 = (bf16[128,1024]{1,0:T(8,128)(2,1)}, bf16[128,1024]{1,0:T(8,128)(2,1)}, u32[]{:S(2)}, u32[]{:S(2)}) collective-permute-start(bf16[128,1024]{1,0:T(8,128)(2,1)} %slice.130), channel_id=1, source_target_pairs={{0,16},{4,20},{8,24},{12,28},{16,0},{20,4},{24,8},{28,12},{1,17},{... | collective-permute-start | bytes 786440 | tf_op jit(solution)/shard_map/ppermute | solution.py:319
  95.8 13.1 %collective-permute-start.14 = (bf16[128,1024]{1,0:T(8,128)(2,1)S(1)}, bf16[128,1024]{1,0:T(8,128)(2,1)S(1)}, u32[]{:S(2)}, u32[]{:S(2)}) collective-permute-start(bf16[128,1024]{1,0:T(8,128)(2,1)S(1)} %slice.131), channel_id=1, source_target_pairs={{0,8},{4,12},{8,0},{12,4},{16,24},{20,28},{24,16},{28,20},{1,9},{5... | collective-permute-start | bytes 786440 | tf_op jit(solution)/shard_map/ppermute | solution.py:319
  103.1 12.0 %copy-start.13 = (bf16[1024,256]{1,0:T(8,128)(2,1)}, bf16[1024,256]{1,0:T(8,128)(2,1)S(1)}, u32[]{:S(2)}) copy-start(bf16[1024,256]{1,0:T(8,128)(2,1)S(1)} %get-tuple-element.147.refs_0_) | copy-start | bytes 1572868
  103.1 12.9 %collective-permute-start.21 = (bf16[1024,256]{1,0:T(8,128)(2,1)S(1)}, bf16[1024,256]{1,0:T(8,128)(2,1)S(1)}, u32[]{:S(2)}, u32[]{:S(2)}) collective-permute-start(bf16[1024,256]{1,0:T(8,128)(2,1)S(1)} %get-tuple-element.147.refs_0_), channel_id=1, source_target_pairs={{1,2},{2,1},{5,6},{6,5},{9,10},{10,9},{13,14},{14,13},{17,18},{18,... | collective-permute-start | bytes 1572872 | tf_op jit(solution)/shard_map/ppermute | solution.py:330
  103.8 14.0 %collective-permute-start.20 = (bf16[1024,256]{1,0:T(8,128)(2,1)S(1)}, bf16[1024,256]{1,0:T(8,128)(2,1)S(1)}, u32[]{:S(2)}, u32[]{:S(2)}) collective-permute-start(bf16[1024,256]{1,0:T(8,128)(2,1)S(1)} %get-tuple-element.147.refs_0_), channel_id=1, source_target_pairs={{0,1},{2,3},{1,0},{3,2},{4,5},{6,7},{5,4},{7,6},{8,9},{10,11},{9,8... | collective-permute-start | bytes 1572872 | tf_op jit(solution)/shard_map/ppermute | solution.py:330
  108.8 6.3 %collective-permute-start.22 = (bf16[512,256]{1,0:T(8,128)(2,1)S(1)}, bf16[512,256]{1,0:T(8,128)(2,1)S(1)}, u32[]{:S(2)}, u32[]{:S(2)}) collective-permute-start(bf16[512,256]{1,0:T(8,128)(2,1)S(1)} %slice.133), channel_id=1, source_target_pairs={{0,4},{4,0},{8,12},{12,8},{16,20},{20,16},{24,28},{28,24},{1,5},{5... | collective-permute-start | bytes 786440 | tf_op jit(solution)/shard_map/ppermute | solution.py:314
  115.9 35.8 %copy-start.20 = (bf16[1024,256]{1,0:T(8,128)(2,1)}, bf16[1024,256]{1,0:T(8,128)(2,1)S(1)}, u32[]{:S(2)}) copy-start(bf16[1024,256]{1,0:T(8,128)(2,1)S(1)} %collective-permute-done.21.refs_2_) | copy-start | bytes 1572868
  117.8 34.0 %copy-start.21 = (bf16[1024,256]{1,0:T(8,128)(2,1)}, bf16[1024,256]{1,0:T(8,128)(2,1)S(1)}, u32[]{:S(2)}) copy-start(bf16[1024,256]{1,0:T(8,128)(2,1)S(1)} %collective-permute-done.20.refs_1_) | copy-start | bytes 1572868
  117.8 8.7 %collective-permute-start.25 = (bf16[1024,256]{1,0:T(8,128)(2,1)S(1)}, bf16[1024,256]{1,0:T(8,128)(2,1)S(1)}, u32[]{:S(2)}, u32[]{:S(2)}) collective-permute-start(bf16[1024,256]{1,0:T(8,128)(2,1)S(1)} %collective-permute-done.20.refs_1_), channel_id=1, source_target_pairs={{1,2},{2,1},{5,6},{6,5},{9,10},{10,9},{13,14},{14,13},{17,18},{18,... | collective-permute-start | bytes 1572872 | tf_op jit(solution)/shard_map/ppermute | solution.py:330
  118.5 14.6 %collective-permute-start.24 = (bf16[1024,256]{1,0:T(8,128)(2,1)S(1)}, bf16[1024,256]{1,0:T(8,128)(2,1)S(1)}, u32[]{:S(2)}, u32[]{:S(2)}) collective-permute-start(bf16[1024,256]{1,0:T(8,128)(2,1)S(1)} %collective-permute-done.21.refs_2_), channel_id=1, source_target_pairs={{2,3},{1,0},{6,7},{5,4},{10,11},{9,8},{14,15},{13,12},{18,19},{17,... | collective-permute-start | bytes 1572872 | tf_op jit(solution)/shard_map/ppermute | solution.py:330
  119.8 42.0 %copy-start.4 = (bf16[1024,256]{1,0:T(8,128)(2,1)S(1)}, bf16[1024,256]{1,0:T(8,128)(2,1)}, u32[]{:S(2)}) copy-start(bf16[1024,256]{1,0:T(8,128)(2,1)} %get-tuple-element.102) | copy-start | bytes 1572868
  119.9 14.6 %collective-permute-start.23 = (bf16[1024,256]{1,0:T(8,128)(2,1)S(1)}, bf16[1024,256]{1,0:T(8,128)(2,1)S(1)}, u32[]{:S(2)}, u32[]{:S(2)}) collective-permute-start(bf16[1024,256]{1,0:T(8,128)(2,1)S(1)} %get-tuple-element.163), channel_id=1, source_target_pairs={{0,1},{3,2},{4,5},{7,6},{8,9},{11,10},{12,13},{15,14},{16,17},{19,... | collective-permute-start | bytes 1572872 | tf_op jit(solution)/shard_map/ppermute | solution.py:330
  126.5 18.3 %copy-start.22 = (bf16[1024,256]{1,0:T(8,128)(2,1)}, bf16[1024,256]{1,0:T(8,128)(2,1)S(1)}, u32[]{:S(2)}) copy-start(bf16[1024,256]{1,0:T(8,128)(2,1)S(1)} %collective-permute-done.25.refs_4_) | copy-start | bytes 1572868
  133.1 11.8 %collective-permute-start.28 = (bf16[1024,256]{1,0:T(8,128)(2,1)S(1)}, bf16[1024,256]{1,0:T(8,128)(2,1)S(1)}, u32[]{:S(2)}, u32[]{:S(2)}) collective-permute-start(bf16[1024,256]{1,0:T(8,128)(2,1)S(1)} %collective-permute-done.25.refs_4_), channel_id=1, source_target_pairs={{2,3},{1,0},{6,7},{5,4},{10,11},{9,8},{14,15},{13,12},{18,19},{17,... | collective-permute-start | bytes 1572872 | tf_op jit(solution)/shard_map/ppermute | solution.py:330
  134.6 10.2 %collective-permute-start.27 = (bf16[1024,256]{1,0:T(8,128)(2,1)S(1)}, bf16[1024,256]{1,0:T(8,128)(2,1)S(1)}, u32[]{:S(2)}, u32[]{:S(2)}) collective-permute-start(bf16[1024,256]{1,0:T(8,128)(2,1)S(1)} %fusion.1), channel_id=1, source_target_pairs={{1,2},{2,1},{5,6},{6,5},{9,10},{10,9},{13,14},{14,13},{17,18},{18,... | collective-permute-start | bytes 1572872 | tf_op jit(solution)/shard_map/ppermute | solution.py:330
  135.3 15.2 %collective-permute-start.26 = (bf16[1024,256]{1,0:T(8,128)(2,1)S(1)}, bf16[1024,256]{1,0:T(8,128)(2,1)S(1)}, u32[]{:S(2)}, u32[]{:S(2)}) collective-permute-start(bf16[1024,256]{1,0:T(8,128)(2,1)S(1)} %get-tuple-element.99), channel_id=1, source_target_pairs={{0,1},{3,2},{4,5},{7,6},{8,9},{11,10},{12,13},{15,14},{16,17},{19,... | collective-permute-start | bytes 1572872 | tf_op jit(solution)/shard_map/ppermute | solution.py:330
  151.8 10.1 %collective-permute-start.29 = (bf16[1024,256]{1,0:T(8,128)(2,1)}, bf16[1024,256]{1,0:T(8,128)(2,1)}, u32[]{:S(2)}, u32[]{:S(2)}) collective-permute-start(bf16[1024,256]{1,0:T(8,128)(2,1)} %get-tuple-element.161), channel_id=1, source_target_pairs={{0,1},{2,3},{1,0},{3,2},{4,5},{6,7},{5,4},{7,6},{8,9},{10,11},{9,8... | collective-permute-start | bytes 1572872 | tf_op jit(solution)/shard_map/ppermute | solution.py:330
  154.3 7.6 %collective-permute-start.30 = (bf16[1024,256]{1,0:T(8,128)(2,1)}, bf16[1024,256]{1,0:T(8,128)(2,1)}, u32[]{:S(2)}, u32[]{:S(2)}) collective-permute-start(bf16[1024,256]{1,0:T(8,128)(2,1)} %get-tuple-element.162), channel_id=1, source_target_pairs={{1,2},{2,1},{5,6},{6,5},{9,10},{10,9},{13,14},{14,13},{17,18},{18,... | collective-permute-start | bytes 1572872 | tf_op jit(solution)/shard_map/ppermute | solution.py:330
  163.4 17.0 %copy-start.14 = (bf16[1024,256]{1,0:T(8,128)(2,1)}, bf16[1024,256]{1,0:T(8,128)(2,1)S(1)}, u32[]{:S(2)}) copy-start(bf16[1024,256]{1,0:T(8,128)(2,1)S(1)} %get-tuple-element.145.refs_0_) | copy-start | bytes 1572868
  163.4 20.6 %collective-permute-start.32 = (bf16[1024,256]{1,0:T(8,128)(2,1)S(1)}, bf16[1024,256]{1,0:T(8,128)(2,1)S(1)}, u32[]{:S(2)}, u32[]{:S(2)}) collective-permute-start(bf16[1024,256]{1,0:T(8,128)(2,1)S(1)} %get-tuple-element.145.refs_0_), channel_id=1, source_target_pairs={{1,2},{2,1},{5,6},{6,5},{9,10},{10,9},{13,14},{14,13},{17,18},{18,... | collective-permute-start | bytes 1572872 | tf_op jit(solution)/shard_map/ppermute | solution.py:330
  164.1 19.9 %collective-permute-start.31 = (bf16[1024,256]{1,0:T(8,128)(2,1)S(1)}, bf16[1024,256]{1,0:T(8,128)(2,1)S(1)}, u32[]{:S(2)}, u32[]{:S(2)}) collective-permute-start(bf16[1024,256]{1,0:T(8,128)(2,1)S(1)} %get-tuple-element.145.refs_0_), channel_id=1, source_target_pairs={{0,1},{2,3},{1,0},{3,2},{4,5},{6,7},{5,4},{7,6},{8,9},{10,11},{9,8... | collective-permute-start | bytes 1572872 | tf_op jit(solution)/shard_map/ppermute | solution.py:330
  180.4 5.9 %collective-permute-start.37 = (bf16[512,256]{1,0:T(8,128)(2,1)S(1)}, bf16[512,256]{1,0:T(8,128)(2,1)S(1)}, u32[]{:S(2)}, u32[]{:S(2)}) collective-permute-start(bf16[512,256]{1,0:T(8,128)(2,1)S(1)} %slice.135), channel_id=1, source_target_pairs={{0,4},{4,0},{8,12},{12,8},{16,20},{20,16},{24,28},{28,24},{1,5},{5... | collective-permute-start | bytes 786440 | tf_op jit(solution)/shard_map/ppermute | solution.py:314
  181.8 19.1 %copy-start.1 = (bf16[4,256,1024]{2,1,0:T(8,128)(2,1)S(1)}, bf16[4,256,1024]{2,1,0:T(8,128)(2,1)}, u32[]{:S(2)}) copy-start(bf16[4,256,1024]{2,1,0:T(8,128)(2,1)} %get-tuple-element.107) | copy-start | bytes 6291460
  181.8 14.4 %collective-permute-start.36 = (bf16[2,128,1024]{2,1,0:T(8,128)(2,1)S(1)}, bf16[2,128,1024]{2,1,0:T(8,128)(2,1)S(1)}, u32[]{:S(2)}, u32[]{:S(2)}) collective-permute-start(bf16[2,128,1024]{2,1,0:T(8,128)(2,1)S(1)} %get-tuple-element.159), channel_id=1, source_target_pairs={{0,16},{4,20},{8,24},{12,28},{16,0},{20,4},{24,8},{28,12},{1,17},{... | collective-permute-start | bytes 1572872 | tf_op jit(solution)/shard_map/ppermute | solution.py:319
  182.9 14.0 %collective-permute-start.35 = (bf16[2,128,1024]{2,1,0:T(8,128)(2,1)S(1)}, bf16[2,128,1024]{2,1,0:T(8,128)(2,1)S(1)}, u32[]{:S(2)}, u32[]{:S(2)}) collective-permute-start(bf16[2,128,1024]{2,1,0:T(8,128)(2,1)S(1)} %get-tuple-element.160), channel_id=1, source_target_pairs={{0,8},{4,12},{8,0},{12,4},{16,24},{20,28},{24,16},{28,20},{1,9},{5... | collective-permute-start | bytes 1572872 | tf_op jit(solution)/shard_map/ppermute | solution.py:319
  184.0 17.2 %copy-start.25 = (bf16[1024,256]{1,0:T(8,128)(2,1)}, bf16[1024,256]{1,0:T(8,128)(2,1)S(1)}, u32[]{:S(2)}) copy-start(bf16[1024,256]{1,0:T(8,128)(2,1)S(1)} %collective-permute-done.32.refs_2_) | copy-start | bytes 1572868
  184.0 17.2 %copy-start.26 = (bf16[1024,256]{1,0:T(8,128)(2,1)}, bf16[1024,256]{1,0:T(8,128)(2,1)S(1)}, u32[]{:S(2)}) copy-start(bf16[1024,256]{1,0:T(8,128)(2,1)S(1)} %collective-permute-done.31.refs_1_) | copy-start | bytes 1572868
  184.0 15.6 %collective-permute-start.33 = (bf16[1024,256]{1,0:T(8,128)(2,1)S(1)}, bf16[1024,256]{1,0:T(8,128)(2,1)S(1)}, u32[]{:S(2)}, u32[]{:S(2)}) collective-permute-start(bf16[1024,256]{1,0:T(8,128)(2,1)S(1)} %collective-permute-done.32.refs_2_), channel_id=1, source_target_pairs={{2,3},{1,0},{6,7},{5,4},{10,11},{9,8},{14,15},{13,12},{18,19},{17,... | collective-permute-start | bytes 1572872 | tf_op jit(solution)/shard_map/ppermute | solution.py:330
  185.3 14.3 %collective-permute-start.34 = (bf16[1024,256]{1,0:T(8,128)(2,1)S(1)}, bf16[1024,256]{1,0:T(8,128)(2,1)S(1)}, u32[]{:S(2)}, u32[]{:S(2)}) collective-permute-start(bf16[1024,256]{1,0:T(8,128)(2,1)S(1)} %collective-permute-done.31.refs_1_), channel_id=1, source_target_pairs={{1,2},{2,1},{5,6},{6,5},{9,10},{10,9},{13,14},{14,13},{17,18},{18,... | collective-permute-start | bytes 1572872 | tf_op jit(solution)/shard_map/ppermute | solution.py:330
  196.2 18.4 %copy-start.9 = (bf16[2,128,1024]{2,1,0:T(8,128)(2,1)}, bf16[2,128,1024]{2,1,0:T(8,128)(2,1)S(1)}, u32[]{:S(2)}) copy-start(bf16[2,128,1024]{2,1,0:T(8,128)(2,1)S(1)} %collective-permute-done.36) | copy-start | bytes 1572868
  197.0 17.6 %copy-start.11 = (bf16[2,128,1024]{2,1,0:T(8,128)(2,1)}, bf16[2,128,1024]{2,1,0:T(8,128)(2,1)S(1)}, u32[]{:S(2)}) copy-start(bf16[2,128,1024]{2,1,0:T(8,128)(2,1)S(1)} %collective-permute-done.35) | copy-start | bytes 1572868
  199.6 15.7 %collective-permute-start.38 = (bf16[1024,256]{1,0:T(8,128)(2,1)S(1)}, bf16[1024,256]{1,0:T(8,128)(2,1)S(1)}, u32[]{:S(2)}, u32[]{:S(2)}) collective-permute-start(bf16[1024,256]{1,0:T(8,128)(2,1)S(1)} %collective-permute-done.34.refs_4_), channel_id=1, source_target_pairs={{2,3},{1,0},{6,7},{5,4},{10,11},{9,8},{14,15},{13,12},{18,19},{17,... | collective-permute-start | bytes 1572872 | tf_op jit(solution)/shard_map/ppermute | solution.py:330
  201.2 13.4 %collective-permute-start.40 = (bf16[128,1024]{1,0:T(8,128)(2,1)S(1)}, bf16[128,1024]{1,0:T(8,128)(2,1)S(1)}, u32[]{:S(2)}, u32[]{:S(2)}) collective-permute-start(bf16[128,1024]{1,0:T(8,128)(2,1)S(1)} %get-tuple-element.157), channel_id=1, source_target_pairs={{0,8},{4,12},{8,0},{12,4},{16,24},{20,28},{24,16},{28,20},{1,9},{5... | collective-permute-start | bytes 786440 | tf_op jit(solution)/shard_map/ppermute | solution.py:319
  202.2 12.3 %collective-permute-start.39 = (bf16[128,1024]{1,0:T(8,128)(2,1)S(1)}, bf16[128,1024]{1,0:T(8,128)(2,1)S(1)}, u32[]{:S(2)}, u32[]{:S(2)}) collective-permute-start(bf16[128,1024]{1,0:T(8,128)(2,1)S(1)} %get-tuple-element.158), channel_id=1, source_target_pairs={{0,16},{4,20},{8,24},{12,28},{16,0},{20,4},{24,8},{28,12},{1,17},{... | collective-permute-start | bytes 786440 | tf_op jit(solution)/shard_map/ppermute | solution.py:319
  221.6 3.6 %collective-permute-start.41 = (bf16[512,1024]{1,0:T(8,128)(2,1)}, bf16[512,1024]{1,0:T(8,128)(2,1)}, u32[]{:S(2)}, u32[]{:S(2)}) collective-permute-start(bf16[512,1024]{1,0:T(8,128)(2,1)} %get-tuple-element.124), channel_id=1, source_target_pairs={{0,4},{4,0},{8,12},{12,8},{16,20},{20,16},{24,28},{28,24},{1,5},{5... | collective-permute-start | bytes 3145736 | tf_op jit(solution)/shard_map/ppermute | solution.py:314
  223.2 21.3 %collective-permute-start.47 = (bf16[2,128,1024]{2,1,0:T(8,128)(2,1)S(1)}, bf16[2,128,1024]{2,1,0:T(8,128)(2,1)S(1)}, u32[]{:S(2)}, u32[]{:S(2)}) collective-permute-start(bf16[2,128,1024]{2,1,0:T(8,128)(2,1)S(1)} %get-tuple-element.155), channel_id=1, source_target_pairs={{0,16},{4,20},{8,24},{12,28},{16,0},{20,4},{24,8},{28,12},{1,17},{... | collective-permute-start | bytes 1572872 | tf_op jit(solution)/shard_map/ppermute | solution.py:319
  224.0 20.5 %collective-permute-start.46 = (bf16[2,128,1024]{2,1,0:T(8,128)(2,1)S(1)}, bf16[2,128,1024]{2,1,0:T(8,128)(2,1)S(1)}, u32[]{:S(2)}, u32[]{:S(2)}) collective-permute-start(bf16[2,128,1024]{2,1,0:T(8,128)(2,1)S(1)} %get-tuple-element.156), channel_id=1, source_target_pairs={{0,8},{4,12},{8,0},{12,4},{16,24},{20,28},{24,16},{28,20},{1,9},{5... | collective-permute-start | bytes 1572872 | tf_op jit(solution)/shard_map/ppermute | solution.py:319
  229.9 1.6 collective-permute-start.42
  231.6 13.1 %copy-start = (bf16[4,256,1024]{2,1,0:T(8,128)(2,1)S(1)}, bf16[4,256,1024]{2,1,0:T(8,128)(2,1)}, u32[]{:S(2)}) copy-start(bf16[4,256,1024]{2,1,0:T(8,128)(2,1)} %get-tuple-element.128) | copy-start | bytes 6291460
  231.6 12.9 %collective-permute-start.45 = (bf16[4,128,128]{2,1,0:T(8,128)(2,1)S(1)}, bf16[4,128,128]{2,1,0:T(8,128)(2,1)S(1)}, u32[]{:S(2)}, u32[]{:S(2)}) collective-permute-start(bf16[4,128,128]{2,1,0:T(8,128)(2,1)S(1)} %fusion.14), channel_id=1, source_target_pairs={{0,24},{4,28},{8,16},{12,20},{16,8},{20,12},{24,0},{28,4},{1,25},{... | collective-permute-start | bytes 393224 | tf_op jit(solution)/shard_map/ppermute | solution.py:319
  233.2 11.3 %collective-permute-start.44 = (bf16[4,128,128]{2,1,0:T(8,128)(2,1)S(1)}, bf16[4,128,128]{2,1,0:T(8,128)(2,1)S(1)}, u32[]{:S(2)}, u32[]{:S(2)}) collective-permute-start(bf16[4,128,128]{2,1,0:T(8,128)(2,1)S(1)} %fusion.14), channel_id=1, source_target_pairs={{0,16},{4,20},{8,24},{12,28},{16,0},{20,4},{24,8},{28,12},{1,17},{... | collective-permute-start | bytes 393224 | tf_op jit(solution)/shard_map/ppermute | solution.py:319
  234.0 10.6 %collective-permute-start.43 = (bf16[4,128,128]{2,1,0:T(8,128)(2,1)S(1)}, bf16[4,128,128]{2,1,0:T(8,128)(2,1)S(1)}, u32[]{:S(2)}, u32[]{:S(2)}) collective-permute-start(bf16[4,128,128]{2,1,0:T(8,128)(2,1)S(1)} %fusion.14), channel_id=1, source_target_pairs={{0,8},{4,12},{8,0},{12,4},{16,24},{20,28},{24,16},{28,20},{1,9},{5... | collective-permute-start | bytes 393224 | tf_op jit(solution)/shard_map/ppermute | solution.py:319
  244.6 2.5 collective-permute-start.50
  244.9 8.8 %collective-permute-start.49 = (bf16[128,1024]{1,0:T(8,128)(2,1)S(1)}, bf16[128,1024]{1,0:T(8,128)(2,1)S(1)}, u32[]{:S(2)}, u32[]{:S(2)}) collective-permute-start(bf16[128,1024]{1,0:T(8,128)(2,1)S(1)} %get-tuple-element.153), channel_id=1, source_target_pairs={{0,8},{4,12},{8,0},{12,4},{16,24},{20,28},{24,16},{28,20},{1,9},{5... | collective-permute-start | bytes 786440 | tf_op jit(solution)/shard_map/ppermute | solution.py:319
  245.8 8.4 %collective-permute-start.48 = (bf16[128,1024]{1,0:T(8,128)(2,1)S(1)}, bf16[128,1024]{1,0:T(8,128)(2,1)S(1)}, u32[]{:S(2)}, u32[]{:S(2)}) collective-permute-start(bf16[128,1024]{1,0:T(8,128)(2,1)S(1)} %get-tuple-element.154), channel_id=1, source_target_pairs={{0,16},{4,20},{8,24},{12,28},{16,0},{20,4},{24,8},{28,12},{1,17},{... | collective-permute-start | bytes 786440 | tf_op jit(solution)/shard_map/ppermute | solution.py:319
  (16 other events, 62.7 us)

commit v4 on v3

--- a/solution.py
+++ b/solution.py
@@ -103,10 +103,11 @@
         step = 1
     specs = {
         "h": pl.BlockSpec((rows, step * DH), lambda h: (0, h)),
+        "v": pl.BlockSpec((rows, step * DH), lambda h: (0, h)),
         "m": pl.BlockSpec((step, DH, DH), lambda h: (h, 0, 0)),
         "s": pl.BlockSpec((rows, 1), lambda h: (0, 0)),
     }
-    shapes = {"h": (rows, heads * DH), "m": (heads, DH, DH)}
+    shapes = {"h": (rows, heads * DH), "v": (rows, heads * DH), "m": (heads, DH, DH)}
     call = pl.pallas_call(
         kernel,
         grid=(heads // step,),
@@ -221,6 +222,7 @@
     step = 256 if width % 256 == 0 else DH
     block = pl.BlockSpec((rows, step), lambda k, unused: (0, k))
     pieces = pl.BlockSpec((chips, part, step), lambda k, unused: (0, 0, k))
+    place = jax.ShapeDtypeStruct if late else pltpu.HBM
     copies = sum(c.shape[1] for c in candidates) // part
     return pl.pallas_call(
         functools.partial(products_kernel, len(candidates), late, chips, len(earlier), factor),
@@ -239,9 +241,9 @@
             ],
         ),
         out_shape=[
-            pltpu.HBM((rows, width), F32),
-            pltpu.HBM((rows, width), F32),
-            pltpu.HBM((chips, part, width), BF16),
+            place((rows, width), F32),
+            place((rows, width), F32),
+            place((chips, part, width), BF16),
         ],
         compiler_params=pltpu.CompilerParams(vmem_limit_bytes=32 * rows * chips * part),
         cost_estimate=pl.CostEstimate(
@@ -295,9 +297,9 @@
             out_specs=[block, block, slot],
         ),
         out_shape=[
-            pltpu.HBM((rows, width), F32),
-            pltpu.HBM((rows, width), second_type),
-            pltpu.HBM(grads.shape, BF16),
+            jax.ShapeDtypeStruct((rows, width), F32),
+            jax.ShapeDtypeStruct((rows, width), second_type),
+            jax.ShapeDtypeStruct(grads.shape, BF16),
         ],
         input_output_aliases={6: 2},
         compiler_params=pltpu.CompilerParams(vmem_limit_bytes=VMEM_LIMIT),
@@ -306,7 +308,7 @@
             bytes_accessed=16 * rows * width,
             transcendentals=0,
         ),
-    )(meta, piece, *in_hbm([own, other, *totals, grads, *weights]))
+    )(meta, piece, own, other, *totals, grads, *weights)
 
 
 def core_swap(value):
@@ -476,11 +478,22 @@
     scale = lax.rsqrt(F32(DH) * positions)[:, None]
     (key_value,) = outer(key_rows, value_rows)
     half, other = swapped_halves(key_value)
+    half, query_rows = barrier((half, query_rows))
     arrived = [chip_swap(half, delta) for delta in range(1, chips)]
     near, rest = near_pieces(out_weight[:part])
     scaled, intra = call(
         forward_kernel, ins="hhhs", outs=[("h", BF16), ("h", F32)], macs=2 * rows * rows * DH
     )(query_rows, key_rows, value_rows, scale)
+    near, scaled, intra = barrier((near, scaled, intra))
+    pieces = rest(near)
+    arrived, scaled = barrier((arrived, scaled))
+    before = sum_of_others(half, arrived, other, True)
+    (attended,) = call(
+        attended_kernel, ins="hhm", outs=[("h", BF16)], macs=2 * rows * DH * DH, step=4
+    )(scaled, intra, before)
+    attended, pieces, target_rows = barrier((attended, pieces, target_rows))
+    other_attended = core_swap(attended)
+
     def features_of(array, group, first, count):
         found = [
             lax.dynamic_slice_in_dim(array, (2 * j + group) * held + first, count, 1)
@@ -499,15 +512,6 @@
         )
         for c in range(chunks)
     ]
-    near, scaled, intra = barrier((near, scaled, intra))
-    pieces = rest(near)
-    arrived, targets, scaled = barrier((arrived, targets, scaled))
-    before = sum_of_others(half, arrived, other, True)
-    before, pieces = barrier((before, pieces))
-    (attended,) = call(
-        attended_kernel, ins="hhm", outs=[("h", BF16)], macs=2 * rows * DH * DH, step=4
-    )(scaled, intra, before)
-    other_attended = core_swap(attended)
 
     outputs, grad_parts = [], []
     gate, totals, sent, gathered = None, (), None, {}
@@ -515,8 +519,8 @@
     for c in range(chunks):
         last = c == chunks - 1
         if c:
-            own_rows, unused = barrier((out_weight[c * part : (c + 1) * part], pieces[-1]))
-            near, rest = near_pieces(own_rows)
+            own_rows, unused = barrier((out_weight, pieces[-1]))
+            near, rest = near_pieces(own_rows[c * part : (c + 1) * part])
             pieces = rest(near)
         partial_out = project(attended, other_attended, pieces)
         if gate is not None:
@@ -608,13 +612,15 @@
         sent, second_step = scatter_start(grads)
 
     grad_attended = (totals[0] + core_swap(totals[1]).astype(F32)).astype(BF16)
-    (query_grad,) = outer(scaled, grad_attended)
+    (query_grad,) = call(outer_kernel, ins="vv", outs=[("m", F32)], macs=rows * DH * DH, step=4)(
+        scaled, grad_attended
+    )
     half, other = swapped_halves(query_grad)
     arrived = [chip_swap(half, delta) for delta in range(1, chips)]
     grad_query, key_part, value_part = call(
         backward_kernel,
-        ins="hhhhsm",
-        outs=[("h", BF16), ("h", F32), ("h", F32)],
+        ins="vvvvsm",
+        outs=[("h", BF16), ("v", F32), ("v", F32)],
         macs=5 * rows * rows * DH,
     )(scaled, key_rows, value_rows, grad_attended, scale, before)
     arrived, key_part, value_part, grad_query, sent = barrier(
@@ -623,7 +629,7 @@
     sent, finish = second_step(sent)
     after = sum_of_others(half, arrived, other, False)
     grad_key, grad_value = call(
-        finish_kernel, ins="hhhhm", outs=[("h", BF16), ("h", BF16)], macs=4 * rows * DH * DH
+        finish_kernel, ins="vvvvm", outs=[("h", BF16), ("h", BF16)], macs=4 * rows * DH * DH
     )(key_rows, value_rows, key_part, value_part, after)
     sent, grad_key, grad_value = barrier((sent, grad_key, grad_value))
     grad_weight = jnp.concatenate([*grad_parts, finish(sent)], axis=0)

time: 258 us -> 250 us (0.969)
  Pallas kernels: 66.7 us -> 60.3 us
  starting transfers between devices: 81.9 us -> 78.8 us
    pallas_call x6, Pallas kernels: 28 us -> 24.2 us  [on_values(): call(*[in_hbm([value])[0] if kind == 'h' else value for kind, value in zi...]
    ppermute x22, waiting for transfers between devices: 25.7 us -> 29 us  [chip_swap(): lax.ppermute(value, 'seq', [(j, j ^ 2 * delta) for j in range(count)])]
    dynamic_slice x2, local copies, waits for them, and re-layouts: 0.9 us -> 3.64 us  [features_of(): lax.dynamic_slice_in_dim(array, (2 * j + group) * held + first, count, 1)]
    ppermute x22, starting transfers between devices: 26.7 us -> 24.1 us  [chip_swap(): lax.ppermute(value, 'seq', [(j, j ^ 2 * delta) for j in range(count)])]
  transfers between devices with their start and end apart: 51 -> 51, of which waited for: 21 -> 26; matrix products, arithmetic and copies ran while one was open for 8% -> 9% of each run, Pallas kernels for 20% -> 19%
where the time goes in v4:
time: 250 us; the launch traced here: 249 us
  starting transfers between devices  78.8 us (32%)
  waiting for transfers between devices  76.4 us (31%)
  Pallas kernels  60.3 us (24%)
  other arithmetic  17.6 us (7%)
  local copies, waits for them, and re-layouts  14.1 us (6%)
    ppermute x20, starting transfers between devices, line_step(): lax.ppermute(value, 'head', pairs)  53.7 us
    ppermute x20, waiting for transfers between devices, line_step(): lax.ppermute(value, 'head', pairs)  43.8 us
    ppermute x22, waiting for transfers between devices, chip_swap(): lax.ppermute(value, 'seq', [(j, j ^ 2 * delta) for j in range(count)])  29 us
    pallas_call x6, Pallas kernels, on_values(): call(*[in_hbm([value])[0] if kind == 'h' else value for kind, value in zi...  24.2 us
    ppermute x22, starting transfers between devices, chip_swap(): lax.ppermute(value, 'seq', [(j, j ^ 2 * delta) for j in range(count)])  24.1 us
    pallas_call x2, Pallas kernels, products(): pl.pallas_call(functools.partial(products_kernel, len(candidates), late,...  20.7 us
    pallas_call x2, Pallas kernels, project(): pl.pallas_call(functools.partial(project_kernel, len(pieces), half), grid...  10.6 us
  transfers between devices with their start and end apart: 51, of which 26 were waited for; matrix products, arithmetic and copies ran while one was open for 9% of the time, Pallas kernels for 19%

profile of v4, /device:TPU:0, one launch (start us, length us, event | category | flops | bytes accessed | tf_op | source)
XLA Modules:
  0.0 248.7 jit_solution(13359127737985814966)
XLA Ops:
  0.6 2.0 shard_map.92
  3.3 2.6 %collective-permute-start.5 = (bf16[256,1024]{1,0:T(8,128)(2,1)S(1)}, bf16[256,1024]{1,0:T(8,128)(2,1)S(1)}, u32[]{:S(2)}, u32[]{:S(2)}) collective-permute-start(bf16[256,1024]{1,0:T(8,128)(2,1)S(1)} %slice.96.refs_0_.refs_8_), channel_id=1, source_target_pairs={{0,16},{4,20},{8,24},{12,28},{16,0},{20,4},{24,8},{28,12},{1,17},{... | collective-permute-start | bytes 1572872 | tf_op jit(solution)/shard_map/ppermute | solution.py:321
  5.9 1.5 collective-permute-start.4
  9.5 1.5 collective-permute-start.1
  11.1 6.2 %shard_map.93 = (bf16[512,1024]{1,0:T(8,128)(2,1)}, f32[512,1024]{1,0:T(8,128)}) custom-call(bf16[512,1024]{1,0:T(8,128)(2,1)} %q_ref, bf16[512,1024]{1,0:T(8,128)(2,1)} %k_ref.5, bf16[512,1024]{1,0:T(8,128)(2,1)} %v_ref.5, f32[512,1]{1,0:T(8,128)S(1)} %multiply_rsqrt_fusion.scale_ref), custom_call_target="tpu_custom_call" | custom-call | flops 1073741824 | bytes 6291456 | tf_op jit(solution)/shard_map/pallas_call | solution.py:129
  17.3 1.4 collective-permute-done.5.refs_2_.refs_10_
  18.7 2.0 collective-permute-done.4.refs_1_.refs_9_
  20.7 2.3 collective-permute-done.3
  24.1 1.5 collective-permute-done.1
  25.8 1.6 collective-permute-start.8
  28.0 3.1 %shard_map.94.own_ref.refs_6_.refs_5_ = bf16[512,1024]{1,0:T(8,128)(2,1)} custom-call(bf16[512,1024]{1,0:T(8,128)(2,1)} %get-tuple-element.81.scaled_ref.a_ref, f32[512,1024]{1,0:T(8,128)} %get-tuple-element.82.intra_ref, f32[8,128,128]{2,1,0:T(8,128)S(1)} %select_add_fusion.1.state_ref), custom_call_target="tpu_custom_call" | custom-call | flops 268435456 | bytes 4194304 | tf_op jit(solution)/shard_map/pallas_call | solution.py:129
  31.1 3.5 %collective-permute-done.8 = bf16[128,1024]{1,0:T(8,128)(2,1)S(1)} collective-permute-done((bf16[128,1024]{1,0:T(8,128)(2,1)S(1)}, bf16[128,1024]{1,0:T(8,128)(2,1)S(1)}, u32[]{:S(2)}, u32[]{:S(2)}) %collective-permute-start.8) | collective-permute-done | bytes 262176 | tf_op jit(solution)/shard_map/ppermute | solution.py:321
  36.6 3.0 %collective-permute-done.9.other_ref.refs_7_.refs_6_ = bf16[512,1024]{1,0:T(8,128)(2,1)} collective-permute-done((bf16[512,1024]{1,0:T(8,128)(2,1)}, bf16[512,1024]{1,0:T(8,128)(2,1)}, u32[]{:S(2)}, u32[]{:S(2)}) %collective-permute-start.9) | collective-permute-done | bytes 1048608 | tf_op jit(solution)/shard_map/ppermute | solution.py:316
  39.6 5.3 %shard_map.96 = bf16[4,1024,256]{2,1,0:T(8,128)(2,1)S(1)} custom-call(bf16[512,1024]{1,0:T(8,128)(2,1)} %shard_map.94.own_ref.refs_6_.refs_5_, bf16[512,1024]{1,0:T(8,128)(2,1)} %collective-permute-done.9.other_ref.refs_7_.refs_6_, bf16[256,1024]{1,0:T(8,128)(2,1)} %copy-done.13, bf16[256,1024]{1,0:T(8,128)(2,1)} %copy-done.23, ...), custom_call_target="tpu_custom_call" | custom-call | flops 2147483648 | bytes 4194304 | tf_op jit(solution)/shard_map/pallas_call | solution.py:150
  46.0 3.5 %collective-permute-start.14 = (bf16[1024,256]{1,0:T(8,128)(2,1)}, bf16[1024,256]{1,0:T(8,128)(2,1)S(1)}, u32[]{:S(2)}, u32[]{:S(2)}) collective-permute-start(bf16[1024,256]{1,0:T(8,128)(2,1)} %get-tuple-element.169), channel_id=1, source_target_pairs={{0,1},{3,2},{4,5},{7,6},{8,9},{11,10},{12,13},{15,14},{16,17},{19,... | collective-permute-start | bytes 1572872 | tf_op jit(solution)/shard_map/ppermute | solution.py:332
  49.5 11.7 %collective-permute-done.14 = bf16[1024,256]{1,0:T(8,128)(2,1)S(1)} collective-permute-done((bf16[1024,256]{1,0:T(8,128)(2,1)}, bf16[1024,256]{1,0:T(8,128)(2,1)S(1)}, u32[]{:S(2)}, u32[]{:S(2)}) %collective-permute-start.14) | collective-permute-done | bytes 524320 | tf_op jit(solution)/shard_map/ppermute | solution.py:332
  62.2 1.5 collective-permute-start.15
  63.6 7.1 %collective-permute-start.17 = (bf16[1024,256]{1,0:T(8,128)(2,1)}, bf16[1024,256]{1,0:T(8,128)(2,1)}, u32[]{:S(2)}, u32[]{:S(2)}) collective-permute-start(bf16[1024,256]{1,0:T(8,128)(2,1)} %get-tuple-element.94), channel_id=1, source_target_pairs={{0,1},{3,2},{4,5},{7,6},{8,9},{11,10},{12,13},{15,14},{16,17},{19,... | collective-permute-start | bytes 1572872 | tf_op jit(solution)/shard_map/ppermute | solution.py:332
  72.9 1.9 constant_dynamic-slice_fusion.1
  74.8 5.8 %collective-permute-done.17 = bf16[1024,256]{1,0:T(8,128)(2,1)} collective-permute-done((bf16[1024,256]{1,0:T(8,128)(2,1)}, bf16[1024,256]{1,0:T(8,128)(2,1)}, u32[]{:S(2)}, u32[]{:S(2)}) %collective-permute-start.17) | collective-permute-done | bytes 524320 | tf_op jit(solution)/shard_map/ppermute | solution.py:332
  80.6 2.4 fusion.7
  83.1 2.5 collective-permute-start.16
  85.5 1.5 collective-permute-start.18
  88.5 1.8 constant_dynamic-slice_fusion.2
  91.9 1.8 fusion.20
  94.4 1.6 collective-permute-done.16
  96.0 1.5 subtract_convert_fusion.1
  98.3 5.4 %collective-permute-start.20 = (bf16[1024,256]{1,0:T(8,128)(2,1)S(1)}, bf16[1024,256]{1,0:T(8,128)(2,1)S(1)}, u32[]{:S(2)}, u32[]{:S(2)}) collective-permute-start(bf16[1024,256]{1,0:T(8,128)(2,1)S(1)} %get-tuple-element.149.refs_0_), channel_id=1, source_target_pairs={{0,1},{2,3},{1,0},{3,2},{4,5},{6,7},{5,4},{7,6},{8,9},{10,11},{9,8... | collective-permute-start | bytes 1572872 | tf_op jit(solution)/shard_map/ppermute | solution.py:332
  104.6 5.3 %shard_map.95 = bf16[4,1024,256]{2,1,0:T(8,128)(2,1)S(1)} custom-call(bf16[512,1024]{1,0:T(8,128)(2,1)} %shard_map.94.own_ref.refs_6_.refs_5_, bf16[512,1024]{1,0:T(8,128)(2,1)} %collective-permute-done.9.other_ref.refs_7_.refs_6_, bf16[256,1024]{1,0:T(8,128)(2,1)} %copy-done.4, bf16[256,1024]{1,0:T(8,128)(2,1)} %collective-permute-done.10.refs_1_.refs_8_, ...), custom_call_target="tpu_custom_call" | custom-call | flops 2147483648 | bytes 4194304 | tf_op jit(solution)/shard_map/pallas_call | solution.py:150
  110.7 2.0 collective-permute-done.20.refs_1_
  113.3 1.3 collective-permute-start.24
  114.7 6.6 %collective-permute-start.23 = (bf16[1024,256]{1,0:T(8,128)(2,1)S(1)}, bf16[1024,256]{1,0:T(8,128)(2,1)S(1)}, u32[]{:S(2)}, u32[]{:S(2)}) collective-permute-start(bf16[1024,256]{1,0:T(8,128)(2,1)S(1)} %get-tuple-element.165), channel_id=1, source_target_pairs={{0,1},{3,2},{4,5},{7,6},{8,9},{11,10},{12,13},{15,14},{16,17},{19,... | collective-permute-start | bytes 1572872 | tf_op jit(solution)/shard_map/ppermute | solution.py:332
  121.4 6.4 %collective-permute-done.24.refs_3_ = bf16[1024,256]{1,0:T(8,128)(2,1)S(1)} collective-permute-done((bf16[1024,256]{1,0:T(8,128)(2,1)S(1)}, bf16[1024,256]{1,0:T(8,128)(2,1)S(1)}, u32[]{:S(2)}, u32[]{:S(2)}) %collective-permute-start.24) | collective-permute-done | bytes 524320 | tf_op jit(solution)/shard_map/ppermute | solution.py:332
  127.8 1.3 collective-permute-start.28
  130.0 7.1 %collective-permute-start.26 = (bf16[1024,256]{1,0:T(8,128)(2,1)S(1)}, bf16[1024,256]{1,0:T(8,128)(2,1)S(1)}, u32[]{:S(2)}, u32[]{:S(2)}) collective-permute-start(bf16[1024,256]{1,0:T(8,128)(2,1)S(1)} %get-tuple-element.102), channel_id=1, source_target_pairs={{0,1},{3,2},{4,5},{7,6},{8,9},{11,10},{12,13},{15,14},{16,17},{19,... | collective-permute-start | bytes 1572872 | tf_op jit(solution)/shard_map/ppermute | solution.py:332
  137.1 2.2 collective-permute-done.28.refs_5_
  139.4 5.8 %collective-permute-done.26 = bf16[1024,256]{1,0:T(8,128)(2,1)S(1)} collective-permute-done((bf16[1024,256]{1,0:T(8,128)(2,1)S(1)}, bf16[1024,256]{1,0:T(8,128)(2,1)S(1)}, u32[]{:S(2)}, u32[]{:S(2)}) %collective-permute-start.26) | collective-permute-done | bytes 524320 | tf_op jit(solution)/shard_map/ppermute | solution.py:332
  145.1 1.3 fusion.2
  146.4 2.5 %collective-permute-start.29 = (bf16[1024,256]{1,0:T(8,128)(2,1)}, bf16[1024,256]{1,0:T(8,128)(2,1)}, u32[]{:S(2)}, u32[]{:S(2)}) collective-permute-start(bf16[1024,256]{1,0:T(8,128)(2,1)} %get-tuple-element.163), channel_id=1, source_target_pairs={{0,1},{2,3},{1,0},{3,2},{4,5},{6,7},{5,4},{7,6},{8,9},{10,11},{9,8... | collective-permute-start | bytes 1572872 | tf_op jit(solution)/shard_map/ppermute | solution.py:332
  149.0 1.5 collective-permute-start.30
  150.5 5.9 %collective-permute-done.29 = bf16[1024,256]{1,0:T(8,128)(2,1)} collective-permute-done((bf16[1024,256]{1,0:T(8,128)(2,1)}, bf16[1024,256]{1,0:T(8,128)(2,1)}, u32[]{:S(2)}, u32[]{:S(2)}) %collective-permute-start.29) | collective-permute-done | bytes 524320 | tf_op jit(solution)/shard_map/ppermute | solution.py:332
  156.4 1.6 subtract_convert_fusion
  158.7 5.8 %collective-permute-start.31 = (bf16[1024,256]{1,0:T(8,128)(2,1)S(1)}, bf16[1024,256]{1,0:T(8,128)(2,1)S(1)}, u32[]{:S(2)}, u32[]{:S(2)}) collective-permute-start(bf16[1024,256]{1,0:T(8,128)(2,1)S(1)} %get-tuple-element.147.refs_0_), channel_id=1, source_target_pairs={{0,1},{2,3},{1,0},{3,2},{4,5},{6,7},{5,4},{7,6},{8,9},{10,11},{9,8... | collective-permute-start | bytes 1572872 | tf_op jit(solution)/shard_map/ppermute | solution.py:332
  164.5 10.6 %shard_map.97 = (f32[512,1024]{1,0:T(8,128)}, f32[512,1024]{1,0:T(8,128)}, bf16[4,256,1024]{2,1,0:T(8,128)(2,1)}) custom-call(s32[12]{0:T(128)S(1)} %stack.93.meta_ref, bf16[1024,256]{1,0:T(8,128)(2,1)} %copy-done.18, bf16[1024,256]{1,0:T(8,128)(2,1)} %copy-done.25, bf16[1024,256]{1,0:T(8,128)(2,1)} %copy-done.24, bf16[1024,256]{1,0:T(8,128)(2,1)} %copy-done.27, ...), custom_call_target="tpu_custom_call" | custom-call | flops 4294967296 | bytes 8388608 | tf_op jit(solution)/shard_map/pallas_call | solution.py:227
  175.2 1.3 fusion.19
  177.7 1.3 collective-permute-start.33
  181.1 9.8 %collective-permute-done.36 = bf16[2,128,1024]{2,1,0:T(8,128)(2,1)S(1)} collective-permute-done((bf16[2,128,1024]{2,1,0:T(8,128)(2,1)S(1)}, bf16[2,128,1024]{2,1,0:T(8,128)(2,1)S(1)}, u32[]{:S(2)}, u32[]{:S(2)}) %collective-permute-start.36) | collective-permute-done | bytes 524320 | tf_op jit(solution)/shard_map/ppermute | solution.py:321
  191.2 2.2 collective-permute-done.33.refs_3_
  193.3 1.3 collective-permute-start.38
  195.9 1.6 collective-permute-start.40
  197.5 1.6 collective-permute-start.39
  199.0 10.2 %shard_map.98 = (f32[512,1024]{1,0:T(8,128)S(1)}, f32[512,1024]{1,0:T(8,128)S(1)}, bf16[4,256,1024]{2,1,0:T(8,128)(2,1)S(1)}) custom-call(s32[12]{0:T(128)S(1)} %stack.93.meta_ref, bf16[1024,256]{1,0:T(8,128)(2,1)} %copy-done.19, bf16[1024,256]{1,0:T(8,128)(2,1)} %copy-done.30, bf16[1024,256]{1,0:T(8,128)(2,1)} %copy-done.29, bf16[1024,256]{1,0:T(8,128)(2,1)} %copy-done.32, ...), custom_call_target="tpu_custom_call" | custom-call | flops 4294967296 | bytes 8388608 | tf_op jit(solution)/shard_map/pallas_call | solution.py:227
  210.0 4.7 %shard_map.99 = (f32[512,1024]{1,0:T(8,128)S(1)}, bf16[512,1024]{1,0:T(8,128)(2,1)}, bf16[4,256,1024]{2,1,0:T(8,128)(2,1)S(1)}) custom-call(s32[2]{0:T(128)S(1)} %pad_add_fusion.meta_ref, bf16[1024,256]{1,0:T(8,128)(2,1)S(1)} %collective-permute-done.38.piece_ref, bf16[512,1024]{1,0:T(8,128)(2,1)S(1)} %copy-done.3, ...), custom_call_target="tpu_custom_call", output_to_operand_aliasing={{2}: (6, {})} | custom-call | flops 1073741824 | bytes 8388608 | tf_op jit(solution)/shard_map/pallas_call | solution.py:290
  214.6 1.3 copy-done.6
  216.8 1.5 collective-permute-start.46
  219.0 1.7 add_convert_fusion.b_ref.g_ref
  222.0 1.4 bitcast_add_fusion.3
  223.5 1.7 collective-permute-start.45
  225.7 1.3 collective-permute-start.43
  227.1 8.7 %shard_map.101 = (bf16[512,1024]{1,0:T(8,128)(2,1)}, f32[512,1024]{1,0:T(8,128)S(1)}, f32[512,1024]{1,0:T(8,128)S(1)}) custom-call(bf16[512,1024]{1,0:T(8,128)(2,1)S(1)} %copy-done.2, bf16[512,1024]{1,0:T(8,128)(2,1)S(1)} %copy-done, bf16[512,1024]{1,0:T(8,128)(2,1)S(1)} %copy-done.1, bf16[512,1024]{1,0:T(8,128)(2,1)S(1)} %add_convert_fusion.b_ref.g_ref, ...), custom_call_target="tpu_custom_call" | custom-call | flops 2684354560 | bytes 9437184 | tf_op jit(solution)/shard_map/pallas_call | solution.py:129
  236.9 1.5 collective-permute-start.49
  239.1 3.4 %shard_map.102 = (bf16[512,1024]{1,0:T(8,128)(2,1)}, bf16[512,1024]{1,0:T(8,128)(2,1)}) custom-call(bf16[512,1024]{1,0:T(8,128)(2,1)S(1)} %copy-done, bf16[512,1024]{1,0:T(8,128)(2,1)S(1)} %copy-done.1, f32[512,1024]{1,0:T(8,128)S(1)} %get-tuple-element.134.dk_part_ref, f32[512,1024]{1,0:T(8,128)S(1)} %get-tuple-element.135.dv_part_ref, ...), custom_call_target="tpu_custom_call" | custom-call | flops 536870912 | bytes 7340032 | tf_op jit(solution)/shard_map/pallas_call | solution.py:129
  242.4 3.2 %collective-permute-done.49 = bf16[128,1024]{1,0:T(8,128)(2,1)S(1)} collective-permute-done((bf16[128,1024]{1,0:T(8,128)(2,1)S(1)}, bf16[128,1024]{1,0:T(8,128)(2,1)S(1)}, u32[]{:S(2)}, u32[]{:S(2)}) %collective-permute-start.49) | collective-permute-done | bytes 262176 | tf_op jit(solution)/shard_map/ppermute | solution.py:321
  247.1 1.6 pad_maximum_fusion
  (163 shorter events, 31.8 us)
Async XLA Ops:
  2.7 4.7 %collective-permute-start = (bf16[8,128,128]{2,1,0:T(8,128)(2,1)S(1)}, bf16[8,128,128]{2,1,0:T(8,128)(2,1)S(1)}, u32[]{:S(2)}, u32[]{:S(2)}) collective-permute-start(bf16[8,128,128]{2,1,0:T(8,128)(2,1)S(1)} %convert_element_type.304), channel_id=1, source_target_pairs={{0,4},{4,0},{8,12},{12,8},{16,20},{20,16},{24,28},{28,24},{1,5},{5... | collective-permute-start | bytes 786440 | tf_op jit(solution)/shard_map/ppermute | solution.py:316
  3.3 14.0 %copy-start.13 = (bf16[256,1024]{1,0:T(8,128)(2,1)}, bf16[256,1024]{1,0:T(8,128)(2,1)S(1)}, u32[]{:S(2)}) copy-start(bf16[256,1024]{1,0:T(8,128)(2,1)S(1)} %slice.96.refs_0_.refs_8_) | copy-start | bytes 1572868
  3.3 15.4 %collective-permute-start.5 = (bf16[256,1024]{1,0:T(8,128)(2,1)S(1)}, bf16[256,1024]{1,0:T(8,128)(2,1)S(1)}, u32[]{:S(2)}, u32[]{:S(2)}) collective-permute-start(bf16[256,1024]{1,0:T(8,128)(2,1)S(1)} %slice.96.refs_0_.refs_8_), channel_id=1, source_target_pairs={{0,16},{4,20},{8,24},{12,28},{16,0},{20,4},{24,8},{28,12},{1,17},{... | collective-permute-start | bytes 1572872 | tf_op jit(solution)/shard_map/ppermute | solution.py:321
  5.9 14.8 %collective-permute-start.4 = (bf16[256,1024]{1,0:T(8,128)(2,1)S(1)}, bf16[256,1024]{1,0:T(8,128)(2,1)S(1)}, u32[]{:S(2)}, u32[]{:S(2)}) collective-permute-start(bf16[256,1024]{1,0:T(8,128)(2,1)S(1)} %slice.96.refs_0_.refs_8_), channel_id=1, source_target_pairs={{0,8},{4,12},{8,0},{12,4},{16,24},{20,28},{24,16},{28,20},{1,9},{5... | collective-permute-start | bytes 1572872 | tf_op jit(solution)/shard_map/ppermute | solution.py:321
  7.5 15.5 %collective-permute-start.3 = (bf16[4,128,128]{2,1,0:T(8,128)(2,1)S(1)}, bf16[4,128,128]{2,1,0:T(8,128)(2,1)S(1)}, u32[]{:S(2)}, u32[]{:S(2)}) collective-permute-start(bf16[4,128,128]{2,1,0:T(8,128)(2,1)S(1)} %fusion.15), channel_id=1, source_target_pairs={{0,24},{4,28},{8,16},{12,20},{16,8},{20,12},{24,0},{28,4},{1,25},{... | collective-permute-start | bytes 393224 | tf_op jit(solution)/shard_map/ppermute | solution.py:321
  8.4 15.7 %collective-permute-start.2 = (bf16[4,128,128]{2,1,0:T(8,128)(2,1)S(1)}, bf16[4,128,128]{2,1,0:T(8,128)(2,1)S(1)}, u32[]{:S(2)}, u32[]{:S(2)}) collective-permute-start(bf16[4,128,128]{2,1,0:T(8,128)(2,1)S(1)} %fusion.15), channel_id=1, source_target_pairs={{0,16},{4,20},{8,24},{12,28},{16,0},{20,4},{24,8},{28,12},{1,17},{... | collective-permute-start | bytes 393224 | tf_op jit(solution)/shard_map/ppermute | solution.py:321
  9.5 16.0 %collective-permute-start.1 = (bf16[4,128,128]{2,1,0:T(8,128)(2,1)S(1)}, bf16[4,128,128]{2,1,0:T(8,128)(2,1)S(1)}, u32[]{:S(2)}, u32[]{:S(2)}) collective-permute-start(bf16[4,128,128]{2,1,0:T(8,128)(2,1)S(1)} %fusion.15), channel_id=1, source_target_pairs={{0,8},{4,12},{8,0},{12,4},{16,24},{20,28},{24,16},{28,20},{1,9},{5... | collective-permute-start | bytes 393224 | tf_op jit(solution)/shard_map/ppermute | solution.py:321
  18.7 12.4 %copy-start.22 = (bf16[256,1024]{1,0:T(8,128)(2,1)}, bf16[256,1024]{1,0:T(8,128)(2,1)S(1)}, u32[]{:S(2)}) copy-start(bf16[256,1024]{1,0:T(8,128)(2,1)S(1)} %collective-permute-done.5.refs_2_.refs_10_) | copy-start | bytes 1572868
  25.7 2.2 collective-permute-start.6
  25.8 8.8 %collective-permute-start.8 = (bf16[128,1024]{1,0:T(8,128)(2,1)S(1)}, bf16[128,1024]{1,0:T(8,128)(2,1)S(1)}, u32[]{:S(2)}, u32[]{:S(2)}) collective-permute-start(bf16[128,1024]{1,0:T(8,128)(2,1)S(1)} %slice.98), channel_id=1, source_target_pairs={{0,8},{4,12},{8,0},{12,4},{16,24},{20,28},{24,16},{28,20},{1,9},{5... | collective-permute-start | bytes 786440 | tf_op jit(solution)/shard_map/ppermute | solution.py:321
  27.4 8.4 %collective-permute-start.7 = (bf16[128,1024]{1,0:T(8,128)(2,1)S(1)}, bf16[128,1024]{1,0:T(8,128)(2,1)S(1)}, u32[]{:S(2)}, u32[]{:S(2)}) collective-permute-start(bf16[128,1024]{1,0:T(8,128)(2,1)S(1)} %slice.97), channel_id=1, source_target_pairs={{0,16},{4,20},{8,24},{12,28},{16,0},{20,4},{24,8},{28,12},{1,17},{... | collective-permute-start | bytes 786440 | tf_op jit(solution)/shard_map/ppermute | solution.py:321
  36.6 3.0 %collective-permute-start.9 = (bf16[512,1024]{1,0:T(8,128)(2,1)}, bf16[512,1024]{1,0:T(8,128)(2,1)}, u32[]{:S(2)}, u32[]{:S(2)}) collective-permute-start(bf16[512,1024]{1,0:T(8,128)(2,1)} %shard_map.94.own_ref.refs_6_.refs_5_), channel_id=1, source_target_pairs={{0,4},{4,0},{8,12},{12,8},{16,20},{20,16},{24,28},{28,24},{1,5},{5... | collective-permute-start | bytes 3145736 | tf_op jit(solution)/shard_map/ppermute | solution.py:316
  46.0 15.3 %collective-permute-start.14 = (bf16[1024,256]{1,0:T(8,128)(2,1)}, bf16[1024,256]{1,0:T(8,128)(2,1)S(1)}, u32[]{:S(2)}, u32[]{:S(2)}) collective-permute-start(bf16[1024,256]{1,0:T(8,128)(2,1)} %get-tuple-element.169), channel_id=1, source_target_pairs={{0,1},{3,2},{4,5},{7,6},{8,9},{11,10},{12,13},{15,14},{16,17},{19,... | collective-permute-start | bytes 1572872 | tf_op jit(solution)/shard_map/ppermute | solution.py:332
  62.2 12.7 %collective-permute-start.15 = (bf16[1024,256]{1,0:T(8,128)(2,1)}, bf16[1024,256]{1,0:T(8,128)(2,1)}, u32[]{:S(2)}, u32[]{:S(2)}) collective-permute-start(bf16[1024,256]{1,0:T(8,128)(2,1)} %fusion.6), channel_id=1, source_target_pairs={{1,2},{2,1},{5,6},{6,5},{9,10},{10,9},{13,14},{14,13},{17,18},{18,... | collective-permute-start | bytes 1572872 | tf_op jit(solution)/shard_map/ppermute | solution.py:332
  63.6 17.0 %collective-permute-start.17 = (bf16[1024,256]{1,0:T(8,128)(2,1)}, bf16[1024,256]{1,0:T(8,128)(2,1)}, u32[]{:S(2)}, u32[]{:S(2)}) collective-permute-start(bf16[1024,256]{1,0:T(8,128)(2,1)} %get-tuple-element.94), channel_id=1, source_target_pairs={{0,1},{3,2},{4,5},{7,6},{8,9},{11,10},{12,13},{15,14},{16,17},{19,... | collective-permute-start | bytes 1572872 | tf_op jit(solution)/shard_map/ppermute | solution.py:332
  71.8 15.2 %collective-permute-start.10 = (bf16[256,1024]{1,0:T(8,128)(2,1)S(1)}, bf16[256,1024]{1,0:T(8,128)(2,1)}, u32[]{:S(2)}, u32[]{:S(2)}) collective-permute-start(bf16[256,1024]{1,0:T(8,128)(2,1)S(1)} %slice.99.refs_0_.refs_7_), channel_id=1, source_target_pairs={{0,8},{4,12},{8,0},{12,4},{16,24},{20,28},{24,16},{28,20},{1,9},{5... | collective-permute-start | bytes 1572872 | tf_op jit(solution)/shard_map/ppermute | solution.py:321
  72.4 17.9 %collective-permute-start.11 = (bf16[256,1024]{1,0:T(8,128)(2,1)S(1)}, bf16[256,1024]{1,0:T(8,128)(2,1)}, u32[]{:S(2)}, u32[]{:S(2)}) collective-permute-start(bf16[256,1024]{1,0:T(8,128)(2,1)S(1)} %slice.99.refs_0_.refs_7_), channel_id=1, source_target_pairs={{0,16},{4,20},{8,24},{12,28},{16,0},{20,4},{24,8},{28,12},{1,17},{... | collective-permute-start | bytes 1572872 | tf_op jit(solution)/shard_map/ppermute | solution.py:321
  74.8 17.1 %collective-permute-start.19 = (bf16[512,512]{1,0:T(8,128)(2,1)}, bf16[512,512]{1,0:T(8,128)(2,1)}, u32[]{:S(2)}, u32[]{:S(2)}) collective-permute-start(bf16[512,512]{1,0:T(8,128)(2,1)} %constant_dynamic-slice_fusion.1), channel_id=1, source_target_pairs={{0,4},{4,0},{8,12},{12,8},{16,20},{20,16},{24,28},{28,24},{1,5},{5... | collective-permute-start | bytes 1572872 | tf_op jit(solution)/shard_map/ppermute | solution.py:316
  83.1 13.0 %collective-permute-start.16 = (bf16[1024,256]{1,0:T(8,128)(2,1)}, bf16[1024,256]{1,0:T(8,128)(2,1)}, u32[]{:S(2)}, u32[]{:S(2)}) collective-permute-start(bf16[1024,256]{1,0:T(8,128)(2,1)} %get-tuple-element.167), channel_id=1, source_target_pairs={{0,1},{2,3},{1,0},{3,2},{4,5},{6,7},{5,4},{7,6},{8,9},{10,11},{9,8... | collective-permute-start | bytes 1572872 | tf_op jit(solution)/shard_map/ppermute | solution.py:332
  85.5 10.5 %collective-permute-start.18 = (bf16[1024,256]{1,0:T(8,128)(2,1)}, bf16[1024,256]{1,0:T(8,128)(2,1)}, u32[]{:S(2)}, u32[]{:S(2)}) collective-permute-start(bf16[1024,256]{1,0:T(8,128)(2,1)} %get-tuple-element.168), channel_id=1, source_target_pairs={{1,2},{2,1},{5,6},{6,5},{9,10},{10,9},{13,14},{14,13},{17,18},{18,... | collective-permute-start | bytes 1572872 | tf_op jit(solution)/shard_map/ppermute | solution.py:332
  88.0 6.4 %collective-permute-start.12 = (bf16[128,1024]{1,0:T(8,128)(2,1)S(1)}, bf16[128,1024]{1,0:T(8,128)(2,1)S(1)}, u32[]{:S(2)}, u32[]{:S(2)}) collective-permute-start(bf16[128,1024]{1,0:T(8,128)(2,1)S(1)} %slice.128), channel_id=1, source_target_pairs={{0,16},{4,20},{8,24},{12,28},{16,0},{20,4},{24,8},{28,12},{1,17},{... | collective-permute-start | bytes 786440 | tf_op jit(solution)/shard_map/ppermute | solution.py:321
  91.3 12.4 %collective-permute-start.13 = (bf16[128,1024]{1,0:T(8,128)(2,1)S(1)}, bf16[128,1024]{1,0:T(8,128)(2,1)S(1)}, u32[]{:S(2)}, u32[]{:S(2)}) collective-permute-start(bf16[128,1024]{1,0:T(8,128)(2,1)S(1)} %slice.129), channel_id=1, source_target_pairs={{0,8},{4,12},{8,0},{12,4},{16,24},{20,28},{24,16},{28,20},{1,9},{5... | collective-permute-start | bytes 786440 | tf_op jit(solution)/shard_map/ppermute | solution.py:321
  97.6 13.1 %collective-permute-start.21 = (bf16[1024,256]{1,0:T(8,128)(2,1)S(1)}, bf16[1024,256]{1,0:T(8,128)(2,1)S(1)}, u32[]{:S(2)}, u32[]{:S(2)}) collective-permute-start(bf16[1024,256]{1,0:T(8,128)(2,1)S(1)} %get-tuple-element.149.refs_0_), channel_id=1, source_target_pairs={{1,2},{2,1},{5,6},{6,5},{9,10},{10,9},{13,14},{14,13},{17,18},{18,... | collective-permute-start | bytes 1572872 | tf_op jit(solution)/shard_map/ppermute | solution.py:332
  98.3 14.3 %collective-permute-start.20 = (bf16[1024,256]{1,0:T(8,128)(2,1)S(1)}, bf16[1024,256]{1,0:T(8,128)(2,1)S(1)}, u32[]{:S(2)}, u32[]{:S(2)}) collective-permute-start(bf16[1024,256]{1,0:T(8,128)(2,1)S(1)} %get-tuple-element.149.refs_0_), channel_id=1, source_target_pairs={{0,1},{2,3},{1,0},{3,2},{4,5},{6,7},{5,4},{7,6},{8,9},{10,11},{9,8... | collective-permute-start | bytes 1572872 | tf_op jit(solution)/shard_map/ppermute | solution.py:332
  103.6 6.3 %collective-permute-start.22 = (bf16[512,256]{1,0:T(8,128)(2,1)S(1)}, bf16[512,256]{1,0:T(8,128)(2,1)S(1)}, u32[]{:S(2)}, u32[]{:S(2)}) collective-permute-start(bf16[512,256]{1,0:T(8,128)(2,1)S(1)} %slice.132), channel_id=1, source_target_pairs={{0,4},{4,0},{8,12},{12,8},{16,20},{20,16},{24,28},{28,24},{1,5},{5... | collective-permute-start | bytes 786440 | tf_op jit(solution)/shard_map/ppermute | solution.py:316
  110.6 28.7 %copy-start.24 = (bf16[1024,256]{1,0:T(8,128)(2,1)}, bf16[1024,256]{1,0:T(8,128)(2,1)S(1)}, u32[]{:S(2)}) copy-start(bf16[1024,256]{1,0:T(8,128)(2,1)S(1)} %collective-permute-done.21.refs_2_) | copy-start | bytes 1572868
  112.6 33.8 %copy-start.25 = (bf16[1024,256]{1,0:T(8,128)(2,1)}, bf16[1024,256]{1,0:T(8,128)(2,1)S(1)}, u32[]{:S(2)}) copy-start(bf16[1024,256]{1,0:T(8,128)(2,1)S(1)} %collective-permute-done.20.refs_1_) | copy-start | bytes 1572868
  112.6 8.7 %collective-permute-start.25 = (bf16[1024,256]{1,0:T(8,128)(2,1)S(1)}, bf16[1024,256]{1,0:T(8,128)(2,1)S(1)}, u32[]{:S(2)}, u32[]{:S(2)}) collective-permute-start(bf16[1024,256]{1,0:T(8,128)(2,1)S(1)} %collective-permute-done.20.refs_1_), channel_id=1, source_target_pairs={{1,2},{2,1},{5,6},{6,5},{9,10},{10,9},{13,14},{14,13},{17,18},{18,... | collective-permute-start | bytes 1572872 | tf_op jit(solution)/shard_map/ppermute | solution.py:332
  113.3 14.4 %collective-permute-start.24 = (bf16[1024,256]{1,0:T(8,128)(2,1)S(1)}, bf16[1024,256]{1,0:T(8,128)(2,1)S(1)}, u32[]{:S(2)}, u32[]{:S(2)}) collective-permute-start(bf16[1024,256]{1,0:T(8,128)(2,1)S(1)} %collective-permute-done.21.refs_2_), channel_id=1, source_target_pairs={{2,3},{1,0},{6,7},{5,4},{10,11},{9,8},{14,15},{13,12},{18,19},{17,... | collective-permute-start | bytes 1572872 | tf_op jit(solution)/shard_map/ppermute | solution.py:332
  114.7 41.7 %copy-start.11 = (bf16[512,256]{1,0:T(8,128)(2,1)S(1)}, bf16[512,256]{1,0:T(8,128)(2,1)}, u32[]{:S(2)}) copy-start(bf16[512,256]{1,0:T(8,128)(2,1)} %get-tuple-element.172) | copy-start | bytes 786436
  114.7 14.5 %collective-permute-start.23 = (bf16[1024,256]{1,0:T(8,128)(2,1)S(1)}, bf16[1024,256]{1,0:T(8,128)(2,1)S(1)}, u32[]{:S(2)}, u32[]{:S(2)}) collective-permute-start(bf16[1024,256]{1,0:T(8,128)(2,1)S(1)} %get-tuple-element.165), channel_id=1, source_target_pairs={{0,1},{3,2},{4,5},{7,6},{8,9},{11,10},{12,13},{15,14},{16,17},{19,... | collective-permute-start | bytes 1572872 | tf_op jit(solution)/shard_map/ppermute | solution.py:332
  121.4 25.0 %copy-start.26 = (bf16[1024,256]{1,0:T(8,128)(2,1)}, bf16[1024,256]{1,0:T(8,128)(2,1)S(1)}, u32[]{:S(2)}) copy-start(bf16[1024,256]{1,0:T(8,128)(2,1)S(1)} %collective-permute-done.25.refs_4_) | copy-start | bytes 1572868
  127.7 18.6 %copy-start.27 = (bf16[1024,256]{1,0:T(8,128)(2,1)}, bf16[1024,256]{1,0:T(8,128)(2,1)S(1)}, u32[]{:S(2)}) copy-start(bf16[1024,256]{1,0:T(8,128)(2,1)S(1)} %collective-permute-done.24.refs_3_) | copy-start | bytes 1572868
  127.8 11.6 %collective-permute-start.28 = (bf16[1024,256]{1,0:T(8,128)(2,1)S(1)}, bf16[1024,256]{1,0:T(8,128)(2,1)S(1)}, u32[]{:S(2)}, u32[]{:S(2)}) collective-permute-start(bf16[1024,256]{1,0:T(8,128)(2,1)S(1)} %collective-permute-done.25.refs_4_), channel_id=1, source_target_pairs={{2,3},{1,0},{6,7},{5,4},{10,11},{9,8},{14,15},{13,12},{18,19},{17,... | collective-permute-start | bytes 1572872 | tf_op jit(solution)/shard_map/ppermute | solution.py:332
  129.3 10.0 %collective-permute-start.27 = (bf16[1024,256]{1,0:T(8,128)(2,1)S(1)}, bf16[1024,256]{1,0:T(8,128)(2,1)S(1)}, u32[]{:S(2)}, u32[]{:S(2)}) collective-permute-start(bf16[1024,256]{1,0:T(8,128)(2,1)S(1)} %fusion.1), channel_id=1, source_target_pairs={{1,2},{2,1},{5,6},{6,5},{9,10},{10,9},{13,14},{14,13},{17,18},{18,... | collective-permute-start | bytes 1572872 | tf_op jit(solution)/shard_map/ppermute | solution.py:332
  130.0 15.1 %collective-permute-start.26 = (bf16[1024,256]{1,0:T(8,128)(2,1)S(1)}, bf16[1024,256]{1,0:T(8,128)(2,1)S(1)}, u32[]{:S(2)}, u32[]{:S(2)}) collective-permute-start(bf16[1024,256]{1,0:T(8,128)(2,1)S(1)} %get-tuple-element.102), channel_id=1, source_target_pairs={{0,1},{3,2},{4,5},{7,6},{8,9},{11,10},{12,13},{15,14},{16,17},{19,... | collective-permute-start | bytes 1572872 | tf_op jit(solution)/shard_map/ppermute | solution.py:332
  146.4 10.0 %collective-permute-start.29 = (bf16[1024,256]{1,0:T(8,128)(2,1)}, bf16[1024,256]{1,0:T(8,128)(2,1)}, u32[]{:S(2)}, u32[]{:S(2)}) collective-permute-start(bf16[1024,256]{1,0:T(8,128)(2,1)} %get-tuple-element.163), channel_id=1, source_target_pairs={{0,1},{2,3},{1,0},{3,2},{4,5},{6,7},{5,4},{7,6},{8,9},{10,11},{9,8... | collective-permute-start | bytes 1572872 | tf_op jit(solution)/shard_map/ppermute | solution.py:332
  149.0 7.5 %collective-permute-start.30 = (bf16[1024,256]{1,0:T(8,128)(2,1)}, bf16[1024,256]{1,0:T(8,128)(2,1)}, u32[]{:S(2)}, u32[]{:S(2)}) collective-permute-start(bf16[1024,256]{1,0:T(8,128)(2,1)} %get-tuple-element.164), channel_id=1, source_target_pairs={{1,2},{2,1},{5,6},{6,5},{9,10},{10,9},{13,14},{14,13},{17,18},{18,... | collective-permute-start | bytes 1572872 | tf_op jit(solution)/shard_map/ppermute | solution.py:332
  158.0 17.1 %copy-start.19 = (bf16[1024,256]{1,0:T(8,128)(2,1)}, bf16[1024,256]{1,0:T(8,128)(2,1)S(1)}, u32[]{:S(2)}) copy-start(bf16[1024,256]{1,0:T(8,128)(2,1)S(1)} %get-tuple-element.147.refs_0_) | copy-start | bytes 1572868
  158.0 19.6 %collective-permute-start.32 = (bf16[1024,256]{1,0:T(8,128)(2,1)S(1)}, bf16[1024,256]{1,0:T(8,128)(2,1)S(1)}, u32[]{:S(2)}, u32[]{:S(2)}) collective-permute-start(bf16[1024,256]{1,0:T(8,128)(2,1)S(1)} %get-tuple-element.147.refs_0_), channel_id=1, source_target_pairs={{1,2},{2,1},{5,6},{6,5},{9,10},{10,9},{13,14},{14,13},{17,18},{18,... | collective-permute-start | bytes 1572872 | tf_op jit(solution)/shard_map/ppermute | solution.py:332
  158.7 18.9 %collective-permute-start.31 = (bf16[1024,256]{1,0:T(8,128)(2,1)S(1)}, bf16[1024,256]{1,0:T(8,128)(2,1)S(1)}, u32[]{:S(2)}, u32[]{:S(2)}) collective-permute-start(bf16[1024,256]{1,0:T(8,128)(2,1)S(1)} %get-tuple-element.147.refs_0_), channel_id=1, source_target_pairs={{0,1},{2,3},{1,0},{3,2},{4,5},{6,7},{5,4},{7,6},{8,9},{10,11},{9,8... | collective-permute-start | bytes 1572872 | tf_op jit(solution)/shard_map/ppermute | solution.py:332
  175.2 4.8 %collective-permute-start.37 = (bf16[512,256]{1,0:T(8,128)(2,1)S(1)}, bf16[512,256]{1,0:T(8,128)(2,1)S(1)}, u32[]{:S(2)}, u32[]{:S(2)}) collective-permute-start(bf16[512,256]{1,0:T(8,128)(2,1)S(1)} %slice.135), channel_id=1, source_target_pairs={{0,4},{4,0},{8,12},{12,8},{16,20},{20,16},{24,28},{28,24},{1,5},{5... | collective-permute-start | bytes 786440 | tf_op jit(solution)/shard_map/ppermute | solution.py:316
  176.5 14.4 %collective-permute-start.36 = (bf16[2,128,1024]{2,1,0:T(8,128)(2,1)S(1)}, bf16[2,128,1024]{2,1,0:T(8,128)(2,1)S(1)}, u32[]{:S(2)}, u32[]{:S(2)}) collective-permute-start(bf16[2,128,1024]{2,1,0:T(8,128)(2,1)S(1)} %get-tuple-element.161), channel_id=1, source_target_pairs={{0,16},{4,20},{8,24},{12,28},{16,0},{20,4},{24,8},{28,12},{1,17},{... | collective-permute-start | bytes 1572872 | tf_op jit(solution)/shard_map/ppermute | solution.py:321
  177.1 14.0 %collective-permute-start.35 = (bf16[2,128,1024]{2,1,0:T(8,128)(2,1)S(1)}, bf16[2,128,1024]{2,1,0:T(8,128)(2,1)S(1)}, u32[]{:S(2)}, u32[]{:S(2)}) collective-permute-start(bf16[2,128,1024]{2,1,0:T(8,128)(2,1)S(1)} %get-tuple-element.162), channel_id=1, source_target_pairs={{0,8},{4,12},{8,0},{12,4},{16,24},{20,28},{24,16},{28,20},{1,9},{5... | collective-permute-start | bytes 1572872 | tf_op jit(solution)/shard_map/ppermute | solution.py:321
  177.6 18.2 %copy-start.29 = (bf16[1024,256]{1,0:T(8,128)(2,1)}, bf16[1024,256]{1,0:T(8,128)(2,1)S(1)}, u32[]{:S(2)}) copy-start(bf16[1024,256]{1,0:T(8,128)(2,1)S(1)} %collective-permute-done.32.refs_2_) | copy-start | bytes 1572868
  177.7 18.2 %copy-start.30 = (bf16[1024,256]{1,0:T(8,128)(2,1)}, bf16[1024,256]{1,0:T(8,128)(2,1)S(1)}, u32[]{:S(2)}) copy-start(bf16[1024,256]{1,0:T(8,128)(2,1)S(1)} %collective-permute-done.31.refs_1_) | copy-start | bytes 1572868
  177.7 15.7 %collective-permute-start.33 = (bf16[1024,256]{1,0:T(8,128)(2,1)S(1)}, bf16[1024,256]{1,0:T(8,128)(2,1)S(1)}, u32[]{:S(2)}, u32[]{:S(2)}) collective-permute-start(bf16[1024,256]{1,0:T(8,128)(2,1)S(1)} %collective-permute-done.32.refs_2_), channel_id=1, source_target_pairs={{2,3},{1,0},{6,7},{5,4},{10,11},{9,8},{14,15},{13,12},{18,19},{17,... | collective-permute-start | bytes 1572872 | tf_op jit(solution)/shard_map/ppermute | solution.py:332
  179.0 14.4 %collective-permute-start.34 = (bf16[1024,256]{1,0:T(8,128)(2,1)S(1)}, bf16[1024,256]{1,0:T(8,128)(2,1)S(1)}, u32[]{:S(2)}, u32[]{:S(2)}) collective-permute-start(bf16[1024,256]{1,0:T(8,128)(2,1)S(1)} %collective-permute-done.31.refs_1_), channel_id=1, source_target_pairs={{1,2},{2,1},{5,6},{6,5},{9,10},{10,9},{13,14},{14,13},{17,18},{18,... | collective-permute-start | bytes 1572872 | tf_op jit(solution)/shard_map/ppermute | solution.py:332
  193.3 15.9 %collective-permute-start.38 = (bf16[1024,256]{1,0:T(8,128)(2,1)S(1)}, bf16[1024,256]{1,0:T(8,128)(2,1)S(1)}, u32[]{:S(2)}, u32[]{:S(2)}) collective-permute-start(bf16[1024,256]{1,0:T(8,128)(2,1)S(1)} %collective-permute-done.34.refs_4_), channel_id=1, source_target_pairs={{2,3},{1,0},{6,7},{5,4},{10,11},{9,8},{14,15},{13,12},{18,19},{17,... | collective-permute-start | bytes 1572872 | tf_op jit(solution)/shard_map/ppermute | solution.py:332
  195.9 13.4 %collective-permute-start.40 = (bf16[128,1024]{1,0:T(8,128)(2,1)S(1)}, bf16[128,1024]{1,0:T(8,128)(2,1)S(1)}, u32[]{:S(2)}, u32[]{:S(2)}) collective-permute-start(bf16[128,1024]{1,0:T(8,128)(2,1)S(1)} %get-tuple-element.159), channel_id=1, source_target_pairs={{0,8},{4,12},{8,0},{12,4},{16,24},{20,28},{24,16},{28,20},{1,9},{5... | collective-permute-start | bytes 786440 | tf_op jit(solution)/shard_map/ppermute | solution.py:321
  197.4 12.5 %copy-start.3 = (bf16[512,1024]{1,0:T(8,128)(2,1)S(1)}, bf16[512,1024]{1,0:T(8,128)(2,1)}, u32[]{:S(2)}) copy-start(bf16[512,1024]{1,0:T(8,128)(2,1)} %shard_map.94.own_ref.refs_6_.refs_5_) | copy-start | bytes 3145732
  197.4 12.5 %copy-start.5 = (bf16[256,1024]{1,0:T(8,128)(2,1)S(1)}, bf16[256,1024]{1,0:T(8,128)(2,1)}, u32[]{:S(2)}) copy-start(bf16[256,1024]{1,0:T(8,128)(2,1)} %copy-done.4) | copy-start | bytes 1572868
  197.4 12.5 %copy-start.9 = (bf16[256,1024]{1,0:T(8,128)(2,1)S(1)}, bf16[256,1024]{1,0:T(8,128)(2,1)}, u32[]{:S(2)}) copy-start(bf16[256,1024]{1,0:T(8,128)(2,1)} %copy-done.8) | copy-start | bytes 1572868
  197.5 11.8 %collective-permute-start.39 = (bf16[128,1024]{1,0:T(8,128)(2,1)S(1)}, bf16[128,1024]{1,0:T(8,128)(2,1)S(1)}, u32[]{:S(2)}, u32[]{:S(2)}) collective-permute-start(bf16[128,1024]{1,0:T(8,128)(2,1)S(1)} %get-tuple-element.160), channel_id=1, source_target_pairs={{0,16},{4,20},{8,24},{12,28},{16,0},{20,4},{24,8},{28,12},{1,17},{... | collective-permute-start | bytes 786440 | tf_op jit(solution)/shard_map/ppermute | solution.py:321
  216.0 3.0 %collective-permute-start.41 = (bf16[512,1024]{1,0:T(8,128)(2,1)}, bf16[512,1024]{1,0:T(8,128)(2,1)}, u32[]{:S(2)}, u32[]{:S(2)}) collective-permute-start(bf16[512,1024]{1,0:T(8,128)(2,1)} %get-tuple-element.126), channel_id=1, source_target_pairs={{0,4},{4,0},{8,12},{12,8},{16,20},{20,16},{24,28},{28,24},{1,5},{5... | collective-permute-start | bytes 3145736 | tf_op jit(solution)/shard_map/ppermute | solution.py:316
  216.0 19.7 %collective-permute-start.47 = (bf16[2,128,1024]{2,1,0:T(8,128)(2,1)S(1)}, bf16[2,128,1024]{2,1,0:T(8,128)(2,1)S(1)}, u32[]{:S(2)}, u32[]{:S(2)}) collective-permute-start(bf16[2,128,1024]{2,1,0:T(8,128)(2,1)S(1)} %get-tuple-element.157), channel_id=1, source_target_pairs={{0,16},{4,20},{8,24},{12,28},{16,0},{20,4},{24,8},{28,12},{1,17},{... | collective-permute-start | bytes 1572872 | tf_op jit(solution)/shard_map/ppermute | solution.py:321
  216.8 18.9 %collective-permute-start.46 = (bf16[2,128,1024]{2,1,0:T(8,128)(2,1)S(1)}, bf16[2,128,1024]{2,1,0:T(8,128)(2,1)S(1)}, u32[]{:S(2)}, u32[]{:S(2)}) collective-permute-start(bf16[2,128,1024]{2,1,0:T(8,128)(2,1)S(1)} %get-tuple-element.158), channel_id=1, source_target_pairs={{0,8},{4,12},{8,0},{12,4},{16,24},{20,28},{24,16},{28,20},{1,9},{5... | collective-permute-start | bytes 1572872 | tf_op jit(solution)/shard_map/ppermute | solution.py:321
  221.7 1.7 collective-permute-start.42
  223.5 12.2 %collective-permute-start.45 = (bf16[4,128,128]{2,1,0:T(8,128)(2,1)S(1)}, bf16[4,128,128]{2,1,0:T(8,128)(2,1)S(1)}, u32[]{:S(2)}, u32[]{:S(2)}) collective-permute-start(bf16[4,128,128]{2,1,0:T(8,128)(2,1)S(1)} %fusion.14), channel_id=1, source_target_pairs={{0,24},{4,28},{8,16},{12,20},{16,8},{20,12},{24,0},{28,4},{1,25},{... | collective-permute-start | bytes 393224 | tf_op jit(solution)/shard_map/ppermute | solution.py:321
  225.2 10.9 %collective-permute-start.44 = (bf16[4,128,128]{2,1,0:T(8,128)(2,1)S(1)}, bf16[4,128,128]{2,1,0:T(8,128)(2,1)S(1)}, u32[]{:S(2)}, u32[]{:S(2)}) collective-permute-start(bf16[4,128,128]{2,1,0:T(8,128)(2,1)S(1)} %fusion.14), channel_id=1, source_target_pairs={{0,16},{4,20},{8,24},{12,28},{16,0},{20,4},{24,8},{28,12},{1,17},{... | collective-permute-start | bytes 393224 | tf_op jit(solution)/shard_map/ppermute | solution.py:321
  225.7 10.8 %collective-permute-start.43 = (bf16[4,128,128]{2,1,0:T(8,128)(2,1)S(1)}, bf16[4,128,128]{2,1,0:T(8,128)(2,1)S(1)}, u32[]{:S(2)}, u32[]{:S(2)}) collective-permute-start(bf16[4,128,128]{2,1,0:T(8,128)(2,1)S(1)} %fusion.14), channel_id=1, source_target_pairs={{0,8},{4,12},{8,0},{12,4},{16,24},{20,28},{24,16},{28,20},{1,9},{5... | collective-permute-start | bytes 393224 | tf_op jit(solution)/shard_map/ppermute | solution.py:321
  236.6 2.3 collective-permute-start.50
  236.9 8.8 %collective-permute-start.49 = (bf16[128,1024]{1,0:T(8,128)(2,1)S(1)}, bf16[128,1024]{1,0:T(8,128)(2,1)S(1)}, u32[]{:S(2)}, u32[]{:S(2)}) collective-permute-start(bf16[128,1024]{1,0:T(8,128)(2,1)S(1)} %get-tuple-element.155), channel_id=1, source_target_pairs={{0,8},{4,12},{8,0},{12,4},{16,24},{20,28},{24,16},{28,20},{1,9},{5... | collective-permute-start | bytes 786440 | tf_op jit(solution)/shard_map/ppermute | solution.py:321
  238.4 8.4 %collective-permute-start.48 = (bf16[128,1024]{1,0:T(8,128)(2,1)S(1)}, bf16[128,1024]{1,0:T(8,128)(2,1)S(1)}, u32[]{:S(2)}, u32[]{:S(2)}) collective-permute-start(bf16[128,1024]{1,0:T(8,128)(2,1)S(1)} %get-tuple-element.156), channel_id=1, source_target_pairs={{0,16},{4,20},{8,24},{12,28},{16,0},{20,4},{24,8},{28,12},{1,17},{... | collective-permute-start | bytes 786440 | tf_op jit(solution)/shard_map/ppermute | solution.py:321
  (20 other events, 94.7 us)

commit v5 on v4

--- a/solution.py
+++ b/solution.py
@@ -133,37 +133,37 @@
     return on_values
 
 
-def project_kernel(pieces, half, own_ref, other_ref, *refs):
-    def fill(a_ref):
-        for piece in range(pieces):
-            refs[-1][piece] = dot(a_ref[...], refs[piece][...], NT).astype(BF16)
-
-    pl.when(pl.program_id(0) < half)(lambda: fill(own_ref))
-    pl.when(pl.program_id(0) >= half)(lambda: fill(other_ref))
-
-
-def project(own, other, pieces):
-    rows, width = own.shape
+def project_kernel(pieces, a_ref, *refs):
+    for piece in range(pieces):
+        refs[-1][piece] = dot(a_ref[...], refs[piece][...], NT).astype(BF16)
+
+
+def project_rows(attended, pieces, half, into):
+    rows, width = attended.shape
     features = pieces[0].shape[0]
     step = min(rows, 256)
-    half = rows // step
+    first = half * (rows // step)
+    more = [] if into is None else [into]
     return pl.pallas_call(
-        functools.partial(project_kernel, len(pieces), half),
-        grid=(2 * half,),
-        in_specs=[
-            pl.BlockSpec((step, width), lambda r: (jnp.minimum(r, half - 1), 0)),
-            pl.BlockSpec((step, width), lambda r: (jnp.maximum(r - half, 0), 0)),
-        ]
-        + [pl.BlockSpec((features, width), lambda r: (0, 0)) for unused in pieces],
-        out_specs=pl.BlockSpec((len(pieces), step, features), lambda r: (0, r, 0)),
+        functools.partial(project_kernel, len(pieces)),
+        grid=(rows // step,),
+        in_specs=[pl.BlockSpec((step, width), lambda r: (r, 0))]
+        + [pl.BlockSpec((features, width), lambda r: (0, 0)) for unused in pieces]
+        + [pl.BlockSpec(memory_space=pl.ANY) for unused in more],
+        out_specs=pl.BlockSpec((len(pieces), step, features), lambda r: (0, r + first, 0)),
         out_shape=jax.ShapeDtypeStruct((len(pieces), 2 * rows, features), BF16),
+        input_output_aliases={len(pieces) + 1: 0} if more else {},
         compiler_params=pltpu.CompilerParams(vmem_limit_bytes=VMEM_LIMIT),
         cost_estimate=pl.CostEstimate(
-            flops=4 * rows * width * features * len(pieces),
-            bytes_accessed=8 * rows * width,
+            flops=2 * rows * width * features * len(pieces),
+            bytes_accessed=4 * rows * width,
             transcendentals=0,
         ),
-    )(*in_hbm([own, other, *pieces]))
+    )(*([attended] if more else in_hbm([attended])), *in_hbm(pieces), *more)
+
+
+def project(own, other, pieces):
+    return project_rows(other, pieces, 1, project_rows(own, pieces, 0, None))
 
 
 def products_kernel(count, late, chips, before, factor, meta_ref, *refs):
@@ -348,9 +348,7 @@
                 continue
             target = jnp.where(mine % 2 == parity, mine + count - step, mine - count + step)
             value = part_for(jnp.clip(target, 0, count - 1))
-            if step > 1 and got[1 - parity] is None:
-                value, unused = lax.optimization_barrier((value, got[parity]))
-            elif step > 1:
+            if got[1 - parity] is not None:
                 value = (value.astype(F32) + got[1 - parity].astype(F32)).astype(BF16)
             values.append(value)
         got = line_step(values, active)
@@ -514,7 +512,7 @@
     ]
 
     outputs, grad_parts = [], []
-    gate, totals, sent, gathered = None, (), None, {}
+    gate, totals, sent, pending, gathered = None, (), None, None, {}
     factor = 1.0 / math.sqrt(rows * seq_count)
     for c in range(chunks):
         last = c == chunks - 1
@@ -554,11 +552,14 @@
                 ],
                 axis=1,
             )
+        if pending is not None:
+            pending, output = barrier((pending, output))
+            sent, second_step = scatter_start(pending)
         found, gathered, tied = line_gather(
-            residual, {1: totals, 2: (sent, output)}
+            residual, {1: totals, 2: output}
         )
-        totals, (sent, output) = tied[1], tied[2]
-        gate = gathered[1]
+        totals, output = tied[1], tied[2]
+        gate = residual
         weights = pieces
         on_time = found[:-1] if last and len(found) > 1 else found
         metas = [
@@ -609,8 +610,9 @@
                     BF16 if j == share - 1 else F32,
                     factor,
                 )
-        sent, second_step = scatter_start(grads)
-
+        pending = grads
+
+    sent, second_step = scatter_start(pending)
     grad_attended = (totals[0] + core_swap(totals[1]).astype(F32)).astype(BF16)
     (query_grad,) = call(outer_kernel, ins="vv", outs=[("m", F32)], macs=rows * DH * DH, step=4)(
         scaled, grad_attended

time: 250 us -> 248 us (level)
  starting transfers between devices: 78.8 us -> 75.2 us
    ppermute x20, waiting for transfers between devices: 43.8 us -> 56.5 us  [line_step(): lax.ppermute(value, 'head', pairs)]
    ppermute x22, waiting for transfers between devices: 29 us -> 17.7 us  [chip_swap(): lax.ppermute(value, 'seq', [(j, j ^ 2 * delta) for j in range(count)])]
    ppermute x22, starting transfers between devices: 24.1 us -> 21.3 us  [chip_swap(): lax.ppermute(value, 'seq', [(j, j ^ 2 * delta) for j in range(count)])]
    pallas_call x2 -> x4, Pallas kernels: 10.6 us -> 13 us  [project_rows(): pl.pallas_call(functools.partial(project_kernel, len(pieces)), grid=(rows...]
  transfers between devices with their start and end apart: 51 -> 51, of which waited for: 26 -> 24; matrix products, arithmetic and copies ran while one was open for 9% -> 9% of each run, Pallas kernels for 19% -> 21%
where the time goes in v5:
time: 248 us; the launch traced here: 247 us
  waiting for transfers between devices  75.8 us (31%)
  starting transfers between devices  75.2 us (30%)
  Pallas kernels  62.3 us (25%)
  other arithmetic  17.8 us (7%)
  local copies, waits for them, and re-layouts  13.9 us (6%)
    ppermute x20, waiting for transfers between devices, line_step(): lax.ppermute(value, 'head', pairs)  56.5 us
    ppermute x20, starting transfers between devices, line_step(): lax.ppermute(value, 'head', pairs)  52.9 us
    pallas_call x6, Pallas kernels, on_values(): call(*[in_hbm([value])[0] if kind == 'h' else value for kind, value in zi...  24.4 us
    ppermute x22, starting transfers between devices, chip_swap(): lax.ppermute(value, 'seq', [(j, j ^ 2 * delta) for j in range(count)])  21.3 us
    pallas_call x2, Pallas kernels, products(): pl.pallas_call(functools.partial(products_kernel, len(candidates), late,...  20.8 us
    ppermute x22, waiting for transfers between devices, chip_swap(): lax.ppermute(value, 'seq', [(j, j ^ 2 * delta) for j in range(count)])  17.7 us
    pallas_call x4, Pallas kernels, project_rows(): pl.pallas_call(functools.partial(project_kernel, len(pieces)), grid=(rows...  13 us
    convert_element_type x4, other arithmetic, line_sum(): value = (value.astype(F32) + got[1 - parity].astype(F32)).astype(BF16)  5.81 us
  transfers between devices with their start and end apart: 51, of which 24 were waited for; matrix products, arithmetic and copies ran while one was open for 9% of the time, Pallas kernels for 21%

profile of v5, /device:TPU:0, one launch (start us, length us, event | category | flops | bytes accessed | tf_op | source)
XLA Modules:
  0.0 246.5 jit_solution(8888289482311314844)
XLA Ops:
  0.6 2.0 shard_map.92
  3.3 2.6 %collective-permute-start.5 = (bf16[256,1024]{1,0:T(8,128)(2,1)S(1)}, bf16[256,1024]{1,0:T(8,128)(2,1)S(1)}, u32[]{:S(2)}, u32[]{:S(2)}) collective-permute-start(bf16[256,1024]{1,0:T(8,128)(2,1)S(1)} %slice.96.refs_0_.refs_8_), channel_id=1, source_target_pairs={{0,16},{4,20},{8,24},{12,28},{16,0},{20,4},{24,8},{28,12},{1,17},{... | collective-permute-start | bytes 1572872 | tf_op jit(solution)/shard_map/ppermute | solution.py:321
  5.9 1.5 collective-permute-start.4
  8.4 1.2 collective-permute-start.2
  9.5 1.5 collective-permute-start.1
  11.1 6.2 %shard_map.93 = (bf16[512,1024]{1,0:T(8,128)(2,1)}, f32[512,1024]{1,0:T(8,128)}) custom-call(bf16[512,1024]{1,0:T(8,128)(2,1)} %q_ref, bf16[512,1024]{1,0:T(8,128)(2,1)} %k_ref.5, bf16[512,1024]{1,0:T(8,128)(2,1)} %v_ref.5, f32[512,1]{1,0:T(8,128)S(1)} %multiply_rsqrt_fusion.scale_ref), custom_call_target="tpu_custom_call" | custom-call | flops 1073741824 | bytes 6291456 | tf_op jit(solution)/shard_map/pallas_call | solution.py:129
  17.3 1.4 collective-permute-done.5.refs_2_.refs_10_
  18.7 2.0 collective-permute-done.4.refs_1_.refs_9_
  20.7 2.3 collective-permute-done.3
  24.1 1.5 collective-permute-done.1
  25.8 1.6 collective-permute-start.8
  28.0 3.3 %shard_map.94.a_ref.refs_6_.refs_5_.own_ref = bf16[512,1024]{1,0:T(8,128)(2,1)} custom-call(bf16[512,1024]{1,0:T(8,128)(2,1)} %get-tuple-element.79.scaled_ref.a_ref, f32[512,1024]{1,0:T(8,128)} %get-tuple-element.80.intra_ref, f32[8,128,128]{2,1,0:T(8,128)S(1)} %select_add_fusion.1.state_ref), custom_call_target="tpu_custom_call" | custom-call | flops 268435456 | bytes 4194304 | tf_op jit(solution)/shard_map/pallas_call | solution.py:129
  31.3 3.3 %collective-permute-done.8 = bf16[128,1024]{1,0:T(8,128)(2,1)S(1)} collective-permute-done((bf16[128,1024]{1,0:T(8,128)(2,1)S(1)}, bf16[128,1024]{1,0:T(8,128)(2,1)S(1)}, u32[]{:S(2)}, u32[]{:S(2)}) %collective-permute-start.8) | collective-permute-done | bytes 262176 | tf_op jit(solution)/shard_map/ppermute | solution.py:321
  34.6 1.2 collective-permute-done.7
  36.6 3.2 %shard_map.97.refs_4_ = bf16[4,1024,256]{2,1,0:T(8,128)(2,1)S(1)} custom-call(bf16[512,1024]{1,0:T(8,128)(2,1)} %shard_map.94.a_ref.refs_6_.refs_5_.own_ref, bf16[256,1024]{1,0:T(8,128)(2,1)} %copy-done.12, bf16[256,1024]{1,0:T(8,128)(2,1)} %copy-done.14, bf16[256,1024]{1,0:T(8,128)(2,1)} %copy-done.13, bf16[256,1024]{1,0:T(8,128)(2,1)} %pad_maximum_fusion.2.refs_3_.refs_11_), custom_call_target="tpu_custom_call" | custom-call | flops 1073741824 | bytes 2097152 | tf_op jit(solution)/shard_map/pallas_call | solution.py:147
  39.9 3.5 %shard_map.98 = bf16[4,1024,256]{2,1,0:T(8,128)(2,1)S(1)} custom-call(bf16[512,1024]{1,0:T(8,128)(2,1)S(1)} %collective-permute-done.9.a_ref.refs_7_.refs_6_.other_ref, bf16[256,1024]{1,0:T(8,128)(2,1)} %copy-done.12, bf16[256,1024]{1,0:T(8,128)(2,1)} %copy-done.14, bf16[256,1024]{1,0:T(8,128)(2,1)} %copy-done.13, ...), custom_call_target="tpu_custom_call", output_to_operand_aliasing={{}: (5, {})} | custom-call | flops 1073741824 | bytes 2097152 | tf_op jit(solution)/shard_map/pallas_call | solution.py:147
  44.4 4.3 %collective-permute-start.14 = (bf16[1024,256]{1,0:T(8,128)(2,1)}, bf16[1024,256]{1,0:T(8,128)(2,1)}, u32[]{:S(2)}, u32[]{:S(2)}) collective-permute-start(bf16[1024,256]{1,0:T(8,128)(2,1)} %get-tuple-element.165), channel_id=1, source_target_pairs={{0,1},{3,2},{4,5},{7,6},{8,9},{11,10},{12,13},{15,14},{16,17},{19,... | collective-permute-start | bytes 1572872 | tf_op jit(solution)/shard_map/ppermute | solution.py:332
  48.7 2.1 collective-permute-start.17
  50.8 9.6 %collective-permute-done.14 = bf16[1024,256]{1,0:T(8,128)(2,1)} collective-permute-done((bf16[1024,256]{1,0:T(8,128)(2,1)}, bf16[1024,256]{1,0:T(8,128)(2,1)}, u32[]{:S(2)}, u32[]{:S(2)}) %collective-permute-start.14) | collective-permute-done | bytes 524320 | tf_op jit(solution)/shard_map/ppermute | solution.py:332
  60.4 2.0 fusion.6
  62.4 1.5 collective-permute-start.15
  63.9 1.9 slice.99.refs_0_.refs_7_
  66.8 1.9 constant_dynamic-slice_fusion.1
  68.6 2.6 %collective-permute-done.17 = bf16[1024,256]{1,0:T(8,128)(2,1)} collective-permute-done((bf16[1024,256]{1,0:T(8,128)(2,1)}, bf16[1024,256]{1,0:T(8,128)(2,1)}, u32[]{:S(2)}, u32[]{:S(2)}) %collective-permute-start.17) | collective-permute-done | bytes 524320 | tf_op jit(solution)/shard_map/ppermute | solution.py:332
  71.3 2.4 fusion.7
  73.7 9.0 %collective-permute-start.16 = (bf16[1024,256]{1,0:T(8,128)(2,1)}, bf16[1024,256]{1,0:T(8,128)(2,1)}, u32[]{:S(2)}, u32[]{:S(2)}) collective-permute-start(bf16[1024,256]{1,0:T(8,128)(2,1)} %get-tuple-element.163), channel_id=1, source_target_pairs={{0,1},{2,3},{1,0},{3,2},{4,5},{6,7},{5,4},{7,6},{8,9},{10,11},{9,8... | collective-permute-start | bytes 1572872 | tf_op jit(solution)/shard_map/ppermute | solution.py:332
  82.7 1.5 collective-permute-start.18
  85.7 1.8 constant_dynamic-slice_fusion.2
  89.1 1.8 fusion.20
  91.6 1.9 collective-permute-done.16
  93.5 1.5 subtract_convert_fusion.1
  95.7 6.5 %collective-permute-start.23 = (bf16[1024,256]{1,0:T(8,128)(2,1)S(1)}, bf16[1024,256]{1,0:T(8,128)(2,1)S(1)}, u32[]{:S(2)}, u32[]{:S(2)}) collective-permute-start(bf16[1024,256]{1,0:T(8,128)(2,1)S(1)} %get-tuple-element.145.refs_0_), channel_id=1, source_target_pairs={{0,1},{2,3},{1,0},{3,2},{4,5},{6,7},{5,4},{7,6},{8,9},{10,11},{9,8... | collective-permute-start | bytes 1572872 | tf_op jit(solution)/shard_map/ppermute | solution.py:332
  103.2 3.2 %shard_map.95.refs_4_ = bf16[4,1024,256]{2,1,0:T(8,128)(2,1)S(1)} custom-call(bf16[512,1024]{1,0:T(8,128)(2,1)} %shard_map.94.a_ref.refs_6_.refs_5_.own_ref, bf16[256,1024]{1,0:T(8,128)(2,1)} %slice.99.refs_0_.refs_7_, bf16[256,1024]{1,0:T(8,128)(2,1)} %collective-permute-done.10.refs_1_.refs_8_, bf16[256,1024]{1,0:T(8,128)(2,1)} %collective-permute-done.11.refs_2_.refs_9_, ...), custom_call_target="tpu_custom_call" | custom-call | flops 1073741824 | bytes 2097152 | tf_op jit(solution)/shard_map/pallas_call | solution.py:147
  106.5 3.1 %shard_map.96 = bf16[4,1024,256]{2,1,0:T(8,128)(2,1)S(1)} custom-call(bf16[512,1024]{1,0:T(8,128)(2,1)S(1)} %collective-permute-done.9.a_ref.refs_7_.refs_6_.other_ref, bf16[256,1024]{1,0:T(8,128)(2,1)} %slice.99.refs_0_.refs_7_, bf16[256,1024]{1,0:T(8,128)(2,1)} %collective-permute-done.10.refs_1_.refs_8_, ...), custom_call_target="tpu_custom_call", output_to_operand_aliasing={{}: (5, {})} | custom-call | flops 1073741824 | bytes 2097152 | tf_op jit(solution)/shard_map/pallas_call | solution.py:147
  111.5 1.3 collective-permute-start.25
  113.6 6.3 %collective-permute-start.22 = (bf16[1024,256]{1,0:T(8,128)(2,1)S(1)}, bf16[1024,256]{1,0:T(8,128)(2,1)S(1)}, u32[]{:S(2)}, u32[]{:S(2)}) collective-permute-start(bf16[1024,256]{1,0:T(8,128)(2,1)S(1)} %get-tuple-element.161), channel_id=1, source_target_pairs={{0,1},{3,2},{4,5},{7,6},{8,9},{11,10},{12,13},{15,14},{16,17},{19,... | collective-permute-start | bytes 1572872 | tf_op jit(solution)/shard_map/ppermute | solution.py:332
  119.9 1.5 collective-permute-start.21
  121.3 5.3 %collective-permute-done.25.refs_3_ = bf16[1024,256]{1,0:T(8,128)(2,1)S(1)} collective-permute-done((bf16[1024,256]{1,0:T(8,128)(2,1)S(1)}, bf16[1024,256]{1,0:T(8,128)(2,1)S(1)}, u32[]{:S(2)}, u32[]{:S(2)}) %collective-permute-start.25) | collective-permute-done | bytes 524320 | tf_op jit(solution)/shard_map/ppermute | solution.py:332
  126.6 1.3 collective-permute-start.28
  127.9 4.2 %collective-permute-done.22 = bf16[1024,256]{1,0:T(8,128)(2,1)S(1)} collective-permute-done((bf16[1024,256]{1,0:T(8,128)(2,1)S(1)}, bf16[1024,256]{1,0:T(8,128)(2,1)S(1)}, u32[]{:S(2)}, u32[]{:S(2)}) %collective-permute-start.22) | collective-permute-done | bytes 524320 | tf_op jit(solution)/shard_map/ppermute | solution.py:332
  133.0 8.2 %collective-permute-done.21 = bf16[1024,256]{1,0:T(8,128)(2,1)S(1)} collective-permute-done((bf16[1024,256]{1,0:T(8,128)(2,1)S(1)}, bf16[1024,256]{1,0:T(8,128)(2,1)S(1)}, u32[]{:S(2)}, u32[]{:S(2)}) %collective-permute-start.21) | collective-permute-done | bytes 524320 | tf_op jit(solution)/shard_map/ppermute | solution.py:332
  141.9 1.3 fusion.2
  143.2 4.5 %collective-permute-start.29 = (bf16[1024,256]{1,0:T(8,128)(2,1)}, bf16[1024,256]{1,0:T(8,128)(2,1)}, u32[]{:S(2)}, u32[]{:S(2)}) collective-permute-start(bf16[1024,256]{1,0:T(8,128)(2,1)} %get-tuple-element.159), channel_id=1, source_target_pairs={{0,1},{2,3},{1,0},{3,2},{4,5},{6,7},{5,4},{7,6},{8,9},{10,11},{9,8... | collective-permute-start | bytes 1572872 | tf_op jit(solution)/shard_map/ppermute | solution.py:332
  148.5 7.0 %collective-permute-done.29 = bf16[1024,256]{1,0:T(8,128)(2,1)} collective-permute-done((bf16[1024,256]{1,0:T(8,128)(2,1)}, bf16[1024,256]{1,0:T(8,128)(2,1)}, u32[]{:S(2)}, u32[]{:S(2)}) %collective-permute-start.29) | collective-permute-done | bytes 524320 | tf_op jit(solution)/shard_map/ppermute | solution.py:332
  156.3 1.6 subtract_convert_fusion
  158.5 6.4 %collective-permute-start.31 = (bf16[1024,256]{1,0:T(8,128)(2,1)S(1)}, bf16[1024,256]{1,0:T(8,128)(2,1)S(1)}, u32[]{:S(2)}, u32[]{:S(2)}) collective-permute-start(bf16[1024,256]{1,0:T(8,128)(2,1)S(1)} %get-tuple-element.143.refs_0_), channel_id=1, source_target_pairs={{0,1},{2,3},{1,0},{3,2},{4,5},{6,7},{5,4},{7,6},{8,9},{10,11},{9,8... | collective-permute-start | bytes 1572872 | tf_op jit(solution)/shard_map/ppermute | solution.py:332
  165.1 10.6 %shard_map.99 = (f32[512,1024]{1,0:T(8,128)}, f32[512,1024]{1,0:T(8,128)}, bf16[4,256,1024]{2,1,0:T(8,128)(2,1)}) custom-call(s32[12]{0:T(128)S(1)} %stack.93.meta_ref, bf16[1024,256]{1,0:T(8,128)(2,1)} %copy-done.24, bf16[1024,256]{1,0:T(8,128)(2,1)} %copy-done.32, bf16[1024,256]{1,0:T(8,128)(2,1)} %copy-done.31, bf16[1024,256]{1,0:T(8,128)(2,1)} %copy-done.33, ...), custom_call_target="tpu_custom_call" | custom-call | flops 4294967296 | bytes 8388608 | tf_op jit(solution)/shard_map/pallas_call | solution.py:227
  176.9 1.3 collective-permute-start.33
  180.4 12.7 %collective-permute-done.33.refs_3_ = bf16[1024,256]{1,0:T(8,128)(2,1)S(1)} collective-permute-done((bf16[1024,256]{1,0:T(8,128)(2,1)S(1)}, bf16[1024,256]{1,0:T(8,128)(2,1)S(1)}, u32[]{:S(2)}, u32[]{:S(2)}) %collective-permute-start.33) | collective-permute-done | bytes 524320 | tf_op jit(solution)/shard_map/ppermute | solution.py:332
  193.1 1.3 collective-permute-start.36
  196.1 10.2 %shard_map.100 = (f32[512,1024]{1,0:T(8,128)S(1)}, f32[512,1024]{1,0:T(8,128)S(1)}, bf16[4,256,1024]{2,1,0:T(8,128)(2,1)S(1)}) custom-call(s32[12]{0:T(128)S(1)} %stack.93.meta_ref, bf16[1024,256]{1,0:T(8,128)(2,1)} %copy-done.25, bf16[1024,256]{1,0:T(8,128)(2,1)} %copy-done.37, bf16[1024,256]{1,0:T(8,128)(2,1)} %copy-done.36, bf16[1024,256]{1,0:T(8,128)(2,1)} %copy-done.39, ...), custom_call_target="tpu_custom_call" | custom-call | flops 4294967296 | bytes 8388608 | tf_op jit(solution)/shard_map/pallas_call | solution.py:227
  206.4 3.2 %collective-permute-done.36.piece_ref = bf16[1024,256]{1,0:T(8,128)(2,1)S(1)} collective-permute-done((bf16[1024,256]{1,0:T(8,128)(2,1)S(1)}, bf16[1024,256]{1,0:T(8,128)(2,1)S(1)}, u32[]{:S(2)}, u32[]{:S(2)}) %collective-permute-start.36) | collective-permute-done | bytes 524320 | tf_op jit(solution)/shard_map/ppermute | solution.py:332
  209.5 4.1 %shard_map.101 = (f32[512,1024]{1,0:T(8,128)S(1)}, bf16[512,1024]{1,0:T(8,128)(2,1)S(1)}, bf16[4,256,1024]{2,1,0:T(8,128)(2,1)S(1)}) custom-call(s32[2]{0:T(128)S(1)} %pad_add_fusion.meta_ref, bf16[1024,256]{1,0:T(8,128)(2,1)S(1)} %collective-permute-done.36.piece_ref, bf16[512,1024]{1,0:T(8,128)(2,1)S(1)} %copy-done, ...), custom_call_target="tpu_custom_call", output_to_operand_aliasing={{2}: (6, {})} | custom-call | flops 1073741824 | bytes 8388608 | tf_op jit(solution)/shard_map/pallas_call | solution.py:290
  213.6 1.3 copy-done.10
  216.2 1.6 collective-permute-done.41
  217.8 1.7 add_convert_fusion.b_ref.g_ref
  220.8 1.5 bitcast_add_fusion.3
  223.3 1.1 collective-permute-start.44
  224.5 1.5 collective-permute-start.43
  226.0 8.6 %shard_map.103 = (bf16[512,1024]{1,0:T(8,128)(2,1)}, f32[512,1024]{1,0:T(8,128)S(1)}, f32[512,1024]{1,0:T(8,128)S(1)}) custom-call(bf16[512,1024]{1,0:T(8,128)(2,1)S(1)} %copy-done.7, bf16[512,1024]{1,0:T(8,128)(2,1)S(1)} %copy-done.5, bf16[512,1024]{1,0:T(8,128)(2,1)S(1)} %copy-done.6, bf16[512,1024]{1,0:T(8,128)(2,1)S(1)} %add_convert_fusion.b_ref.g_ref, ...), custom_call_target="tpu_custom_call" | custom-call | flops 2684354560 | bytes 9437184 | tf_op jit(solution)/shard_map/pallas_call | solution.py:129
  236.3 1.5 collective-permute-start.48
  237.9 3.4 %shard_map.104 = (bf16[512,1024]{1,0:T(8,128)(2,1)}, bf16[512,1024]{1,0:T(8,128)(2,1)}) custom-call(bf16[512,1024]{1,0:T(8,128)(2,1)S(1)} %copy-done.5, bf16[512,1024]{1,0:T(8,128)(2,1)S(1)} %copy-done.6, f32[512,1024]{1,0:T(8,128)S(1)} %get-tuple-element.130.dk_part_ref, f32[512,1024]{1,0:T(8,128)S(1)} %get-tuple-element.131.dv_part_ref, ...), custom_call_target="tpu_custom_call" | custom-call | flops 536870912 | bytes 7340032 | tf_op jit(solution)/shard_map/pallas_call | solution.py:129
  241.3 3.2 %collective-permute-done.49 = bf16[128,1024]{1,0:T(8,128)(2,1)S(1)} collective-permute-done((bf16[128,1024]{1,0:T(8,128)(2,1)S(1)}, bf16[128,1024]{1,0:T(8,128)(2,1)S(1)}, u32[]{:S(2)}, u32[]{:S(2)}) %collective-permute-start.49) | collective-permute-done | bytes 262176 | tf_op jit(solution)/shard_map/ppermute | solution.py:321
  245.0 1.5 pad_maximum_fusion
  (179 shorter events, 29.4 us)
Async XLA Ops:
  2.7 4.7 %collective-permute-start = (bf16[8,128,128]{2,1,0:T(8,128)(2,1)S(1)}, bf16[8,128,128]{2,1,0:T(8,128)(2,1)S(1)}, u32[]{:S(2)}, u32[]{:S(2)}) collective-permute-start(bf16[8,128,128]{2,1,0:T(8,128)(2,1)S(1)} %convert_element_type.304), channel_id=1, source_target_pairs={{0,4},{4,0},{8,12},{12,8},{16,20},{20,16},{24,28},{28,24},{1,5},{5... | collective-permute-start | bytes 786440 | tf_op jit(solution)/shard_map/ppermute | solution.py:316
  3.3 14.0 %copy-start.12 = (bf16[256,1024]{1,0:T(8,128)(2,1)}, bf16[256,1024]{1,0:T(8,128)(2,1)S(1)}, u32[]{:S(2)}) copy-start(bf16[256,1024]{1,0:T(8,128)(2,1)S(1)} %slice.96.refs_0_.refs_8_) | copy-start | bytes 1572868
  3.3 15.4 %collective-permute-start.5 = (bf16[256,1024]{1,0:T(8,128)(2,1)S(1)}, bf16[256,1024]{1,0:T(8,128)(2,1)S(1)}, u32[]{:S(2)}, u32[]{:S(2)}) collective-permute-start(bf16[256,1024]{1,0:T(8,128)(2,1)S(1)} %slice.96.refs_0_.refs_8_), channel_id=1, source_target_pairs={{0,16},{4,20},{8,24},{12,28},{16,0},{20,4},{24,8},{28,12},{1,17},{... | collective-permute-start | bytes 1572872 | tf_op jit(solution)/shard_map/ppermute | solution.py:321
  5.9 14.8 %collective-permute-start.4 = (bf16[256,1024]{1,0:T(8,128)(2,1)S(1)}, bf16[256,1024]{1,0:T(8,128)(2,1)S(1)}, u32[]{:S(2)}, u32[]{:S(2)}) collective-permute-start(bf16[256,1024]{1,0:T(8,128)(2,1)S(1)} %slice.96.refs_0_.refs_8_), channel_id=1, source_target_pairs={{0,8},{4,12},{8,0},{12,4},{16,24},{20,28},{24,16},{28,20},{1,9},{5... | collective-permute-start | bytes 1572872 | tf_op jit(solution)/shard_map/ppermute | solution.py:321
  7.5 15.5 %collective-permute-start.3 = (bf16[4,128,128]{2,1,0:T(8,128)(2,1)S(1)}, bf16[4,128,128]{2,1,0:T(8,128)(2,1)S(1)}, u32[]{:S(2)}, u32[]{:S(2)}) collective-permute-start(bf16[4,128,128]{2,1,0:T(8,128)(2,1)S(1)} %fusion.15), channel_id=1, source_target_pairs={{0,24},{4,28},{8,16},{12,20},{16,8},{20,12},{24,0},{28,4},{1,25},{... | collective-permute-start | bytes 393224 | tf_op jit(solution)/shard_map/ppermute | solution.py:321
  8.4 15.7 %collective-permute-start.2 = (bf16[4,128,128]{2,1,0:T(8,128)(2,1)S(1)}, bf16[4,128,128]{2,1,0:T(8,128)(2,1)S(1)}, u32[]{:S(2)}, u32[]{:S(2)}) collective-permute-start(bf16[4,128,128]{2,1,0:T(8,128)(2,1)S(1)} %fusion.15), channel_id=1, source_target_pairs={{0,16},{4,20},{8,24},{12,28},{16,0},{20,4},{24,8},{28,12},{1,17},{... | collective-permute-start | bytes 393224 | tf_op jit(solution)/shard_map/ppermute | solution.py:321
  9.5 16.0 %collective-permute-start.1 = (bf16[4,128,128]{2,1,0:T(8,128)(2,1)S(1)}, bf16[4,128,128]{2,1,0:T(8,128)(2,1)S(1)}, u32[]{:S(2)}, u32[]{:S(2)}) collective-permute-start(bf16[4,128,128]{2,1,0:T(8,128)(2,1)S(1)} %fusion.15), channel_id=1, source_target_pairs={{0,8},{4,12},{8,0},{12,4},{16,24},{20,28},{24,16},{28,20},{1,9},{5... | collective-permute-start | bytes 393224 | tf_op jit(solution)/shard_map/ppermute | solution.py:321
  25.7 2.2 collective-permute-start.6
  25.8 8.8 %collective-permute-start.8 = (bf16[128,1024]{1,0:T(8,128)(2,1)S(1)}, bf16[128,1024]{1,0:T(8,128)(2,1)S(1)}, u32[]{:S(2)}, u32[]{:S(2)}) collective-permute-start(bf16[128,1024]{1,0:T(8,128)(2,1)S(1)} %slice.98), channel_id=1, source_target_pairs={{0,8},{4,12},{8,0},{12,4},{16,24},{20,28},{24,16},{28,20},{1,9},{5... | collective-permute-start | bytes 786440 | tf_op jit(solution)/shard_map/ppermute | solution.py:321
  27.4 8.4 %collective-permute-start.7 = (bf16[128,1024]{1,0:T(8,128)(2,1)S(1)}, bf16[128,1024]{1,0:T(8,128)(2,1)S(1)}, u32[]{:S(2)}, u32[]{:S(2)}) collective-permute-start(bf16[128,1024]{1,0:T(8,128)(2,1)S(1)} %slice.97), channel_id=1, source_target_pairs={{0,16},{4,20},{8,24},{12,28},{16,0},{20,4},{24,8},{28,12},{1,17},{... | collective-permute-start | bytes 786440 | tf_op jit(solution)/shard_map/ppermute | solution.py:321
  36.6 3.3 %collective-permute-start.9 = (bf16[512,1024]{1,0:T(8,128)(2,1)}, bf16[512,1024]{1,0:T(8,128)(2,1)S(1)}, u32[]{:S(2)}, u32[]{:S(2)}) collective-permute-start(bf16[512,1024]{1,0:T(8,128)(2,1)} %shard_map.94.a_ref.refs_6_.refs_5_.own_ref), channel_id=1, source_target_pairs={{0,4},{4,0},{8,12},{12,8},{16,20},{20,16},{24,28},{28,24},{1,5},{5... | collective-permute-start | bytes 3145736 | tf_op jit(solution)/shard_map/ppermute | solution.py:316
  39.9 66.5 %copy-start.1 = (bf16[512,1024]{1,0:T(8,128)(2,1)}, bf16[512,1024]{1,0:T(8,128)(2,1)S(1)}, u32[]{:S(2)}) copy-start(bf16[512,1024]{1,0:T(8,128)(2,1)S(1)} %collective-permute-done.9.a_ref.refs_7_.refs_6_.other_ref) | copy-start | bytes 3145732
  44.4 16.0 %collective-permute-start.14 = (bf16[1024,256]{1,0:T(8,128)(2,1)}, bf16[1024,256]{1,0:T(8,128)(2,1)}, u32[]{:S(2)}, u32[]{:S(2)}) collective-permute-start(bf16[1024,256]{1,0:T(8,128)(2,1)} %get-tuple-element.165), channel_id=1, source_target_pairs={{0,1},{3,2},{4,5},{7,6},{8,9},{11,10},{12,13},{15,14},{16,17},{19,... | collective-permute-start | bytes 1572872 | tf_op jit(solution)/shard_map/ppermute | solution.py:332
  48.7 22.6 %collective-permute-start.17 = (bf16[1024,256]{1,0:T(8,128)(2,1)}, bf16[1024,256]{1,0:T(8,128)(2,1)}, u32[]{:S(2)}, u32[]{:S(2)}) collective-permute-start(bf16[1024,256]{1,0:T(8,128)(2,1)} %get-tuple-element.166), channel_id=1, source_target_pairs={{0,1},{3,2},{4,5},{7,6},{8,9},{11,10},{12,13},{15,14},{16,17},{19,... | collective-permute-start | bytes 1572872 | tf_op jit(solution)/shard_map/ppermute | solution.py:332
  62.4 8.9 %collective-permute-start.15 = (bf16[1024,256]{1,0:T(8,128)(2,1)}, bf16[1024,256]{1,0:T(8,128)(2,1)}, u32[]{:S(2)}, u32[]{:S(2)}) collective-permute-start(bf16[1024,256]{1,0:T(8,128)(2,1)} %fusion.6), channel_id=1, source_target_pairs={{1,2},{2,1},{5,6},{6,5},{9,10},{10,9},{13,14},{14,13},{17,18},{18,... | collective-permute-start | bytes 1572872 | tf_op jit(solution)/shard_map/ppermute | solution.py:332
  65.7 18.4 %collective-permute-start.10 = (bf16[256,1024]{1,0:T(8,128)(2,1)}, bf16[256,1024]{1,0:T(8,128)(2,1)}, u32[]{:S(2)}, u32[]{:S(2)}) collective-permute-start(bf16[256,1024]{1,0:T(8,128)(2,1)} %slice.99.refs_0_.refs_7_), channel_id=1, source_target_pairs={{0,8},{4,12},{8,0},{12,4},{16,24},{20,28},{24,16},{28,20},{1,9},{5... | collective-permute-start | bytes 1572872 | tf_op jit(solution)/shard_map/ppermute | solution.py:321
  66.3 21.2 %collective-permute-start.11 = (bf16[256,1024]{1,0:T(8,128)(2,1)}, bf16[256,1024]{1,0:T(8,128)(2,1)}, u32[]{:S(2)}, u32[]{:S(2)}) collective-permute-start(bf16[256,1024]{1,0:T(8,128)(2,1)} %slice.99.refs_0_.refs_7_), channel_id=1, source_target_pairs={{0,16},{4,20},{8,24},{12,28},{16,0},{20,4},{24,8},{28,12},{1,17},{... | collective-permute-start | bytes 1572872 | tf_op jit(solution)/shard_map/ppermute | solution.py:321
  68.6 20.4 %collective-permute-start.19 = (bf16[512,512]{1,0:T(8,128)(2,1)}, bf16[512,512]{1,0:T(8,128)(2,1)}, u32[]{:S(2)}, u32[]{:S(2)}) collective-permute-start(bf16[512,512]{1,0:T(8,128)(2,1)} %constant_dynamic-slice_fusion.1), channel_id=1, source_target_pairs={{0,4},{4,0},{8,12},{12,8},{16,20},{20,16},{24,28},{28,24},{1,5},{5... | collective-permute-start | bytes 1572872 | tf_op jit(solution)/shard_map/ppermute | solution.py:316
  73.7 19.8 %collective-permute-start.16 = (bf16[1024,256]{1,0:T(8,128)(2,1)}, bf16[1024,256]{1,0:T(8,128)(2,1)}, u32[]{:S(2)}, u32[]{:S(2)}) collective-permute-start(bf16[1024,256]{1,0:T(8,128)(2,1)} %get-tuple-element.163), channel_id=1, source_target_pairs={{0,1},{2,3},{1,0},{3,2},{4,5},{6,7},{5,4},{7,6},{8,9},{10,11},{9,8... | collective-permute-start | bytes 1572872 | tf_op jit(solution)/shard_map/ppermute | solution.py:332
  82.7 10.8 %collective-permute-start.18 = (bf16[1024,256]{1,0:T(8,128)(2,1)}, bf16[1024,256]{1,0:T(8,128)(2,1)}, u32[]{:S(2)}, u32[]{:S(2)}) collective-permute-start(bf16[1024,256]{1,0:T(8,128)(2,1)} %get-tuple-element.164), channel_id=1, source_target_pairs={{1,2},{2,1},{5,6},{6,5},{9,10},{10,9},{13,14},{14,13},{17,18},{18,... | collective-permute-start | bytes 1572872 | tf_op jit(solution)/shard_map/ppermute | solution.py:332
  85.1 6.4 %collective-permute-start.12 = (bf16[128,1024]{1,0:T(8,128)(2,1)S(1)}, bf16[128,1024]{1,0:T(8,128)(2,1)S(1)}, u32[]{:S(2)}, u32[]{:S(2)}) collective-permute-start(bf16[128,1024]{1,0:T(8,128)(2,1)S(1)} %slice.128), channel_id=1, source_target_pairs={{0,16},{4,20},{8,24},{12,28},{16,0},{20,4},{24,8},{28,12},{1,17},{... | collective-permute-start | bytes 786440 | tf_op jit(solution)/shard_map/ppermute | solution.py:321
  88.4 13.9 %collective-permute-start.13 = (bf16[128,1024]{1,0:T(8,128)(2,1)S(1)}, bf16[128,1024]{1,0:T(8,128)(2,1)S(1)}, u32[]{:S(2)}, u32[]{:S(2)}) collective-permute-start(bf16[128,1024]{1,0:T(8,128)(2,1)S(1)} %slice.129), channel_id=1, source_target_pairs={{0,8},{4,12},{8,0},{12,4},{16,24},{20,28},{24,16},{28,20},{1,9},{5... | collective-permute-start | bytes 786440 | tf_op jit(solution)/shard_map/ppermute | solution.py:321
  95.0 15.4 %collective-permute-start.24 = (bf16[1024,256]{1,0:T(8,128)(2,1)S(1)}, bf16[1024,256]{1,0:T(8,128)(2,1)S(1)}, u32[]{:S(2)}, u32[]{:S(2)}) collective-permute-start(bf16[1024,256]{1,0:T(8,128)(2,1)S(1)} %get-tuple-element.145.refs_0_), channel_id=1, source_target_pairs={{1,2},{2,1},{5,6},{6,5},{9,10},{10,9},{13,14},{14,13},{17,18},{18,... | collective-permute-start | bytes 1572872 | tf_op jit(solution)/shard_map/ppermute | solution.py:332
  95.7 15.8 %collective-permute-start.23 = (bf16[1024,256]{1,0:T(8,128)(2,1)S(1)}, bf16[1024,256]{1,0:T(8,128)(2,1)S(1)}, u32[]{:S(2)}, u32[]{:S(2)}) collective-permute-start(bf16[1024,256]{1,0:T(8,128)(2,1)S(1)} %get-tuple-element.145.refs_0_), channel_id=1, source_target_pairs={{0,1},{2,3},{1,0},{3,2},{4,5},{6,7},{5,4},{7,6},{8,9},{10,11},{9,8... | collective-permute-start | bytes 1572872 | tf_op jit(solution)/shard_map/ppermute | solution.py:332
  102.2 7.3 %collective-permute-start.20 = (bf16[512,256]{1,0:T(8,128)(2,1)S(1)}, bf16[512,256]{1,0:T(8,128)(2,1)S(1)}, u32[]{:S(2)}, u32[]{:S(2)}) collective-permute-start(bf16[512,256]{1,0:T(8,128)(2,1)S(1)} %slice.132), channel_id=1, source_target_pairs={{0,4},{4,0},{8,12},{12,8},{16,20},{20,16},{24,28},{28,24},{1,5},{5... | collective-permute-start | bytes 786440 | tf_op jit(solution)/shard_map/ppermute | solution.py:316
  110.4 30.8 %copy-start.31 = (bf16[1024,256]{1,0:T(8,128)(2,1)}, bf16[1024,256]{1,0:T(8,128)(2,1)S(1)}, u32[]{:S(2)}) copy-start(bf16[1024,256]{1,0:T(8,128)(2,1)S(1)} %collective-permute-done.24.refs_2_) | copy-start | bytes 1572868
  111.5 31.7 %copy-start.32 = (bf16[1024,256]{1,0:T(8,128)(2,1)}, bf16[1024,256]{1,0:T(8,128)(2,1)S(1)}, u32[]{:S(2)}) copy-start(bf16[1024,256]{1,0:T(8,128)(2,1)S(1)} %collective-permute-done.23.refs_1_) | copy-start | bytes 1572868
  111.5 15.1 %collective-permute-start.25 = (bf16[1024,256]{1,0:T(8,128)(2,1)S(1)}, bf16[1024,256]{1,0:T(8,128)(2,1)S(1)}, u32[]{:S(2)}, u32[]{:S(2)}) collective-permute-start(bf16[1024,256]{1,0:T(8,128)(2,1)S(1)} %collective-permute-done.24.refs_2_), channel_id=1, source_target_pairs={{2,3},{1,0},{6,7},{5,4},{10,11},{9,8},{14,15},{13,12},{18,19},{17,... | collective-permute-start | bytes 1572872 | tf_op jit(solution)/shard_map/ppermute | solution.py:332
  112.8 13.9 %collective-permute-start.26 = (bf16[1024,256]{1,0:T(8,128)(2,1)S(1)}, bf16[1024,256]{1,0:T(8,128)(2,1)S(1)}, u32[]{:S(2)}, u32[]{:S(2)}) collective-permute-start(bf16[1024,256]{1,0:T(8,128)(2,1)S(1)} %collective-permute-done.23.refs_1_), channel_id=1, source_target_pairs={{1,2},{2,1},{5,6},{6,5},{9,10},{10,9},{13,14},{14,13},{17,18},{18,... | collective-permute-start | bytes 1572872 | tf_op jit(solution)/shard_map/ppermute | solution.py:332
  113.6 18.6 %collective-permute-start.22 = (bf16[1024,256]{1,0:T(8,128)(2,1)S(1)}, bf16[1024,256]{1,0:T(8,128)(2,1)S(1)}, u32[]{:S(2)}, u32[]{:S(2)}) collective-permute-start(bf16[1024,256]{1,0:T(8,128)(2,1)S(1)} %get-tuple-element.161), channel_id=1, source_target_pairs={{0,1},{3,2},{4,5},{7,6},{8,9},{11,10},{12,13},{15,14},{16,17},{19,... | collective-permute-start | bytes 1572872 | tf_op jit(solution)/shard_map/ppermute | solution.py:332
  119.9 36.4 %copy-start.17 = (bf16[512,256]{1,0:T(8,128)(2,1)S(1)}, bf16[512,256]{1,0:T(8,128)(2,1)}, u32[]{:S(2)}) copy-start(bf16[512,256]{1,0:T(8,128)(2,1)} %get-tuple-element.168) | copy-start | bytes 786436
  119.9 21.4 %collective-permute-start.21 = (bf16[1024,256]{1,0:T(8,128)(2,1)S(1)}, bf16[1024,256]{1,0:T(8,128)(2,1)S(1)}, u32[]{:S(2)}, u32[]{:S(2)}) collective-permute-start(bf16[1024,256]{1,0:T(8,128)(2,1)S(1)} %get-tuple-element.162), channel_id=1, source_target_pairs={{0,1},{3,2},{4,5},{7,6},{8,9},{11,10},{12,13},{15,14},{16,17},{19,... | collective-permute-start | bytes 1572872 | tf_op jit(solution)/shard_map/ppermute | solution.py:332
  126.6 16.5 %copy-start.33 = (bf16[1024,256]{1,0:T(8,128)(2,1)}, bf16[1024,256]{1,0:T(8,128)(2,1)S(1)}, u32[]{:S(2)}) copy-start(bf16[1024,256]{1,0:T(8,128)(2,1)S(1)} %collective-permute-done.25.refs_3_) | copy-start | bytes 1572868
  126.6 16.5 %copy-start.34 = (bf16[1024,256]{1,0:T(8,128)(2,1)}, bf16[1024,256]{1,0:T(8,128)(2,1)S(1)}, u32[]{:S(2)}) copy-start(bf16[1024,256]{1,0:T(8,128)(2,1)S(1)} %collective-permute-done.26.refs_4_) | copy-start | bytes 1572868
  126.6 15.3 %collective-permute-start.28 = (bf16[1024,256]{1,0:T(8,128)(2,1)S(1)}, bf16[1024,256]{1,0:T(8,128)(2,1)S(1)}, u32[]{:S(2)}, u32[]{:S(2)}) collective-permute-start(bf16[1024,256]{1,0:T(8,128)(2,1)S(1)} %collective-permute-done.26.refs_4_), channel_id=1, source_target_pairs={{2,3},{1,0},{6,7},{5,4},{10,11},{9,8},{14,15},{13,12},{18,19},{17,... | collective-permute-start | bytes 1572872 | tf_op jit(solution)/shard_map/ppermute | solution.py:332
  132.3 9.6 %collective-permute-start.27 = (bf16[1024,256]{1,0:T(8,128)(2,1)S(1)}, bf16[1024,256]{1,0:T(8,128)(2,1)S(1)}, u32[]{:S(2)}, u32[]{:S(2)}) collective-permute-start(bf16[1024,256]{1,0:T(8,128)(2,1)S(1)} %fusion.1), channel_id=1, source_target_pairs={{1,2},{2,1},{5,6},{6,5},{9,10},{10,9},{13,14},{14,13},{17,18},{18,... | collective-permute-start | bytes 1572872 | tf_op jit(solution)/shard_map/ppermute | solution.py:332
  143.2 12.3 %collective-permute-start.29 = (bf16[1024,256]{1,0:T(8,128)(2,1)}, bf16[1024,256]{1,0:T(8,128)(2,1)}, u32[]{:S(2)}, u32[]{:S(2)}) collective-permute-start(bf16[1024,256]{1,0:T(8,128)(2,1)} %get-tuple-element.159), channel_id=1, source_target_pairs={{0,1},{2,3},{1,0},{3,2},{4,5},{6,7},{5,4},{7,6},{8,9},{10,11},{9,8... | collective-permute-start | bytes 1572872 | tf_op jit(solution)/shard_map/ppermute | solution.py:332
  147.7 7.8 %collective-permute-start.30 = (bf16[1024,256]{1,0:T(8,128)(2,1)}, bf16[1024,256]{1,0:T(8,128)(2,1)S(1)}, u32[]{:S(2)}, u32[]{:S(2)}) collective-permute-start(bf16[1024,256]{1,0:T(8,128)(2,1)} %get-tuple-element.160), channel_id=1, source_target_pairs={{1,2},{2,1},{5,6},{6,5},{9,10},{10,9},{13,14},{14,13},{17,18},{18,... | collective-permute-start | bytes 1572872 | tf_op jit(solution)/shard_map/ppermute | solution.py:332
  157.8 17.8 %copy-start.25 = (bf16[1024,256]{1,0:T(8,128)(2,1)}, bf16[1024,256]{1,0:T(8,128)(2,1)S(1)}, u32[]{:S(2)}) copy-start(bf16[1024,256]{1,0:T(8,128)(2,1)S(1)} %get-tuple-element.143.refs_0_) | copy-start | bytes 1572868
  157.8 19.0 %collective-permute-start.32 = (bf16[1024,256]{1,0:T(8,128)(2,1)S(1)}, bf16[1024,256]{1,0:T(8,128)(2,1)S(1)}, u32[]{:S(2)}, u32[]{:S(2)}) collective-permute-start(bf16[1024,256]{1,0:T(8,128)(2,1)S(1)} %get-tuple-element.143.refs_0_), channel_id=1, source_target_pairs={{1,2},{2,1},{5,6},{6,5},{9,10},{10,9},{13,14},{14,13},{17,18},{18,... | collective-permute-start | bytes 1572872 | tf_op jit(solution)/shard_map/ppermute | solution.py:332
  158.5 18.3 %collective-permute-start.31 = (bf16[1024,256]{1,0:T(8,128)(2,1)S(1)}, bf16[1024,256]{1,0:T(8,128)(2,1)S(1)}, u32[]{:S(2)}, u32[]{:S(2)}) collective-permute-start(bf16[1024,256]{1,0:T(8,128)(2,1)S(1)} %get-tuple-element.143.refs_0_), channel_id=1, source_target_pairs={{0,1},{2,3},{1,0},{3,2},{4,5},{6,7},{5,4},{7,6},{8,9},{10,11},{9,8... | collective-permute-start | bytes 1572872 | tf_op jit(solution)/shard_map/ppermute | solution.py:332
  165.0 10.7 %collective-permute-start.35 = (bf16[512,256]{1,0:T(8,128)(2,1)S(1)}, bf16[512,256]{1,0:T(8,128)(2,1)S(1)}, u32[]{:S(2)}, u32[]{:S(2)}) collective-permute-start(bf16[512,256]{1,0:T(8,128)(2,1)S(1)} %slice.135), channel_id=1, source_target_pairs={{0,4},{4,0},{8,12},{12,8},{16,20},{20,16},{24,28},{28,24},{1,5},{5... | collective-permute-start | bytes 786440 | tf_op jit(solution)/shard_map/ppermute | solution.py:316
  176.9 19.2 %copy-start.36 = (bf16[1024,256]{1,0:T(8,128)(2,1)}, bf16[1024,256]{1,0:T(8,128)(2,1)S(1)}, u32[]{:S(2)}) copy-start(bf16[1024,256]{1,0:T(8,128)(2,1)S(1)} %collective-permute-done.32.refs_2_) | copy-start | bytes 1572868
  176.9 19.2 %copy-start.37 = (bf16[1024,256]{1,0:T(8,128)(2,1)}, bf16[1024,256]{1,0:T(8,128)(2,1)S(1)}, u32[]{:S(2)}) copy-start(bf16[1024,256]{1,0:T(8,128)(2,1)S(1)} %collective-permute-done.31.refs_1_) | copy-start | bytes 1572868
  176.9 16.2 %collective-permute-start.33 = (bf16[1024,256]{1,0:T(8,128)(2,1)S(1)}, bf16[1024,256]{1,0:T(8,128)(2,1)S(1)}, u32[]{:S(2)}, u32[]{:S(2)}) collective-permute-start(bf16[1024,256]{1,0:T(8,128)(2,1)S(1)} %collective-permute-done.32.refs_2_), channel_id=1, source_target_pairs={{2,3},{1,0},{6,7},{5,4},{10,11},{9,8},{14,15},{13,12},{18,19},{17,... | collective-permute-start | bytes 1572872 | tf_op jit(solution)/shard_map/ppermute | solution.py:332
  178.2 14.9 %collective-permute-start.34 = (bf16[1024,256]{1,0:T(8,128)(2,1)S(1)}, bf16[1024,256]{1,0:T(8,128)(2,1)S(1)}, u32[]{:S(2)}, u32[]{:S(2)}) collective-permute-start(bf16[1024,256]{1,0:T(8,128)(2,1)S(1)} %collective-permute-done.31.refs_1_), channel_id=1, source_target_pairs={{1,2},{2,1},{5,6},{6,5},{9,10},{10,9},{13,14},{14,13},{17,18},{18,... | collective-permute-start | bytes 1572872 | tf_op jit(solution)/shard_map/ppermute | solution.py:332
  179.2 15.2 %collective-permute-start.39 = (bf16[2,128,1024]{2,1,0:T(8,128)(2,1)S(1)}, bf16[2,128,1024]{2,1,0:T(8,128)(2,1)S(1)}, u32[]{:S(2)}, u32[]{:S(2)}) collective-permute-start(bf16[2,128,1024]{2,1,0:T(8,128)(2,1)S(1)} %get-tuple-element.157), channel_id=1, source_target_pairs={{0,16},{4,20},{8,24},{12,28},{16,0},{20,4},{24,8},{28,12},{1,17},{... | collective-permute-start | bytes 1572872 | tf_op jit(solution)/shard_map/ppermute | solution.py:321
  179.7 14.7 %collective-permute-start.37 = (bf16[2,128,1024]{2,1,0:T(8,128)(2,1)S(1)}, bf16[2,128,1024]{2,1,0:T(8,128)(2,1)S(1)}, u32[]{:S(2)}, u32[]{:S(2)}) collective-permute-start(bf16[2,128,1024]{2,1,0:T(8,128)(2,1)S(1)} %get-tuple-element.158), channel_id=1, source_target_pairs={{0,8},{4,12},{8,0},{12,4},{16,24},{20,28},{24,16},{28,20},{1,9},{5... | collective-permute-start | bytes 1572872 | tf_op jit(solution)/shard_map/ppermute | solution.py:321
  193.1 16.4 %collective-permute-start.36 = (bf16[1024,256]{1,0:T(8,128)(2,1)S(1)}, bf16[1024,256]{1,0:T(8,128)(2,1)S(1)}, u32[]{:S(2)}, u32[]{:S(2)}) collective-permute-start(bf16[1024,256]{1,0:T(8,128)(2,1)S(1)} %collective-permute-done.34.refs_4_), channel_id=1, source_target_pairs={{2,3},{1,0},{6,7},{5,4},{10,11},{9,8},{14,15},{13,12},{18,19},{17,... | collective-permute-start | bytes 1572872 | tf_op jit(solution)/shard_map/ppermute | solution.py:332
  194.6 11.7 %collective-permute-start.40 = (bf16[128,1024]{1,0:T(8,128)(2,1)S(1)}, bf16[128,1024]{1,0:T(8,128)(2,1)S(1)}, u32[]{:S(2)}, u32[]{:S(2)}) collective-permute-start(bf16[128,1024]{1,0:T(8,128)(2,1)S(1)} %get-tuple-element.155), channel_id=1, source_target_pairs={{0,8},{4,12},{8,0},{12,4},{16,24},{20,28},{24,16},{28,20},{1,9},{5... | collective-permute-start | bytes 786440 | tf_op jit(solution)/shard_map/ppermute | solution.py:321
  195.2 14.3 %copy-start = (bf16[512,1024]{1,0:T(8,128)(2,1)S(1)}, bf16[512,1024]{1,0:T(8,128)(2,1)}, u32[]{:S(2)}) copy-start(bf16[512,1024]{1,0:T(8,128)(2,1)} %shard_map.94.a_ref.refs_6_.refs_5_.own_ref) | copy-start | bytes 3145732
  195.2 14.3 %copy-start.2 = (bf16[512,1024]{1,0:T(8,128)(2,1)S(1)}, bf16[512,1024]{1,0:T(8,128)(2,1)}, u32[]{:S(2)}) copy-start(bf16[512,1024]{1,0:T(8,128)(2,1)} %copy-done.1) | copy-start | bytes 3145732
  195.2 14.3 %copy-start.4 = (bf16[256,1024]{1,0:T(8,128)(2,1)S(1)}, bf16[256,1024]{1,0:T(8,128)(2,1)}, u32[]{:S(2)}) copy-start(bf16[256,1024]{1,0:T(8,128)(2,1)} %copy-done.3) | copy-start | bytes 1572868
  195.2 11.1 %collective-permute-start.38 = (bf16[128,1024]{1,0:T(8,128)(2,1)S(1)}, bf16[128,1024]{1,0:T(8,128)(2,1)S(1)}, u32[]{:S(2)}, u32[]{:S(2)}) collective-permute-start(bf16[128,1024]{1,0:T(8,128)(2,1)S(1)} %get-tuple-element.156), channel_id=1, source_target_pairs={{0,16},{4,20},{8,24},{12,28},{16,0},{20,4},{24,8},{28,12},{1,17},{... | collective-permute-start | bytes 786440 | tf_op jit(solution)/shard_map/ppermute | solution.py:321
  215.0 2.8 %collective-permute-start.41 = (bf16[512,1024]{1,0:T(8,128)(2,1)S(1)}, bf16[512,1024]{1,0:T(8,128)(2,1)}, u32[]{:S(2)}, u32[]{:S(2)}) collective-permute-start(bf16[512,1024]{1,0:T(8,128)(2,1)S(1)} %get-tuple-element.122), channel_id=1, source_target_pairs={{0,4},{4,0},{8,12},{12,8},{16,20},{20,16},{24,28},{28,24},{1,5},{5... | collective-permute-start | bytes 3145736 | tf_op jit(solution)/shard_map/ppermute | solution.py:316
  215.0 19.6 %collective-permute-start.47 = (bf16[2,128,1024]{2,1,0:T(8,128)(2,1)S(1)}, bf16[2,128,1024]{2,1,0:T(8,128)(2,1)S(1)}, u32[]{:S(2)}, u32[]{:S(2)}) collective-permute-start(bf16[2,128,1024]{2,1,0:T(8,128)(2,1)S(1)} %get-tuple-element.153), channel_id=1, source_target_pairs={{0,16},{4,20},{8,24},{12,28},{16,0},{20,4},{24,8},{28,12},{1,17},{... | collective-permute-start | bytes 1572872 | tf_op jit(solution)/shard_map/ppermute | solution.py:321
  215.6 19.0 %collective-permute-start.46 = (bf16[2,128,1024]{2,1,0:T(8,128)(2,1)S(1)}, bf16[2,128,1024]{2,1,0:T(8,128)(2,1)S(1)}, u32[]{:S(2)}, u32[]{:S(2)}) collective-permute-start(bf16[2,128,1024]{2,1,0:T(8,128)(2,1)S(1)} %get-tuple-element.154), channel_id=1, source_target_pairs={{0,8},{4,12},{8,0},{12,4},{16,24},{20,28},{24,16},{28,20},{1,9},{5... | collective-permute-start | bytes 1572872 | tf_op jit(solution)/shard_map/ppermute | solution.py:321
  220.5 1.8 collective-permute-start.42
  222.4 12.2 %collective-permute-start.45 = (bf16[4,128,128]{2,1,0:T(8,128)(2,1)S(1)}, bf16[4,128,128]{2,1,0:T(8,128)(2,1)S(1)}, u32[]{:S(2)}, u32[]{:S(2)}) collective-permute-start(bf16[4,128,128]{2,1,0:T(8,128)(2,1)S(1)} %fusion.14), channel_id=1, source_target_pairs={{0,24},{4,28},{8,16},{12,20},{16,8},{20,12},{24,0},{28,4},{1,25},{... | collective-permute-start | bytes 393224 | tf_op jit(solution)/shard_map/ppermute | solution.py:321
  223.3 11.7 %collective-permute-start.44 = (bf16[4,128,128]{2,1,0:T(8,128)(2,1)S(1)}, bf16[4,128,128]{2,1,0:T(8,128)(2,1)S(1)}, u32[]{:S(2)}, u32[]{:S(2)}) collective-permute-start(bf16[4,128,128]{2,1,0:T(8,128)(2,1)S(1)} %fusion.14), channel_id=1, source_target_pairs={{0,16},{4,20},{8,24},{12,28},{16,0},{20,4},{24,8},{28,12},{1,17},{... | collective-permute-start | bytes 393224 | tf_op jit(solution)/shard_map/ppermute | solution.py:321
  224.5 10.9 %collective-permute-start.43 = (bf16[4,128,128]{2,1,0:T(8,128)(2,1)S(1)}, bf16[4,128,128]{2,1,0:T(8,128)(2,1)S(1)}, u32[]{:S(2)}, u32[]{:S(2)}) collective-permute-start(bf16[4,128,128]{2,1,0:T(8,128)(2,1)S(1)} %fusion.14), channel_id=1, source_target_pairs={{0,8},{4,12},{8,0},{12,4},{16,24},{20,28},{24,16},{28,20},{1,9},{5... | collective-permute-start | bytes 393224 | tf_op jit(solution)/shard_map/ppermute | solution.py:321
  235.4 2.4 collective-permute-start.50
  235.7 8.8 %collective-permute-start.49 = (bf16[128,1024]{1,0:T(8,128)(2,1)S(1)}, bf16[128,1024]{1,0:T(8,128)(2,1)S(1)}, u32[]{:S(2)}, u32[]{:S(2)}) collective-permute-start(bf16[128,1024]{1,0:T(8,128)(2,1)S(1)} %get-tuple-element.151), channel_id=1, source_target_pairs={{0,8},{4,12},{8,0},{12,4},{16,24},{20,28},{24,16},{28,20},{1,9},{5... | collective-permute-start | bytes 786440 | tf_op jit(solution)/shard_map/ppermute | solution.py:321
  236.3 8.4 %collective-permute-start.48 = (bf16[128,1024]{1,0:T(8,128)(2,1)S(1)}, bf16[128,1024]{1,0:T(8,128)(2,1)S(1)}, u32[]{:S(2)}, u32[]{:S(2)}) collective-permute-start(bf16[128,1024]{1,0:T(8,128)(2,1)S(1)} %get-tuple-element.152), channel_id=1, source_target_pairs={{0,16},{4,20},{8,24},{12,28},{16,0},{20,4},{24,8},{28,12},{1,17},{... | collective-permute-start | bytes 786440 | tf_op jit(solution)/shard_map/ppermute | solution.py:321
  (27 other events, 136.3 us)

commit v6 on v5

--- a/solution.py
+++ b/solution.py
@@ -12,7 +12,7 @@
 CHUNKS = 2
 F32 = jnp.float32
 BF16 = jnp.bfloat16
-VMEM_LIMIT = 16 * 1024 * 1024
+VMEM_LIMIT = 12 * 1024 * 1024
 
 NT = (((1,), (1,)), ((), ()))
 TN = (((0,), (0,)), ((), ()))
@@ -117,7 +117,7 @@
             (pltpu.HBM if kind == "h" else jax.ShapeDtypeStruct)(shapes[kind], dtype)
             for kind, dtype in outs
         ],
-        compiler_params=pltpu.CompilerParams(vmem_limit_bytes=VMEM_LIMIT),
+        compiler_params=pltpu.CompilerParams(vmem_limit_bytes=VMEM_LIMIT // 2),
         cost_estimate=pl.CostEstimate(
             flops=2 * macs * heads,
             bytes_accessed=rows * heads * DH * 2 * (len(ins) + len(outs)),
@@ -245,7 +245,7 @@
             place((rows, width), F32),
             place((chips, part, width), BF16),
         ],
-        compiler_params=pltpu.CompilerParams(vmem_limit_bytes=32 * rows * chips * part),
+        compiler_params=pltpu.CompilerParams(vmem_limit_bytes=24 * rows * chips * part),
         cost_estimate=pl.CostEstimate(
             flops=8 * rows * width * part * chips,
             bytes_accessed=16 * rows * width,
@@ -297,8 +297,8 @@
             out_specs=[block, block, slot],
         ),
         out_shape=[
-            jax.ShapeDtypeStruct((rows, width), F32),
-            jax.ShapeDtypeStruct((rows, width), second_type),
+            pltpu.HBM((rows, width), F32),
+            pltpu.HBM((rows, width), second_type),
             jax.ShapeDtypeStruct(grads.shape, BF16),
         ],
         input_output_aliases={6: 2},

time: 248 us -> 246 us (level)
  transfers between devices with their start and end apart: 51 -> 51, of which waited for: 24 -> 23; matrix products, arithmetic and copies ran while one was open for 9% -> 8% of each run, Pallas kernels for 21% -> 22%
where the time goes in v6:
time: 246 us; the launch traced here: 245 us
  starting transfers between devices  76.4 us (31%)
  waiting for transfers between devices  74.6 us (30%)
  Pallas kernels  63.1 us (26%)
  other arithmetic  15.7 us (6%)
  local copies, waits for them, and re-layouts  13.6 us (6%)
    ppermute x20, waiting for transfers between devices, line_step(): lax.ppermute(value, 'head', pairs)  54.8 us
    ppermute x20, starting transfers between devices, line_step(): lax.ppermute(value, 'head', pairs)  54.2 us
    pallas_call x6, Pallas kernels, on_values(): call(*[in_hbm([value])[0] if kind == 'h' else value for kind, value in zi...  24.4 us
    ppermute x22, starting transfers between devices, chip_swap(): lax.ppermute(value, 'seq', [(j, j ^ 2 * delta) for j in range(count)])  21.2 us
    pallas_call x2, Pallas kernels, products(): pl.pallas_call(functools.partial(products_kernel, len(candidates), late,...  20.8 us
    ppermute x22, waiting for transfers between devices, chip_swap(): lax.ppermute(value, 'seq', [(j, j ^ 2 * delta) for j in range(count)])  18.1 us
    pallas_call x4, Pallas kernels, project_rows(): pl.pallas_call(functools.partial(project_kernel, len(pieces)), grid=(rows...  13 us
    convert_element_type x4, other arithmetic, line_sum(): value = (value.astype(F32) + got[1 - parity].astype(F32)).astype(BF16)  5.84 us
  transfers between devices with their start and end apart: 51, of which 23 were waited for; matrix products, arithmetic and copies ran while one was open for 8% of the time, Pallas kernels for 22%

profile of v6, /device:TPU:0, one launch (start us, length us, event | category | flops | bytes accessed | tf_op | source)
XLA Modules:
  0.0 244.8 jit_solution(12022491995093374877)
XLA Ops:
  0.6 2.0 shard_map.92
  3.3 2.6 %collective-permute-start.5 = (bf16[256,1024]{1,0:T(8,128)(2,1)S(1)}, bf16[256,1024]{1,0:T(8,128)(2,1)S(1)}, u32[]{:S(2)}, u32[]{:S(2)}) collective-permute-start(bf16[256,1024]{1,0:T(8,128)(2,1)S(1)} %slice.96.refs_0_.refs_8_), channel_id=1, source_target_pairs={{0,16},{4,20},{8,24},{12,28},{16,0},{20,4},{24,8},{28,12},{1,17},{... | collective-permute-start | bytes 1572872 | tf_op jit(solution)/shard_map/ppermute | solution.py:321
  5.9 1.5 collective-permute-start.4
  8.4 1.2 collective-permute-start.2
  9.5 1.5 collective-permute-start.1
  11.1 6.2 %shard_map.93 = (bf16[512,1024]{1,0:T(8,128)(2,1)}, f32[512,1024]{1,0:T(8,128)}) custom-call(bf16[512,1024]{1,0:T(8,128)(2,1)} %q_ref, bf16[512,1024]{1,0:T(8,128)(2,1)} %k_ref.5, bf16[512,1024]{1,0:T(8,128)(2,1)} %v_ref.5, f32[512,1]{1,0:T(8,128)S(1)} %multiply_rsqrt_fusion.scale_ref), custom_call_target="tpu_custom_call" | custom-call | flops 1073741824 | bytes 6291456 | tf_op jit(solution)/shard_map/pallas_call | solution.py:129
  17.3 1.4 collective-permute-done.5.refs_2_.refs_10_
  18.7 2.0 collective-permute-done.4.refs_1_.refs_9_
  20.7 2.3 collective-permute-done.3
  24.1 1.5 collective-permute-done.1
  25.8 1.6 collective-permute-start.8
  28.0 3.3 %shard_map.94.a_ref.refs_6_.refs_5_.own_ref = bf16[512,1024]{1,0:T(8,128)(2,1)} custom-call(bf16[512,1024]{1,0:T(8,128)(2,1)} %get-tuple-element.79.scaled_ref.a_ref, f32[512,1024]{1,0:T(8,128)} %get-tuple-element.80.intra_ref, f32[8,128,128]{2,1,0:T(8,128)S(1)} %select_add_fusion.1.state_ref), custom_call_target="tpu_custom_call" | custom-call | flops 268435456 | bytes 4194304 | tf_op jit(solution)/shard_map/pallas_call | solution.py:129
  31.3 3.3 %collective-permute-done.8 = bf16[128,1024]{1,0:T(8,128)(2,1)S(1)} collective-permute-done((bf16[128,1024]{1,0:T(8,128)(2,1)S(1)}, bf16[128,1024]{1,0:T(8,128)(2,1)S(1)}, u32[]{:S(2)}, u32[]{:S(2)}) %collective-permute-start.8) | collective-permute-done | bytes 262176 | tf_op jit(solution)/shard_map/ppermute | solution.py:321
  34.6 1.2 collective-permute-done.7
  36.6 3.2 %shard_map.97.refs_4_ = bf16[4,1024,256]{2,1,0:T(8,128)(2,1)S(1)} custom-call(bf16[512,1024]{1,0:T(8,128)(2,1)} %shard_map.94.a_ref.refs_6_.refs_5_.own_ref, bf16[256,1024]{1,0:T(8,128)(2,1)} %copy-done.10, bf16[256,1024]{1,0:T(8,128)(2,1)} %copy-done.12, bf16[256,1024]{1,0:T(8,128)(2,1)} %copy-done.11, bf16[256,1024]{1,0:T(8,128)(2,1)} %pad_maximum_fusion.2.refs_3_.refs_11_), custom_call_target="tpu_custom_call" | custom-call | flops 1073741824 | bytes 2097152 | tf_op jit(solution)/shard_map/pallas_call | solution.py:147
  39.9 3.5 %shard_map.98 = bf16[4,1024,256]{2,1,0:T(8,128)(2,1)S(1)} custom-call(bf16[512,1024]{1,0:T(8,128)(2,1)S(1)} %collective-permute-done.9.a_ref.refs_7_.refs_6_.other_ref, bf16[256,1024]{1,0:T(8,128)(2,1)} %copy-done.10, bf16[256,1024]{1,0:T(8,128)(2,1)} %copy-done.12, bf16[256,1024]{1,0:T(8,128)(2,1)} %copy-done.11, ...), custom_call_target="tpu_custom_call", output_to_operand_aliasing={{}: (5, {})} | custom-call | flops 1073741824 | bytes 2097152 | tf_op jit(solution)/shard_map/pallas_call | solution.py:147
  44.4 4.3 %collective-permute-start.14 = (bf16[1024,256]{1,0:T(8,128)(2,1)}, bf16[1024,256]{1,0:T(8,128)(2,1)}, u32[]{:S(2)}, u32[]{:S(2)}) collective-permute-start(bf16[1024,256]{1,0:T(8,128)(2,1)} %get-tuple-element.165), channel_id=1, source_target_pairs={{0,1},{3,2},{4,5},{7,6},{8,9},{11,10},{12,13},{15,14},{16,17},{19,... | collective-permute-start | bytes 1572872 | tf_op jit(solution)/shard_map/ppermute | solution.py:332
  48.7 2.1 collective-permute-start.17
  50.8 9.6 %collective-permute-done.14 = bf16[1024,256]{1,0:T(8,128)(2,1)} collective-permute-done((bf16[1024,256]{1,0:T(8,128)(2,1)}, bf16[1024,256]{1,0:T(8,128)(2,1)}, u32[]{:S(2)}, u32[]{:S(2)}) %collective-permute-start.14) | collective-permute-done | bytes 524320 | tf_op jit(solution)/shard_map/ppermute | solution.py:332
  60.4 2.0 fusion.6
  62.4 1.5 collective-permute-start.15
  63.9 1.9 slice.99.refs_0_.refs_7_
  66.8 1.9 constant_dynamic-slice_fusion.1
  68.7 2.6 %collective-permute-done.17 = bf16[1024,256]{1,0:T(8,128)(2,1)} collective-permute-done((bf16[1024,256]{1,0:T(8,128)(2,1)}, bf16[1024,256]{1,0:T(8,128)(2,1)}, u32[]{:S(2)}, u32[]{:S(2)}) %collective-permute-start.17) | collective-permute-done | bytes 524320 | tf_op jit(solution)/shard_map/ppermute | solution.py:332
  71.3 2.5 %fusion.7 = (bf16[1024,256]{1,0:T(8,128)(2,1)}, bf16[1024,256]{1,0:T(8,128)(2,1)}) fusion(bf16[1024,256]{1,0:T(8,128)(2,1)} %collective-permute-done.15, bf16[4,1024,256]{2,1,0:T(8,128)(2,1)S(1)} %shard_map.98, s32[]{:T(128)S(6)} %select_n.220, bf16[1024,256]{1,0:T(8,128)(2,1)} %collective-permute-done.17, s32[]{:T(128)S(6)} %select_n.226), kind=kLoop, calls=%fused_computation.17 | loop fusion | flops 2097152 | bytes 3145736 | tf_op jit(solution)/shard_map/convert_element_type | solution.py:352
  73.7 9.0 %collective-permute-start.16 = (bf16[1024,256]{1,0:T(8,128)(2,1)}, bf16[1024,256]{1,0:T(8,128)(2,1)}, u32[]{:S(2)}, u32[]{:S(2)}) collective-permute-start(bf16[1024,256]{1,0:T(8,128)(2,1)} %get-tuple-element.163), channel_id=1, source_target_pairs={{0,1},{2,3},{1,0},{3,2},{4,5},{6,7},{5,4},{7,6},{8,9},{10,11},{9,8... | collective-permute-start | bytes 1572872 | tf_op jit(solution)/shard_map/ppermute | solution.py:332
  82.7 1.5 collective-permute-start.18
  85.7 1.8 constant_dynamic-slice_fusion.2
  89.1 1.8 fusion.20
  91.6 1.9 collective-permute-done.16
  93.5 1.5 subtract_convert_fusion.1
  95.8 6.5 %collective-permute-start.23 = (bf16[1024,256]{1,0:T(8,128)(2,1)S(1)}, bf16[1024,256]{1,0:T(8,128)(2,1)S(1)}, u32[]{:S(2)}, u32[]{:S(2)}) collective-permute-start(bf16[1024,256]{1,0:T(8,128)(2,1)S(1)} %get-tuple-element.145.refs_0_), channel_id=1, source_target_pairs={{0,1},{2,3},{1,0},{3,2},{4,5},{6,7},{5,4},{7,6},{8,9},{10,11},{9,8... | collective-permute-start | bytes 1572872 | tf_op jit(solution)/shard_map/ppermute | solution.py:332
  103.2 3.2 %shard_map.95.refs_4_ = bf16[4,1024,256]{2,1,0:T(8,128)(2,1)S(1)} custom-call(bf16[512,1024]{1,0:T(8,128)(2,1)} %shard_map.94.a_ref.refs_6_.refs_5_.own_ref, bf16[256,1024]{1,0:T(8,128)(2,1)} %slice.99.refs_0_.refs_7_, bf16[256,1024]{1,0:T(8,128)(2,1)} %collective-permute-done.10.refs_1_.refs_8_, bf16[256,1024]{1,0:T(8,128)(2,1)} %collective-permute-done.11.refs_2_.refs_9_, ...), custom_call_target="tpu_custom_call" | custom-call | flops 1073741824 | bytes 2097152 | tf_op jit(solution)/shard_map/pallas_call | solution.py:147
  106.5 3.1 %shard_map.96 = bf16[4,1024,256]{2,1,0:T(8,128)(2,1)S(1)} custom-call(bf16[512,1024]{1,0:T(8,128)(2,1)S(1)} %collective-permute-done.9.a_ref.refs_7_.refs_6_.other_ref, bf16[256,1024]{1,0:T(8,128)(2,1)} %slice.99.refs_0_.refs_7_, bf16[256,1024]{1,0:T(8,128)(2,1)} %collective-permute-done.10.refs_1_.refs_8_, ...), custom_call_target="tpu_custom_call", output_to_operand_aliasing={{}: (5, {})} | custom-call | flops 1073741824 | bytes 2097152 | tf_op jit(solution)/shard_map/pallas_call | solution.py:147
  109.6 1.9 collective-permute-done.23.refs_1_
  111.6 1.3 collective-permute-start.25
  113.6 6.3 %collective-permute-start.22 = (bf16[1024,256]{1,0:T(8,128)(2,1)S(1)}, bf16[1024,256]{1,0:T(8,128)(2,1)S(1)}, u32[]{:S(2)}, u32[]{:S(2)}) collective-permute-start(bf16[1024,256]{1,0:T(8,128)(2,1)S(1)} %get-tuple-element.161), channel_id=1, source_target_pairs={{0,1},{3,2},{4,5},{7,6},{8,9},{11,10},{12,13},{15,14},{16,17},{19,... | collective-permute-start | bytes 1572872 | tf_op jit(solution)/shard_map/ppermute | solution.py:332
  119.9 1.5 collective-permute-start.21
  121.4 4.5 %collective-permute-done.25.refs_3_ = bf16[1024,256]{1,0:T(8,128)(2,1)S(1)} collective-permute-done((bf16[1024,256]{1,0:T(8,128)(2,1)S(1)}, bf16[1024,256]{1,0:T(8,128)(2,1)S(1)}, u32[]{:S(2)}, u32[]{:S(2)}) %collective-permute-start.25) | collective-permute-done | bytes 524320 | tf_op jit(solution)/shard_map/ppermute | solution.py:332
  125.9 1.3 collective-permute-start.28
  127.2 5.1 %collective-permute-done.22 = bf16[1024,256]{1,0:T(8,128)(2,1)S(1)} collective-permute-done((bf16[1024,256]{1,0:T(8,128)(2,1)S(1)}, bf16[1024,256]{1,0:T(8,128)(2,1)S(1)}, u32[]{:S(2)}, u32[]{:S(2)}) %collective-permute-start.22) | collective-permute-done | bytes 524320 | tf_op jit(solution)/shard_map/ppermute | solution.py:332
  133.1 7.4 %collective-permute-done.21 = bf16[1024,256]{1,0:T(8,128)(2,1)S(1)} collective-permute-done((bf16[1024,256]{1,0:T(8,128)(2,1)S(1)}, bf16[1024,256]{1,0:T(8,128)(2,1)S(1)}, u32[]{:S(2)}, u32[]{:S(2)}) %collective-permute-start.21) | collective-permute-done | bytes 524320 | tf_op jit(solution)/shard_map/ppermute | solution.py:332
  141.3 1.3 fusion.2
  142.6 4.6 %collective-permute-start.29 = (bf16[1024,256]{1,0:T(8,128)(2,1)}, bf16[1024,256]{1,0:T(8,128)(2,1)}, u32[]{:S(2)}, u32[]{:S(2)}) collective-permute-start(bf16[1024,256]{1,0:T(8,128)(2,1)} %get-tuple-element.159), channel_id=1, source_target_pairs={{0,1},{2,3},{1,0},{3,2},{4,5},{6,7},{5,4},{7,6},{8,9},{10,11},{9,8... | collective-permute-start | bytes 1572872 | tf_op jit(solution)/shard_map/ppermute | solution.py:332
  147.2 1.5 collective-permute-start.30
  148.8 5.9 %collective-permute-done.29 = bf16[1024,256]{1,0:T(8,128)(2,1)} collective-permute-done((bf16[1024,256]{1,0:T(8,128)(2,1)}, bf16[1024,256]{1,0:T(8,128)(2,1)}, u32[]{:S(2)}, u32[]{:S(2)}) %collective-permute-start.29) | collective-permute-done | bytes 524320 | tf_op jit(solution)/shard_map/ppermute | solution.py:332
  154.7 1.5 subtract_convert_fusion
  156.9 6.8 %collective-permute-start.31 = (bf16[1024,256]{1,0:T(8,128)(2,1)S(1)}, bf16[1024,256]{1,0:T(8,128)(2,1)S(1)}, u32[]{:S(2)}, u32[]{:S(2)}) collective-permute-start(bf16[1024,256]{1,0:T(8,128)(2,1)S(1)} %get-tuple-element.143.refs_0_), channel_id=1, source_target_pairs={{0,1},{2,3},{1,0},{3,2},{4,5},{6,7},{5,4},{7,6},{8,9},{10,11},{9,8... | collective-permute-start | bytes 1572872 | tf_op jit(solution)/shard_map/ppermute | solution.py:332
  163.8 10.6 %shard_map.99 = (f32[512,1024]{1,0:T(8,128)}, f32[512,1024]{1,0:T(8,128)}, bf16[4,256,1024]{2,1,0:T(8,128)(2,1)}) custom-call(s32[12]{0:T(128)S(1)} %stack.93.meta_ref, bf16[1024,256]{1,0:T(8,128)(2,1)} %copy-done.22, bf16[1024,256]{1,0:T(8,128)(2,1)} %copy-done.29, bf16[1024,256]{1,0:T(8,128)(2,1)} %copy-done.28, bf16[1024,256]{1,0:T(8,128)(2,1)} %copy-done.30, ...), custom_call_target="tpu_custom_call" | custom-call | flops 4294967296 | bytes 8388608 | tf_op jit(solution)/shard_map/pallas_call | solution.py:227
  175.6 1.3 collective-permute-start.33
  179.0 12.7 %collective-permute-done.33.refs_3_ = bf16[1024,256]{1,0:T(8,128)(2,1)S(1)} collective-permute-done((bf16[1024,256]{1,0:T(8,128)(2,1)S(1)}, bf16[1024,256]{1,0:T(8,128)(2,1)S(1)}, u32[]{:S(2)}, u32[]{:S(2)}) %collective-permute-start.33) | collective-permute-done | bytes 524320 | tf_op jit(solution)/shard_map/ppermute | solution.py:332
  191.8 1.3 collective-permute-start.36
  194.9 10.2 %shard_map.100 = (f32[512,1024]{1,0:T(8,128)S(1)}, f32[512,1024]{1,0:T(8,128)S(1)}, bf16[4,256,1024]{2,1,0:T(8,128)(2,1)S(1)}) custom-call(s32[12]{0:T(128)S(1)} %stack.93.meta_ref, bf16[1024,256]{1,0:T(8,128)(2,1)} %copy-done.23, bf16[1024,256]{1,0:T(8,128)(2,1)} %copy-done.34, bf16[1024,256]{1,0:T(8,128)(2,1)} %copy-done.33, bf16[1024,256]{1,0:T(8,128)(2,1)} %copy-done.36, ...), custom_call_target="tpu_custom_call" | custom-call | flops 4294967296 | bytes 8388608 | tf_op jit(solution)/shard_map/pallas_call | solution.py:227
  205.1 3.1 %collective-permute-done.36.piece_ref = bf16[1024,256]{1,0:T(8,128)(2,1)S(1)} collective-permute-done((bf16[1024,256]{1,0:T(8,128)(2,1)S(1)}, bf16[1024,256]{1,0:T(8,128)(2,1)S(1)}, u32[]{:S(2)}, u32[]{:S(2)}) %collective-permute-start.36) | collective-permute-done | bytes 524320 | tf_op jit(solution)/shard_map/ppermute | solution.py:332
  208.2 5.0 %shard_map.101 = (f32[512,1024]{1,0:T(8,128)}, bf16[512,1024]{1,0:T(8,128)(2,1)}, bf16[4,256,1024]{2,1,0:T(8,128)(2,1)S(1)}) custom-call(s32[2]{0:T(128)S(1)} %pad_add_fusion.meta_ref, bf16[1024,256]{1,0:T(8,128)(2,1)S(1)} %collective-permute-done.36.piece_ref, bf16[512,1024]{1,0:T(8,128)(2,1)S(1)} %copy-done, ...), custom_call_target="tpu_custom_call", output_to_operand_aliasing={{2}: (6, {})} | custom-call | flops 1073741824 | bytes 8388608 | tf_op jit(solution)/shard_map/pallas_call | solution.py:290
  214.4 1.6 collective-permute-done.41
  218.6 1.5 bitcast_add_fusion.3
  221.0 1.2 collective-permute-start.44
  222.2 1.5 collective-permute-start.43
  223.7 8.7 %shard_map.103 = (bf16[512,1024]{1,0:T(8,128)(2,1)}, f32[512,1024]{1,0:T(8,128)S(1)}, f32[512,1024]{1,0:T(8,128)S(1)}) custom-call(bf16[512,1024]{1,0:T(8,128)(2,1)S(1)} %copy-done.7, bf16[512,1024]{1,0:T(8,128)(2,1)S(1)} %copy-done.5, bf16[512,1024]{1,0:T(8,128)(2,1)S(1)} %copy-done.6, bf16[512,1024]{1,0:T(8,128)(2,1)S(1)} %add_convert_fusion.b_ref.g_ref, ...), custom_call_target="tpu_custom_call" | custom-call | flops 2684354560 | bytes 9437184 | tf_op jit(solution)/shard_map/pallas_call | solution.py:129
  234.5 1.5 collective-permute-start.48
  236.1 3.4 %shard_map.104 = (bf16[512,1024]{1,0:T(8,128)(2,1)}, bf16[512,1024]{1,0:T(8,128)(2,1)}) custom-call(bf16[512,1024]{1,0:T(8,128)(2,1)S(1)} %copy-done.5, bf16[512,1024]{1,0:T(8,128)(2,1)S(1)} %copy-done.6, f32[512,1024]{1,0:T(8,128)S(1)} %get-tuple-element.130.dk_part_ref, f32[512,1024]{1,0:T(8,128)S(1)} %get-tuple-element.131.dv_part_ref, ...), custom_call_target="tpu_custom_call" | custom-call | flops 536870912 | bytes 7340032 | tf_op jit(solution)/shard_map/pallas_call | solution.py:129
  239.5 3.2 %collective-permute-done.49 = bf16[128,1024]{1,0:T(8,128)(2,1)S(1)} collective-permute-done((bf16[128,1024]{1,0:T(8,128)(2,1)S(1)}, bf16[128,1024]{1,0:T(8,128)(2,1)S(1)}, u32[]{:S(2)}, u32[]{:S(2)}) %collective-permute-start.49) | collective-permute-done | bytes 262176 | tf_op jit(solution)/shard_map/ppermute | solution.py:321
  243.2 1.6 pad_maximum_fusion
  (173 shorter events, 27.9 us)
Async XLA Ops:
  2.7 4.7 %collective-permute-start = (bf16[8,128,128]{2,1,0:T(8,128)(2,1)S(1)}, bf16[8,128,128]{2,1,0:T(8,128)(2,1)S(1)}, u32[]{:S(2)}, u32[]{:S(2)}) collective-permute-start(bf16[8,128,128]{2,1,0:T(8,128)(2,1)S(1)} %convert_element_type.304), channel_id=1, source_target_pairs={{0,4},{4,0},{8,12},{12,8},{16,20},{20,16},{24,28},{28,24},{1,5},{5... | collective-permute-start | bytes 786440 | tf_op jit(solution)/shard_map/ppermute | solution.py:316
  3.3 14.0 %copy-start.10 = (bf16[256,1024]{1,0:T(8,128)(2,1)}, bf16[256,1024]{1,0:T(8,128)(2,1)S(1)}, u32[]{:S(2)}) copy-start(bf16[256,1024]{1,0:T(8,128)(2,1)S(1)} %slice.96.refs_0_.refs_8_) | copy-start | bytes 1572868
  3.3 15.4 %collective-permute-start.5 = (bf16[256,1024]{1,0:T(8,128)(2,1)S(1)}, bf16[256,1024]{1,0:T(8,128)(2,1)S(1)}, u32[]{:S(2)}, u32[]{:S(2)}) collective-permute-start(bf16[256,1024]{1,0:T(8,128)(2,1)S(1)} %slice.96.refs_0_.refs_8_), channel_id=1, source_target_pairs={{0,16},{4,20},{8,24},{12,28},{16,0},{20,4},{24,8},{28,12},{1,17},{... | collective-permute-start | bytes 1572872 | tf_op jit(solution)/shard_map/ppermute | solution.py:321
  5.9 14.8 %collective-permute-start.4 = (bf16[256,1024]{1,0:T(8,128)(2,1)S(1)}, bf16[256,1024]{1,0:T(8,128)(2,1)S(1)}, u32[]{:S(2)}, u32[]{:S(2)}) collective-permute-start(bf16[256,1024]{1,0:T(8,128)(2,1)S(1)} %slice.96.refs_0_.refs_8_), channel_id=1, source_target_pairs={{0,8},{4,12},{8,0},{12,4},{16,24},{20,28},{24,16},{28,20},{1,9},{5... | collective-permute-start | bytes 1572872 | tf_op jit(solution)/shard_map/ppermute | solution.py:321
  7.5 15.5 %collective-permute-start.3 = (bf16[4,128,128]{2,1,0:T(8,128)(2,1)S(1)}, bf16[4,128,128]{2,1,0:T(8,128)(2,1)S(1)}, u32[]{:S(2)}, u32[]{:S(2)}) collective-permute-start(bf16[4,128,128]{2,1,0:T(8,128)(2,1)S(1)} %fusion.15), channel_id=1, source_target_pairs={{0,24},{4,28},{8,16},{12,20},{16,8},{20,12},{24,0},{28,4},{1,25},{... | collective-permute-start | bytes 393224 | tf_op jit(solution)/shard_map/ppermute | solution.py:321
  8.4 15.7 %collective-permute-start.2 = (bf16[4,128,128]{2,1,0:T(8,128)(2,1)S(1)}, bf16[4,128,128]{2,1,0:T(8,128)(2,1)S(1)}, u32[]{:S(2)}, u32[]{:S(2)}) collective-permute-start(bf16[4,128,128]{2,1,0:T(8,128)(2,1)S(1)} %fusion.15), channel_id=1, source_target_pairs={{0,16},{4,20},{8,24},{12,28},{16,0},{20,4},{24,8},{28,12},{1,17},{... | collective-permute-start | bytes 393224 | tf_op jit(solution)/shard_map/ppermute | solution.py:321
  9.5 16.0 %collective-permute-start.1 = (bf16[4,128,128]{2,1,0:T(8,128)(2,1)S(1)}, bf16[4,128,128]{2,1,0:T(8,128)(2,1)S(1)}, u32[]{:S(2)}, u32[]{:S(2)}) collective-permute-start(bf16[4,128,128]{2,1,0:T(8,128)(2,1)S(1)} %fusion.15), channel_id=1, source_target_pairs={{0,8},{4,12},{8,0},{12,4},{16,24},{20,28},{24,16},{28,20},{1,9},{5... | collective-permute-start | bytes 393224 | tf_op jit(solution)/shard_map/ppermute | solution.py:321
  25.7 2.2 collective-permute-start.6
  25.8 8.8 %collective-permute-start.8 = (bf16[128,1024]{1,0:T(8,128)(2,1)S(1)}, bf16[128,1024]{1,0:T(8,128)(2,1)S(1)}, u32[]{:S(2)}, u32[]{:S(2)}) collective-permute-start(bf16[128,1024]{1,0:T(8,128)(2,1)S(1)} %slice.98), channel_id=1, source_target_pairs={{0,8},{4,12},{8,0},{12,4},{16,24},{20,28},{24,16},{28,20},{1,9},{5... | collective-permute-start | bytes 786440 | tf_op jit(solution)/shard_map/ppermute | solution.py:321
  27.4 8.4 %collective-permute-start.7 = (bf16[128,1024]{1,0:T(8,128)(2,1)S(1)}, bf16[128,1024]{1,0:T(8,128)(2,1)S(1)}, u32[]{:S(2)}, u32[]{:S(2)}) collective-permute-start(bf16[128,1024]{1,0:T(8,128)(2,1)S(1)} %slice.97), channel_id=1, source_target_pairs={{0,16},{4,20},{8,24},{12,28},{16,0},{20,4},{24,8},{28,12},{1,17},{... | collective-permute-start | bytes 786440 | tf_op jit(solution)/shard_map/ppermute | solution.py:321
  36.6 3.3 %collective-permute-start.9 = (bf16[512,1024]{1,0:T(8,128)(2,1)}, bf16[512,1024]{1,0:T(8,128)(2,1)S(1)}, u32[]{:S(2)}, u32[]{:S(2)}) collective-permute-start(bf16[512,1024]{1,0:T(8,128)(2,1)} %shard_map.94.a_ref.refs_6_.refs_5_.own_ref), channel_id=1, source_target_pairs={{0,4},{4,0},{8,12},{12,8},{16,20},{20,16},{24,28},{28,24},{1,5},{5... | collective-permute-start | bytes 3145736 | tf_op jit(solution)/shard_map/ppermute | solution.py:316
  39.9 66.6 %copy-start.1 = (bf16[512,1024]{1,0:T(8,128)(2,1)}, bf16[512,1024]{1,0:T(8,128)(2,1)S(1)}, u32[]{:S(2)}) copy-start(bf16[512,1024]{1,0:T(8,128)(2,1)S(1)} %collective-permute-done.9.a_ref.refs_7_.refs_6_.other_ref) | copy-start | bytes 3145732
  44.4 16.0 %collective-permute-start.14 = (bf16[1024,256]{1,0:T(8,128)(2,1)}, bf16[1024,256]{1,0:T(8,128)(2,1)}, u32[]{:S(2)}, u32[]{:S(2)}) collective-permute-start(bf16[1024,256]{1,0:T(8,128)(2,1)} %get-tuple-element.165), channel_id=1, source_target_pairs={{0,1},{3,2},{4,5},{7,6},{8,9},{11,10},{12,13},{15,14},{16,17},{19,... | collective-permute-start | bytes 1572872 | tf_op jit(solution)/shard_map/ppermute | solution.py:332
  48.7 22.6 %collective-permute-start.17 = (bf16[1024,256]{1,0:T(8,128)(2,1)}, bf16[1024,256]{1,0:T(8,128)(2,1)}, u32[]{:S(2)}, u32[]{:S(2)}) collective-permute-start(bf16[1024,256]{1,0:T(8,128)(2,1)} %get-tuple-element.166), channel_id=1, source_target_pairs={{0,1},{3,2},{4,5},{7,6},{8,9},{11,10},{12,13},{15,14},{16,17},{19,... | collective-permute-start | bytes 1572872 | tf_op jit(solution)/shard_map/ppermute | solution.py:332
  62.4 8.9 %collective-permute-start.15 = (bf16[1024,256]{1,0:T(8,128)(2,1)}, bf16[1024,256]{1,0:T(8,128)(2,1)}, u32[]{:S(2)}, u32[]{:S(2)}) collective-permute-start(bf16[1024,256]{1,0:T(8,128)(2,1)} %fusion.6), channel_id=1, source_target_pairs={{1,2},{2,1},{5,6},{6,5},{9,10},{10,9},{13,14},{14,13},{17,18},{18,... | collective-permute-start | bytes 1572872 | tf_op jit(solution)/shard_map/ppermute | solution.py:332
  65.8 18.4 %collective-permute-start.10 = (bf16[256,1024]{1,0:T(8,128)(2,1)}, bf16[256,1024]{1,0:T(8,128)(2,1)}, u32[]{:S(2)}, u32[]{:S(2)}) collective-permute-start(bf16[256,1024]{1,0:T(8,128)(2,1)} %slice.99.refs_0_.refs_7_), channel_id=1, source_target_pairs={{0,8},{4,12},{8,0},{12,4},{16,24},{20,28},{24,16},{28,20},{1,9},{5... | collective-permute-start | bytes 1572872 | tf_op jit(solution)/shard_map/ppermute | solution.py:321
  66.3 21.2 %collective-permute-start.11 = (bf16[256,1024]{1,0:T(8,128)(2,1)}, bf16[256,1024]{1,0:T(8,128)(2,1)}, u32[]{:S(2)}, u32[]{:S(2)}) collective-permute-start(bf16[256,1024]{1,0:T(8,128)(2,1)} %slice.99.refs_0_.refs_7_), channel_id=1, source_target_pairs={{0,16},{4,20},{8,24},{12,28},{16,0},{20,4},{24,8},{28,12},{1,17},{... | collective-permute-start | bytes 1572872 | tf_op jit(solution)/shard_map/ppermute | solution.py:321
  68.7 20.4 %collective-permute-start.19 = (bf16[512,512]{1,0:T(8,128)(2,1)}, bf16[512,512]{1,0:T(8,128)(2,1)}, u32[]{:S(2)}, u32[]{:S(2)}) collective-permute-start(bf16[512,512]{1,0:T(8,128)(2,1)} %constant_dynamic-slice_fusion.1), channel_id=1, source_target_pairs={{0,4},{4,0},{8,12},{12,8},{16,20},{20,16},{24,28},{28,24},{1,5},{5... | collective-permute-start | bytes 1572872 | tf_op jit(solution)/shard_map/ppermute | solution.py:316
  73.7 19.8 %collective-permute-start.16 = (bf16[1024,256]{1,0:T(8,128)(2,1)}, bf16[1024,256]{1,0:T(8,128)(2,1)}, u32[]{:S(2)}, u32[]{:S(2)}) collective-permute-start(bf16[1024,256]{1,0:T(8,128)(2,1)} %get-tuple-element.163), channel_id=1, source_target_pairs={{0,1},{2,3},{1,0},{3,2},{4,5},{6,7},{5,4},{7,6},{8,9},{10,11},{9,8... | collective-permute-start | bytes 1572872 | tf_op jit(solution)/shard_map/ppermute | solution.py:332
  82.7 10.8 %collective-permute-start.18 = (bf16[1024,256]{1,0:T(8,128)(2,1)}, bf16[1024,256]{1,0:T(8,128)(2,1)}, u32[]{:S(2)}, u32[]{:S(2)}) collective-permute-start(bf16[1024,256]{1,0:T(8,128)(2,1)} %get-tuple-element.164), channel_id=1, source_target_pairs={{1,2},{2,1},{5,6},{6,5},{9,10},{10,9},{13,14},{14,13},{17,18},{18,... | collective-permute-start | bytes 1572872 | tf_op jit(solution)/shard_map/ppermute | solution.py:332
  85.2 6.4 %collective-permute-start.12 = (bf16[128,1024]{1,0:T(8,128)(2,1)S(1)}, bf16[128,1024]{1,0:T(8,128)(2,1)S(1)}, u32[]{:S(2)}, u32[]{:S(2)}) collective-permute-start(bf16[128,1024]{1,0:T(8,128)(2,1)S(1)} %slice.128), channel_id=1, source_target_pairs={{0,16},{4,20},{8,24},{12,28},{16,0},{20,4},{24,8},{28,12},{1,17},{... | collective-permute-start | bytes 786440 | tf_op jit(solution)/shard_map/ppermute | solution.py:321
  88.5 13.9 %collective-permute-start.13 = (bf16[128,1024]{1,0:T(8,128)(2,1)S(1)}, bf16[128,1024]{1,0:T(8,128)(2,1)S(1)}, u32[]{:S(2)}, u32[]{:S(2)}) collective-permute-start(bf16[128,1024]{1,0:T(8,128)(2,1)S(1)} %slice.129), channel_id=1, source_target_pairs={{0,8},{4,12},{8,0},{12,4},{16,24},{20,28},{24,16},{28,20},{1,9},{5... | collective-permute-start | bytes 786440 | tf_op jit(solution)/shard_map/ppermute | solution.py:321
  95.1 14.6 %collective-permute-start.24 = (bf16[1024,256]{1,0:T(8,128)(2,1)S(1)}, bf16[1024,256]{1,0:T(8,128)(2,1)S(1)}, u32[]{:S(2)}, u32[]{:S(2)}) collective-permute-start(bf16[1024,256]{1,0:T(8,128)(2,1)S(1)} %get-tuple-element.145.refs_0_), channel_id=1, source_target_pairs={{1,2},{2,1},{5,6},{6,5},{9,10},{10,9},{13,14},{14,13},{17,18},{18,... | collective-permute-start | bytes 1572872 | tf_op jit(solution)/shard_map/ppermute | solution.py:332
  95.8 15.8 %collective-permute-start.23 = (bf16[1024,256]{1,0:T(8,128)(2,1)S(1)}, bf16[1024,256]{1,0:T(8,128)(2,1)S(1)}, u32[]{:S(2)}, u32[]{:S(2)}) collective-permute-start(bf16[1024,256]{1,0:T(8,128)(2,1)S(1)} %get-tuple-element.145.refs_0_), channel_id=1, source_target_pairs={{0,1},{2,3},{1,0},{3,2},{4,5},{6,7},{5,4},{7,6},{8,9},{10,11},{9,8... | collective-permute-start | bytes 1572872 | tf_op jit(solution)/shard_map/ppermute | solution.py:332
  102.3 7.3 %collective-permute-start.20 = (bf16[512,256]{1,0:T(8,128)(2,1)S(1)}, bf16[512,256]{1,0:T(8,128)(2,1)S(1)}, u32[]{:S(2)}, u32[]{:S(2)}) collective-permute-start(bf16[512,256]{1,0:T(8,128)(2,1)S(1)} %slice.132), channel_id=1, source_target_pairs={{0,4},{4,0},{8,12},{12,8},{16,20},{20,16},{24,28},{28,24},{1,5},{5... | collective-permute-start | bytes 786440 | tf_op jit(solution)/shard_map/ppermute | solution.py:316
  109.6 30.9 %copy-start.28 = (bf16[1024,256]{1,0:T(8,128)(2,1)}, bf16[1024,256]{1,0:T(8,128)(2,1)S(1)}, u32[]{:S(2)}) copy-start(bf16[1024,256]{1,0:T(8,128)(2,1)S(1)} %collective-permute-done.24.refs_2_) | copy-start | bytes 1572868
  111.6 31.0 %copy-start.29 = (bf16[1024,256]{1,0:T(8,128)(2,1)}, bf16[1024,256]{1,0:T(8,128)(2,1)S(1)}, u32[]{:S(2)}) copy-start(bf16[1024,256]{1,0:T(8,128)(2,1)S(1)} %collective-permute-done.23.refs_1_) | copy-start | bytes 1572868
  111.6 14.3 %collective-permute-start.25 = (bf16[1024,256]{1,0:T(8,128)(2,1)S(1)}, bf16[1024,256]{1,0:T(8,128)(2,1)S(1)}, u32[]{:S(2)}, u32[]{:S(2)}) collective-permute-start(bf16[1024,256]{1,0:T(8,128)(2,1)S(1)} %collective-permute-done.24.refs_2_), channel_id=1, source_target_pairs={{2,3},{1,0},{6,7},{5,4},{10,11},{9,8},{14,15},{13,12},{18,19},{17,... | collective-permute-start | bytes 1572872 | tf_op jit(solution)/shard_map/ppermute | solution.py:332
  112.8 13.0 %collective-permute-start.26 = (bf16[1024,256]{1,0:T(8,128)(2,1)S(1)}, bf16[1024,256]{1,0:T(8,128)(2,1)S(1)}, u32[]{:S(2)}, u32[]{:S(2)}) collective-permute-start(bf16[1024,256]{1,0:T(8,128)(2,1)S(1)} %collective-permute-done.23.refs_1_), channel_id=1, source_target_pairs={{1,2},{2,1},{5,6},{6,5},{9,10},{10,9},{13,14},{14,13},{17,18},{18,... | collective-permute-start | bytes 1572872 | tf_op jit(solution)/shard_map/ppermute | solution.py:332
  113.6 18.6 %collective-permute-start.22 = (bf16[1024,256]{1,0:T(8,128)(2,1)S(1)}, bf16[1024,256]{1,0:T(8,128)(2,1)S(1)}, u32[]{:S(2)}, u32[]{:S(2)}) collective-permute-start(bf16[1024,256]{1,0:T(8,128)(2,1)S(1)} %get-tuple-element.161), channel_id=1, source_target_pairs={{0,1},{3,2},{4,5},{7,6},{8,9},{11,10},{12,13},{15,14},{16,17},{19,... | collective-permute-start | bytes 1572872 | tf_op jit(solution)/shard_map/ppermute | solution.py:332
  119.9 34.8 %copy-start.16 = (bf16[512,256]{1,0:T(8,128)(2,1)S(1)}, bf16[512,256]{1,0:T(8,128)(2,1)}, u32[]{:S(2)}) copy-start(bf16[512,256]{1,0:T(8,128)(2,1)} %get-tuple-element.168) | copy-start | bytes 786436
  119.9 34.8 %copy-start.17 = (bf16[512,256]{1,0:T(8,128)(2,1)S(1)}, bf16[512,256]{1,0:T(8,128)(2,1)}, u32[]{:S(2)}) copy-start(bf16[512,256]{1,0:T(8,128)(2,1)} %get-tuple-element.174) | copy-start | bytes 786436
  119.9 20.5 %collective-permute-start.21 = (bf16[1024,256]{1,0:T(8,128)(2,1)S(1)}, bf16[1024,256]{1,0:T(8,128)(2,1)S(1)}, u32[]{:S(2)}, u32[]{:S(2)}) collective-permute-start(bf16[1024,256]{1,0:T(8,128)(2,1)S(1)} %get-tuple-element.162), channel_id=1, source_target_pairs={{0,1},{3,2},{4,5},{7,6},{8,9},{11,10},{12,13},{15,14},{16,17},{19,... | collective-permute-start | bytes 1572872 | tf_op jit(solution)/shard_map/ppermute | solution.py:332
  125.9 16.7 %copy-start.31 = (bf16[1024,256]{1,0:T(8,128)(2,1)}, bf16[1024,256]{1,0:T(8,128)(2,1)S(1)}, u32[]{:S(2)}) copy-start(bf16[1024,256]{1,0:T(8,128)(2,1)S(1)} %collective-permute-done.26.refs_4_) | copy-start | bytes 1572868
  125.9 14.6 %collective-permute-start.28 = (bf16[1024,256]{1,0:T(8,128)(2,1)S(1)}, bf16[1024,256]{1,0:T(8,128)(2,1)S(1)}, u32[]{:S(2)}, u32[]{:S(2)}) collective-permute-start(bf16[1024,256]{1,0:T(8,128)(2,1)S(1)} %collective-permute-done.26.refs_4_), channel_id=1, source_target_pairs={{2,3},{1,0},{6,7},{5,4},{10,11},{9,8},{14,15},{13,12},{18,19},{17,... | collective-permute-start | bytes 1572872 | tf_op jit(solution)/shard_map/ppermute | solution.py:332
  132.4 8.9 %collective-permute-start.27 = (bf16[1024,256]{1,0:T(8,128)(2,1)S(1)}, bf16[1024,256]{1,0:T(8,128)(2,1)S(1)}, u32[]{:S(2)}, u32[]{:S(2)}) collective-permute-start(bf16[1024,256]{1,0:T(8,128)(2,1)S(1)} %fusion.1), channel_id=1, source_target_pairs={{1,2},{2,1},{5,6},{6,5},{9,10},{10,9},{13,14},{14,13},{17,18},{18,... | collective-permute-start | bytes 1572872 | tf_op jit(solution)/shard_map/ppermute | solution.py:332
  142.6 12.1 %collective-permute-start.29 = (bf16[1024,256]{1,0:T(8,128)(2,1)}, bf16[1024,256]{1,0:T(8,128)(2,1)}, u32[]{:S(2)}, u32[]{:S(2)}) collective-permute-start(bf16[1024,256]{1,0:T(8,128)(2,1)} %get-tuple-element.159), channel_id=1, source_target_pairs={{0,1},{2,3},{1,0},{3,2},{4,5},{6,7},{5,4},{7,6},{8,9},{10,11},{9,8... | collective-permute-start | bytes 1572872 | tf_op jit(solution)/shard_map/ppermute | solution.py:332
  147.2 7.5 %collective-permute-start.30 = (bf16[1024,256]{1,0:T(8,128)(2,1)}, bf16[1024,256]{1,0:T(8,128)(2,1)}, u32[]{:S(2)}, u32[]{:S(2)}) collective-permute-start(bf16[1024,256]{1,0:T(8,128)(2,1)} %get-tuple-element.160), channel_id=1, source_target_pairs={{1,2},{2,1},{5,6},{6,5},{9,10},{10,9},{13,14},{14,13},{17,18},{18,... | collective-permute-start | bytes 1572872 | tf_op jit(solution)/shard_map/ppermute | solution.py:332
  156.2 18.2 %copy-start.23 = (bf16[1024,256]{1,0:T(8,128)(2,1)}, bf16[1024,256]{1,0:T(8,128)(2,1)S(1)}, u32[]{:S(2)}) copy-start(bf16[1024,256]{1,0:T(8,128)(2,1)S(1)} %get-tuple-element.143.refs_0_) | copy-start | bytes 1572868
  156.2 19.4 %collective-permute-start.32 = (bf16[1024,256]{1,0:T(8,128)(2,1)S(1)}, bf16[1024,256]{1,0:T(8,128)(2,1)S(1)}, u32[]{:S(2)}, u32[]{:S(2)}) collective-permute-start(bf16[1024,256]{1,0:T(8,128)(2,1)S(1)} %get-tuple-element.143.refs_0_), channel_id=1, source_target_pairs={{1,2},{2,1},{5,6},{6,5},{9,10},{10,9},{13,14},{14,13},{17,18},{18,... | collective-permute-start | bytes 1572872 | tf_op jit(solution)/shard_map/ppermute | solution.py:332
  156.9 18.7 %collective-permute-start.31 = (bf16[1024,256]{1,0:T(8,128)(2,1)S(1)}, bf16[1024,256]{1,0:T(8,128)(2,1)S(1)}, u32[]{:S(2)}, u32[]{:S(2)}) collective-permute-start(bf16[1024,256]{1,0:T(8,128)(2,1)S(1)} %get-tuple-element.143.refs_0_), channel_id=1, source_target_pairs={{0,1},{2,3},{1,0},{3,2},{4,5},{6,7},{5,4},{7,6},{8,9},{10,11},{9,8... | collective-permute-start | bytes 1572872 | tf_op jit(solution)/shard_map/ppermute | solution.py:332
  163.7 10.7 %collective-permute-start.35 = (bf16[512,256]{1,0:T(8,128)(2,1)S(1)}, bf16[512,256]{1,0:T(8,128)(2,1)S(1)}, u32[]{:S(2)}, u32[]{:S(2)}) collective-permute-start(bf16[512,256]{1,0:T(8,128)(2,1)S(1)} %slice.135), channel_id=1, source_target_pairs={{0,4},{4,0},{8,12},{12,8},{16,20},{20,16},{24,28},{28,24},{1,5},{5... | collective-permute-start | bytes 786440 | tf_op jit(solution)/shard_map/ppermute | solution.py:316
  175.5 19.3 %copy-start.33 = (bf16[1024,256]{1,0:T(8,128)(2,1)}, bf16[1024,256]{1,0:T(8,128)(2,1)S(1)}, u32[]{:S(2)}) copy-start(bf16[1024,256]{1,0:T(8,128)(2,1)S(1)} %collective-permute-done.32.refs_2_) | copy-start | bytes 1572868
  175.5 19.3 %copy-start.34 = (bf16[1024,256]{1,0:T(8,128)(2,1)}, bf16[1024,256]{1,0:T(8,128)(2,1)S(1)}, u32[]{:S(2)}) copy-start(bf16[1024,256]{1,0:T(8,128)(2,1)S(1)} %collective-permute-done.31.refs_1_) | copy-start | bytes 1572868
  175.6 16.2 %collective-permute-start.33 = (bf16[1024,256]{1,0:T(8,128)(2,1)S(1)}, bf16[1024,256]{1,0:T(8,128)(2,1)S(1)}, u32[]{:S(2)}, u32[]{:S(2)}) collective-permute-start(bf16[1024,256]{1,0:T(8,128)(2,1)S(1)} %collective-permute-done.32.refs_2_), channel_id=1, source_target_pairs={{2,3},{1,0},{6,7},{5,4},{10,11},{9,8},{14,15},{13,12},{18,19},{17,... | collective-permute-start | bytes 1572872 | tf_op jit(solution)/shard_map/ppermute | solution.py:332
  176.9 14.9 %collective-permute-start.34 = (bf16[1024,256]{1,0:T(8,128)(2,1)S(1)}, bf16[1024,256]{1,0:T(8,128)(2,1)S(1)}, u32[]{:S(2)}, u32[]{:S(2)}) collective-permute-start(bf16[1024,256]{1,0:T(8,128)(2,1)S(1)} %collective-permute-done.31.refs_1_), channel_id=1, source_target_pairs={{1,2},{2,1},{5,6},{6,5},{9,10},{10,9},{13,14},{14,13},{17,18},{18,... | collective-permute-start | bytes 1572872 | tf_op jit(solution)/shard_map/ppermute | solution.py:332
  177.8 15.2 %collective-permute-start.39 = (bf16[2,128,1024]{2,1,0:T(8,128)(2,1)S(1)}, bf16[2,128,1024]{2,1,0:T(8,128)(2,1)S(1)}, u32[]{:S(2)}, u32[]{:S(2)}) collective-permute-start(bf16[2,128,1024]{2,1,0:T(8,128)(2,1)S(1)} %get-tuple-element.157), channel_id=1, source_target_pairs={{0,16},{4,20},{8,24},{12,28},{16,0},{20,4},{24,8},{28,12},{1,17},{... | collective-permute-start | bytes 1572872 | tf_op jit(solution)/shard_map/ppermute | solution.py:321
  178.4 14.7 %collective-permute-start.37 = (bf16[2,128,1024]{2,1,0:T(8,128)(2,1)S(1)}, bf16[2,128,1024]{2,1,0:T(8,128)(2,1)S(1)}, u32[]{:S(2)}, u32[]{:S(2)}) collective-permute-start(bf16[2,128,1024]{2,1,0:T(8,128)(2,1)S(1)} %get-tuple-element.158), channel_id=1, source_target_pairs={{0,8},{4,12},{8,0},{12,4},{16,24},{20,28},{24,16},{28,20},{1,9},{5... | collective-permute-start | bytes 1572872 | tf_op jit(solution)/shard_map/ppermute | solution.py:321
  191.8 16.4 %collective-permute-start.36 = (bf16[1024,256]{1,0:T(8,128)(2,1)S(1)}, bf16[1024,256]{1,0:T(8,128)(2,1)S(1)}, u32[]{:S(2)}, u32[]{:S(2)}) collective-permute-start(bf16[1024,256]{1,0:T(8,128)(2,1)S(1)} %collective-permute-done.34.refs_4_), channel_id=1, source_target_pairs={{2,3},{1,0},{6,7},{5,4},{10,11},{9,8},{14,15},{13,12},{18,19},{17,... | collective-permute-start | bytes 1572872 | tf_op jit(solution)/shard_map/ppermute | solution.py:332
  193.3 11.7 %collective-permute-start.40 = (bf16[128,1024]{1,0:T(8,128)(2,1)S(1)}, bf16[128,1024]{1,0:T(8,128)(2,1)S(1)}, u32[]{:S(2)}, u32[]{:S(2)}) collective-permute-start(bf16[128,1024]{1,0:T(8,128)(2,1)S(1)} %get-tuple-element.155), channel_id=1, source_target_pairs={{0,8},{4,12},{8,0},{12,4},{16,24},{20,28},{24,16},{28,20},{1,9},{5... | collective-permute-start | bytes 786440 | tf_op jit(solution)/shard_map/ppermute | solution.py:321
  194.1 14.1 %copy-start = (bf16[512,1024]{1,0:T(8,128)(2,1)S(1)}, bf16[512,1024]{1,0:T(8,128)(2,1)}, u32[]{:S(2)}) copy-start(bf16[512,1024]{1,0:T(8,128)(2,1)} %shard_map.94.a_ref.refs_6_.refs_5_.own_ref) | copy-start | bytes 3145732
  194.1 14.1 %copy-start.2 = (bf16[512,1024]{1,0:T(8,128)(2,1)S(1)}, bf16[512,1024]{1,0:T(8,128)(2,1)}, u32[]{:S(2)}) copy-start(bf16[512,1024]{1,0:T(8,128)(2,1)} %copy-done.1) | copy-start | bytes 3145732
  194.1 14.1 %copy-start.4 = (bf16[256,1024]{1,0:T(8,128)(2,1)S(1)}, bf16[256,1024]{1,0:T(8,128)(2,1)}, u32[]{:S(2)}) copy-start(bf16[256,1024]{1,0:T(8,128)(2,1)} %copy-done.3) | copy-start | bytes 1572868
  194.1 11.0 %collective-permute-start.38 = (bf16[128,1024]{1,0:T(8,128)(2,1)S(1)}, bf16[128,1024]{1,0:T(8,128)(2,1)S(1)}, u32[]{:S(2)}, u32[]{:S(2)}) collective-permute-start(bf16[128,1024]{1,0:T(8,128)(2,1)S(1)} %get-tuple-element.156), channel_id=1, source_target_pairs={{0,16},{4,20},{8,24},{12,28},{16,0},{20,4},{24,8},{28,12},{1,17},{... | collective-permute-start | bytes 786440 | tf_op jit(solution)/shard_map/ppermute | solution.py:321
  213.2 2.9 %collective-permute-start.41 = (bf16[512,1024]{1,0:T(8,128)(2,1)}, bf16[512,1024]{1,0:T(8,128)(2,1)S(1)}, u32[]{:S(2)}, u32[]{:S(2)}) collective-permute-start(bf16[512,1024]{1,0:T(8,128)(2,1)} %get-tuple-element.122), channel_id=1, source_target_pairs={{0,4},{4,0},{8,12},{12,8},{16,20},{20,16},{24,28},{28,24},{1,5},{5... | collective-permute-start | bytes 3145736 | tf_op jit(solution)/shard_map/ppermute | solution.py:316
  213.3 19.1 %collective-permute-start.47 = (bf16[2,128,1024]{2,1,0:T(8,128)(2,1)S(1)}, bf16[2,128,1024]{2,1,0:T(8,128)(2,1)S(1)}, u32[]{:S(2)}, u32[]{:S(2)}) collective-permute-start(bf16[2,128,1024]{2,1,0:T(8,128)(2,1)S(1)} %get-tuple-element.153), channel_id=1, source_target_pairs={{0,16},{4,20},{8,24},{12,28},{16,0},{20,4},{24,8},{28,12},{1,17},{... | collective-permute-start | bytes 1572872 | tf_op jit(solution)/shard_map/ppermute | solution.py:321
  213.9 18.5 %collective-permute-start.46 = (bf16[2,128,1024]{2,1,0:T(8,128)(2,1)S(1)}, bf16[2,128,1024]{2,1,0:T(8,128)(2,1)S(1)}, u32[]{:S(2)}, u32[]{:S(2)}) collective-permute-start(bf16[2,128,1024]{2,1,0:T(8,128)(2,1)S(1)} %get-tuple-element.154), channel_id=1, source_target_pairs={{0,8},{4,12},{8,0},{12,4},{16,24},{20,28},{24,16},{28,20},{1,9},{5... | collective-permute-start | bytes 1572872 | tf_op jit(solution)/shard_map/ppermute | solution.py:321
  218.2 1.8 collective-permute-start.42
  220.2 12.2 %collective-permute-start.45 = (bf16[4,128,128]{2,1,0:T(8,128)(2,1)S(1)}, bf16[4,128,128]{2,1,0:T(8,128)(2,1)S(1)}, u32[]{:S(2)}, u32[]{:S(2)}) collective-permute-start(bf16[4,128,128]{2,1,0:T(8,128)(2,1)S(1)} %fusion.14), channel_id=1, source_target_pairs={{0,24},{4,28},{8,16},{12,20},{16,8},{20,12},{24,0},{28,4},{1,25},{... | collective-permute-start | bytes 393224 | tf_op jit(solution)/shard_map/ppermute | solution.py:321
  221.0 12.2 %collective-permute-start.44 = (bf16[4,128,128]{2,1,0:T(8,128)(2,1)S(1)}, bf16[4,128,128]{2,1,0:T(8,128)(2,1)S(1)}, u32[]{:S(2)}, u32[]{:S(2)}) collective-permute-start(bf16[4,128,128]{2,1,0:T(8,128)(2,1)S(1)} %fusion.14), channel_id=1, source_target_pairs={{0,16},{4,20},{8,24},{12,28},{16,0},{20,4},{24,8},{28,12},{1,17},{... | collective-permute-start | bytes 393224 | tf_op jit(solution)/shard_map/ppermute | solution.py:321
  222.2 11.3 %collective-permute-start.43 = (bf16[4,128,128]{2,1,0:T(8,128)(2,1)S(1)}, bf16[4,128,128]{2,1,0:T(8,128)(2,1)S(1)}, u32[]{:S(2)}, u32[]{:S(2)}) collective-permute-start(bf16[4,128,128]{2,1,0:T(8,128)(2,1)S(1)} %fusion.14), channel_id=1, source_target_pairs={{0,8},{4,12},{8,0},{12,4},{16,24},{20,28},{24,16},{28,20},{1,9},{5... | collective-permute-start | bytes 393224 | tf_op jit(solution)/shard_map/ppermute | solution.py:321
  233.6 2.4 collective-permute-start.50
  233.9 8.8 %collective-permute-start.49 = (bf16[128,1024]{1,0:T(8,128)(2,1)S(1)}, bf16[128,1024]{1,0:T(8,128)(2,1)S(1)}, u32[]{:S(2)}, u32[]{:S(2)}) collective-permute-start(bf16[128,1024]{1,0:T(8,128)(2,1)S(1)} %get-tuple-element.151), channel_id=1, source_target_pairs={{0,8},{4,12},{8,0},{12,4},{16,24},{20,28},{24,16},{28,20},{1,9},{5... | collective-permute-start | bytes 786440 | tf_op jit(solution)/shard_map/ppermute | solution.py:321
  234.5 8.4 %collective-permute-start.48 = (bf16[128,1024]{1,0:T(8,128)(2,1)S(1)}, bf16[128,1024]{1,0:T(8,128)(2,1)S(1)}, u32[]{:S(2)}, u32[]{:S(2)}) collective-permute-start(bf16[128,1024]{1,0:T(8,128)(2,1)S(1)} %get-tuple-element.152), channel_id=1, source_target_pairs={{0,16},{4,20},{8,24},{12,28},{16,0},{20,4},{24,8},{28,12},{1,17},{... | collective-permute-start | bytes 786440 | tf_op jit(solution)/shard_map/ppermute | solution.py:321
  (24 other events, 96.8 us)

commit v7 on v6

--- a/solution.py
+++ b/solution.py
@@ -117,7 +117,7 @@
             (pltpu.HBM if kind == "h" else jax.ShapeDtypeStruct)(shapes[kind], dtype)
             for kind, dtype in outs
         ],
-        compiler_params=pltpu.CompilerParams(vmem_limit_bytes=VMEM_LIMIT // 2),
+        compiler_params=pltpu.CompilerParams(vmem_limit_bytes=VMEM_LIMIT),
         cost_estimate=pl.CostEstimate(
             flops=2 * macs * heads,
             bytes_accessed=rows * heads * DH * 2 * (len(ins) + len(outs)),
@@ -631,7 +631,7 @@
     sent, finish = second_step(sent)
     after = sum_of_others(half, arrived, other, False)
     grad_key, grad_value = call(
-        finish_kernel, ins="vvvvm", outs=[("h", BF16), ("h", BF16)], macs=4 * rows * DH * DH
+        finish_kernel, ins="vvvvm", outs=[("h", BF16), ("h", BF16)], macs=4 * rows * DH * DH, step=4
     )(key_rows, value_rows, key_part, value_part, after)
     sent, grad_key, grad_value = barrier((sent, grad_key, grad_value))
     grad_weight = jnp.concatenate([*grad_parts, finish(sent)], axis=0)

time: 246 us -> 246 us (level)
  transfers between devices with their start and end apart: 51 -> 51, of which waited for: 23 -> 23; matrix products, arithmetic and copies ran while one was open for 8% -> 8% of each run, Pallas kernels for 22% -> 21%
where the time goes in v7:
time: 246 us; the launch traced here: 245 us
  starting transfers between devices  76.4 us (31%)
  waiting for transfers between devices  75 us (30%)
  Pallas kernels  62.7 us (25%)
  other arithmetic  15.7 us (6%)
  local copies, waits for them, and re-layouts  13.6 us (6%)
    ppermute x20, waiting for transfers between devices, line_step(): lax.ppermute(value, 'head', pairs)  54.8 us
    ppermute x20, starting transfers between devices, line_step(): lax.ppermute(value, 'head', pairs)  54.2 us
    pallas_call x6, Pallas kernels, on_values(): call(*[in_hbm([value])[0] if kind == 'h' else value for kind, value in zi...  23.9 us
    ppermute x22, starting transfers between devices, chip_swap(): lax.ppermute(value, 'seq', [(j, j ^ 2 * delta) for j in range(count)])  21.2 us
    pallas_call x2, Pallas kernels, products(): pl.pallas_call(functools.partial(products_kernel, len(candidates), late,...  20.8 us
    ppermute x22, waiting for transfers between devices, chip_swap(): lax.ppermute(value, 'seq', [(j, j ^ 2 * delta) for j in range(count)])  18.6 us
    pallas_call x4, Pallas kernels, project_rows(): pl.pallas_call(functools.partial(project_kernel, len(pieces)), grid=(rows...  13 us
    convert_element_type x4, other arithmetic, line_sum(): value = (value.astype(F32) + got[1 - parity].astype(F32)).astype(BF16)  5.84 us
  transfers between devices with their start and end apart: 51, of which 23 were waited for; matrix products, arithmetic and copies ran while one was open for 8% of the time, Pallas kernels for 21%

profile of v7, /device:TPU:0, one launch (start us, length us, event | category | flops | bytes accessed | tf_op | source)
XLA Modules:
  0.0 244.8 jit_solution(3249613465524420519)
XLA Ops:
  0.6 2.0 shard_map.92
  3.3 2.6 %collective-permute-start.5 = (bf16[256,1024]{1,0:T(8,128)(2,1)S(1)}, bf16[256,1024]{1,0:T(8,128)(2,1)S(1)}, u32[]{:S(2)}, u32[]{:S(2)}) collective-permute-start(bf16[256,1024]{1,0:T(8,128)(2,1)S(1)} %slice.96.refs_0_.refs_8_), channel_id=1, source_target_pairs={{0,16},{4,20},{8,24},{12,28},{16,0},{20,4},{24,8},{28,12},{1,17},{... | collective-permute-start | bytes 1572872 | tf_op jit(solution)/shard_map/ppermute | solution.py:321
  5.9 1.5 collective-permute-start.4
  8.4 1.2 collective-permute-start.2
  9.5 1.5 collective-permute-start.1
  11.1 6.2 %shard_map.93 = (bf16[512,1024]{1,0:T(8,128)(2,1)}, f32[512,1024]{1,0:T(8,128)}) custom-call(bf16[512,1024]{1,0:T(8,128)(2,1)} %q_ref, bf16[512,1024]{1,0:T(8,128)(2,1)} %k_ref.5, bf16[512,1024]{1,0:T(8,128)(2,1)} %v_ref.5, f32[512,1]{1,0:T(8,128)S(1)} %multiply_rsqrt_fusion.scale_ref), custom_call_target="tpu_custom_call" | custom-call | flops 1073741824 | bytes 6291456 | tf_op jit(solution)/shard_map/pallas_call | solution.py:129
  17.3 1.4 collective-permute-done.5.refs_2_.refs_10_
  18.7 2.0 collective-permute-done.4.refs_1_.refs_9_
  20.7 2.3 collective-permute-done.3
  24.1 1.5 collective-permute-done.1
  25.8 1.6 collective-permute-start.8
  28.0 3.3 %shard_map.94.a_ref.refs_6_.refs_5_.own_ref = bf16[512,1024]{1,0:T(8,128)(2,1)} custom-call(bf16[512,1024]{1,0:T(8,128)(2,1)} %get-tuple-element.79.scaled_ref.a_ref, f32[512,1024]{1,0:T(8,128)} %get-tuple-element.80.intra_ref, f32[8,128,128]{2,1,0:T(8,128)S(1)} %select_add_fusion.1.state_ref), custom_call_target="tpu_custom_call" | custom-call | flops 268435456 | bytes 4194304 | tf_op jit(solution)/shard_map/pallas_call | solution.py:129
  31.3 3.3 %collective-permute-done.8 = bf16[128,1024]{1,0:T(8,128)(2,1)S(1)} collective-permute-done((bf16[128,1024]{1,0:T(8,128)(2,1)S(1)}, bf16[128,1024]{1,0:T(8,128)(2,1)S(1)}, u32[]{:S(2)}, u32[]{:S(2)}) %collective-permute-start.8) | collective-permute-done | bytes 262176 | tf_op jit(solution)/shard_map/ppermute | solution.py:321
  34.6 1.2 collective-permute-done.7
  36.6 3.2 %shard_map.97.refs_4_ = bf16[4,1024,256]{2,1,0:T(8,128)(2,1)S(1)} custom-call(bf16[512,1024]{1,0:T(8,128)(2,1)} %shard_map.94.a_ref.refs_6_.refs_5_.own_ref, bf16[256,1024]{1,0:T(8,128)(2,1)} %copy-done.10, bf16[256,1024]{1,0:T(8,128)(2,1)} %copy-done.12, bf16[256,1024]{1,0:T(8,128)(2,1)} %copy-done.11, bf16[256,1024]{1,0:T(8,128)(2,1)} %pad_maximum_fusion.2.refs_3_.refs_11_), custom_call_target="tpu_custom_call" | custom-call | flops 1073741824 | bytes 2097152 | tf_op jit(solution)/shard_map/pallas_call | solution.py:147
  39.9 3.5 %shard_map.98 = bf16[4,1024,256]{2,1,0:T(8,128)(2,1)S(1)} custom-call(bf16[512,1024]{1,0:T(8,128)(2,1)S(1)} %collective-permute-done.9.a_ref.refs_7_.refs_6_.other_ref, bf16[256,1024]{1,0:T(8,128)(2,1)} %copy-done.10, bf16[256,1024]{1,0:T(8,128)(2,1)} %copy-done.12, bf16[256,1024]{1,0:T(8,128)(2,1)} %copy-done.11, ...), custom_call_target="tpu_custom_call", output_to_operand_aliasing={{}: (5, {})} | custom-call | flops 1073741824 | bytes 2097152 | tf_op jit(solution)/shard_map/pallas_call | solution.py:147
  44.4 4.3 %collective-permute-start.14 = (bf16[1024,256]{1,0:T(8,128)(2,1)}, bf16[1024,256]{1,0:T(8,128)(2,1)}, u32[]{:S(2)}, u32[]{:S(2)}) collective-permute-start(bf16[1024,256]{1,0:T(8,128)(2,1)} %get-tuple-element.165), channel_id=1, source_target_pairs={{0,1},{3,2},{4,5},{7,6},{8,9},{11,10},{12,13},{15,14},{16,17},{19,... | collective-permute-start | bytes 1572872 | tf_op jit(solution)/shard_map/ppermute | solution.py:332
  48.7 2.1 collective-permute-start.17
  50.8 9.6 %collective-permute-done.14 = bf16[1024,256]{1,0:T(8,128)(2,1)} collective-permute-done((bf16[1024,256]{1,0:T(8,128)(2,1)}, bf16[1024,256]{1,0:T(8,128)(2,1)}, u32[]{:S(2)}, u32[]{:S(2)}) %collective-permute-start.14) | collective-permute-done | bytes 524320 | tf_op jit(solution)/shard_map/ppermute | solution.py:332
  60.4 2.0 fusion.6
  62.4 1.5 collective-permute-start.15
  63.9 1.9 slice.99.refs_0_.refs_7_
  66.8 1.9 constant_dynamic-slice_fusion.1
  68.7 2.6 %collective-permute-done.17 = bf16[1024,256]{1,0:T(8,128)(2,1)} collective-permute-done((bf16[1024,256]{1,0:T(8,128)(2,1)}, bf16[1024,256]{1,0:T(8,128)(2,1)}, u32[]{:S(2)}, u32[]{:S(2)}) %collective-permute-start.17) | collective-permute-done | bytes 524320 | tf_op jit(solution)/shard_map/ppermute | solution.py:332
  71.3 2.5 %fusion.7 = (bf16[1024,256]{1,0:T(8,128)(2,1)}, bf16[1024,256]{1,0:T(8,128)(2,1)}) fusion(bf16[1024,256]{1,0:T(8,128)(2,1)} %collective-permute-done.15, bf16[4,1024,256]{2,1,0:T(8,128)(2,1)S(1)} %shard_map.98, s32[]{:T(128)S(6)} %select_n.220, bf16[1024,256]{1,0:T(8,128)(2,1)} %collective-permute-done.17, s32[]{:T(128)S(6)} %select_n.226), kind=kLoop, calls=%fused_computation.17 | loop fusion | flops 2097152 | bytes 3145736 | tf_op jit(solution)/shard_map/convert_element_type | solution.py:352
  73.7 9.0 %collective-permute-start.16 = (bf16[1024,256]{1,0:T(8,128)(2,1)}, bf16[1024,256]{1,0:T(8,128)(2,1)}, u32[]{:S(2)}, u32[]{:S(2)}) collective-permute-start(bf16[1024,256]{1,0:T(8,128)(2,1)} %get-tuple-element.163), channel_id=1, source_target_pairs={{0,1},{2,3},{1,0},{3,2},{4,5},{6,7},{5,4},{7,6},{8,9},{10,11},{9,8... | collective-permute-start | bytes 1572872 | tf_op jit(solution)/shard_map/ppermute | solution.py:332
  82.7 1.5 collective-permute-start.18
  85.7 1.8 constant_dynamic-slice_fusion.2
  89.1 1.8 fusion.20
  91.6 1.9 collective-permute-done.16
  93.5 1.5 subtract_convert_fusion.1
  95.8 6.5 %collective-permute-start.23 = (bf16[1024,256]{1,0:T(8,128)(2,1)S(1)}, bf16[1024,256]{1,0:T(8,128)(2,1)S(1)}, u32[]{:S(2)}, u32[]{:S(2)}) collective-permute-start(bf16[1024,256]{1,0:T(8,128)(2,1)S(1)} %get-tuple-element.145.refs_0_), channel_id=1, source_target_pairs={{0,1},{2,3},{1,0},{3,2},{4,5},{6,7},{5,4},{7,6},{8,9},{10,11},{9,8... | collective-permute-start | bytes 1572872 | tf_op jit(solution)/shard_map/ppermute | solution.py:332
  103.2 3.2 %shard_map.95.refs_4_ = bf16[4,1024,256]{2,1,0:T(8,128)(2,1)S(1)} custom-call(bf16[512,1024]{1,0:T(8,128)(2,1)} %shard_map.94.a_ref.refs_6_.refs_5_.own_ref, bf16[256,1024]{1,0:T(8,128)(2,1)} %slice.99.refs_0_.refs_7_, bf16[256,1024]{1,0:T(8,128)(2,1)} %collective-permute-done.10.refs_1_.refs_8_, bf16[256,1024]{1,0:T(8,128)(2,1)} %collective-permute-done.11.refs_2_.refs_9_, ...), custom_call_target="tpu_custom_call" | custom-call | flops 1073741824 | bytes 2097152 | tf_op jit(solution)/shard_map/pallas_call | solution.py:147
  106.5 3.1 %shard_map.96 = bf16[4,1024,256]{2,1,0:T(8,128)(2,1)S(1)} custom-call(bf16[512,1024]{1,0:T(8,128)(2,1)S(1)} %collective-permute-done.9.a_ref.refs_7_.refs_6_.other_ref, bf16[256,1024]{1,0:T(8,128)(2,1)} %slice.99.refs_0_.refs_7_, bf16[256,1024]{1,0:T(8,128)(2,1)} %collective-permute-done.10.refs_1_.refs_8_, ...), custom_call_target="tpu_custom_call", output_to_operand_aliasing={{}: (5, {})} | custom-call | flops 1073741824 | bytes 2097152 | tf_op jit(solution)/shard_map/pallas_call | solution.py:147
  109.6 1.9 collective-permute-done.23.refs_1_
  111.6 1.3 collective-permute-start.25
  113.6 6.3 %collective-permute-start.22 = (bf16[1024,256]{1,0:T(8,128)(2,1)S(1)}, bf16[1024,256]{1,0:T(8,128)(2,1)S(1)}, u32[]{:S(2)}, u32[]{:S(2)}) collective-permute-start(bf16[1024,256]{1,0:T(8,128)(2,1)S(1)} %get-tuple-element.161), channel_id=1, source_target_pairs={{0,1},{3,2},{4,5},{7,6},{8,9},{11,10},{12,13},{15,14},{16,17},{19,... | collective-permute-start | bytes 1572872 | tf_op jit(solution)/shard_map/ppermute | solution.py:332
  119.9 1.5 collective-permute-start.21
  121.4 4.5 %collective-permute-done.25.refs_3_ = bf16[1024,256]{1,0:T(8,128)(2,1)S(1)} collective-permute-done((bf16[1024,256]{1,0:T(8,128)(2,1)S(1)}, bf16[1024,256]{1,0:T(8,128)(2,1)S(1)}, u32[]{:S(2)}, u32[]{:S(2)}) %collective-permute-start.25) | collective-permute-done | bytes 524320 | tf_op jit(solution)/shard_map/ppermute | solution.py:332
  125.9 1.3 collective-permute-start.28
  127.2 5.1 %collective-permute-done.22 = bf16[1024,256]{1,0:T(8,128)(2,1)S(1)} collective-permute-done((bf16[1024,256]{1,0:T(8,128)(2,1)S(1)}, bf16[1024,256]{1,0:T(8,128)(2,1)S(1)}, u32[]{:S(2)}, u32[]{:S(2)}) %collective-permute-start.22) | collective-permute-done | bytes 524320 | tf_op jit(solution)/shard_map/ppermute | solution.py:332
  133.1 7.4 %collective-permute-done.21 = bf16[1024,256]{1,0:T(8,128)(2,1)S(1)} collective-permute-done((bf16[1024,256]{1,0:T(8,128)(2,1)S(1)}, bf16[1024,256]{1,0:T(8,128)(2,1)S(1)}, u32[]{:S(2)}, u32[]{:S(2)}) %collective-permute-start.21) | collective-permute-done | bytes 524320 | tf_op jit(solution)/shard_map/ppermute | solution.py:332
  141.3 1.3 fusion.2
  142.6 4.6 %collective-permute-start.29 = (bf16[1024,256]{1,0:T(8,128)(2,1)}, bf16[1024,256]{1,0:T(8,128)(2,1)}, u32[]{:S(2)}, u32[]{:S(2)}) collective-permute-start(bf16[1024,256]{1,0:T(8,128)(2,1)} %get-tuple-element.159), channel_id=1, source_target_pairs={{0,1},{2,3},{1,0},{3,2},{4,5},{6,7},{5,4},{7,6},{8,9},{10,11},{9,8... | collective-permute-start | bytes 1572872 | tf_op jit(solution)/shard_map/ppermute | solution.py:332
  147.2 1.5 collective-permute-start.30
  148.8 5.9 %collective-permute-done.29 = bf16[1024,256]{1,0:T(8,128)(2,1)} collective-permute-done((bf16[1024,256]{1,0:T(8,128)(2,1)}, bf16[1024,256]{1,0:T(8,128)(2,1)}, u32[]{:S(2)}, u32[]{:S(2)}) %collective-permute-start.29) | collective-permute-done | bytes 524320 | tf_op jit(solution)/shard_map/ppermute | solution.py:332
  154.7 1.5 subtract_convert_fusion
  156.9 6.8 %collective-permute-start.31 = (bf16[1024,256]{1,0:T(8,128)(2,1)S(1)}, bf16[1024,256]{1,0:T(8,128)(2,1)S(1)}, u32[]{:S(2)}, u32[]{:S(2)}) collective-permute-start(bf16[1024,256]{1,0:T(8,128)(2,1)S(1)} %get-tuple-element.143.refs_0_), channel_id=1, source_target_pairs={{0,1},{2,3},{1,0},{3,2},{4,5},{6,7},{5,4},{7,6},{8,9},{10,11},{9,8... | collective-permute-start | bytes 1572872 | tf_op jit(solution)/shard_map/ppermute | solution.py:332
  163.8 10.6 %shard_map.99 = (f32[512,1024]{1,0:T(8,128)}, f32[512,1024]{1,0:T(8,128)}, bf16[4,256,1024]{2,1,0:T(8,128)(2,1)}) custom-call(s32[12]{0:T(128)S(1)} %stack.93.meta_ref, bf16[1024,256]{1,0:T(8,128)(2,1)} %copy-done.22, bf16[1024,256]{1,0:T(8,128)(2,1)} %copy-done.29, bf16[1024,256]{1,0:T(8,128)(2,1)} %copy-done.28, bf16[1024,256]{1,0:T(8,128)(2,1)} %copy-done.30, ...), custom_call_target="tpu_custom_call" | custom-call | flops 4294967296 | bytes 8388608 | tf_op jit(solution)/shard_map/pallas_call | solution.py:227
  175.6 1.3 collective-permute-start.33
  179.0 12.7 %collective-permute-done.33.refs_3_ = bf16[1024,256]{1,0:T(8,128)(2,1)S(1)} collective-permute-done((bf16[1024,256]{1,0:T(8,128)(2,1)S(1)}, bf16[1024,256]{1,0:T(8,128)(2,1)S(1)}, u32[]{:S(2)}, u32[]{:S(2)}) %collective-permute-start.33) | collective-permute-done | bytes 524320 | tf_op jit(solution)/shard_map/ppermute | solution.py:332
  191.8 1.3 collective-permute-start.36
  194.9 10.2 %shard_map.100 = (f32[512,1024]{1,0:T(8,128)S(1)}, f32[512,1024]{1,0:T(8,128)S(1)}, bf16[4,256,1024]{2,1,0:T(8,128)(2,1)S(1)}) custom-call(s32[12]{0:T(128)S(1)} %stack.93.meta_ref, bf16[1024,256]{1,0:T(8,128)(2,1)} %copy-done.23, bf16[1024,256]{1,0:T(8,128)(2,1)} %copy-done.34, bf16[1024,256]{1,0:T(8,128)(2,1)} %copy-done.33, bf16[1024,256]{1,0:T(8,128)(2,1)} %copy-done.36, ...), custom_call_target="tpu_custom_call" | custom-call | flops 4294967296 | bytes 8388608 | tf_op jit(solution)/shard_map/pallas_call | solution.py:227
  205.1 3.1 %collective-permute-done.36.piece_ref = bf16[1024,256]{1,0:T(8,128)(2,1)S(1)} collective-permute-done((bf16[1024,256]{1,0:T(8,128)(2,1)S(1)}, bf16[1024,256]{1,0:T(8,128)(2,1)S(1)}, u32[]{:S(2)}, u32[]{:S(2)}) %collective-permute-start.36) | collective-permute-done | bytes 524320 | tf_op jit(solution)/shard_map/ppermute | solution.py:332
  208.2 5.0 %shard_map.101 = (f32[512,1024]{1,0:T(8,128)}, bf16[512,1024]{1,0:T(8,128)(2,1)}, bf16[4,256,1024]{2,1,0:T(8,128)(2,1)S(1)}) custom-call(s32[2]{0:T(128)S(1)} %pad_add_fusion.meta_ref, bf16[1024,256]{1,0:T(8,128)(2,1)S(1)} %collective-permute-done.36.piece_ref, bf16[512,1024]{1,0:T(8,128)(2,1)S(1)} %copy-done, ...), custom_call_target="tpu_custom_call", output_to_operand_aliasing={{2}: (6, {})} | custom-call | flops 1073741824 | bytes 8388608 | tf_op jit(solution)/shard_map/pallas_call | solution.py:290
  214.4 1.6 collective-permute-done.41
  218.6 1.5 bitcast_add_fusion.3
  221.0 1.2 collective-permute-start.44
  222.2 1.5 collective-permute-start.43
  223.7 8.7 %shard_map.103 = (bf16[512,1024]{1,0:T(8,128)(2,1)}, f32[512,1024]{1,0:T(8,128)S(1)}, f32[512,1024]{1,0:T(8,128)S(1)}) custom-call(bf16[512,1024]{1,0:T(8,128)(2,1)S(1)} %copy-done.7, bf16[512,1024]{1,0:T(8,128)(2,1)S(1)} %copy-done.5, bf16[512,1024]{1,0:T(8,128)(2,1)S(1)} %copy-done.6, bf16[512,1024]{1,0:T(8,128)(2,1)S(1)} %add_convert_fusion.b_ref.g_ref, ...), custom_call_target="tpu_custom_call" | custom-call | flops 2684354560 | bytes 9437184 | tf_op jit(solution)/shard_map/pallas_call | solution.py:129
  234.5 1.5 collective-permute-start.48
  236.1 2.9 %shard_map.104 = (bf16[512,1024]{1,0:T(8,128)(2,1)}, bf16[512,1024]{1,0:T(8,128)(2,1)}) custom-call(bf16[512,1024]{1,0:T(8,128)(2,1)S(1)} %copy-done.5, bf16[512,1024]{1,0:T(8,128)(2,1)S(1)} %copy-done.6, f32[512,1024]{1,0:T(8,128)S(1)} %get-tuple-element.130.dk_part_ref, f32[512,1024]{1,0:T(8,128)S(1)} %get-tuple-element.131.dv_part_ref, ...), custom_call_target="tpu_custom_call" | custom-call | flops 536870912 | bytes 7340032 | tf_op jit(solution)/shard_map/pallas_call | solution.py:129
  239.0 3.7 %collective-permute-done.49 = bf16[128,1024]{1,0:T(8,128)(2,1)S(1)} collective-permute-done((bf16[128,1024]{1,0:T(8,128)(2,1)S(1)}, bf16[128,1024]{1,0:T(8,128)(2,1)S(1)}, u32[]{:S(2)}, u32[]{:S(2)}) %collective-permute-start.49) | collective-permute-done | bytes 262176 | tf_op jit(solution)/shard_map/ppermute | solution.py:321
  243.2 1.6 pad_maximum_fusion
  (173 shorter events, 27.9 us)
Async XLA Ops:
  2.7 4.7 %collective-permute-start = (bf16[8,128,128]{2,1,0:T(8,128)(2,1)S(1)}, bf16[8,128,128]{2,1,0:T(8,128)(2,1)S(1)}, u32[]{:S(2)}, u32[]{:S(2)}) collective-permute-start(bf16[8,128,128]{2,1,0:T(8,128)(2,1)S(1)} %convert_element_type.304), channel_id=1, source_target_pairs={{0,4},{4,0},{8,12},{12,8},{16,20},{20,16},{24,28},{28,24},{1,5},{5... | collective-permute-start | bytes 786440 | tf_op jit(solution)/shard_map/ppermute | solution.py:316
  3.3 14.0 %copy-start.10 = (bf16[256,1024]{1,0:T(8,128)(2,1)}, bf16[256,1024]{1,0:T(8,128)(2,1)S(1)}, u32[]{:S(2)}) copy-start(bf16[256,1024]{1,0:T(8,128)(2,1)S(1)} %slice.96.refs_0_.refs_8_) | copy-start | bytes 1572868
  3.3 15.4 %collective-permute-start.5 = (bf16[256,1024]{1,0:T(8,128)(2,1)S(1)}, bf16[256,1024]{1,0:T(8,128)(2,1)S(1)}, u32[]{:S(2)}, u32[]{:S(2)}) collective-permute-start(bf16[256,1024]{1,0:T(8,128)(2,1)S(1)} %slice.96.refs_0_.refs_8_), channel_id=1, source_target_pairs={{0,16},{4,20},{8,24},{12,28},{16,0},{20,4},{24,8},{28,12},{1,17},{... | collective-permute-start | bytes 1572872 | tf_op jit(solution)/shard_map/ppermute | solution.py:321
  5.9 14.8 %collective-permute-start.4 = (bf16[256,1024]{1,0:T(8,128)(2,1)S(1)}, bf16[256,1024]{1,0:T(8,128)(2,1)S(1)}, u32[]{:S(2)}, u32[]{:S(2)}) collective-permute-start(bf16[256,1024]{1,0:T(8,128)(2,1)S(1)} %slice.96.refs_0_.refs_8_), channel_id=1, source_target_pairs={{0,8},{4,12},{8,0},{12,4},{16,24},{20,28},{24,16},{28,20},{1,9},{5... | collective-permute-start | bytes 1572872 | tf_op jit(solution)/shard_map/ppermute | solution.py:321
  7.5 15.5 %collective-permute-start.3 = (bf16[4,128,128]{2,1,0:T(8,128)(2,1)S(1)}, bf16[4,128,128]{2,1,0:T(8,128)(2,1)S(1)}, u32[]{:S(2)}, u32[]{:S(2)}) collective-permute-start(bf16[4,128,128]{2,1,0:T(8,128)(2,1)S(1)} %fusion.15), channel_id=1, source_target_pairs={{0,24},{4,28},{8,16},{12,20},{16,8},{20,12},{24,0},{28,4},{1,25},{... | collective-permute-start | bytes 393224 | tf_op jit(solution)/shard_map/ppermute | solution.py:321
  8.4 15.7 %collective-permute-start.2 = (bf16[4,128,128]{2,1,0:T(8,128)(2,1)S(1)}, bf16[4,128,128]{2,1,0:T(8,128)(2,1)S(1)}, u32[]{:S(2)}, u32[]{:S(2)}) collective-permute-start(bf16[4,128,128]{2,1,0:T(8,128)(2,1)S(1)} %fusion.15), channel_id=1, source_target_pairs={{0,16},{4,20},{8,24},{12,28},{16,0},{20,4},{24,8},{28,12},{1,17},{... | collective-permute-start | bytes 393224 | tf_op jit(solution)/shard_map/ppermute | solution.py:321
  9.5 16.0 %collective-permute-start.1 = (bf16[4,128,128]{2,1,0:T(8,128)(2,1)S(1)}, bf16[4,128,128]{2,1,0:T(8,128)(2,1)S(1)}, u32[]{:S(2)}, u32[]{:S(2)}) collective-permute-start(bf16[4,128,128]{2,1,0:T(8,128)(2,1)S(1)} %fusion.15), channel_id=1, source_target_pairs={{0,8},{4,12},{8,0},{12,4},{16,24},{20,28},{24,16},{28,20},{1,9},{5... | collective-permute-start | bytes 393224 | tf_op jit(solution)/shard_map/ppermute | solution.py:321
  25.7 2.2 collective-permute-start.6
  25.8 8.8 %collective-permute-start.8 = (bf16[128,1024]{1,0:T(8,128)(2,1)S(1)}, bf16[128,1024]{1,0:T(8,128)(2,1)S(1)}, u32[]{:S(2)}, u32[]{:S(2)}) collective-permute-start(bf16[128,1024]{1,0:T(8,128)(2,1)S(1)} %slice.98), channel_id=1, source_target_pairs={{0,8},{4,12},{8,0},{12,4},{16,24},{20,28},{24,16},{28,20},{1,9},{5... | collective-permute-start | bytes 786440 | tf_op jit(solution)/shard_map/ppermute | solution.py:321
  27.4 8.4 %collective-permute-start.7 = (bf16[128,1024]{1,0:T(8,128)(2,1)S(1)}, bf16[128,1024]{1,0:T(8,128)(2,1)S(1)}, u32[]{:S(2)}, u32[]{:S(2)}) collective-permute-start(bf16[128,1024]{1,0:T(8,128)(2,1)S(1)} %slice.97), channel_id=1, source_target_pairs={{0,16},{4,20},{8,24},{12,28},{16,0},{20,4},{24,8},{28,12},{1,17},{... | collective-permute-start | bytes 786440 | tf_op jit(solution)/shard_map/ppermute | solution.py:321
  36.6 3.3 %collective-permute-start.9 = (bf16[512,1024]{1,0:T(8,128)(2,1)}, bf16[512,1024]{1,0:T(8,128)(2,1)S(1)}, u32[]{:S(2)}, u32[]{:S(2)}) collective-permute-start(bf16[512,1024]{1,0:T(8,128)(2,1)} %shard_map.94.a_ref.refs_6_.refs_5_.own_ref), channel_id=1, source_target_pairs={{0,4},{4,0},{8,12},{12,8},{16,20},{20,16},{24,28},{28,24},{1,5},{5... | collective-permute-start | bytes 3145736 | tf_op jit(solution)/shard_map/ppermute | solution.py:316
  39.9 66.6 %copy-start.1 = (bf16[512,1024]{1,0:T(8,128)(2,1)}, bf16[512,1024]{1,0:T(8,128)(2,1)S(1)}, u32[]{:S(2)}) copy-start(bf16[512,1024]{1,0:T(8,128)(2,1)S(1)} %collective-permute-done.9.a_ref.refs_7_.refs_6_.other_ref) | copy-start | bytes 3145732
  44.4 16.0 %collective-permute-start.14 = (bf16[1024,256]{1,0:T(8,128)(2,1)}, bf16[1024,256]{1,0:T(8,128)(2,1)}, u32[]{:S(2)}, u32[]{:S(2)}) collective-permute-start(bf16[1024,256]{1,0:T(8,128)(2,1)} %get-tuple-element.165), channel_id=1, source_target_pairs={{0,1},{3,2},{4,5},{7,6},{8,9},{11,10},{12,13},{15,14},{16,17},{19,... | collective-permute-start | bytes 1572872 | tf_op jit(solution)/shard_map/ppermute | solution.py:332
  48.7 22.6 %collective-permute-start.17 = (bf16[1024,256]{1,0:T(8,128)(2,1)}, bf16[1024,256]{1,0:T(8,128)(2,1)}, u32[]{:S(2)}, u32[]{:S(2)}) collective-permute-start(bf16[1024,256]{1,0:T(8,128)(2,1)} %get-tuple-element.166), channel_id=1, source_target_pairs={{0,1},{3,2},{4,5},{7,6},{8,9},{11,10},{12,13},{15,14},{16,17},{19,... | collective-permute-start | bytes 1572872 | tf_op jit(solution)/shard_map/ppermute | solution.py:332
  62.4 8.9 %collective-permute-start.15 = (bf16[1024,256]{1,0:T(8,128)(2,1)}, bf16[1024,256]{1,0:T(8,128)(2,1)}, u32[]{:S(2)}, u32[]{:S(2)}) collective-permute-start(bf16[1024,256]{1,0:T(8,128)(2,1)} %fusion.6), channel_id=1, source_target_pairs={{1,2},{2,1},{5,6},{6,5},{9,10},{10,9},{13,14},{14,13},{17,18},{18,... | collective-permute-start | bytes 1572872 | tf_op jit(solution)/shard_map/ppermute | solution.py:332
  65.8 18.4 %collective-permute-start.10 = (bf16[256,1024]{1,0:T(8,128)(2,1)}, bf16[256,1024]{1,0:T(8,128)(2,1)}, u32[]{:S(2)}, u32[]{:S(2)}) collective-permute-start(bf16[256,1024]{1,0:T(8,128)(2,1)} %slice.99.refs_0_.refs_7_), channel_id=1, source_target_pairs={{0,8},{4,12},{8,0},{12,4},{16,24},{20,28},{24,16},{28,20},{1,9},{5... | collective-permute-start | bytes 1572872 | tf_op jit(solution)/shard_map/ppermute | solution.py:321
  66.3 21.2 %collective-permute-start.11 = (bf16[256,1024]{1,0:T(8,128)(2,1)}, bf16[256,1024]{1,0:T(8,128)(2,1)}, u32[]{:S(2)}, u32[]{:S(2)}) collective-permute-start(bf16[256,1024]{1,0:T(8,128)(2,1)} %slice.99.refs_0_.refs_7_), channel_id=1, source_target_pairs={{0,16},{4,20},{8,24},{12,28},{16,0},{20,4},{24,8},{28,12},{1,17},{... | collective-permute-start | bytes 1572872 | tf_op jit(solution)/shard_map/ppermute | solution.py:321
  68.7 20.4 %collective-permute-start.19 = (bf16[512,512]{1,0:T(8,128)(2,1)}, bf16[512,512]{1,0:T(8,128)(2,1)}, u32[]{:S(2)}, u32[]{:S(2)}) collective-permute-start(bf16[512,512]{1,0:T(8,128)(2,1)} %constant_dynamic-slice_fusion.1), channel_id=1, source_target_pairs={{0,4},{4,0},{8,12},{12,8},{16,20},{20,16},{24,28},{28,24},{1,5},{5... | collective-permute-start | bytes 1572872 | tf_op jit(solution)/shard_map/ppermute | solution.py:316
  73.7 19.8 %collective-permute-start.16 = (bf16[1024,256]{1,0:T(8,128)(2,1)}, bf16[1024,256]{1,0:T(8,128)(2,1)}, u32[]{:S(2)}, u32[]{:S(2)}) collective-permute-start(bf16[1024,256]{1,0:T(8,128)(2,1)} %get-tuple-element.163), channel_id=1, source_target_pairs={{0,1},{2,3},{1,0},{3,2},{4,5},{6,7},{5,4},{7,6},{8,9},{10,11},{9,8... | collective-permute-start | bytes 1572872 | tf_op jit(solution)/shard_map/ppermute | solution.py:332
  82.7 10.8 %collective-permute-start.18 = (bf16[1024,256]{1,0:T(8,128)(2,1)}, bf16[1024,256]{1,0:T(8,128)(2,1)}, u32[]{:S(2)}, u32[]{:S(2)}) collective-permute-start(bf16[1024,256]{1,0:T(8,128)(2,1)} %get-tuple-element.164), channel_id=1, source_target_pairs={{1,2},{2,1},{5,6},{6,5},{9,10},{10,9},{13,14},{14,13},{17,18},{18,... | collective-permute-start | bytes 1572872 | tf_op jit(solution)/shard_map/ppermute | solution.py:332
  85.2 6.4 %collective-permute-start.12 = (bf16[128,1024]{1,0:T(8,128)(2,1)S(1)}, bf16[128,1024]{1,0:T(8,128)(2,1)S(1)}, u32[]{:S(2)}, u32[]{:S(2)}) collective-permute-start(bf16[128,1024]{1,0:T(8,128)(2,1)S(1)} %slice.128), channel_id=1, source_target_pairs={{0,16},{4,20},{8,24},{12,28},{16,0},{20,4},{24,8},{28,12},{1,17},{... | collective-permute-start | bytes 786440 | tf_op jit(solution)/shard_map/ppermute | solution.py:321
  88.5 13.9 %collective-permute-start.13 = (bf16[128,1024]{1,0:T(8,128)(2,1)S(1)}, bf16[128,1024]{1,0:T(8,128)(2,1)S(1)}, u32[]{:S(2)}, u32[]{:S(2)}) collective-permute-start(bf16[128,1024]{1,0:T(8,128)(2,1)S(1)} %slice.129), channel_id=1, source_target_pairs={{0,8},{4,12},{8,0},{12,4},{16,24},{20,28},{24,16},{28,20},{1,9},{5... | collective-permute-start | bytes 786440 | tf_op jit(solution)/shard_map/ppermute | solution.py:321
  95.1 14.6 %collective-permute-start.24 = (bf16[1024,256]{1,0:T(8,128)(2,1)S(1)}, bf16[1024,256]{1,0:T(8,128)(2,1)S(1)}, u32[]{:S(2)}, u32[]{:S(2)}) collective-permute-start(bf16[1024,256]{1,0:T(8,128)(2,1)S(1)} %get-tuple-element.145.refs_0_), channel_id=1, source_target_pairs={{1,2},{2,1},{5,6},{6,5},{9,10},{10,9},{13,14},{14,13},{17,18},{18,... | collective-permute-start | bytes 1572872 | tf_op jit(solution)/shard_map/ppermute | solution.py:332
  95.8 15.8 %collective-permute-start.23 = (bf16[1024,256]{1,0:T(8,128)(2,1)S(1)}, bf16[1024,256]{1,0:T(8,128)(2,1)S(1)}, u32[]{:S(2)}, u32[]{:S(2)}) collective-permute-start(bf16[1024,256]{1,0:T(8,128)(2,1)S(1)} %get-tuple-element.145.refs_0_), channel_id=1, source_target_pairs={{0,1},{2,3},{1,0},{3,2},{4,5},{6,7},{5,4},{7,6},{8,9},{10,11},{9,8... | collective-permute-start | bytes 1572872 | tf_op jit(solution)/shard_map/ppermute | solution.py:332
  102.3 7.3 %collective-permute-start.20 = (bf16[512,256]{1,0:T(8,128)(2,1)S(1)}, bf16[512,256]{1,0:T(8,128)(2,1)S(1)}, u32[]{:S(2)}, u32[]{:S(2)}) collective-permute-start(bf16[512,256]{1,0:T(8,128)(2,1)S(1)} %slice.132), channel_id=1, source_target_pairs={{0,4},{4,0},{8,12},{12,8},{16,20},{20,16},{24,28},{28,24},{1,5},{5... | collective-permute-start | bytes 786440 | tf_op jit(solution)/shard_map/ppermute | solution.py:316
  109.6 30.9 %copy-start.28 = (bf16[1024,256]{1,0:T(8,128)(2,1)}, bf16[1024,256]{1,0:T(8,128)(2,1)S(1)}, u32[]{:S(2)}) copy-start(bf16[1024,256]{1,0:T(8,128)(2,1)S(1)} %collective-permute-done.24.refs_2_) | copy-start | bytes 1572868
  111.6 31.0 %copy-start.29 = (bf16[1024,256]{1,0:T(8,128)(2,1)}, bf16[1024,256]{1,0:T(8,128)(2,1)S(1)}, u32[]{:S(2)}) copy-start(bf16[1024,256]{1,0:T(8,128)(2,1)S(1)} %collective-permute-done.23.refs_1_) | copy-start | bytes 1572868
  111.6 14.3 %collective-permute-start.25 = (bf16[1024,256]{1,0:T(8,128)(2,1)S(1)}, bf16[1024,256]{1,0:T(8,128)(2,1)S(1)}, u32[]{:S(2)}, u32[]{:S(2)}) collective-permute-start(bf16[1024,256]{1,0:T(8,128)(2,1)S(1)} %collective-permute-done.24.refs_2_), channel_id=1, source_target_pairs={{2,3},{1,0},{6,7},{5,4},{10,11},{9,8},{14,15},{13,12},{18,19},{17,... | collective-permute-start | bytes 1572872 | tf_op jit(solution)/shard_map/ppermute | solution.py:332
  112.8 13.0 %collective-permute-start.26 = (bf16[1024,256]{1,0:T(8,128)(2,1)S(1)}, bf16[1024,256]{1,0:T(8,128)(2,1)S(1)}, u32[]{:S(2)}, u32[]{:S(2)}) collective-permute-start(bf16[1024,256]{1,0:T(8,128)(2,1)S(1)} %collective-permute-done.23.refs_1_), channel_id=1, source_target_pairs={{1,2},{2,1},{5,6},{6,5},{9,10},{10,9},{13,14},{14,13},{17,18},{18,... | collective-permute-start | bytes 1572872 | tf_op jit(solution)/shard_map/ppermute | solution.py:332
  113.6 18.6 %collective-permute-start.22 = (bf16[1024,256]{1,0:T(8,128)(2,1)S(1)}, bf16[1024,256]{1,0:T(8,128)(2,1)S(1)}, u32[]{:S(2)}, u32[]{:S(2)}) collective-permute-start(bf16[1024,256]{1,0:T(8,128)(2,1)S(1)} %get-tuple-element.161), channel_id=1, source_target_pairs={{0,1},{3,2},{4,5},{7,6},{8,9},{11,10},{12,13},{15,14},{16,17},{19,... | collective-permute-start | bytes 1572872 | tf_op jit(solution)/shard_map/ppermute | solution.py:332
  119.9 34.8 %copy-start.16 = (bf16[512,256]{1,0:T(8,128)(2,1)S(1)}, bf16[512,256]{1,0:T(8,128)(2,1)}, u32[]{:S(2)}) copy-start(bf16[512,256]{1,0:T(8,128)(2,1)} %get-tuple-element.168) | copy-start | bytes 786436
  119.9 34.8 %copy-start.17 = (bf16[512,256]{1,0:T(8,128)(2,1)S(1)}, bf16[512,256]{1,0:T(8,128)(2,1)}, u32[]{:S(2)}) copy-start(bf16[512,256]{1,0:T(8,128)(2,1)} %get-tuple-element.174) | copy-start | bytes 786436
  119.9 20.5 %collective-permute-start.21 = (bf16[1024,256]{1,0:T(8,128)(2,1)S(1)}, bf16[1024,256]{1,0:T(8,128)(2,1)S(1)}, u32[]{:S(2)}, u32[]{:S(2)}) collective-permute-start(bf16[1024,256]{1,0:T(8,128)(2,1)S(1)} %get-tuple-element.162), channel_id=1, source_target_pairs={{0,1},{3,2},{4,5},{7,6},{8,9},{11,10},{12,13},{15,14},{16,17},{19,... | collective-permute-start | bytes 1572872 | tf_op jit(solution)/shard_map/ppermute | solution.py:332
  125.9 16.7 %copy-start.31 = (bf16[1024,256]{1,0:T(8,128)(2,1)}, bf16[1024,256]{1,0:T(8,128)(2,1)S(1)}, u32[]{:S(2)}) copy-start(bf16[1024,256]{1,0:T(8,128)(2,1)S(1)} %collective-permute-done.26.refs_4_) | copy-start | bytes 1572868
  125.9 14.6 %collective-permute-start.28 = (bf16[1024,256]{1,0:T(8,128)(2,1)S(1)}, bf16[1024,256]{1,0:T(8,128)(2,1)S(1)}, u32[]{:S(2)}, u32[]{:S(2)}) collective-permute-start(bf16[1024,256]{1,0:T(8,128)(2,1)S(1)} %collective-permute-done.26.refs_4_), channel_id=1, source_target_pairs={{2,3},{1,0},{6,7},{5,4},{10,11},{9,8},{14,15},{13,12},{18,19},{17,... | collective-permute-start | bytes 1572872 | tf_op jit(solution)/shard_map/ppermute | solution.py:332
  132.4 8.9 %collective-permute-start.27 = (bf16[1024,256]{1,0:T(8,128)(2,1)S(1)}, bf16[1024,256]{1,0:T(8,128)(2,1)S(1)}, u32[]{:S(2)}, u32[]{:S(2)}) collective-permute-start(bf16[1024,256]{1,0:T(8,128)(2,1)S(1)} %fusion.1), channel_id=1, source_target_pairs={{1,2},{2,1},{5,6},{6,5},{9,10},{10,9},{13,14},{14,13},{17,18},{18,... | collective-permute-start | bytes 1572872 | tf_op jit(solution)/shard_map/ppermute | solution.py:332
  142.6 12.1 %collective-permute-start.29 = (bf16[1024,256]{1,0:T(8,128)(2,1)}, bf16[1024,256]{1,0:T(8,128)(2,1)}, u32[]{:S(2)}, u32[]{:S(2)}) collective-permute-start(bf16[1024,256]{1,0:T(8,128)(2,1)} %get-tuple-element.159), channel_id=1, source_target_pairs={{0,1},{2,3},{1,0},{3,2},{4,5},{6,7},{5,4},{7,6},{8,9},{10,11},{9,8... | collective-permute-start | bytes 1572872 | tf_op jit(solution)/shard_map/ppermute | solution.py:332
  147.2 7.5 %collective-permute-start.30 = (bf16[1024,256]{1,0:T(8,128)(2,1)}, bf16[1024,256]{1,0:T(8,128)(2,1)}, u32[]{:S(2)}, u32[]{:S(2)}) collective-permute-start(bf16[1024,256]{1,0:T(8,128)(2,1)} %get-tuple-element.160), channel_id=1, source_target_pairs={{1,2},{2,1},{5,6},{6,5},{9,10},{10,9},{13,14},{14,13},{17,18},{18,... | collective-permute-start | bytes 1572872 | tf_op jit(solution)/shard_map/ppermute | solution.py:332
  156.2 18.2 %copy-start.23 = (bf16[1024,256]{1,0:T(8,128)(2,1)}, bf16[1024,256]{1,0:T(8,128)(2,1)S(1)}, u32[]{:S(2)}) copy-start(bf16[1024,256]{1,0:T(8,128)(2,1)S(1)} %get-tuple-element.143.refs_0_) | copy-start | bytes 1572868
  156.2 19.4 %collective-permute-start.32 = (bf16[1024,256]{1,0:T(8,128)(2,1)S(1)}, bf16[1024,256]{1,0:T(8,128)(2,1)S(1)}, u32[]{:S(2)}, u32[]{:S(2)}) collective-permute-start(bf16[1024,256]{1,0:T(8,128)(2,1)S(1)} %get-tuple-element.143.refs_0_), channel_id=1, source_target_pairs={{1,2},{2,1},{5,6},{6,5},{9,10},{10,9},{13,14},{14,13},{17,18},{18,... | collective-permute-start | bytes 1572872 | tf_op jit(solution)/shard_map/ppermute | solution.py:332
  156.9 18.7 %collective-permute-start.31 = (bf16[1024,256]{1,0:T(8,128)(2,1)S(1)}, bf16[1024,256]{1,0:T(8,128)(2,1)S(1)}, u32[]{:S(2)}, u32[]{:S(2)}) collective-permute-start(bf16[1024,256]{1,0:T(8,128)(2,1)S(1)} %get-tuple-element.143.refs_0_), channel_id=1, source_target_pairs={{0,1},{2,3},{1,0},{3,2},{4,5},{6,7},{5,4},{7,6},{8,9},{10,11},{9,8... | collective-permute-start | bytes 1572872 | tf_op jit(solution)/shard_map/ppermute | solution.py:332
  163.7 10.7 %collective-permute-start.35 = (bf16[512,256]{1,0:T(8,128)(2,1)S(1)}, bf16[512,256]{1,0:T(8,128)(2,1)S(1)}, u32[]{:S(2)}, u32[]{:S(2)}) collective-permute-start(bf16[512,256]{1,0:T(8,128)(2,1)S(1)} %slice.135), channel_id=1, source_target_pairs={{0,4},{4,0},{8,12},{12,8},{16,20},{20,16},{24,28},{28,24},{1,5},{5... | collective-permute-start | bytes 786440 | tf_op jit(solution)/shard_map/ppermute | solution.py:316
  175.5 19.3 %copy-start.33 = (bf16[1024,256]{1,0:T(8,128)(2,1)}, bf16[1024,256]{1,0:T(8,128)(2,1)S(1)}, u32[]{:S(2)}) copy-start(bf16[1024,256]{1,0:T(8,128)(2,1)S(1)} %collective-permute-done.32.refs_2_) | copy-start | bytes 1572868
  175.5 19.3 %copy-start.34 = (bf16[1024,256]{1,0:T(8,128)(2,1)}, bf16[1024,256]{1,0:T(8,128)(2,1)S(1)}, u32[]{:S(2)}) copy-start(bf16[1024,256]{1,0:T(8,128)(2,1)S(1)} %collective-permute-done.31.refs_1_) | copy-start | bytes 1572868
  175.6 16.2 %collective-permute-start.33 = (bf16[1024,256]{1,0:T(8,128)(2,1)S(1)}, bf16[1024,256]{1,0:T(8,128)(2,1)S(1)}, u32[]{:S(2)}, u32[]{:S(2)}) collective-permute-start(bf16[1024,256]{1,0:T(8,128)(2,1)S(1)} %collective-permute-done.32.refs_2_), channel_id=1, source_target_pairs={{2,3},{1,0},{6,7},{5,4},{10,11},{9,8},{14,15},{13,12},{18,19},{17,... | collective-permute-start | bytes 1572872 | tf_op jit(solution)/shard_map/ppermute | solution.py:332
  176.9 14.9 %collective-permute-start.34 = (bf16[1024,256]{1,0:T(8,128)(2,1)S(1)}, bf16[1024,256]{1,0:T(8,128)(2,1)S(1)}, u32[]{:S(2)}, u32[]{:S(2)}) collective-permute-start(bf16[1024,256]{1,0:T(8,128)(2,1)S(1)} %collective-permute-done.31.refs_1_), channel_id=1, source_target_pairs={{1,2},{2,1},{5,6},{6,5},{9,10},{10,9},{13,14},{14,13},{17,18},{18,... | collective-permute-start | bytes 1572872 | tf_op jit(solution)/shard_map/ppermute | solution.py:332
  177.8 15.2 %collective-permute-start.39 = (bf16[2,128,1024]{2,1,0:T(8,128)(2,1)S(1)}, bf16[2,128,1024]{2,1,0:T(8,128)(2,1)S(1)}, u32[]{:S(2)}, u32[]{:S(2)}) collective-permute-start(bf16[2,128,1024]{2,1,0:T(8,128)(2,1)S(1)} %get-tuple-element.157), channel_id=1, source_target_pairs={{0,16},{4,20},{8,24},{12,28},{16,0},{20,4},{24,8},{28,12},{1,17},{... | collective-permute-start | bytes 1572872 | tf_op jit(solution)/shard_map/ppermute | solution.py:321
  178.4 14.7 %collective-permute-start.37 = (bf16[2,128,1024]{2,1,0:T(8,128)(2,1)S(1)}, bf16[2,128,1024]{2,1,0:T(8,128)(2,1)S(1)}, u32[]{:S(2)}, u32[]{:S(2)}) collective-permute-start(bf16[2,128,1024]{2,1,0:T(8,128)(2,1)S(1)} %get-tuple-element.158), channel_id=1, source_target_pairs={{0,8},{4,12},{8,0},{12,4},{16,24},{20,28},{24,16},{28,20},{1,9},{5... | collective-permute-start | bytes 1572872 | tf_op jit(solution)/shard_map/ppermute | solution.py:321
  191.8 16.4 %collective-permute-start.36 = (bf16[1024,256]{1,0:T(8,128)(2,1)S(1)}, bf16[1024,256]{1,0:T(8,128)(2,1)S(1)}, u32[]{:S(2)}, u32[]{:S(2)}) collective-permute-start(bf16[1024,256]{1,0:T(8,128)(2,1)S(1)} %collective-permute-done.34.refs_4_), channel_id=1, source_target_pairs={{2,3},{1,0},{6,7},{5,4},{10,11},{9,8},{14,15},{13,12},{18,19},{17,... | collective-permute-start | bytes 1572872 | tf_op jit(solution)/shard_map/ppermute | solution.py:332
  193.3 11.7 %collective-permute-start.40 = (bf16[128,1024]{1,0:T(8,128)(2,1)S(1)}, bf16[128,1024]{1,0:T(8,128)(2,1)S(1)}, u32[]{:S(2)}, u32[]{:S(2)}) collective-permute-start(bf16[128,1024]{1,0:T(8,128)(2,1)S(1)} %get-tuple-element.155), channel_id=1, source_target_pairs={{0,8},{4,12},{8,0},{12,4},{16,24},{20,28},{24,16},{28,20},{1,9},{5... | collective-permute-start | bytes 786440 | tf_op jit(solution)/shard_map/ppermute | solution.py:321
  194.1 14.1 %copy-start = (bf16[512,1024]{1,0:T(8,128)(2,1)S(1)}, bf16[512,1024]{1,0:T(8,128)(2,1)}, u32[]{:S(2)}) copy-start(bf16[512,1024]{1,0:T(8,128)(2,1)} %shard_map.94.a_ref.refs_6_.refs_5_.own_ref) | copy-start | bytes 3145732
  194.1 14.1 %copy-start.2 = (bf16[512,1024]{1,0:T(8,128)(2,1)S(1)}, bf16[512,1024]{1,0:T(8,128)(2,1)}, u32[]{:S(2)}) copy-start(bf16[512,1024]{1,0:T(8,128)(2,1)} %copy-done.1) | copy-start | bytes 3145732
  194.1 14.1 %copy-start.4 = (bf16[256,1024]{1,0:T(8,128)(2,1)S(1)}, bf16[256,1024]{1,0:T(8,128)(2,1)}, u32[]{:S(2)}) copy-start(bf16[256,1024]{1,0:T(8,128)(2,1)} %copy-done.3) | copy-start | bytes 1572868
  194.1 11.0 %collective-permute-start.38 = (bf16[128,1024]{1,0:T(8,128)(2,1)S(1)}, bf16[128,1024]{1,0:T(8,128)(2,1)S(1)}, u32[]{:S(2)}, u32[]{:S(2)}) collective-permute-start(bf16[128,1024]{1,0:T(8,128)(2,1)S(1)} %get-tuple-element.156), channel_id=1, source_target_pairs={{0,16},{4,20},{8,24},{12,28},{16,0},{20,4},{24,8},{28,12},{1,17},{... | collective-permute-start | bytes 786440 | tf_op jit(solution)/shard_map/ppermute | solution.py:321
  213.2 2.9 %collective-permute-start.41 = (bf16[512,1024]{1,0:T(8,128)(2,1)}, bf16[512,1024]{1,0:T(8,128)(2,1)S(1)}, u32[]{:S(2)}, u32[]{:S(2)}) collective-permute-start(bf16[512,1024]{1,0:T(8,128)(2,1)} %get-tuple-element.122), channel_id=1, source_target_pairs={{0,4},{4,0},{8,12},{12,8},{16,20},{20,16},{24,28},{28,24},{1,5},{5... | collective-permute-start | bytes 3145736 | tf_op jit(solution)/shard_map/ppermute | solution.py:316
  213.3 19.1 %collective-permute-start.47 = (bf16[2,128,1024]{2,1,0:T(8,128)(2,1)S(1)}, bf16[2,128,1024]{2,1,0:T(8,128)(2,1)S(1)}, u32[]{:S(2)}, u32[]{:S(2)}) collective-permute-start(bf16[2,128,1024]{2,1,0:T(8,128)(2,1)S(1)} %get-tuple-element.153), channel_id=1, source_target_pairs={{0,16},{4,20},{8,24},{12,28},{16,0},{20,4},{24,8},{28,12},{1,17},{... | collective-permute-start | bytes 1572872 | tf_op jit(solution)/shard_map/ppermute | solution.py:321
  213.9 18.5 %collective-permute-start.46 = (bf16[2,128,1024]{2,1,0:T(8,128)(2,1)S(1)}, bf16[2,128,1024]{2,1,0:T(8,128)(2,1)S(1)}, u32[]{:S(2)}, u32[]{:S(2)}) collective-permute-start(bf16[2,128,1024]{2,1,0:T(8,128)(2,1)S(1)} %get-tuple-element.154), channel_id=1, source_target_pairs={{0,8},{4,12},{8,0},{12,4},{16,24},{20,28},{24,16},{28,20},{1,9},{5... | collective-permute-start | bytes 1572872 | tf_op jit(solution)/shard_map/ppermute | solution.py:321
  218.2 1.8 collective-permute-start.42
  220.2 12.2 %collective-permute-start.45 = (bf16[4,128,128]{2,1,0:T(8,128)(2,1)S(1)}, bf16[4,128,128]{2,1,0:T(8,128)(2,1)S(1)}, u32[]{:S(2)}, u32[]{:S(2)}) collective-permute-start(bf16[4,128,128]{2,1,0:T(8,128)(2,1)S(1)} %fusion.14), channel_id=1, source_target_pairs={{0,24},{4,28},{8,16},{12,20},{16,8},{20,12},{24,0},{28,4},{1,25},{... | collective-permute-start | bytes 393224 | tf_op jit(solution)/shard_map/ppermute | solution.py:321
  221.0 12.2 %collective-permute-start.44 = (bf16[4,128,128]{2,1,0:T(8,128)(2,1)S(1)}, bf16[4,128,128]{2,1,0:T(8,128)(2,1)S(1)}, u32[]{:S(2)}, u32[]{:S(2)}) collective-permute-start(bf16[4,128,128]{2,1,0:T(8,128)(2,1)S(1)} %fusion.14), channel_id=1, source_target_pairs={{0,16},{4,20},{8,24},{12,28},{16,0},{20,4},{24,8},{28,12},{1,17},{... | collective-permute-start | bytes 393224 | tf_op jit(solution)/shard_map/ppermute | solution.py:321
  222.2 11.3 %collective-permute-start.43 = (bf16[4,128,128]{2,1,0:T(8,128)(2,1)S(1)}, bf16[4,128,128]{2,1,0:T(8,128)(2,1)S(1)}, u32[]{:S(2)}, u32[]{:S(2)}) collective-permute-start(bf16[4,128,128]{2,1,0:T(8,128)(2,1)S(1)} %fusion.14), channel_id=1, source_target_pairs={{0,8},{4,12},{8,0},{12,4},{16,24},{20,28},{24,16},{28,20},{1,9},{5... | collective-permute-start | bytes 393224 | tf_op jit(solution)/shard_map/ppermute | solution.py:321
  233.6 2.4 collective-permute-start.50
  233.9 8.8 %collective-permute-start.49 = (bf16[128,1024]{1,0:T(8,128)(2,1)S(1)}, bf16[128,1024]{1,0:T(8,128)(2,1)S(1)}, u32[]{:S(2)}, u32[]{:S(2)}) collective-permute-start(bf16[128,1024]{1,0:T(8,128)(2,1)S(1)} %get-tuple-element.151), channel_id=1, source_target_pairs={{0,8},{4,12},{8,0},{12,4},{16,24},{20,28},{24,16},{28,20},{1,9},{5... | collective-permute-start | bytes 786440 | tf_op jit(solution)/shard_map/ppermute | solution.py:321
  234.5 8.4 %collective-permute-start.48 = (bf16[128,1024]{1,0:T(8,128)(2,1)S(1)}, bf16[128,1024]{1,0:T(8,128)(2,1)S(1)}, u32[]{:S(2)}, u32[]{:S(2)}) collective-permute-start(bf16[128,1024]{1,0:T(8,128)(2,1)S(1)} %get-tuple-element.152), channel_id=1, source_target_pairs={{0,16},{4,20},{8,24},{12,28},{16,0},{20,4},{24,8},{28,12},{1,17},{... | collective-permute-start | bytes 786440 | tf_op jit(solution)/shard_map/ppermute | solution.py:321
  (24 other events, 96.8 us)
